TPU v7x, 32 devices: a whole 2x2x4 slice. The times are simulated.
32 devices in a mesh: rep: 4 (over y, core), fsdp: 8 (over z, x).
Axes of the slice: x: 2, y: 2, z: 4, core: 2. Of those that a mesh axis runs over, the one named last changes fastest.
Arguments:
- tokens: bfloat16 [1536, 64, 512], P(('rep', 'fsdp')), may hold values from -6 to 6
- counts: int32 [4, 8], P('rep', 'fsdp'), may hold values from 1 to 48, 240 in all within a row
- attn_gain: float32 [512], P('fsdp'), may hold values from 0.5 to 1.5
- w_query: float32 [512, 384], P('fsdp'), may hold values from -0.125 to 0.125
- w_key: float32 [512, 384], P('fsdp'), may hold values from -0.125 to 0.125
- w_value: float32 [512, 384], P('fsdp'), may hold values from -0.25 to 0.25
- attention_output_weight: float32 [384, 512], P('fsdp'), may hold values from -0.875 to 0.875
- rel_bias: float32 [192], P('fsdp'), may hold values from -4 to 4
- ffn_gain: float32 [512], P('fsdp'), may hold values from 0.5 to 1.5
- gate_weight: float32 [512, 1024], P('fsdp'), may hold values from -0.25 to 0.25
- up_weight: float32 [512, 1024], P('fsdp'), may hold values from -0.25 to 0.25
- down_weight: float32 [1024, 512], P('fsdp'), may hold values from -0.25 to 0.25
- cotangent: bfloat16 [1536, 64, 512], P(('rep', 'fsdp')), may hold values from -6 to 6
Outputs:
- layer_out: bfloat16 [1536, 64, 512], P(('rep', 'fsdp'))
- grad_tokens: bfloat16 [1536, 64, 512], P(('rep', 'fsdp'))
- grad_attn_gain: float32 [512], P('fsdp')
- grad_query: float32 [512, 384], P('fsdp')
- grad_key: float32 [512, 384], P('fsdp')
- grad_value: float32 [512, 384], P('fsdp')
- grad_out: float32 [384, 512], P('fsdp')
- grad_bias: float32 [192], P('fsdp')
- grad_ffn_gain: float32 [512], P('fsdp')
- grad_gate: float32 [512, 1024], P('fsdp')
- grad_up: float32 [512, 1024], P('fsdp')
- grad_down: float32 [1024, 512], P('fsdp')
Inputs may be any that keep to these rules, and one draw needn't show every extreme that they name: Each row of counts (one index of rep) sums to 240, and each row holds an entry equal to 48.
All inputs are finite; a program needn't handle non-finite values. No bound on the sum of `counts` on one device may be relied on, other than what follows from the above.
Results may differ from a plain program's by a relative error of at most 0.02.
Values may be sent and summed in bfloat16 or wider, within the bound.
No kernel may reach another device: no remote copies, remote signals or barrier semaphores. Data moves between devices by JAX's collectives and lax.ppermute only.
A program may use at most 192 MiB of HBM per device.

v0:
```python
import jax
import jax.numpy as jnp
import numpy as np
from jax import lax
from jax.sharding import PartitionSpec as P

HEADS = 6
HDIM = 64
BUCKETS = 32


epsilon = 1e-06
PRECISION_TOP = lax.Precision.HIGHEST


def distance_bucket(distance, half_count, exact_count):
    if distance < exact_count:
        return distance
    reached = 0
    for higher in range(1, half_count - exact_count):
        if distance ** (
            half_count - exact_count
        ) * exact_count**higher >= 128**higher * exact_count ** (half_count - exact_count):
            reached = higher
    return exact_count + reached


def bucket_onehot(length, buckets):
    half_count = buckets // 2
    exact_count = half_count // 2
    bucket_ids = np.array(
        [
            [
                (half_count if column > row_index else 0)
                + distance_bucket(abs(column - row_index), half_count, exact_count)
                for column in range(length)
            ]
            for row_index in range(length)
        ],
        dtype=np.int32,
    ).reshape(-1)
    return (bucket_ids[:, None] == np.arange(buckets)[None, :]).astype(np.float32)


def rms_scale(values):
    return lax.rsqrt(jnp.mean(values * values, axis=-1, keepdims=True) + epsilon)


def norm_piece(values, gain_in):
    return values * rms_scale(values) * gain_in


def gated_piece(gate_in, up_in):
    return jax.nn.gelu(gate_in, approximate=True) * up_in


def product_of(left, right):
    return jnp.dot(left, right, preferred_element_type=jnp.float32)


def contract_rows(left, right):
    return lax.dot_general(
        left, right, (((0,), (0,)), ((), ())), preferred_element_type=jnp.float32
    )


def times_transposed(left, right):
    return lax.dot_general(
        left, right, (((1,), (1,)), ((), ())), preferred_element_type=jnp.float32
    )


def scores_of(queries, keys_all, bias_values, onehot, length):
    table_bias = jnp.dot(
        onehot.astype(jnp.bfloat16),
        bias_values.reshape(BUCKETS, HEADS),
        preferred_element_type=jnp.float32,
    )
    head_bias = jnp.transpose(table_bias.reshape(length, length, HEADS), (2, 0, 1))
    return (
        jnp.einsum("sihe,sjhe->shij", queries, keys_all, preferred_element_type=jnp.float32)
        + head_bias[None]
    )


def body(
    tokens,
    counts,
    attn_gain,
    w_query,
    w_key,
    w_value,
    attention_output_weight,
    rel_bias,
    ffn_gain,
    gate_weight,
    up_weight,
    down_weight,
    cotangent,
):
    forward_set = (
        lax.all_gather(attn_gain.astype(jnp.bfloat16), "fsdp", axis=0, tiled=True),
        lax.all_gather(w_query.astype(jnp.bfloat16), "fsdp", axis=0, tiled=True),
        lax.all_gather(w_key.astype(jnp.bfloat16), "fsdp", axis=0, tiled=True),
        lax.all_gather(w_value.astype(jnp.bfloat16), "fsdp", axis=0, tiled=True),
        lax.all_gather(attention_output_weight.astype(jnp.bfloat16), "fsdp", axis=0, tiled=True),
        lax.all_gather(rel_bias.astype(jnp.bfloat16), "fsdp", axis=0, tiled=True),
        lax.all_gather(ffn_gain.astype(jnp.bfloat16), "fsdp", axis=0, tiled=True),
        lax.all_gather(gate_weight.astype(jnp.bfloat16), "fsdp", axis=0, tiled=True),
        lax.all_gather(up_weight.astype(jnp.bfloat16), "fsdp", axis=0, tiled=True),
        lax.all_gather(down_weight.astype(jnp.bfloat16), "fsdp", axis=0, tiled=True),
    )
    gain_one, query_w, key_w, value_w, out_w, bias_w, gain_two, gate_w, up_w, down_w = forward_set
    series_count, length, model_width = tokens.shape
    inner_width = HEADS * HDIM
    row_count = series_count * length
    slot_ids = jnp.arange(series_count, dtype=jnp.int32)
    live_slots = (slot_ids < counts[0, 0]).astype(jnp.float32)
    live_rows = jnp.repeat(live_slots, length)[:, None]
    onehot = jnp.asarray(bucket_onehot(length, BUCKETS))
    flat_in = tokens.reshape(row_count, model_width).astype(jnp.float32)
    normed_first = norm_piece(flat_in, gain_one.astype(jnp.float32)).astype(jnp.bfloat16)
    queries = (
        product_of(normed_first, query_w)
        .astype(jnp.bfloat16)
        .reshape(series_count, length, HEADS, HDIM)
    )
    keys_all = (
        product_of(normed_first, key_w)
        .astype(jnp.bfloat16)
        .reshape(series_count, length, HEADS, HDIM)
    )
    values_all = (
        product_of(normed_first, value_w)
        .astype(jnp.bfloat16)
        .reshape(series_count, length, HEADS, HDIM)
    )
    scores = scores_of(queries, keys_all, bias_w, onehot, length)
    row_peak = jnp.max(scores, axis=-1, keepdims=True)
    exponent = jnp.exp(scores - row_peak)
    row_total = jnp.sum(exponent, axis=-1, keepdims=True)
    log_total = row_peak + jnp.log(row_total)
    probs_low = (exponent / row_total).astype(jnp.bfloat16)
    merged_head_rows = (
        jnp.einsum("shij,sjhe->sihe", probs_low, values_all, preferred_element_type=jnp.float32)
        .astype(jnp.bfloat16)
        .reshape(row_count, inner_width)
    )
    hidden_state = flat_in + product_of(merged_head_rows, out_w)
    normed_second = norm_piece(hidden_state, gain_two.astype(jnp.float32)).astype(jnp.bfloat16)
    gate_before_activation = product_of(normed_second, gate_w)
    up_projected = product_of(normed_second, up_w)
    activated_rows = gated_piece(gate_before_activation, up_projected).astype(jnp.bfloat16)
    result = (hidden_state + product_of(activated_rows, down_w)) * live_rows
    layer_out = result.reshape(tokens.shape).astype(jnp.bfloat16)
    back_set = (
        lax.all_gather(attn_gain.astype(jnp.bfloat16), "fsdp", axis=0, tiled=True),
        lax.all_gather(w_query.astype(jnp.bfloat16), "fsdp", axis=0, tiled=True),
        lax.all_gather(w_key.astype(jnp.bfloat16), "fsdp", axis=0, tiled=True),
        lax.all_gather(w_value.astype(jnp.bfloat16), "fsdp", axis=0, tiled=True),
        lax.all_gather(attention_output_weight.astype(jnp.bfloat16), "fsdp", axis=0, tiled=True),
        lax.all_gather(rel_bias.astype(jnp.bfloat16), "fsdp", axis=0, tiled=True),
        lax.all_gather(ffn_gain.astype(jnp.bfloat16), "fsdp", axis=0, tiled=True),
        lax.all_gather(gate_weight.astype(jnp.bfloat16), "fsdp", axis=0, tiled=True),
        lax.all_gather(up_weight.astype(jnp.bfloat16), "fsdp", axis=0, tiled=True),
        lax.all_gather(down_weight.astype(jnp.bfloat16), "fsdp", axis=0, tiled=True),
    )
    (
        gain_one_back,
        query_back,
        key_back,
        value_back,
        out_back,
        bias_back,
        gain_two_back,
        gate_back,
        up_back,
        down_back,
    ) = back_set
    grad_y = cotangent.reshape(row_count, model_width).astype(jnp.float32) * live_rows
    grad_branch = grad_y.astype(jnp.bfloat16)
    grad_down = contract_rows(activated_rows, grad_branch)
    grad_activ = times_transposed(grad_branch, down_back)
    unused, gated_pull = jax.vjp(gated_piece, gate_before_activation, up_projected)
    grad_gate_in, grad_up_in = gated_pull(grad_activ)
    grad_gate_low = grad_gate_in.astype(jnp.bfloat16)
    grad_up_low = grad_up_in.astype(jnp.bfloat16)
    grad_gate = contract_rows(normed_second, grad_gate_low)
    grad_upw = contract_rows(normed_second, grad_up_low)
    grad_normed_two = times_transposed(grad_gate_low, gate_back) + times_transposed(
        grad_up_low, up_back
    )
    unused, norm_pull_two = jax.vjp(norm_piece, hidden_state, gain_two_back.astype(jnp.float32))
    grad_from_norm, grad_gain_two = norm_pull_two(grad_normed_two)
    grad_hidden = grad_y + grad_from_norm
    grad_attn = grad_hidden.astype(jnp.bfloat16)
    grad_outw = contract_rows(merged_head_rows, grad_attn)
    grad_mixed = (
        times_transposed(grad_attn, out_back)
        .astype(jnp.bfloat16)
        .reshape(series_count, length, HEADS, HDIM)
    )
    scores_again = scores_of(queries, keys_all, bias_back, onehot, length)
    probs_again = jnp.exp(scores_again - log_total)
    grad_probs = jnp.einsum(
        "sihe,sjhe->shij", grad_mixed, values_all, preferred_element_type=jnp.float32
    )
    grad_scores = probs_again * (
        grad_probs - jnp.sum(probs_again * grad_probs, axis=-1, keepdims=True)
    )
    grad_values_in = (
        jnp.einsum(
            "shij,sihe->sjhe",
            probs_again.astype(jnp.bfloat16),
            grad_mixed,
            preferred_element_type=jnp.float32,
        )
        .astype(jnp.bfloat16)
        .reshape(row_count, inner_width)
    )
    head_sums = jnp.sum(grad_scores, axis=0).reshape(HEADS, length * length)
    grad_biasw = lax.dot_general(
        onehot, head_sums, (((0,), (1,)), ((), ())), precision=PRECISION_TOP
    ).reshape(-1)
    scores_low = grad_scores.astype(jnp.bfloat16)
    grad_queries_in = (
        jnp.einsum("shij,sjhe->sihe", scores_low, keys_all, preferred_element_type=jnp.float32)
        .astype(jnp.bfloat16)
        .reshape(row_count, inner_width)
    )
    grad_keys_in = (
        jnp.einsum("shij,sihe->sjhe", scores_low, queries, preferred_element_type=jnp.float32)
        .astype(jnp.bfloat16)
        .reshape(row_count, inner_width)
    )
    grad_queryw = contract_rows(normed_first, grad_queries_in)
    grad_keyw = contract_rows(normed_first, grad_keys_in)
    grad_valuew = contract_rows(normed_first, grad_values_in)
    grad_normed = (
        times_transposed(grad_queries_in, query_back)
        + times_transposed(grad_keys_in, key_back)
        + times_transposed(grad_values_in, value_back)
    )
    unused, norm_pull_one = jax.vjp(norm_piece, flat_in, gain_one_back.astype(jnp.float32))
    grad_from_first, grad_gain_one = norm_pull_one(grad_normed)
    grad_tokens = (grad_hidden + grad_from_first).reshape(tokens.shape).astype(jnp.bfloat16)
    shards = (
        lax.psum_scatter(
            grad_gain_one.astype(jnp.bfloat16), "fsdp", scatter_dimension=0, tiled=True
        ).astype(jnp.float32),
        lax.psum_scatter(
            grad_queryw.astype(jnp.bfloat16), "fsdp", scatter_dimension=0, tiled=True
        ).astype(jnp.float32),
        lax.psum_scatter(
            grad_keyw.astype(jnp.bfloat16), "fsdp", scatter_dimension=0, tiled=True
        ).astype(jnp.float32),
        lax.psum_scatter(
            grad_valuew.astype(jnp.bfloat16), "fsdp", scatter_dimension=0, tiled=True
        ).astype(jnp.float32),
        lax.psum_scatter(
            grad_outw.astype(jnp.bfloat16), "fsdp", scatter_dimension=0, tiled=True
        ).astype(jnp.float32),
        lax.psum_scatter(
            grad_biasw.astype(jnp.bfloat16), "fsdp", scatter_dimension=0, tiled=True
        ).astype(jnp.float32),
        lax.psum_scatter(
            grad_gain_two.astype(jnp.bfloat16), "fsdp", scatter_dimension=0, tiled=True
        ).astype(jnp.float32),
        lax.psum_scatter(
            grad_gate.astype(jnp.bfloat16), "fsdp", scatter_dimension=0, tiled=True
        ).astype(jnp.float32),
        lax.psum_scatter(
            grad_upw.astype(jnp.bfloat16), "fsdp", scatter_dimension=0, tiled=True
        ).astype(jnp.float32),
        lax.psum_scatter(
            grad_down.astype(jnp.bfloat16), "fsdp", scatter_dimension=0, tiled=True
        ).astype(jnp.float32),
    )
    summed = tuple(
        (
            lax.psum(shards[0].astype(jnp.bfloat16), "rep").astype(jnp.float32),
            lax.psum(shards[1].astype(jnp.bfloat16), "rep").astype(jnp.float32),
            lax.psum(shards[2].astype(jnp.bfloat16), "rep").astype(jnp.float32),
            lax.psum(shards[3].astype(jnp.bfloat16), "rep").astype(jnp.float32),
            lax.psum(shards[4].astype(jnp.bfloat16), "rep").astype(jnp.float32),
            lax.psum(shards[5].astype(jnp.bfloat16), "rep").astype(jnp.float32),
            lax.psum(shards[6].astype(jnp.bfloat16), "rep").astype(jnp.float32),
            lax.psum(shards[7].astype(jnp.bfloat16), "rep").astype(jnp.float32),
            lax.psum(shards[8].astype(jnp.bfloat16), "rep").astype(jnp.float32),
            lax.psum(shards[9].astype(jnp.bfloat16), "rep").astype(jnp.float32),
        )
    )
    return (layer_out, grad_tokens) + summed


def solution(mesh):
    in_specs = (
        P(("rep", "fsdp"), None, None),
        P("rep", "fsdp"),
        P("fsdp"),
        P("fsdp", None),
        P("fsdp", None),
        P("fsdp", None),
        P("fsdp", None),
        P("fsdp"),
        P("fsdp"),
        P("fsdp", None),
        P("fsdp", None),
        P("fsdp", None),
        P(("rep", "fsdp"), None, None),
    )
    out_specs = (
        P(("rep", "fsdp"), None, None),
        P(("rep", "fsdp"), None, None),
        P("fsdp"),
        P("fsdp", None),
        P("fsdp", None),
        P("fsdp", None),
        P("fsdp", None),
        P("fsdp"),
        P("fsdp"),
        P("fsdp", None),
        P("fsdp", None),
        P("fsdp", None),
    )
    return jax.shard_map(body, mesh=mesh, in_specs=in_specs, out_specs=out_specs, check_vma=False)
```

profile of v0, /device:TPU:0, one launch (start us, length us, event | category | flops | bytes accessed | tf_op | source)
XLA Modules:
  0.0 952.9 jit_solution(16890557091442584892)
XLA Ops:
  17.7 23.8 %all-reduce.7 = (bf16[512]{0:T(512)(128)(2,1)S(1)}, bf16[192]{0:T(256)(128)(2,1)S(1)}, bf16[512]{0:T(512)(128)(2,1)}) all-reduce(bf16[512]{0:T(512)(128)(2,1)S(1)} %dynamic-update-slice, bf16[192]{0:T(256)(128)(2,1)S(1)} %dynamic-update-slice.1, bf16[512]{0:T(512)(128)(2,1)S(1)} %dynamic-update-slice.2), channel_id=1, replica_groups=mesh['rep'=4,'fsdp'=8] {'fsdp'}, use_global_device_ids=true, to_apply=%add | all-reduce | flops 1216 | bytes 4864
  45.7 31.3 %all_gather.43 = bf16[512,384]{1,0:T(8,128)(2,1)S(1)} all-gather(bf16[64,384]{1,0:T(8,128)(2,1)S(1)} %convert_element_type.254), channel_id=1, replica_groups=mesh['rep'=4,'fsdp'=8] {'fsdp'}, dimensions={0}, use_global_device_ids=true | all-gather | bytes 442368 | tf_op jit(solution)/shard_map/all_gather | solution.py:104
  91.4 8.3 copy.122
  99.7 31.6 %all_gather.42 = bf16[512,384]{1,0:T(8,128)(2,1)S(1)} all-gather(bf16[64,384]{1,0:T(8,128)(2,1)S(1)} %convert_element_type.252), channel_id=1, replica_groups=mesh['rep'=4,'fsdp'=8] {'fsdp'}, dimensions={0}, use_global_device_ids=true | all-gather | bytes 442368 | tf_op jit(solution)/shard_map/all_gather | solution.py:103
  145.3 8.3 copy.125
  156.8 31.0 %all_gather.41 = bf16[512,384]{1,0:T(8,128)(2,1)S(1)} all-gather(bf16[64,384]{1,0:T(8,128)(2,1)S(1)} %convert_element_type.250), channel_id=1, replica_groups=mesh['rep'=4,'fsdp'=8] {'fsdp'}, dimensions={0}, use_global_device_ids=true | all-gather | bytes 442368 | tf_op jit(solution)/shard_map/all_gather | solution.py:105
  193.6 8.4 reshape.192
  214.8 10.5 %convert_bitcast_fusion.3 = bf16[48,64,6,64]{1,3,2,0:T(8,128)(2,1)} fusion(f32[48,6,64,64]{2,3,1,0:T(8,128)} %copy-done, f32[48,6,64]{2,1,0:T(8,128)} %fusion.7, f32[48,6,64]{2,1,0:T(8,128)S(1)} %get-tuple-element.41, f32[6,64,64]{1,2,0:T(8,128)S(1)} %copy.115, bf16[48,64,6,64]{3,2,1,0:T(8,128)(2,1)} %reshape.192), kind=kOutput, calls=%fused_computation.52 | convolution fusion | flops 156893184 | bytes 9682944 | tf_op jit(solution)/shard_map/shij,sjhe->sihe/dot_general | solution.py:145
  232.8 16.8 %reshape.165 = bf16[3072,384]{0,1:T(8,128)(2,1)} reshape(bf16[48,64,6,64]{1,0,3,2:T(8,128)(2,1)} %copy.118) | data formatting | bytes 4718592 | tf_op jit(solution)/shard_map/reshape | solution.py:147
  249.6 31.0 %all_gather.45 = bf16[384,512]{1,0:T(8,128)(2,1)S(1)} all-gather(bf16[48,512]{1,0:T(8,128)(2,1)S(1)} %convert_element_type.261), channel_id=1, replica_groups=mesh['rep'=4,'fsdp'=8] {'fsdp'}, dimensions={0}, use_global_device_ids=true | all-gather | bytes 442368 | tf_op jit(solution)/shard_map/all_gather | solution.py:106
  297.4 10.1 %fusion.48 = f32[3072,1024]{1,0:T(8,128)} fusion(bf16[3072,512]{1,0:T(8,128)(2,1)} %multiply_convert_fusion.3, bf16[512,1024]{1,0:T(8,128)(2,1)} %all-gather.4.cloned.1.call-done), kind=kOutput, calls=%fused_computation.89 | convolution fusion | flops 3221225472 | bytes 16777216 | tf_op jit(solution)/shard_map/dot_general | solution.py:58
  307.5 10.3 %fusion.49 = f32[3072,1024]{1,0:T(8,128)} fusion(bf16[3072,512]{1,0:T(8,128)(2,1)} %multiply_convert_fusion.3, bf16[512,1024]{1,0:T(8,128)(2,1)} %all-gather.6.cloned.1.call-done), kind=kOutput, calls=%fused_computation.90 | convolution fusion | flops 3221225472 | bytes 16777216 | tf_op jit(solution)/shard_map/dot_general | solution.py:58
  317.8 18.3 %multiply_convert_fusion = (bf16[3072,1024]{1,0:T(8,128)(2,1)S(1)}, bf16[3072,1024]{1,0:T(8,128)(2,1)}, bf16[3072,1024]{1,0:T(8,128)(2,1)}) fusion(f32[3072,1024]{1,0:T(8,128)} %fusion.48, f32[3072,1024]{1,0:T(8,128)} %fusion.49, bf16[3072,512]{1,0:T(8,128)(2,1)S(1)} %copy-done.15, bf16[1024,512]{1,0:T(8,128)(2,1)} %all-gather.8.cloned.1.call-done), kind=kOutput, calls=%fused_computation.9 | convolution fusion | flops 3303014400 | bytes 48234496 | tf_op jit(solution)/shard_map/dot_general | solution.py:68
  336.1 8.5 fusion.50
  344.7 8.6 multiply_reduce_fusion.1
  368.0 8.3 copy.128
  376.3 13.5 %multiply_reduce_fusion = (f32[48,6,64]{2,1,0:T(8,128)S(1)}, f32[48,6,64,64]{2,3,1,0:T(8,128)}) fusion(f32[48,6,64,64]{2,3,1,0:T(8,128)} %copy-done, f32[48,6,64]{2,1,0:T(8,128)S(1)} %log_add_fusion, f32[6,64,64]{1,2,0:T(8,128)S(1)} %copy.115, bf16[48,64,6,64]{1,3,2,0:T(8,128)(2,1)} %copy.128, bf16[48,64,6,64]{3,2,1,0:T(8,128)(2,1)} %reshape.192), kind=kOutput, calls=%fused_computation.15 | convolution fusion | flops 155695104 | bytes 14401536 | tf_op jit(solution)/shard_map/sihe,sjhe->shij/dot_general | solution.py:205
  389.9 8.6 fusion.46
  449.4 9.9 %convert_bitcast_fusion = bf16[48,64,6,64]{1,3,2,0:T(8,128)(2,1)} fusion(bf16[48,64,6,64]{1,3,2,0:T(8,128)(2,1)} %copy.128, f32[48,6,64,64]{2,3,1,0:T(8,128)} %copy-done, f32[48,6,64]{2,1,0:T(8,128)S(1)} %log_add_fusion, f32[6,64,64]{1,2,0:T(8,128)S(1)} %copy.115), kind=kOutput, calls=%fused_computation.48 | convolution fusion | flops 155713536 | bytes 9609216 | tf_op jit(solution)/shard_map/shij,sihe->sjhe/dot_general | solution.py:212
  478.0 8.2 convolution_convert_fusion.6
  486.4 8.2 convolution_convert_fusion.5
  497.5 8.3 convolution_convert_fusion.4
  516.3 17.5 %all-reduce.6 = (bf16[512]{0:T(512)(128)(2,1)S(1)}, bf16[192]{0:T(256)(128)(2,1)S(1)}, bf16[512]{0:T(512)(128)(2,1)S(1)}) all-reduce(bf16[512]{0:T(512)(128)(2,1)S(1)} %get-tuple-element.14, bf16[192]{0:T(256)(128)(2,1)S(1)} %copy-done.43, bf16[512]{0:T(512)(128)(2,1)S(1)} %copy-done.42), channel_id=2, replica_groups=mesh['rep'=4,'fsdp'=8] {'fsdp'}, use_global_device_ids=true, to_apply=%region_8.0.clone | all-reduce | flops 1216 | bytes 4864
  535.6 9.2 reduce-scatter.14.cloned.1.call-done
  544.8 63.5 %reduce-scatter.8.cloned.1.call-done = bf16[64,384]{1,0:T(8,128)(2,1)} async-done(((bf16[512,384]{1,0:T(8,128)(2,1)}), bf16[64,384]{1,0:T(8,128)(2,1)}) %reduce-scatter.8.cloned.1.call-update) | async-done | bytes 49168 | tf_op jit(solution)/shard_map/reduce_scatter | solution.py:251
  608.3 63.7 %reduce-scatter.12.cloned.1.call-done = bf16[64,384]{1,0:T(8,128)(2,1)} async-done(((bf16[512,384]{1,0:T(8,128)(2,1)}), bf16[64,384]{1,0:T(8,128)(2,1)}) %reduce-scatter.12.cloned.1.call-update) | async-done | bytes 49168 | tf_op jit(solution)/shard_map/reduce_scatter | solution.py:257
  679.0 58.9 %reduce-scatter.16.cloned.1.call-done = bf16[64,1024]{1,0:T(8,128)(2,1)} async-done(((bf16[512,1024]{1,0:T(8,128)(2,1)}), bf16[64,1024]{1,0:T(8,128)(2,1)}) %reduce-scatter.16.cloned.1.call-update) | async-done | bytes 131088 | tf_op jit(solution)/shard_map/reduce_scatter | solution.py:269
  737.9 66.2 %reduce-scatter.18.cloned.1.call-done = bf16[64,1024]{1,0:T(8,128)(2,1)} async-done(((bf16[512,1024]{1,0:T(8,128)(2,1)}), bf16[64,1024]{1,0:T(8,128)(2,1)}) %reduce-scatter.18.cloned.1.call-update) | async-done | bytes 131088 | tf_op jit(solution)/shard_map/reduce_scatter | solution.py:272
  804.1 65.8 %reduce-scatter.20.cloned.1.call-done = bf16[128,512]{1,0:T(8,128)(2,1)} async-done(((bf16[1024,512]{1,0:T(8,128)(2,1)}), bf16[128,512]{1,0:T(8,128)(2,1)}) %reduce-scatter.20.cloned.1.call-update) | async-done | bytes 131088 | tf_op jit(solution)/shard_map/reduce_scatter | solution.py:275
  870.0 10.0 %multiply_convert_fusion.2 = bf16[3072,512]{1,0:T(8,128)(2,1)} fusion(f32[3072,512]{1,0:T(8,128)} %get-tuple-element.44, bf16[3072,1024]{1,0:T(8,128)(2,1)} %get-tuple-element.36, bf16[1024,512]{1,0:T(8,128)(2,1)} %all-gather.8.cloned.1.call-done, f32[3072]{0:T(1024)S(1)} %copy-done.34), kind=kOutput, calls=%fused_computation.43 | convolution fusion | flops 3225944064 | bytes 16789504 | tf_op jit(solution)/shard_map/dot_general | solution.py:58
  880.0 24.1 %all-reduce.13.cloned.1.call-done = (bf16[64]{0:T(256)(128)(2,1)}, bf16[64,384]{1,0:T(8,128)(2,1)}, bf16[64,384]{1,0:T(8,128)(2,1)}, bf16[64,384]{1,0:T(8,128)(2...) async-done(((bf16[64]{0:T(256)(128)(2,1)}, bf16[64,384]{1,0:T(8,128)(2,1)}, bf16[64,384]{1,0:T(8,128)(2,1)}, bf16[64,384]{1,0:T(8,128)(2,1)}, ...) | async-done | bytes 196928 | tf_op jit(solution)/shard_map/psum | solution.py:281
  913.4 27.6 %all-reduce.15.cloned.1.call-done = (bf16[64,1024]{1,0:T(8,128)(2,1)}, bf16[64,1024]{1,0:T(8,128)(2,1)}, bf16[128,512]{1,0:T(8,128)(2,1)}) async-done(((bf16[64,1024]{1,0:T(8,128)(2,1)}, bf16[64,1024]{1,0:T(8,128)(2,1)}, bf16[128,512]{1,0:T(8,128)(2,1)}), (bf16[64,1024]{1,0:T(8,128)(2,1)}, bf16[64,1024]{1,0:T(8,128)(2,1)}, bf16[128,512]{1,0:T(8,128)(2,1)})) %all-reduce.15.cloned.1.call-update) | async-done | bytes 393232 | tf_op jit(solution)/shard_map/psum | solution.py:288
  (215 shorter events, 206.4 us)
Async XLA Ops:
  7.2 69.8 %copy-start.3 = (bf16[48,64,512]{2,1,0:T(8,128)(2,1)S(1)}, bf16[48,64,512]{2,1,0:T(8,128)(2,1)}, u32[]{:S(2)}) copy-start(bf16[48,64,512]{2,1,0:T(8,128)(2,1)} %param.14) | copy-start | bytes 9437188
  7.2 290.2 %all-gather.4.cloned.1.call-start = ((), (), s32[]{:S(2)}) async-start(), calls=%async_computation.7 | async-start | bytes 1179648 | tf_op jit(solution)/shard_map/all_gather | solution.py:109
  9.0 298.5 %all-gather.6.cloned.1.call-start = ((), (), s32[]{:S(2)}) async-start(), calls=%async_computation.8 | async-start | bytes 1179648 | tf_op jit(solution)/shard_map/all_gather | solution.py:110
  10.7 307.1 %all-gather.8.cloned.1.call-start = ((), (), s32[]{:S(2)}) async-start(), calls=%async_computation.9 | async-start | bytes 1179648 | tf_op jit(solution)/shard_map/all_gather | solution.py:111
  12.4 523.2 %reduce-scatter.10.cloned.1.call-start = ((), (), s32[]{:S(2)}) async-start(), calls=%async_computation.11 | async-start | bytes 442368 | tf_op jit(solution)/shard_map/reduce_scatter | solution.py:254
  41.5 41.8 %copy-start.39 = (f32[512]{0:T(512)}, f32[512]{0:T(512)S(1)}, u32[]{:S(2)}) copy-start(f32[512]{0:T(512)S(1)} %convert_element_type.248) | copy-start | bytes 6148
  44.8 38.5 %copy-start.30 = (f32[3072]{0:T(1024)}, f32[3072]{0:T(1024)S(1)}, u32[]{:S(2)}) copy-start(f32[3072]{0:T(1024)S(1)} %add.117) | copy-start | bytes 36868
  44.8 32.2 %copy-start.26 = (f32[3072]{0:T(1024)}, f32[3072]{0:T(1024)S(1)}, u32[]{:S(2)}) copy-start(f32[3072]{0:T(1024)S(1)} %rsqrt.25) | copy-start | bytes 36868
  145.3 11.5 %copy-start.37 = (f32[64,384]{1,0:T(8,128)S(1)}, f32[64,384]{1,0:T(8,128)}, u32[]{:S(2)}) copy-start(f32[64,384]{1,0:T(8,128)} %param.19) | copy-start | bytes 294916
  207.9 17.5 %copy-start.16 = (f32[48,6,64]{2,1,0:T(8,128)}, f32[48,6,64]{2,1,0:T(8,128)S(1)}, u32[]{:S(2)}) copy-start(f32[48,6,64]{2,1,0:T(8,128)S(1)} %get-tuple-element.41) | copy-start | bytes 221188
  232.8 16.8 %copy-start.38 = (f32[48,512]{1,0:T(8,128)S(1)}, f32[48,512]{1,0:T(8,128)}, u32[]{:S(2)}) copy-start(f32[48,512]{1,0:T(8,128)} %param.20) | copy-start | bytes 294916
  307.5 10.3 %copy-start.15 = (bf16[3072,512]{1,0:T(8,128)(2,1)S(1)}, bf16[3072,512]{1,0:T(8,128)(2,1)}, u32[]{:S(2)}) copy-start(bf16[3072,512]{1,0:T(8,128)(2,1)} %fusion.11) | copy-start | bytes 9437188
  317.8 18.3 %copy-start.45 = (bf16[512,1024]{1,0:T(8,128)(2,1)S(1)}, bf16[512,1024]{1,0:T(8,128)(2,1)}, u32[]{:S(2)}) copy-start(bf16[512,1024]{1,0:T(8,128)(2,1)} %all-gather.4.cloned.1.call-done) | copy-start | bytes 3145732
  336.1 17.1 %slice-start.3 = ((s8[6291456]{0:T(1024)(128)(4,1)}), s8[4194304]{0:T(1024)(128)(4,1)S(1)}, s32[]{:S(2)}) async-start(s8[6291456]{0:T(1024)(128)(4,1)} %bitcast.111), calls=%async_computation.22 | async-start | bytes 8388608
  344.7 8.6 slice-start.4
  368.0 21.9 %slice-start = ((s8[9437184]{0:T(1024)(128)(4,1)}), s8[1048576]{0:T(1024)(128)(4,1)S(1)}, s32[]{:S(2)}) async-start(s8[9437184]{0:T(1024)(128)(4,1)} %bitcast.109), calls=%async_computation.19 | async-start | bytes 2097152
  376.3 13.6 %slice-start.1 = ((s8[9437184]{0:T(1024)(128)(4,1)}), s8[4194304]{0:T(1024)(128)(4,1)S(1)}, s32[]{:S(2)}) async-start(s8[9437184]{0:T(1024)(128)(4,1)} %bitcast.109), calls=%async_computation.20 | async-start | bytes 8388608
  376.3 13.6 %slice-start.2 = ((s8[9437184]{0:T(1024)(128)(4,1)}), s8[4194304]{0:T(1024)(128)(4,1)S(1)}, s32[]{:S(2)}) async-start(s8[9437184]{0:T(1024)(128)(4,1)} %bitcast.109), calls=%async_computation.21 | async-start | bytes 8388608
  410.1 12.3 %copy-start.5 = (bf16[3072,384]{0,1:T(8,128)(2,1)S(1)}, bf16[3072,384]{0,1:T(8,128)(2,1)}, u32[]{:S(2)}) copy-start(bf16[3072,384]{0,1:T(8,128)(2,1)} %reshape.165) | copy-start | bytes 7077892
  422.3 122.5 %reduce-scatter.14.cloned.1.call-start = ((), (), s32[]{:S(2)}) async-start(), calls=%async_computation.13 | async-start | bytes 442368 | tf_op jit(solution)/shard_map/reduce_scatter | solution.py:260
  427.3 180.9 %reduce-scatter.8.cloned.1.call-start = ((), (), s32[]{:S(2)}) async-start(), calls=%async_computation.10 | async-start | bytes 442368 | tf_op jit(solution)/shard_map/reduce_scatter | solution.py:251
  443.5 15.7 %copy-start.8 = (bf16[3072,384]{0,1:T(8,128)(2,1)}, bf16[3072,384]{0,1:T(8,128)(2,1)S(1)}, u32[]{:S(2)}) copy-start(bf16[3072,384]{0,1:T(8,128)(2,1)S(1)} %reshape.167) | copy-start | bytes 7077892
  448.9 223.1 %reduce-scatter.12.cloned.1.call-start = ((), (), s32[]{:S(2)}) async-start(), calls=%async_computation.12 | async-start | bytes 442368 | tf_op jit(solution)/shard_map/reduce_scatter | solution.py:257
  472.5 13.6 %copy-start.10 = (bf16[3072,384]{0,1:T(8,128)(2,1)}, bf16[3072,384]{0,1:T(8,128)(2,1)S(1)}, u32[]{:S(2)}) copy-start(bf16[3072,384]{0,1:T(8,128)(2,1)S(1)} %reshape.169) | copy-start | bytes 7077892
  477.9 260.0 %reduce-scatter.16.cloned.1.call-start = ((), (), s32[]{:S(2)}) async-start(), calls=%async_computation.14 | async-start | bytes 1179648 | tf_op jit(solution)/shard_map/reduce_scatter | solution.py:269
  486.2 10.1 %copy-start.25 = (f32[4096,32]{0,1:T(8,128)S(1)}, f32[4096,32]{0,1:T(8,128)}, u32[]{:S(2)}) copy-start(f32[4096,32]{0,1:T(8,128)} %constant.28.clone) | copy-start | bytes 1572868
  486.2 317.9 %reduce-scatter.18.cloned.1.call-start = ((), (), s32[]{:S(2)}) async-start(), calls=%async_computation.15 | async-start | bytes 1179648 | tf_op jit(solution)/shard_map/reduce_scatter | solution.py:272
  494.7 375.3 %reduce-scatter.20.cloned.1.call-start = ((), (), s32[]{:S(2)}) async-start(), calls=%async_computation.16 | async-start | bytes 1179648 | tf_op jit(solution)/shard_map/reduce_scatter | solution.py:275
  505.9 398.3 %all-reduce.13.cloned.1.call-start = ((), (), s32[]{:S(2)}) async-start(), calls=%async_computation.17 | async-start | bytes 396288 | tf_op jit(solution)/shard_map/psum | solution.py:281
  510.5 25.1 %copy-start.31 = (f32[3072]{0:T(1024)S(1)}, f32[3072]{0:T(1024)}, u32[]{:S(2)}) copy-start(f32[3072]{0:T(1024)} %copy-done.30) | copy-start | bytes 36868
  672.0 268.9 %all-reduce.15.cloned.1.call-start = ((), (), s32[]{:S(2)}) async-start(), calls=%async_computation.18 | async-start | bytes 786432 | tf_op jit(solution)/shard_map/psum | solution.py:288
  672.3 197.7 %copy-start.34 = (f32[3072]{0:T(1024)S(1)}, f32[3072]{0:T(1024)}, u32[]{:S(2)}) copy-start(f32[3072]{0:T(1024)} %copy-done.32) | copy-start | bytes 36868
  (31 other events, 136.8 us)
Sparse Core Ops, SparseCore 0:
  10.7 44.5 all-gather.3
  57.4 38.9 all-gather.5
  98.5 40.2 all-gather.7
  422.4 58.6 reduce-scatter.9
  484.3 60.4 reduce-scatter.13
  547.9 60.3 reduce-scatter.7
  611.5 60.4 reduce-scatter.11
  675.4 62.4 reduce-scatter.15
  741.7 62.3 reduce-scatter.17
  807.4 62.5 reduce-scatter.19
  874.2 29.9 all-reduce.12
  906.5 34.3 all-reduce.14
where the time goes:
time: 958 us; the launch traced here: 953 us
  waiting for transfers between devices  379 us (40%)
  matrix products  196 us (20%)
  blocking collectives  166 us (17%)
  local copies, waits for them, and re-layouts  133 us (14%)
  other arithmetic  58.7 us (6%)
  between operations  18.3 us (2%)
    reduce_scatter x1, waiting for transfers between devices, body(): lax.psum_scatter(grad_upw.astype(jnp.bfloat16), 'fsdp', scatter_dimension...  66.2 us
    reduce_scatter x1, waiting for transfers between devices, body(): lax.psum_scatter(grad_down.astype(jnp.bfloat16), 'fsdp', scatter_dimensio...  65.8 us
    reduce_scatter x1, waiting for transfers between devices, body(): lax.psum_scatter(grad_valuew.astype(jnp.bfloat16), 'fsdp', scatter_dimens...  63.7 us
    reduce_scatter x1, waiting for transfers between devices, body(): lax.psum_scatter(grad_queryw.astype(jnp.bfloat16), 'fsdp', scatter_dimens...  63.5 us
    reduce_scatter x1, waiting for transfers between devices, body(): lax.psum_scatter(grad_gate.astype(jnp.bfloat16), 'fsdp', scatter_dimensio...  58.9 us
    dot_general x7, matrix products, product_of(): return jnp.dot(left, right, preferred_element_type=jnp.float32)  50.2 us
    dot_general x7, matrix products, times_transposed(): lax.dot_general(left, right, (((1,), (1,)), ((), ())), preferred_element_...  46.7 us
    dot_general x7, matrix products, contract_rows(): lax.dot_general(left, right, (((0,), (0,)), ((), ())), preferred_element_...  45.6 us
  transfers between devices with their start and end apart: 12, of which 8 were waited for; matrix products, arithmetic and copies ran while one was open for 28% of the time, Pallas kernels for 0%

commit v1 on v0

v1 whole, which is shorter than its diff:
```python
import functools

import jax
import jax.numpy as jnp
import numpy as np
from jax import lax
from jax.experimental import pallas as pl
from jax.experimental.pallas import tpu as pltpu
from jax.sharding import PartitionSpec as P

HEADS, HDIM, BUCKETS = 6, 64, 32
INNER = HEADS * HDIM
PAIRS = HEADS // 2
PAIR = 2 * HDIM
CUT = 640
GROUP = 8
EPS = 1e-6
VMEM_LIMIT = 56 * 1024 * 1024
bf16, f32 = jnp.bfloat16, jnp.float32
sds = jax.ShapeDtypeStruct


def nn(a, b):
    return jnp.dot(a, b, preferred_element_type=f32)


def nt(a, b):
    return lax.dot_general(a, b, (((1,), (1,)), ((), ())), preferred_element_type=f32)


def tn(a, b):
    return lax.dot_general(a, b, (((0,), (0,)), ((), ())), preferred_element_type=f32)


def distance_bucket(distance, half_count, exact_count):
    if distance < exact_count:
        return distance
    reached = 0
    for higher in range(1, half_count - exact_count):
        if distance ** (
            half_count - exact_count
        ) * exact_count**higher >= 128**higher * exact_count ** (half_count - exact_count):
            reached = higher
    return exact_count + reached


def bucket_table(length):
    half = BUCKETS // 2
    ids = np.array(
        [
            [(half if j > i else 0) + distance_bucket(abs(j - i), half, half // 2) for i in range(length)]
            for j in range(length)
        ],
        dtype=np.int32,
    )
    return np.concatenate([ids, ids], axis=1)


def lane_low(shape):
    return lax.broadcasted_iota(jnp.int32, shape, 1) < HDIM


def split_heads(pair):
    low, zero = lane_low(pair.shape), jnp.zeros_like(pair)
    return jnp.concatenate([jnp.where(low, pair, zero), jnp.where(low, zero, pair)], axis=0)


def join_heads(both):
    rows = both.shape[0] // 2
    return jnp.where(lane_low((rows, PAIR)), both[:rows], both[rows:])


def row_sums(values):
    rows, width = values.shape
    return jnp.sum(values.reshape(rows // 8, 8, width), axis=0)


def inverse_rms(values):
    return lax.rsqrt(jnp.mean(values * values, axis=-1, keepdims=True) + EPS)


class Place:
    def __init__(self, ref, n_z):
        self.count, self.core, self.x, self.z = ref[0], ref[1], ref[2], ref[3]
        self.n_z = n_z

    def shards(self):
        for xx in range(2):
            for k in range(self.n_z):
                yield xx, k, jnp.bitwise_xor(self.z, k) * 2 + jnp.bitwise_xor(self.x, xx)


def at(shard, size):
    return pl.ds(pl.multiple_of(shard * size, size), size)


def interleaved(values, n_f, chunk):
    width = values.shape[1] // n_f // 2
    return jnp.concatenate(
        [values[:, (2 * f + chunk) * width : (2 * f + chunk + 1) * width] for f in range(n_f)], axis=1
    )


def prepare(n_f, place_ref, bias_ref, wq, wk, wv, wo, wg, wu, wd, ga, gf, a_ref, p0_ref, p1_ref):
    core = place_ref[1]
    ds, is_, fh = wq.shape[0], wo.shape[0], wd.shape[0] // 2
    half = wo.shape[1] // 2
    joined = jnp.concatenate([wq[...], wk[...], wv[...]], axis=1)
    row = lax.broadcasted_iota(jnp.int32, (ds, PAIR), 0)
    low = lane_low((1, PAIR))
    small = jnp.zeros((ds, PAIR), f32)
    n_b = BUCKETS // n_f
    for b in range(n_b):
        for p in range(PAIRS):
            value = jnp.where(low, bias_ref[b * HEADS + 2 * p], bias_ref[b * HEADS + 2 * p + 1])
            small = jnp.where(row == b * PAIRS + p, value, small)
    for i, gain in enumerate((ga, gf)):
        tiled = jnp.concatenate([gain[...]] * (PAIR // ds), axis=1)
        small = jnp.where(row == n_b * PAIRS + i, tiled, small)

    def write(c):
        if c == 0:
            a_ref[...] = joined[:, :CUT].astype(bf16)
        else:
            a_ref[:, : 3 * INNER - CUT] = joined[:, CUT:].astype(bf16)
            a_ref[:, 3 * INNER - CUT :] = small.astype(bf16)
        cols = slice(c * half, (c + 1) * half)
        for chunk, ref in enumerate((p0_ref, p1_ref)):
            g = interleaved((wg, wu)[c][...], n_f, chunk).astype(bf16)
            ref[:ds, :] = g[:, :half]
            ref[ds : 2 * ds, :] = g[:, half:]
            ref[2 * ds : 2 * ds + fh, :] = wd[chunk * fh : (chunk + 1) * fh, cols].astype(bf16)
        tail = wo[:, cols]
        pad = p0_ref.shape[0] - (2 * ds + fh + is_)
        if pad:
            tail = jnp.concatenate([tail, jnp.zeros((pad, half), f32)], axis=0)
        p0_ref[2 * ds + fh :, :] = tail.astype(bf16)

    for c in range(2):
        pl.when(core == c)(functools.partial(write, c))


def padded(rows):
    return -(-rows // 16) * 16


def call_prepare(place, n_f, attn_gain, wq, wk, wv, wo, rel_bias, ffn_gain, wg, wu, wd):
    ds, fh, half = wq.shape[0], wd.shape[0] // 2, wo.shape[1] // 2
    vm, sm = pl.BlockSpec(memory_space=pltpu.VMEM), pl.BlockSpec(memory_space=pltpu.SMEM)
    return pl.pallas_call(
        functools.partial(prepare, n_f),
        out_shape=(
            sds((ds, CUT), bf16),
            sds((2 * ds + fh + padded(wo.shape[0]), half), bf16),
            sds((2 * ds + fh, half), bf16),
        ),
        in_specs=[sm, sm] + [vm] * 9,
        out_specs=[vm] * 3,
        name="prepare",
    )(place, rel_bias, wq, wk, wv, wo, wg, wu, wd, attn_gain.reshape(1, -1), ffn_gain.reshape(1, -1))


def attention_forward(G, L, n_z, place_ref, idx_ref, tok_ref, z_ref, x_ref, zc_ref, xc_ref,
                      qkv_ref, probs_ref, mixed_ref, w_ref, gains_ref, table_ref, st_ref, small_ref):
    step = pl.program_id(0)
    place = Place(place_ref, n_z)
    D = tok_ref.shape[-1]
    n_f = 2 * n_z
    ds = D // n_f
    rest = 3 * INNER - CUT

    def assemble(c):
        for xx, k, f in place.shards():
            here, there = ((z_ref, zc_ref), (x_ref, xc_ref))[xx]
            one, two = (here, there) if c == 0 else (there, here)
            w_ref[at(f, ds), :CUT] = one[k]
            w_ref[at(f, ds), CUT:] = two[k, :, :rest]
            small_ref[at(f, ds), :] = two[k, :, rest:].astype(f32)

    @pl.when(step == 0)
    def _():
        for c in range(2):
            pl.when(place.core == c)(functools.partial(assemble, c))
        n_b = BUCKETS // n_f
        ids = idx_ref[...]
        for p in range(PAIRS):
            total = jnp.zeros(ids.shape, f32)
            for b in range(BUCKETS):
                row = b // n_b * ds + (b % n_b) * PAIRS + p
                total = jnp.where(ids == b, small_ref[row : row + 1, :], total)
            table_ref[p] = total
        per = PAIR // ds
        lane = lax.broadcasted_iota(jnp.int32, (1, PAIR), 1) // ds
        gains_ref[...] = jnp.zeros_like(gains_ref)
        for i in range(2):
            for v in range(D // PAIR):
                total = jnp.zeros((1, PAIR), f32)
                for f in range(per):
                    row = (v * per + f) * ds + n_b * PAIRS + i
                    total = jnp.where(lane == f, small_ref[row : row + 1, :], total)
                gains_ref[i : i + 1, v * PAIR : (v + 1) * PAIR] = total

    @pl.when(step * G < place.count)
    def _():
        x = tok_ref[...].reshape(G * L, D).astype(f32)
        normed = (x * inverse_rms(x) * gains_ref[0:1, :]).astype(bf16)
        qkv_ref[...] = nn(normed, w_ref[...]).astype(bf16)
        for s in range(G):
            rows = pl.ds(s * L, L)
            for p in range(PAIRS):
                q = qkv_ref[rows, pl.ds(p * PAIR, PAIR)]
                k = qkv_ref[rows, pl.ds(INNER + p * PAIR, PAIR)]
                st_ref[s, p] = nt(k, split_heads(q))
        for s in range(G):
            for p in range(PAIRS):
                st = st_ref[s, p] + table_ref[p]
                e = jnp.exp(st - jnp.max(st, axis=0, keepdims=True))
                probs_ref[s, p] = (e * (1.0 / jnp.sum(e, axis=0, keepdims=True))).astype(bf16)
        for s in range(G):
            rows = pl.ds(s * L, L)
            for p in range(PAIRS):
                v = qkv_ref[rows, pl.ds(2 * INNER + p * PAIR, PAIR)]
                mixed_ref[rows, pl.ds(p * PAIR, PAIR)] = join_heads(tn(probs_ref[s, p], v)).astype(bf16)


def params():
    return pltpu.CompilerParams(dimension_semantics=("arbitrary",), vmem_limit_bytes=VMEM_LIMIT)


def whole(shape):
    return pl.BlockSpec(shape, lambda i, *_: (0,) * len(shape), pipeline_mode=pl.Buffered(1))


def live_group(i, place, G):
    return jnp.minimum(i, jnp.maximum((place[0] + G - 1) // G - 1, 0))


def series_spec(G, shape, every=False):
    tail = (0,) * (len(shape) - 1)
    return pl.BlockSpec((G,) + shape[1:], lambda i, c: ((i if every else live_group(i, c, G)),) + tail)


def row_spec(G, L, width):
    return pl.BlockSpec((G * L, width), lambda i, c: (live_group(i, c, G), 0))


def cost(rows, per_row, nbytes, exps=0):
    return pl.CostEstimate(flops=2 * rows * per_row, bytes_accessed=nbytes, transcendentals=exps)


def call_attention_forward(place, tokens, pieces):
    S, L, D = tokens.shape
    G, n_z = GROUP, pieces[0].shape[0]
    return pl.pallas_call(
        functools.partial(attention_forward, G, L, n_z),
        out_shape=(
            sds((S * L, 3 * INNER), bf16),
            sds((S, PAIRS, L, PAIR), bf16),
            sds((S * L, INNER), bf16),
            sds((D, 3 * INNER), bf16),
            sds((8, D), f32),
        ),
        grid_spec=pltpu.PrefetchScalarGridSpec(
            num_scalar_prefetch=1,
            grid=(S // G,),
            in_specs=[whole((L, PAIR)), series_spec(G, tokens.shape)] + [whole(piece.shape) for piece in pieces],
            out_specs=[
                row_spec(G, L, 3 * INNER),
                series_spec(G, (S, PAIRS, L, PAIR)),
                row_spec(G, L, INNER),
                whole((D, 3 * INNER)),
                whole((8, D)),
            ],
            scratch_shapes=[
                pltpu.VMEM((PAIRS, L, PAIR), f32),
                pltpu.VMEM((G, PAIRS, L, PAIR), f32),
                pltpu.VMEM((D, PAIR), f32),
            ],
        ),
        compiler_params=params(),
        cost_estimate=cost(S * L, D * 3 * INNER * 4, S * L * 5000),
        name="attention_forward",
    )(place, jnp.asarray(bucket_table(L)), tokens, *pieces)


def gelu_parts(v):
    c = 0.7978845608028654
    v2 = v * v
    t = jnp.tanh(v * (c + (c * 0.044715) * v2))
    half = 0.5 + 0.5 * t
    return v * half, half + (0.5 * v) * (1.0 - t * t) * (c + (3 * c * 0.044715) * v2)


def put_weights(place, first, n_z, pieces, wg, wu, wd, wo):
    z_ref, x_ref, zc_ref, xc_ref = pieces
    n_f = 2 * n_z
    D, FW = wg.shape
    ds, fh, half = D // n_f, FW // n_f, FW // 2

    def assemble(c):
        for xx, k, f in place.shards():
            here, there = ((z_ref, zc_ref), (x_ref, xc_ref))[xx]
            for which, piece in enumerate((here, there) if c == 0 else (there, here)):
                gated = (wg, wu)[which]
                gated[at(f, ds), :half] = piece[k, :ds, :]
                gated[at(f, ds), half:] = piece[k, ds : 2 * ds, :]
                cols = slice(which * half, (which + 1) * half)
                wd[at(f, fh), cols] = piece[k, 2 * ds : 2 * ds + fh, :]
                if first:
                    is_ = INNER // n_f
                    if is_ % 16 == 0:
                        wo[at(f, is_), cols] = piece[k, 2 * ds + fh : 2 * ds + fh + is_, :]
                    else:
                        wo[f, :, cols] = piece[k, 2 * ds + fh :, :]

    for c in range(2):
        pl.when(place.core == c)(functools.partial(assemble, c))


def put_grads(place, n_z, keep, send, ag, au, ad, ao=None):
    n_f = 2 * n_z
    D, FW = ag.shape
    ds, fh, half = D // n_f, FW // n_f, FW // 2

    def write(c):
        for xx, k, f in place.shards():
            for which, ref in enumerate((keep, send) if c == 0 else (send, keep)):
                gated = (ag, au)[which]
                cols = slice(which * half, (which + 1) * half)
                ref[xx, k, :ds, :] = gated[at(f, ds), :half].astype(bf16)
                ref[xx, k, ds : 2 * ds, :] = gated[at(f, ds), half:].astype(bf16)
                ref[xx, k, 2 * ds : 2 * ds + fh, :] = ad[at(f, fh), cols].astype(bf16)
                if ao is not None:
                    is_ = INNER // n_f
                    if is_ % 16 == 0:
                        ref[xx, k, 2 * ds + fh :, :] = ao[at(f, is_), cols].astype(bf16)
                    else:
                        ref[xx, k, 2 * ds + fh :, :] = ao[f, :, cols].astype(bf16)

    for c in range(2):
        pl.when(place.core == c)(functools.partial(write, c))


def ffn_half(G, L, CH, n_z, first, place_ref, *refs):
    if first:
        (tok_ref, ct_ref, mixed_ref, z_ref, x_ref, zc_ref, xc_ref, gains_ref,
         hid_ref, part_ref, gpart_ref, wo_out, keep, send,
         ag, au, ad, wg, wu, wd, n2, gb, gate, up, ga, act, ggr, gur, acc, gn, spread) = refs
    else:
        (hid_ref, ct_ref, mixed_ref, part_ref, gpart_ref, z_ref, x_ref, zc_ref, xc_ref, gains_ref, wo_in,
         out_ref, gh_ref, gm_ref, keep, send, gf_ref,
         ag, au, ad, wg, wu, wd, n2, gb, gate, up, ga, act, ggr, gur, acc, gn, ao, spread) = refs
    step = pl.program_id(0)
    last = pl.num_programs(0) - 1
    R = G * L
    D = ct_ref.shape[-1]
    FW = wg.shape[1]
    n_f = 2 * n_z
    is_ = INNER // n_f
    place = Place(place_ref, n_z)
    count = place.count

    @pl.when(step == 0)
    def _():
        wo = (wo_out if is_ % 16 == 0 else spread) if first else None
        put_weights(place, first, n_z, (z_ref, x_ref, zc_ref, xc_ref), wg, wu, wd, wo)
        if first and is_ % 16:
            wo_out[...] = jnp.concatenate([spread[f, :is_, :].astype(f32) for f in range(n_f)], axis=0).astype(bf16)
        for ref in (ag, au, ad) if first else (ag, au, ad, ao, gf_ref):
            ref[...] = jnp.zeros_like(ref)

    if not first:

        @pl.when(step * G >= count)
        def _():
            out_ref[...] = jnp.zeros_like(out_ref)

    @pl.when(step * G < count)
    def _():
        if first:
            hid_ref[...] = tok_ref[...].reshape(R, D).astype(f32) + nn(mixed_ref[...], wo_out[...])
        h = hid_ref[...]
        n2[...] = (h * inverse_rms(h) * gains_ref[1:2, :]).astype(bf16)
        live = (step * G + lax.broadcasted_iota(jnp.int32, (R, 1), 0) // L) < count
        gb[...] = jnp.where(live, ct_ref[...].reshape(R, D), jnp.zeros((), bf16))
        for c in range(FW // CH):
            cols = pl.ds(c * CH, CH)
            gate[...] = nn(n2[...], wg[:, cols])
            up[...] = nn(n2[...], wu[:, cols])
            ga[...] = nt(gb[...], wd[cols, :])
            for r in range(0, R, L):
                rows = pl.ds(r, L)
                u = up[rows, :]
                a = ga[rows, :]
                g, dg = gelu_parts(gate[rows, :])
                act[rows, :] = (g * u).astype(bf16)
                ggr[rows, :] = (a * u * dg).astype(bf16)
                gur[rows, :] = (a * g).astype(bf16)
            if c == 0:
                acc[...] = nn(act[...], wd[cols, :])
                gn[...] = nt(ggr[...], wg[:, cols]) + nt(gur[...], wu[:, cols])
            else:
                acc[...] += nn(act[...], wd[cols, :])
                gn[...] += nt(ggr[...], wg[:, cols]) + nt(gur[...], wu[:, cols])
            ad[cols, :] += tn(act[...], gb[...])
            ag[:, cols] += tn(n2[...], ggr[...])
            au[:, cols] += tn(n2[...], gur[...])
        if first:
            part_ref[...] = acc[...].astype(bf16)
            gpart_ref[...] = gn[...].astype(bf16)
        else:
            h = hid_ref[...]
            out = h + part_ref[...].astype(f32) + acc[...]
            out_ref[...] = jnp.where(live, out, 0.0).astype(bf16).reshape(G, L, D)
            scale = inverse_rms(h)
            hs = h * scale
            g2 = gn[...] + gpart_ref[...].astype(f32)
            gf_ref[...] += row_sums(g2 * hs)
            g2 = g2 * gains_ref[1:2, :]
            dot = jnp.mean(g2 * hs, axis=-1, keepdims=True)
            gh = (gb[...].astype(f32) + scale * (g2 - hs * dot)).astype(bf16)
            gh_ref[...] = gh
            ao[...] += tn(mixed_ref[...], gh)
            gm_ref[...] = nt(gh, wo_in[...]).astype(bf16)

    @pl.when(step == last)
    def _():
        if first:
            put_grads(place, n_z, keep, send, ag, au, ad)
        elif is_ % 16 == 0:
            put_grads(place, n_z, keep, send, ag, au, ad, ao)
        else:
            for f in range(n_f):
                spread[f, :is_, :] = ao[f * is_ : (f + 1) * is_, :]
            put_grads(place, n_z, keep, send, ag, au, ad, spread)


def call_ffn_half(first, place, pieces, gains, arrays, S, L, D, CH=256):
    G, n_z = GROUP, pieces[0].shape[0]
    R, n_f = G * L, 2 * n_z
    FW = D
    ds, fh, half, is_ = D // n_f, FW // n_f, FW // 2, INNER // n_f
    series = series_spec(G, (S, L, D))
    piece_specs = [whole(piece.shape) for piece in pieces] + [whole(gains.shape)]
    rows = functools.partial(row_spec, G, L)
    extra = 0 if first else padded(is_)
    pack = (2, n_z, 2 * ds + fh + extra, half)
    if first:
        in_specs = [series, series, rows(INNER)] + piece_specs
        out_shape = [sds((S * L, D), f32), sds((S * L, D), bf16), sds((S * L, D), bf16), sds((INNER, D), bf16),
                     sds(pack, bf16), sds(pack, bf16)]
        out_specs = [rows(D), rows(D), rows(D), whole((INNER, D)), whole(pack), whole(pack)]
        operands = arrays + tuple(pieces) + (gains,)
    else:
        *arrays, wo = arrays
        in_specs = [rows(D), series, rows(INNER), rows(D), rows(D)] + piece_specs + [whole(wo.shape)]
        out_shape = [sds((S, L, D), bf16), sds((S * L, D), bf16), sds((S * L, INNER), bf16),
                     sds(pack, bf16), sds(pack, bf16), sds((8, D), f32)]
        out_specs = [series_spec(G, (S, L, D), True), rows(D), rows(INNER), whole(pack), whole(pack), whole((8, D))]
        operands = tuple(arrays) + tuple(pieces) + (gains, wo)
    vm = pltpu.VMEM
    scratch = (
        [vm((D, FW), f32)] * 2 + [vm((FW, D), f32)]
        + [vm((D, FW), bf16)] * 2 + [vm((FW, D), bf16)]
        + [vm((R, D), bf16)] * 2 + [vm((R, CH), f32)] * 3 + [vm((R, CH), bf16)] * 3 + [vm((R, D), f32)] * 2
        + ([] if first else [vm((INNER, D), f32)])
        + [vm((n_f, padded(is_), D) if is_ % 16 else (1, 16, 128), bf16 if first else f32)]
    )
    return pl.pallas_call(
        functools.partial(ffn_half, G, L, CH, n_z, first),
        out_shape=tuple(out_shape),
        grid_spec=pltpu.PrefetchScalarGridSpec(
            num_scalar_prefetch=1, grid=(S // G,), in_specs=in_specs, out_specs=out_specs, scratch_shapes=scratch
        ),
        compiler_params=params(),
        cost_estimate=cost(S * L, 12 * D * FW, S * L * 9000),
        name="ffn_first" if first else "ffn_second",
    )(place, *operands)


def attention_backward(G, L, n_z, place_ref, idx_ref, tok_ref, qkv_ref, probs_ref, gm_ref, gh_ref, w_ref, gains_ref, gf_ref,
                       gt_ref, keep, send, aw, aq, ab, dqkv, dp_ref, ds_ref, small):
    step = pl.program_id(0)
    last = pl.num_programs(0) - 1
    R = G * L
    D = tok_ref.shape[-1]
    place = Place(place_ref, n_z)
    count = place.count

    @pl.when(step == 0)
    def _():
        for ref in (aw, aq, ab):
            ref[...] = jnp.zeros_like(ref)

    @pl.when(step * G >= count)
    def _():
        gt_ref[...] = jnp.zeros_like(gt_ref)

    @pl.when(step * G < count)
    def _():
        cols = [[pl.ds(b * INNER + p * PAIR, PAIR) for b in range(3)] for p in range(PAIRS)]
        for p in range(PAIRS):
            for s in range(G):
                rows = pl.ds(s * L, L)
                dm = split_heads(gm_ref[rows, pl.ds(p * PAIR, PAIR)])
                dp_ref[s, p] = nt(qkv_ref[rows, cols[p][2]], dm)
                dqkv[rows, cols[p][2]] = nn(probs_ref[s, p], dm).astype(bf16)
        for p in range(PAIRS):
            total = ab[p]
            for s in range(G):
                prf = probs_ref[s, p].astype(f32)
                dp = dp_ref[s, p]
                ds = prf * (dp - jnp.sum(prf * dp, axis=0, keepdims=True))
                total = total + ds
                ds_ref[s, p] = ds.astype(bf16)
            ab[p] = total
        for p in range(PAIRS):
            for s in range(G):
                rows = pl.ds(s * L, L)
                low = ds_ref[s, p]
                dqkv[rows, cols[p][1]] = nn(low, split_heads(qkv_ref[rows, cols[p][0]])).astype(bf16)
                dqkv[rows, cols[p][0]] = join_heads(tn(low, qkv_ref[rows, cols[p][1]])).astype(bf16)
        x = tok_ref[...].reshape(R, D).astype(f32)
        scale = inverse_rms(x)
        xs = x * scale
        aw[...] += tn((xs * gains_ref[0:1, :]).astype(bf16), dqkv[...])
        g = nt(dqkv[...], w_ref[...])
        aq[...] += row_sums(g * xs)
        g = g * gains_ref[0:1, :]
        dot = jnp.mean(g * xs, axis=-1, keepdims=True)
        gt_ref[...] = (gh_ref[...].astype(f32) + scale * (g - xs * dot)).astype(bf16).reshape(G, L, D)

    @pl.when(step == last)
    def _():
        n_f = 2 * n_z
        ds, n_b, rest = D // n_f, BUCKETS // n_f, 3 * INNER - CUT
        ids = idx_ref[...]
        low = lane_low((1, PAIR))
        small[...] = jnp.zeros_like(small)
        for p in range(PAIRS):
            t = ab[p]
            for b in range(BUCKETS):
                by_lane = jnp.sum(jnp.where(ids == b, t, 0.0), axis=0, keepdims=True)
                one = jnp.sum(jnp.where(low, by_lane, 0.0), axis=1, keepdims=True)
                two = jnp.sum(jnp.where(low, 0.0, by_lane), axis=1, keepdims=True)
                row = b // n_b * ds + (b % n_b) * PAIRS + p
                small[row : row + 1, :] = jnp.where(low, one, two)
        for i, ref in enumerate((aq, gf_ref)):
            total = jnp.sum(ref[...], axis=0, keepdims=True)
            for f in range(n_f):
                row = f * ds + n_b * PAIRS + i
                start = f * ds // PAIR * PAIR
                small[row : row + 1, :] = total[:, start : start + PAIR]

        def write(c):
            for xx, k, f in place.shards():
                one, two = (keep, send) if c == 0 else (send, keep)
                one[xx, k] = aw[at(f, ds), :CUT].astype(bf16)
                two[xx, k, :, :rest] = aw[at(f, ds), CUT:].astype(bf16)
                two[xx, k, :, rest:] = small[at(f, ds), :].astype(bf16)

        for c in range(2):
            pl.when(place.core == c)(functools.partial(write, c))


def call_attention_backward(place, n_z, tokens, qkv, probs, gm, gh, w, gains, gf):
    S, L, D = tokens.shape
    G = GROUP
    R = G * L
    rows = functools.partial(row_spec, G, L)
    pack = (2, n_z, D // (2 * n_z), CUT)
    vm = pltpu.VMEM
    return pl.pallas_call(
        functools.partial(attention_backward, G, L, n_z),
        out_shape=(sds((S, L, D), bf16), sds(pack, bf16), sds(pack, bf16)),
        grid_spec=pltpu.PrefetchScalarGridSpec(
            num_scalar_prefetch=1,
            grid=(S // G,),
            in_specs=[whole((L, PAIR)), series_spec(G, tokens.shape), rows(3 * INNER), series_spec(G, probs.shape),
                      rows(INNER), rows(D), whole(w.shape), whole(gains.shape), whole(gf.shape)],
            out_specs=[series_spec(G, tokens.shape, True), whole(pack), whole(pack)],
            scratch_shapes=[
                vm(w.shape, f32), vm((8, D), f32), vm((PAIRS, L, PAIR), f32), vm((R, 3 * INNER), bf16),
                vm((G, PAIRS, L, PAIR), f32), vm((G, PAIRS, L, PAIR), bf16), vm((D, PAIR), f32),
            ],
        ),
        compiler_params=params(),
        cost_estimate=cost(S * L, D * 3 * INNER * 6, S * L * 6000),
        name="attention_backward",
    )(place, jnp.asarray(bucket_table(L)), tokens, qkv, probs, gm, gh, w, gains, gf)


def tree(values):
    while len(values) > 1:
        values = [a + b for a, b in zip(values[0::2], values[1::2])]
    return values[0]


def finish(n_f, n_r, place_ref, *refs):
    packs = [refs[i * n_r : (i + 1) * n_r] for i in range(3)]
    gq, gk, gv, go, gg, gu, gd, gs = refs[3 * n_r :]
    core = place_ref[1]
    ds, is_, fh = gq.shape[0], go.shape[0], gd.shape[0] // 2
    half = go.shape[1] // 2

    def halves(pack):
        here = tree([ref[...].astype(f32) for ref in pack[0::2]])
        there = tree([ref[...].astype(f32) for ref in pack[1::2]])
        return jnp.where(core == 0, here, there), jnp.where(core == 0, there, here)

    one, two = halves(packs[2])
    gq[...] = one[:, :INNER]
    gk[...] = jnp.concatenate([one[:, INNER:CUT], two[:, : 2 * INNER - CUT]], axis=1)
    gv[...] = two[:, 2 * INNER - CUT : 3 * INNER - CUT]
    gs[...] = two[:, 3 * INNER - CUT :]
    chunks = [halves(packs[0]), halves(packs[1])]
    for which, ref in enumerate((gg, gu)):
        wide = [jnp.concatenate([c[which][:ds], c[which][ds : 2 * ds]], axis=1) for c in chunks]
        width = wide[0].shape[1] // n_f
        ref[...] = jnp.concatenate(
            [w[:, f * width : (f + 1) * width] for f in range(n_f) for w in wide], axis=1
        )
    for chunk, pair in enumerate(chunks):
        for which in range(2):
            gd[chunk * fh : (chunk + 1) * fh, which * half : (which + 1) * half] = pair[which][2 * ds : 2 * ds + fh]
    for which in range(2):
        go[:, which * half : (which + 1) * half] = chunks[1][which][2 * ds + fh : 2 * ds + fh + is_]


def call_finish(place, n_f, n_r, packs, shapes):
    vm, sm = pl.BlockSpec(memory_space=pltpu.VMEM), pl.BlockSpec(memory_space=pltpu.SMEM)
    flat = [piece for pack in packs for piece in pack]
    return pl.pallas_call(
        functools.partial(finish, n_f, n_r),
        out_shape=tuple(sds(shape, f32) for shape in shapes),
        in_specs=[sm] + [vm] * len(flat),
        out_specs=[vm] * len(shapes),
        name="finish",
    )(place, *flat)


def solution(mesh):
    n_r, n_f = mesh.shape["rep"], mesh.shape["fsdp"]
    n_z = n_f // 2

    def over_fsdp(value, distance):
        return lax.ppermute(value, "fsdp", [(i, i ^ distance) for i in range(n_f)])

    def over_rep(value, distance):
        return lax.ppermute(value, "rep", [(i, i ^ distance) for i in range(n_r)])

    def gather(pack):
        near = jnp.stack([pack] + [over_fsdp(pack, 2 * k) for k in range(1, n_z)])
        far = over_fsdp(near, 1)
        return near, far, over_rep(near, 1), over_rep(far, 1)

    def scatter(keep, send):
        got = over_rep(send, 1)
        away = (keep[1].astype(f32) + got[1].astype(f32)).astype(bf16)
        here = keep[0].astype(f32) + got[0].astype(f32) + over_fsdp(away, 1).astype(f32)
        own = here[0]
        for k in range(1, n_z):
            own = own + over_fsdp(here[k].astype(bf16), 2 * k).astype(f32)
        own = own.astype(bf16)
        return [own] + [over_rep(own, m) for m in range(1, n_r)]

    def body(tokens, counts, attn_gain, wq, wk, wv, wo, rel_bias, ffn_gain, wg, wu, wd, cotangent):
        S, L, D = tokens.shape
        r, f = lax.axis_index("rep"), lax.axis_index("fsdp")
        place = jnp.stack([counts[0, 0], r % 2, f % 2, f // 2]).astype(jnp.int32)
        pack_a, pack_0, pack_1 = call_prepare(place, n_f, attn_gain, wq, wk, wv, wo, rel_bias, ffn_gain, wg, wu, wd)
        qkv, probs, mixed, w_all, gains = call_attention_forward(place, tokens, gather(pack_a))
        hidden, part, gpart, wo_all, keep_0, send_0 = call_ffn_half(
            True, place, gather(pack_0), gains, (tokens, cotangent, mixed), S, L, D
        )
        sums_0 = scatter(keep_0, send_0)
        layer_out, gh, gm, keep_1, send_1, gf = call_ffn_half(
            False, place, gather(pack_1), gains, (hidden, cotangent, mixed, part, gpart, wo_all), S, L, D
        )
        sums_1 = scatter(keep_1, send_1)
        grad_tokens, keep_2, send_2 = call_attention_backward(
            place, n_z, tokens, qkv, probs, gm, gh, w_all, gains, gf
        )
        sums_2 = scatter(keep_2, send_2)
        ds, n_b = wq.shape[0], BUCKETS // n_f
        gq, gk, gv, go, gg, gu, gd, small = call_finish(
            place, n_f, n_r, (sums_0, sums_1, sums_2),
            (wq.shape, wk.shape, wv.shape, wo.shape, wg.shape, wu.shape, wd.shape, (ds, PAIR)),
        )
        grad_bias = small[: n_b * PAIRS, ::HDIM].reshape(-1)
        gain_rows = small[n_b * PAIRS : n_b * PAIRS + 2].reshape(2, PAIR // ds, ds)
        gain_rows = lax.dynamic_index_in_dim(gain_rows, f % (PAIR // ds), axis=1, keepdims=False)
        return (layer_out, grad_tokens, gain_rows[0], gq, gk, gv, go, grad_bias, gain_rows[1], gg, gu, gd)

    rows, cols, flat = P(("rep", "fsdp"), None, None), P("fsdp", None), P("fsdp")
    return jax.shard_map(
        body,
        mesh=mesh,
        in_specs=(rows, P("rep", "fsdp"), flat, cols, cols, cols, cols, flat, flat, cols, cols, cols, rows),
        out_specs=(rows, rows, flat, cols, cols, cols, cols, flat, flat, cols, cols, cols),
        check_vma=False,
    )
```

time: 958 us -> 213 us (0.22)
  waiting for transfers between devices: 379 us -> 49.5 us
  matrix products: 196 us -> 0 us
  blocking collectives: 166 us -> 0 us
  local copies, waits for them, and re-layouts: 133 us -> 6.66 us
  Pallas kernels: 0 us -> 85.4 us
  starting transfers between devices: 1.29 us -> 61.9 us
  other arithmetic: 58.7 us -> 6.35 us
  between operations: 18.3 us -> 1.76 us
    reduce_scatter x7 -> x0, waiting for transfers between devices: 327 us -> none  [the longest x1 66.2 us: body(): lax.psum_scatter(grad_upw.astype(jnp.bfloat16), 'fsdp', scatter_dimension...]
    dot_general x29 -> x0, matrix products: 196 us -> none  [the longest x7 50.2 us: product_of(): return jnp.dot(left, right, preferred_element_type=jnp.float32)]
    all_gather x4 -> x0, blocking collectives: 125 us -> none  [the longest x1 31.6 us: body(): lax.all_gather(w_query.astype(jnp.bfloat16), 'fsdp', axis=0, tiled=True)]
    reshape x13 -> x2, local copies, waits for them, and re-layouts: 90.7 us -> 0.68 us  [the longest x1 0.59 us: body(): grad_bias = small[:n_b * PAIRS, ::HDIM].reshape(-1)]
    pallas_call x0 -> x6, Pallas kernels: none -> 85.4 us  [the longest x2 47.4 us: call_ffn_half(): pl.pallas_call(functools.partial(ffn_half, G, L, CH, n_z, first), out_sha...]
    ppermute x0 -> x42, starting transfers between devices: none -> 61.9 us  [the longest x24 43.3 us: over_fsdp(): return lax.ppermute(value, 'fsdp', [(i, i ^ distance) for i in range(n_f)])]
    psum x2 -> x0, waiting for transfers between devices: 51.7 us -> none  [the longest x1 27.6 us: body(): lax.psum(shards[7].astype(jnp.bfloat16), 'rep').astype(jnp.float32)]
    ppermute x0 -> x42, waiting for transfers between devices: none -> 49.5 us  [the longest x24 39 us: over_fsdp(): return lax.ppermute(value, 'fsdp', [(i, i ^ distance) for i in range(n_f)])]
  transfers between devices with their start and end apart: 12 -> 42, of which waited for: 8 -> 14; matrix products, arithmetic and copies ran while one was open for 28% -> 3% of each run, Pallas kernels for 0% -> 17%
where the time goes in v1:
time: 213 us; the launch traced here: 212 us
  Pallas kernels  85.4 us (40%)
  starting transfers between devices  61.9 us (29%)
  waiting for transfers between devices  49.5 us (23%)
  local copies, waits for them, and re-layouts  6.66 us (3%)
  other arithmetic  6.35 us (3%)
    pallas_call x2, Pallas kernels, call_ffn_half(): pl.pallas_call(functools.partial(ffn_half, G, L, CH, n_z, first), out_sha...  47.4 us
    ppermute x24, starting transfers between devices, over_fsdp(): return lax.ppermute(value, 'fsdp', [(i, i ^ distance) for i in range(n_f)])  43.3 us
    ppermute x24, waiting for transfers between devices, over_fsdp(): return lax.ppermute(value, 'fsdp', [(i, i ^ distance) for i in range(n_f)])  39 us
    pallas_call x1, Pallas kernels, call_attention_backward(): pl.pallas_call(functools.partial(attention_backward, G, L, n_z), out_shap...  20.3 us
    ppermute x18, starting transfers between devices, over_rep(): return lax.ppermute(value, 'rep', [(i, i ^ distance) for i in range(n_r)])  18.6 us
    pallas_call x1, Pallas kernels, call_attention_forward(): pl.pallas_call(functools.partial(attention_forward, G, L, n_z), out_shape...  13.1 us
    ppermute x18, waiting for transfers between devices, over_rep(): return lax.ppermute(value, 'rep', [(i, i ^ distance) for i in range(n_r)])  10.5 us
  transfers between devices with their start and end apart: 42, of which 14 were waited for; matrix products, arithmetic and copies ran while one was open for 3% of the time, Pallas kernels for 17%

profile of v1, /device:TPU:0, one launch (start us, length us, event | category | flops | bytes accessed | tf_op | source)
XLA Modules:
  0.0 211.6 jit_solution(6573239926856906824)
XLA Ops:
  2.0 2.2 %prepare.1 = (bf16[64,640]{1,0:T(8,128)(2,1)}, bf16[240,256]{1,0:T(8,128)(2,1)}, bf16[192,256]{1,0:T(8,128)(2,1)}) custom-call(s32[4]{0:T(128)} %pad_add_fusion.place_ref, f32[24]{0:T(128)} %bias_ref.1, f32[64,384]{1,0:T(8,128)} %wq.1, f32[64,384]{1,0:T(8,128)} %wk.1, f32[64,384]{1,0:T(8,128)} %wv.1, f32[48,512]{1,0:T(8,128)} %wo.1, f32[64,1024]{1,0:T(8,128)} %wg.1, ...), custom_call_target="tpu_custom_call" | custom-call | tf_op jit(solution)/shard_map/prepare/pallas_call | solution.py:150
  4.2 3.0 %collective-permute-start = (bf16[64,640]{1,0:T(8,128)(2,1)}, bf16[64,640]{1,0:T(8,128)(2,1)S(1)}, u32[]{:S(2)}, u32[]{:S(2)}) collective-permute-start(bf16[64,640]{1,0:T(8,128)(2,1)} %get-tuple-element.43), channel_id=1, source_target_pairs={{0,2},{1,3},{2,0},{3,1},{4,6},{5,7},{6,4},{7,5},{8,10},{9,11},{10,... | collective-permute-start | bytes 245768 | tf_op jit(solution)/shard_map/ppermute | solution.py:647
  7.2 2.6 %collective-permute-start.1 = (bf16[64,640]{1,0:T(8,128)(2,1)}, bf16[64,640]{1,0:T(8,128)(2,1)S(1)}, u32[]{:S(2)}, u32[]{:S(2)}) collective-permute-start(bf16[64,640]{1,0:T(8,128)(2,1)} %get-tuple-element.43), channel_id=1, source_target_pairs={{0,4},{1,5},{2,6},{3,7},{4,0},{5,1},{6,2},{7,3},{8,12},{9,13},{10,... | collective-permute-start | bytes 245768 | tf_op jit(solution)/shard_map/ppermute | solution.py:647
  10.7 3.5 %collective-permute-start.7 = (bf16[240,256]{1,0:T(8,128)(2,1)}, bf16[240,256]{1,0:T(8,128)(2,1)S(1)}, u32[]{:S(2)}, u32[]{:S(2)}) collective-permute-start(bf16[240,256]{1,0:T(8,128)(2,1)} %get-tuple-element.45), channel_id=1, source_target_pairs={{0,4},{1,5},{2,6},{3,7},{4,0},{5,1},{6,2},{7,3},{8,12},{9,13},{10,... | collective-permute-start | bytes 368648 | tf_op jit(solution)/shard_map/ppermute | solution.py:647
  14.7 1.6 collective-permute-done.1
  18.2 1.6 collective-permute-start.3
  19.8 5.6 %collective-permute-start.12 = (bf16[192,256]{1,0:T(8,128)(2,1)}, bf16[192,256]{1,0:T(8,128)(2,1)S(1)}, u32[]{:S(2)}, u32[]{:S(2)}) collective-permute-start(bf16[192,256]{1,0:T(8,128)(2,1)} %get-tuple-element.50), channel_id=1, source_target_pairs={{0,2},{1,3},{2,0},{3,1},{4,6},{5,7},{6,4},{7,5},{8,10},{9,11},{10,... | collective-permute-start | bytes 294920 | tf_op jit(solution)/shard_map/ppermute | solution.py:647
  25.4 2.1 %collective-permute-start.13 = (bf16[192,256]{1,0:T(8,128)(2,1)}, bf16[192,256]{1,0:T(8,128)(2,1)S(1)}, u32[]{:S(2)}, u32[]{:S(2)}) collective-permute-start(bf16[192,256]{1,0:T(8,128)(2,1)} %get-tuple-element.50), channel_id=1, source_target_pairs={{0,4},{1,5},{2,6},{3,7},{4,0},{5,1},{6,2},{7,3},{8,12},{9,13},{10,... | collective-permute-start | bytes 294920 | tf_op jit(solution)/shard_map/ppermute | solution.py:647
  27.6 2.5 %collective-permute-start.14 = (bf16[192,256]{1,0:T(8,128)(2,1)}, bf16[192,256]{1,0:T(8,128)(2,1)S(1)}, u32[]{:S(2)}, u32[]{:S(2)}) collective-permute-start(bf16[192,256]{1,0:T(8,128)(2,1)} %get-tuple-element.50), channel_id=1, source_target_pairs={{0,6},{1,7},{2,4},{3,5},{4,2},{5,3},{6,0},{7,1},{8,14},{9,15},{10,... | collective-permute-start | bytes 294920 | tf_op jit(solution)/shard_map/ppermute | solution.py:647
  31.1 1.6 collective-permute-start.9
  32.6 2.7 %collective-permute-done.13 = bf16[192,256]{1,0:T(8,128)(2,1)S(1)} collective-permute-done((bf16[192,256]{1,0:T(8,128)(2,1)}, bf16[192,256]{1,0:T(8,128)(2,1)S(1)}, u32[]{:S(2)}, u32[]{:S(2)}) %collective-permute-start.13) | collective-permute-done | bytes 98336 | tf_op jit(solution)/shard_map/ppermute | solution.py:647
  36.3 1.6 collective-permute-start.15
  39.6 10.6 %collective-permute-done.15.refs_6_ = bf16[4,192,256]{2,1,0:T(8,128)(2,1)S(1)} collective-permute-done((bf16[4,192,256]{2,1,0:T(8,128)(2,1)S(1)}, bf16[4,192,256]{2,1,0:T(8,128)(2,1)S(1)}, u32[]{:S(2)}, u32[]{:S(2)}) %collective-permute-start.15) | collective-permute-done | bytes 393248 | tf_op jit(solution)/shard_map/ppermute | solution.py:647
  51.5 13.1 %attention_forward.1 = (bf16[3072,1152]{1,0:T(8,128)(2,1)}, bf16[48,3,64,128]{3,2,1,0:T(8,128)(2,1)}, bf16[3072,384]{1,0:T(8,128)(2,1)}, bf16[512,1152]{1,0:T(8,128)(2,1)}, f32[8,512]{1,0:T(8,128)}) custom-call(s32[4]{0:T(128)} %pad_add_fusion.place_ref, s32[64,128]{1,0:T(8,128)} %constant.44.clone.idx_ref, bf16[48,64,512]{2,1,0:T(8,128)(2,1)} %tok_ref.3, ...), custom_call_target="tpu_custom_call" | custom-call | flops 14495514624 | bytes 15360000 | tf_op jit(solution)/shard_map/attention_forward/pallas_call | solution.py:254
  65.5 22.3 %ffn_first.1 = (f32[3072,512]{1,0:T(8,128)}, bf16[3072,512]{1,0:T(8,128)(2,1)}, bf16[3072,512]{1,0:T(8,128)(2,1)}, bf16[384,512]{1,0:T(8,128)(2,1)}, bf16[2,4,19...) custom-call(s32[4]{0:T(128)} %pad_add_fusion.place_ref, bf16[48,64,512]{2,1,0:T(8,128)(2,1)} %tok_ref.3, ...), custom_call_target="tpu_custom_call" | custom-call | flops 19327352832 | bytes 27648000 | tf_op jit(solution)/shard_map/ffn_first/pallas_call | solution.py:469
  88.7 25.1 %ffn_second.1 = (bf16[48,64,512]{2,1,0:T(8,128)(2,1)}, bf16[3072,512]{1,0:T(8,128)(2,1)}, bf16[3072,384]{1,0:T(8,128)(2,1)}, bf16[2,4,240,256]{3,2,1,0:T(8,128)(...) custom-call(s32[4]{0:T(128)} %pad_add_fusion.place_ref, f32[3072,512]{1,0:T(8,128)} %get-tuple-element.47.refs_0_, ...), custom_call_target="tpu_custom_call" | custom-call | flops 19327352832 | bytes 27648000 | tf_op jit(solution)/shard_map/ffn_second/pallas_call | solution.py:469
  113.8 20.3 %attention_backward.1 = (bf16[48,64,512]{2,1,0:T(8,128)(2,1)}, bf16[2,4,64,640]{3,2,1,0:T(8,128)(2,1)}, bf16[2,4,64,640]{3,2,1,0:T(8,128)(2,1)}) custom-call(s32[4]{0:T(128)} %pad_add_fusion.place_ref, s32[64,128]{1,0:T(8,128)} %constant.44.clone.idx_ref, bf16[48,64,512]{2,1,0:T(8,128)(2,1)} %tok_ref.3, bf16[3072,1152]{1,0:T(8,128)(2,1)} %get-tuple-element.53.qkv_ref, ...), custom_call_target="tpu_custom_call" | custom-call | flops 21743271936 | bytes 18432000 | tf_op jit(solution)/shard_map/attention_backward/pallas_call | solution.py:573
  134.1 11.6 %collective-permute-start.34 = (bf16[2,4,64,640]{3,2,1,0:T(8,128)(2,1)}, bf16[2,4,64,640]{3,2,1,0:T(8,128)(2,1)S(1)}, u32[]{:S(2)}, u32[]{:S(2)}) collective-permute-start(bf16[2,4,64,640]{3,2,1,0:T(8,128)(2,1)} %get-tuple-element.65), channel_id=1, source_target_pairs={{0,8},{8,0},{16,24},{24,16},{1,9},{9,1},{17,25},{25,17},{2,10},{10... | collective-permute-start | bytes 1966088 | tf_op jit(solution)/shard_map/ppermute | solution.py:650
  148.8 1.6 collective-permute-start.35
  151.1 8.3 %collective-permute-done.35 = bf16[4,64,640]{2,1,0:T(8,128)(2,1)S(1)} collective-permute-done((bf16[4,64,640]{2,1,0:T(8,128)(2,1)S(1)}, bf16[4,64,640]{2,1,0:T(8,128)(2,1)S(1)}, u32[]{:S(2)}, u32[]{:S(2)}) %collective-permute-start.35) | collective-permute-done | bytes 327712 | tf_op jit(solution)/shard_map/ppermute | solution.py:647
  161.5 3.5 %collective-permute-start.38 = (bf16[64,640]{1,0:T(8,128)(2,1)S(1)}, bf16[64,640]{1,0:T(8,128)(2,1)S(1)}, u32[]{:S(2)}, u32[]{:S(2)}) collective-permute-start(bf16[64,640]{1,0:T(8,128)(2,1)S(1)} %get-tuple-element.87), channel_id=1, source_target_pairs={{0,6},{1,7},{2,4},{3,5},{4,2},{5,3},{6,0},{7,1},{8,14},{9,15},{10,... | collective-permute-start | bytes 245768 | tf_op jit(solution)/shard_map/ppermute | solution.py:647
  165.1 1.6 collective-permute-start.27
  166.7 3.0 %collective-permute-done.37 = bf16[64,640]{1,0:T(8,128)(2,1)S(1)} collective-permute-done((bf16[64,640]{1,0:T(8,128)(2,1)S(1)}, bf16[64,640]{1,0:T(8,128)(2,1)S(1)}, u32[]{:S(2)}, u32[]{:S(2)}) %collective-permute-start.37) | collective-permute-done | bytes 81952 | tf_op jit(solution)/shard_map/ppermute | solution.py:647
  171.1 1.9 collective-permute-start.20
  174.3 3.5 %collective-permute-done.27 = bf16[4,240,256]{2,1,0:T(8,128)(2,1)S(1)} collective-permute-done((bf16[4,240,256]{2,1,0:T(8,128)(2,1)S(1)}, bf16[4,240,256]{2,1,0:T(8,128)(2,1)S(1)}, u32[]{:S(2)}, u32[]{:S(2)}) %collective-permute-start.27) | collective-permute-done | bytes 491552 | tf_op jit(solution)/shard_map/ppermute | solution.py:647
  179.2 3.3 %collective-permute-start.29 = (bf16[240,256]{1,0:T(8,128)(2,1)S(1)}, bf16[240,256]{1,0:T(8,128)(2,1)S(1)}, u32[]{:S(2)}, u32[]{:S(2)}) collective-permute-start(bf16[240,256]{1,0:T(8,128)(2,1)S(1)} %get-tuple-element.82), channel_id=1, source_target_pairs={{0,4},{1,5},{2,6},{3,7},{4,0},{5,1},{6,2},{7,3},{8,12},{9,13},{10,... | collective-permute-start | bytes 368648 | tf_op jit(solution)/shard_map/ppermute | solution.py:647
  182.5 1.8 collective-permute-done.22
  184.3 2.2 %collective-permute-start.30 = (bf16[240,256]{1,0:T(8,128)(2,1)S(1)}, bf16[240,256]{1,0:T(8,128)(2,1)S(1)}, u32[]{:S(2)}, u32[]{:S(2)}) collective-permute-start(bf16[240,256]{1,0:T(8,128)(2,1)S(1)} %get-tuple-element.81), channel_id=1, source_target_pairs={{0,6},{1,7},{2,4},{3,5},{4,2},{5,3},{6,0},{7,1},{8,14},{9,15},{10,... | collective-permute-start | bytes 368648 | tf_op jit(solution)/shard_map/ppermute | solution.py:647
  186.7 6.3 %collective-permute-done.29 = bf16[240,256]{1,0:T(8,128)(2,1)S(1)} collective-permute-done((bf16[240,256]{1,0:T(8,128)(2,1)S(1)}, bf16[240,256]{1,0:T(8,128)(2,1)S(1)}, u32[]{:S(2)}, u32[]{:S(2)}) %collective-permute-start.29) | collective-permute-done | bytes 122912 | tf_op jit(solution)/shard_map/ppermute | solution.py:647
  193.6 1.6 collective-permute-start.32
  197.1 7.3 %collective-permute-done.24.refs_2_ = bf16[192,256]{1,0:T(8,128)(2,1)S(1)} collective-permute-done((bf16[192,256]{1,0:T(8,128)(2,1)S(1)}, bf16[192,256]{1,0:T(8,128)(2,1)S(1)}, u32[]{:S(2)}, u32[]{:S(2)}) %collective-permute-start.24) | collective-permute-done | bytes 98336 | tf_op jit(solution)/shard_map/ppermute | solution.py:650
  206.4 2.5 %finish.1 = (f32[64,384]{1,0:T(8,128)}, f32[64,384]{1,0:T(8,128)}, f32[64,384]{1,0:T(8,128)}, f32[48,512]{1,0:T(8,128)}, f32[64,1024]{1,0:T(8,128)}, /*index=5*/...) custom-call(s32[4]{0:T(128)} %pad_add_fusion.place_ref, bf16[192,256]{1,0:T(8,128)(2,1)} %copy-done.4, ...), custom_call_target="tpu_custom_call" | custom-call | tf_op jit(solution)/shard_map/finish/pallas_call | solution.py:633
  (135 shorter events, 28.1 us)
Async XLA Ops:
  4.2 10.0 %collective-permute-start = (bf16[64,640]{1,0:T(8,128)(2,1)}, bf16[64,640]{1,0:T(8,128)(2,1)S(1)}, u32[]{:S(2)}, u32[]{:S(2)}) collective-permute-start(bf16[64,640]{1,0:T(8,128)(2,1)} %get-tuple-element.43), channel_id=1, source_target_pairs={{0,2},{1,3},{2,0},{3,1},{4,6},{5,7},{6,4},{7,5},{8,10},{9,11},{10,... | collective-permute-start | bytes 245768 | tf_op jit(solution)/shard_map/ppermute | solution.py:647
  7.2 9.0 %collective-permute-start.1 = (bf16[64,640]{1,0:T(8,128)(2,1)}, bf16[64,640]{1,0:T(8,128)(2,1)S(1)}, u32[]{:S(2)}, u32[]{:S(2)}) collective-permute-start(bf16[64,640]{1,0:T(8,128)(2,1)} %get-tuple-element.43), channel_id=1, source_target_pairs={{0,4},{1,5},{2,6},{3,7},{4,0},{5,1},{6,2},{7,3},{8,12},{9,13},{10,... | collective-permute-start | bytes 245768 | tf_op jit(solution)/shard_map/ppermute | solution.py:647
  9.8 15.6 %collective-permute-start.6 = (bf16[240,256]{1,0:T(8,128)(2,1)}, bf16[240,256]{1,0:T(8,128)(2,1)S(1)}, u32[]{:S(2)}, u32[]{:S(2)}) collective-permute-start(bf16[240,256]{1,0:T(8,128)(2,1)} %get-tuple-element.45), channel_id=1, source_target_pairs={{0,2},{1,3},{2,0},{3,1},{4,6},{5,7},{6,4},{7,5},{8,10},{9,11},{10,... | collective-permute-start | bytes 368648 | tf_op jit(solution)/shard_map/ppermute | solution.py:647
  10.7 16.9 %collective-permute-start.7 = (bf16[240,256]{1,0:T(8,128)(2,1)}, bf16[240,256]{1,0:T(8,128)(2,1)S(1)}, u32[]{:S(2)}, u32[]{:S(2)}) collective-permute-start(bf16[240,256]{1,0:T(8,128)(2,1)} %get-tuple-element.45), channel_id=1, source_target_pairs={{0,4},{1,5},{2,6},{3,7},{4,0},{5,1},{6,2},{7,3},{8,12},{9,13},{10,... | collective-permute-start | bytes 368648 | tf_op jit(solution)/shard_map/ppermute | solution.py:647
  14.2 15.9 %collective-permute-start.8 = (bf16[240,256]{1,0:T(8,128)(2,1)}, bf16[240,256]{1,0:T(8,128)(2,1)S(1)}, u32[]{:S(2)}, u32[]{:S(2)}) collective-permute-start(bf16[240,256]{1,0:T(8,128)(2,1)} %get-tuple-element.45), channel_id=1, source_target_pairs={{0,6},{1,7},{2,4},{3,5},{4,2},{5,3},{6,0},{7,1},{8,14},{9,15},{10,... | collective-permute-start | bytes 368648 | tf_op jit(solution)/shard_map/ppermute | solution.py:647
  18.2 19.6 %collective-permute-start.3 = (bf16[4,64,640]{2,1,0:T(8,128)(2,1)S(1)}, bf16[4,64,640]{2,1,0:T(8,128)(2,1)S(1)}, u32[]{:S(2)}, u32[]{:S(2)}) collective-permute-start(bf16[4,64,640]{2,1,0:T(8,128)(2,1)S(1)} %pad_maximum_fusion.2.z_ref), channel_id=1, source_target_pairs={{0,1},{1,0},{2,3},{3,2},{4,5},{5,4},{6,7},{7,6},{8,9},{9,8},{10,11... | collective-permute-start | bytes 983048 | tf_op jit(solution)/shard_map/ppermute | solution.py:647
  19.8 12.8 %collective-permute-start.12 = (bf16[192,256]{1,0:T(8,128)(2,1)}, bf16[192,256]{1,0:T(8,128)(2,1)S(1)}, u32[]{:S(2)}, u32[]{:S(2)}) collective-permute-start(bf16[192,256]{1,0:T(8,128)(2,1)} %get-tuple-element.50), channel_id=1, source_target_pairs={{0,2},{1,3},{2,0},{3,1},{4,6},{5,7},{6,4},{7,5},{8,10},{9,11},{10,... | collective-permute-start | bytes 294920 | tf_op jit(solution)/shard_map/ppermute | solution.py:647
  25.4 9.9 %collective-permute-start.13 = (bf16[192,256]{1,0:T(8,128)(2,1)}, bf16[192,256]{1,0:T(8,128)(2,1)S(1)}, u32[]{:S(2)}, u32[]{:S(2)}) collective-permute-start(bf16[192,256]{1,0:T(8,128)(2,1)} %get-tuple-element.50), channel_id=1, source_target_pairs={{0,4},{1,5},{2,6},{3,7},{4,0},{5,1},{6,2},{7,3},{8,12},{9,13},{10,... | collective-permute-start | bytes 294920 | tf_op jit(solution)/shard_map/ppermute | solution.py:647
  31.1 19.1 %collective-permute-start.9 = (bf16[4,240,256]{2,1,0:T(8,128)(2,1)S(1)}, bf16[4,240,256]{2,1,0:T(8,128)(2,1)S(1)}, u32[]{:S(2)}, u32[]{:S(2)}) collective-permute-start(bf16[4,240,256]{2,1,0:T(8,128)(2,1)S(1)} %pad_maximum_fusion.refs_3_), channel_id=1, source_target_pairs={{0,1},{1,0},{2,3},{3,2},{4,5},{5,4},{6,7},{7,6},{8,9},{9,8},{10,11... | collective-permute-start | bytes 1474568 | tf_op jit(solution)/shard_map/ppermute | solution.py:647
  36.3 13.9 %collective-permute-start.15 = (bf16[4,192,256]{2,1,0:T(8,128)(2,1)S(1)}, bf16[4,192,256]{2,1,0:T(8,128)(2,1)S(1)}, u32[]{:S(2)}, u32[]{:S(2)}) collective-permute-start(bf16[4,192,256]{2,1,0:T(8,128)(2,1)S(1)} %pad_maximum_fusion.1.refs_5_), channel_id=1, source_target_pairs={{0,1},{1,0},{2,3},{3,2},{4,5},{5,4},{6,7},{7,6},{8,9},{9,8},{10,11... | collective-permute-start | bytes 1179656 | tf_op jit(solution)/shard_map/ppermute | solution.py:647
  37.8 12.9 %collective-permute-start.5 = (bf16[4,64,640]{2,1,0:T(8,128)(2,1)S(1)}, bf16[4,64,640]{2,1,0:T(8,128)(2,1)S(1)}, u32[]{:S(2)}, u32[]{:S(2)}) collective-permute-start(bf16[4,64,640]{2,1,0:T(8,128)(2,1)S(1)} %collective-permute-done.3.x_ref), channel_id=1, source_target_pairs={{0,8},{8,0},{16,24},{24,16},{1,9},{9,1},{17,25},{25,17},{2,10},{10... | collective-permute-start | bytes 983048 | tf_op jit(solution)/shard_map/ppermute | solution.py:650
  38.3 49.5 %collective-permute-start.16 = (bf16[4,192,256]{2,1,0:T(8,128)(2,1)S(1)}, bf16[4,192,256]{2,1,0:T(8,128)(2,1)S(1)}, u32[]{:S(2)}, u32[]{:S(2)}) collective-permute-start(bf16[4,192,256]{2,1,0:T(8,128)(2,1)S(1)} %pad_maximum_fusion.1.refs_5_), channel_id=1, source_target_pairs={{0,8},{8,0},{16,24},{24,16},{1,9},{9,1},{17,25},{25,17},{2,10},{10... | collective-permute-start | bytes 1179656 | tf_op jit(solution)/shard_map/ppermute | solution.py:650
  39.5 25.1 %collective-permute-start.10 = (bf16[4,240,256]{2,1,0:T(8,128)(2,1)S(1)}, bf16[4,240,256]{2,1,0:T(8,128)(2,1)S(1)}, u32[]{:S(2)}, u32[]{:S(2)}) collective-permute-start(bf16[4,240,256]{2,1,0:T(8,128)(2,1)S(1)} %pad_maximum_fusion.refs_3_), channel_id=1, source_target_pairs={{0,8},{8,0},{16,24},{24,16},{1,9},{9,1},{17,25},{25,17},{2,10},{10... | collective-permute-start | bytes 1474568 | tf_op jit(solution)/shard_map/ppermute | solution.py:650
  50.2 37.6 %collective-permute-start.17 = (bf16[4,192,256]{2,1,0:T(8,128)(2,1)S(1)}, bf16[4,192,256]{2,1,0:T(8,128)(2,1)S(1)}, u32[]{:S(2)}, u32[]{:S(2)}) collective-permute-start(bf16[4,192,256]{2,1,0:T(8,128)(2,1)S(1)} %collective-permute-done.15.refs_6_), channel_id=1, source_target_pairs={{0,8},{8,0},{16,24},{24,16},{1,9},{9,1},{17,25},{25,17},{2,10},{10... | collective-permute-start | bytes 1179656 | tf_op jit(solution)/shard_map/ppermute | solution.py:650
  50.2 14.3 %collective-permute-start.11 = (bf16[4,240,256]{2,1,0:T(8,128)(2,1)S(1)}, bf16[4,240,256]{2,1,0:T(8,128)(2,1)S(1)}, u32[]{:S(2)}, u32[]{:S(2)}) collective-permute-start(bf16[4,240,256]{2,1,0:T(8,128)(2,1)S(1)} %collective-permute-done.9.refs_4_), channel_id=1, source_target_pairs={{0,8},{8,0},{16,24},{24,16},{1,9},{9,1},{17,25},{25,17},{2,10},{10... | collective-permute-start | bytes 1474568 | tf_op jit(solution)/shard_map/ppermute | solution.py:650
  134.1 13.6 %collective-permute-start.34 = (bf16[2,4,64,640]{3,2,1,0:T(8,128)(2,1)}, bf16[2,4,64,640]{3,2,1,0:T(8,128)(2,1)S(1)}, u32[]{:S(2)}, u32[]{:S(2)}) collective-permute-start(bf16[2,4,64,640]{3,2,1,0:T(8,128)(2,1)} %get-tuple-element.65), channel_id=1, source_target_pairs={{0,8},{8,0},{16,24},{24,16},{1,9},{9,1},{17,25},{25,17},{2,10},{10... | collective-permute-start | bytes 1966088 | tf_op jit(solution)/shard_map/ppermute | solution.py:650
  145.8 19.1 %collective-permute-start.26 = (bf16[2,4,240,256]{3,2,1,0:T(8,128)(2,1)S(1)}, bf16[2,4,240,256]{3,2,1,0:T(8,128)(2,1)S(1)}, u32[]{:S(2)}, u32[]{:S(2)}) collective-permute-start(bf16[2,4,240,256]{3,2,1,0:T(8,128)(2,1)S(1)} %copy-done.17), channel_id=1, source_target_pairs={{0,8},{8,0},{16,24},{24,16},{1,9},{9,1},{17,25},{25,17},{2,10},{10... | collective-permute-start | bytes 2949128 | tf_op jit(solution)/shard_map/ppermute | solution.py:650
  148.8 10.6 %collective-permute-start.35 = (bf16[4,64,640]{2,1,0:T(8,128)(2,1)S(1)}, bf16[4,64,640]{2,1,0:T(8,128)(2,1)S(1)}, u32[]{:S(2)}, u32[]{:S(2)}) collective-permute-start(bf16[4,64,640]{2,1,0:T(8,128)(2,1)S(1)} %fusion.2), channel_id=1, source_target_pairs={{0,1},{1,0},{2,3},{3,2},{4,5},{5,4},{6,7},{7,6},{8,9},{9,8},{10,11... | collective-permute-start | bytes 983048 | tf_op jit(solution)/shard_map/ppermute | solution.py:647
  150.5 20.4 %collective-permute-start.19 = (bf16[4,192,256]{2,1,0:T(8,128)(2,1)S(1)}, bf16[4,192,256]{2,1,0:T(8,128)(2,1)S(1)}, u32[]{:S(2)}, u32[]{:S(2)}) collective-permute-start(bf16[4,192,256]{2,1,0:T(8,128)(2,1)S(1)} %fusion.1), channel_id=1, source_target_pairs={{0,1},{1,0},{2,3},{3,2},{4,5},{5,4},{6,7},{7,6},{8,9},{9,8},{10,11... | collective-permute-start | bytes 1179656 | tf_op jit(solution)/shard_map/ppermute | solution.py:647
  161.5 8.2 %collective-permute-start.37 = (bf16[64,640]{1,0:T(8,128)(2,1)S(1)}, bf16[64,640]{1,0:T(8,128)(2,1)S(1)}, u32[]{:S(2)}, u32[]{:S(2)}) collective-permute-start(bf16[64,640]{1,0:T(8,128)(2,1)S(1)} %get-tuple-element.88), channel_id=1, source_target_pairs={{0,4},{1,5},{2,6},{3,7},{4,0},{5,1},{6,2},{7,3},{8,12},{9,13},{10,... | collective-permute-start | bytes 245768 | tf_op jit(solution)/shard_map/ppermute | solution.py:647
  165.1 12.7 %collective-permute-start.27 = (bf16[4,240,256]{2,1,0:T(8,128)(2,1)S(1)}, bf16[4,240,256]{2,1,0:T(8,128)(2,1)S(1)}, u32[]{:S(2)}, u32[]{:S(2)}) collective-permute-start(bf16[4,240,256]{2,1,0:T(8,128)(2,1)S(1)} %fusion), channel_id=1, source_target_pairs={{0,1},{1,0},{2,3},{3,2},{4,5},{5,4},{6,7},{7,6},{8,9},{9,8},{10,11... | collective-permute-start | bytes 1474568 | tf_op jit(solution)/shard_map/ppermute | solution.py:647
  169.8 23.8 %collective-permute-start.39 = (bf16[64,640]{1,0:T(8,128)(2,1)S(1)}, bf16[64,640]{1,0:T(8,128)(2,1)S(1)}, u32[]{:S(2)}, u32[]{:S(2)}) collective-permute-start(bf16[64,640]{1,0:T(8,128)(2,1)S(1)} %fusion.14.refs_8_), channel_id=1, source_target_pairs={{0,8},{8,0},{16,24},{24,16},{1,9},{9,1},{17,25},{25,17},{2,10},{10... | collective-permute-start | bytes 245768 | tf_op jit(solution)/shard_map/ppermute | solution.py:650
  169.8 25.3 %collective-permute-start.40 = (bf16[64,640]{1,0:T(8,128)(2,1)S(1)}, bf16[64,640]{1,0:T(8,128)(2,1)S(1)}, u32[]{:S(2)}, u32[]{:S(2)}) collective-permute-start(bf16[64,640]{1,0:T(8,128)(2,1)S(1)} %fusion.14.refs_8_), channel_id=1, source_target_pairs={{0,16},{8,24},{16,0},{24,8},{1,17},{9,25},{17,1},{25,9},{2,18},{10... | collective-permute-start | bytes 245768 | tf_op jit(solution)/shard_map/ppermute | solution.py:650
  178.3 8.2 %collective-permute-start.28 = (bf16[240,256]{1,0:T(8,128)(2,1)S(1)}, bf16[240,256]{1,0:T(8,128)(2,1)S(1)}, u32[]{:S(2)}, u32[]{:S(2)}) collective-permute-start(bf16[240,256]{1,0:T(8,128)(2,1)S(1)} %get-tuple-element.80), channel_id=1, source_target_pairs={{0,2},{1,3},{2,0},{3,1},{4,6},{5,7},{6,4},{7,5},{8,10},{9,11},{10,... | collective-permute-start | bytes 368648 | tf_op jit(solution)/shard_map/ppermute | solution.py:647
  179.2 13.7 %collective-permute-start.29 = (bf16[240,256]{1,0:T(8,128)(2,1)S(1)}, bf16[240,256]{1,0:T(8,128)(2,1)S(1)}, u32[]{:S(2)}, u32[]{:S(2)}) collective-permute-start(bf16[240,256]{1,0:T(8,128)(2,1)S(1)} %get-tuple-element.82), channel_id=1, source_target_pairs={{0,4},{1,5},{2,6},{3,7},{4,0},{5,1},{6,2},{7,3},{8,12},{9,13},{10,... | collective-permute-start | bytes 368648 | tf_op jit(solution)/shard_map/ppermute | solution.py:647
  184.3 8.6 %collective-permute-start.30 = (bf16[240,256]{1,0:T(8,128)(2,1)S(1)}, bf16[240,256]{1,0:T(8,128)(2,1)S(1)}, u32[]{:S(2)}, u32[]{:S(2)}) collective-permute-start(bf16[240,256]{1,0:T(8,128)(2,1)S(1)} %get-tuple-element.81), channel_id=1, source_target_pairs={{0,6},{1,7},{2,4},{3,5},{4,2},{5,3},{6,0},{7,1},{8,14},{9,15},{10,... | collective-permute-start | bytes 368648 | tf_op jit(solution)/shard_map/ppermute | solution.py:647
  186.6 8.6 %collective-permute-start.41 = (bf16[64,640]{1,0:T(8,128)(2,1)S(1)}, bf16[64,640]{1,0:T(8,128)(2,1)S(1)}, u32[]{:S(2)}, u32[]{:S(2)}) collective-permute-start(bf16[64,640]{1,0:T(8,128)(2,1)S(1)} %fusion.14.refs_8_), channel_id=1, source_target_pairs={{0,24},{8,16},{16,8},{24,0},{1,25},{9,17},{17,9},{25,1},{2,26},{10... | collective-permute-start | bytes 245768 | tf_op jit(solution)/shard_map/ppermute | solution.py:650
  193.0 12.0 %collective-permute-start.31 = (bf16[240,256]{1,0:T(8,128)(2,1)S(1)}, bf16[240,256]{1,0:T(8,128)(2,1)S(1)}, u32[]{:S(2)}, u32[]{:S(2)}) collective-permute-start(bf16[240,256]{1,0:T(8,128)(2,1)S(1)} %fusion.6.refs_4_), channel_id=1, source_target_pairs={{0,8},{8,0},{16,24},{24,16},{1,9},{9,1},{17,25},{25,17},{2,10},{10... | collective-permute-start | bytes 368648 | tf_op jit(solution)/shard_map/ppermute | solution.py:650
  193.6 11.4 %collective-permute-start.32 = (bf16[240,256]{1,0:T(8,128)(2,1)S(1)}, bf16[240,256]{1,0:T(8,128)(2,1)S(1)}, u32[]{:S(2)}, u32[]{:S(2)}) collective-permute-start(bf16[240,256]{1,0:T(8,128)(2,1)S(1)} %fusion.6.refs_4_), channel_id=1, source_target_pairs={{0,16},{8,24},{16,0},{24,8},{1,17},{9,25},{17,1},{25,9},{2,18},{10... | collective-permute-start | bytes 368648 | tf_op jit(solution)/shard_map/ppermute | solution.py:650
  195.2 9.9 %collective-permute-start.33 = (bf16[240,256]{1,0:T(8,128)(2,1)S(1)}, bf16[240,256]{1,0:T(8,128)(2,1)S(1)}, u32[]{:S(2)}, u32[]{:S(2)}) collective-permute-start(bf16[240,256]{1,0:T(8,128)(2,1)S(1)} %fusion.6.refs_4_), channel_id=1, source_target_pairs={{0,24},{8,16},{16,8},{24,0},{1,25},{9,17},{17,9},{25,1},{2,26},{10... | collective-permute-start | bytes 368648 | tf_op jit(solution)/shard_map/ppermute | solution.py:650
  195.2 9.2 %collective-permute-start.24 = (bf16[192,256]{1,0:T(8,128)(2,1)S(1)}, bf16[192,256]{1,0:T(8,128)(2,1)S(1)}, u32[]{:S(2)}, u32[]{:S(2)}) collective-permute-start(bf16[192,256]{1,0:T(8,128)(2,1)S(1)} %fusion.10.refs_0_), channel_id=1, source_target_pairs={{0,16},{8,24},{16,0},{24,8},{1,17},{9,25},{17,1},{25,9},{2,18},{10... | collective-permute-start | bytes 294920 | tf_op jit(solution)/shard_map/ppermute | solution.py:650
  196.6 8.4 %collective-permute-start.25 = (bf16[192,256]{1,0:T(8,128)(2,1)S(1)}, bf16[192,256]{1,0:T(8,128)(2,1)S(1)}, u32[]{:S(2)}, u32[]{:S(2)}) collective-permute-start(bf16[192,256]{1,0:T(8,128)(2,1)S(1)} %fusion.10.refs_0_), channel_id=1, source_target_pairs={{0,24},{8,16},{16,8},{24,0},{1,25},{9,17},{17,9},{25,1},{2,26},{10... | collective-permute-start | bytes 294920 | tf_op jit(solution)/shard_map/ppermute | solution.py:650
  (38 other events, 432.6 us)

commit v2 on v1

--- a/solution.py
+++ b/solution.py
@@ -478,8 +478,8 @@
     )(place, *operands)
 
 
-def attention_backward(G, L, n_z, place_ref, idx_ref, tok_ref, qkv_ref, probs_ref, gm_ref, gh_ref, w_ref, gains_ref, gf_ref,
-                       gt_ref, keep, send, aw, aq, ab, dqkv, dp_ref, ds_ref, small):
+def attention_backward(G, L, n_z, place_ref, idx_ref, tok_ref, qkv_ref, probs_ref, gm_ref, w_ref, gains_ref, gf_ref,
+                       dqkv, keep, send, aw, ab, dp_ref, ds_ref, small):
     step = pl.program_id(0)
     last = pl.num_programs(0) - 1
     R = G * L
@@ -489,12 +489,8 @@
 
     @pl.when(step == 0)
     def _():
-        for ref in (aw, aq, ab):
+        for ref in (aw, ab):
             ref[...] = jnp.zeros_like(ref)
-
-    @pl.when(step * G >= count)
-    def _():
-        gt_ref[...] = jnp.zeros_like(gt_ref)
 
     @pl.when(step * G < count)
     def _():
@@ -521,14 +517,7 @@
                 dqkv[rows, cols[p][1]] = nn(low, split_heads(qkv_ref[rows, cols[p][0]])).astype(bf16)
                 dqkv[rows, cols[p][0]] = join_heads(tn(low, qkv_ref[rows, cols[p][1]])).astype(bf16)
         x = tok_ref[...].reshape(R, D).astype(f32)
-        scale = inverse_rms(x)
-        xs = x * scale
-        aw[...] += tn((xs * gains_ref[0:1, :]).astype(bf16), dqkv[...])
-        g = nt(dqkv[...], w_ref[...])
-        aq[...] += row_sums(g * xs)
-        g = g * gains_ref[0:1, :]
-        dot = jnp.mean(g * xs, axis=-1, keepdims=True)
-        gt_ref[...] = (gh_ref[...].astype(f32) + scale * (g - xs * dot)).astype(bf16).reshape(G, L, D)
+        aw[...] += tn((x * inverse_rms(x) * gains_ref[0:1, :]).astype(bf16), dqkv[...])
 
     @pl.when(step == last)
     def _():
@@ -536,6 +525,7 @@
         ds, n_b, rest = D // n_f, BUCKETS // n_f, 3 * INNER - CUT
         ids = idx_ref[...]
         low = lane_low((1, PAIR))
+        lane = lax.broadcasted_iota(jnp.int32, (1, PAIR), 1)
         small[...] = jnp.zeros_like(small)
         for p in range(PAIRS):
             t = ab[p]
@@ -544,13 +534,12 @@
                 one = jnp.sum(jnp.where(low, by_lane, 0.0), axis=1, keepdims=True)
                 two = jnp.sum(jnp.where(low, 0.0, by_lane), axis=1, keepdims=True)
                 row = b // n_b * ds + (b % n_b) * PAIRS + p
-                small[row : row + 1, :] = jnp.where(low, one, two)
-        for i, ref in enumerate((aq, gf_ref)):
-            total = jnp.sum(ref[...], axis=0, keepdims=True)
-            for f in range(n_f):
-                row = f * ds + n_b * PAIRS + i
-                start = f * ds // PAIR * PAIR
-                small[row : row + 1, :] = total[:, start : start + PAIR]
+                small[row : row + 1, :] = jnp.where(lane == 2, one, two)
+        gain = jnp.transpose(gains_ref[...])[:, 0:1]
+        one = jnp.sum(aw[...] * w_ref[...].astype(f32), axis=1, keepdims=True) / gain
+        two = jnp.sum(jnp.transpose(gf_ref[...]), axis=1, keepdims=True)
+        lane = lax.broadcasted_iota(jnp.int32, (D, PAIR), 1)
+        small[...] = jnp.where(lane == 0, one, jnp.where(lane == 1, two, small[...]))
 
         def write(c):
             for xx, k, f in place.shards():
@@ -563,31 +552,67 @@
             pl.when(place.core == c)(functools.partial(write, c))
 
 
-def call_attention_backward(place, n_z, tokens, qkv, probs, gm, gh, w, gains, gf):
+def call_attention_backward(place, n_z, tokens, qkv, probs, gm, w, gains, gf):
     S, L, D = tokens.shape
     G = GROUP
-    R = G * L
     rows = functools.partial(row_spec, G, L)
     pack = (2, n_z, D // (2 * n_z), CUT)
     vm = pltpu.VMEM
     return pl.pallas_call(
         functools.partial(attention_backward, G, L, n_z),
-        out_shape=(sds((S, L, D), bf16), sds(pack, bf16), sds(pack, bf16)),
+        out_shape=(sds((S * L, 3 * INNER), bf16), sds(pack, bf16), sds(pack, bf16)),
         grid_spec=pltpu.PrefetchScalarGridSpec(
             num_scalar_prefetch=1,
             grid=(S // G,),
             in_specs=[whole((L, PAIR)), series_spec(G, tokens.shape), rows(3 * INNER), series_spec(G, probs.shape),
-                      rows(INNER), rows(D), whole(w.shape), whole(gains.shape), whole(gf.shape)],
-            out_specs=[series_spec(G, tokens.shape, True), whole(pack), whole(pack)],
+                      rows(INNER), whole(w.shape), whole(gains.shape), whole(gf.shape)],
+            out_specs=[rows(3 * INNER), whole(pack), whole(pack)],
             scratch_shapes=[
-                vm(w.shape, f32), vm((8, D), f32), vm((PAIRS, L, PAIR), f32), vm((R, 3 * INNER), bf16),
+                vm(w.shape, f32), vm((PAIRS, L, PAIR), f32),
                 vm((G, PAIRS, L, PAIR), f32), vm((G, PAIRS, L, PAIR), bf16), vm((D, PAIR), f32),
             ],
         ),
         compiler_params=params(),
-        cost_estimate=cost(S * L, D * 3 * INNER * 6, S * L * 6000),
+        cost_estimate=cost(S * L, D * 3 * INNER * 4, S * L * 6000),
         name="attention_backward",
-    )(place, jnp.asarray(bucket_table(L)), tokens, qkv, probs, gm, gh, w, gains, gf)
+    )(place, jnp.asarray(bucket_table(L)), tokens, qkv, probs, gm, w, gains, gf)
+
+
+def token_gradient(G, L, place_ref, tok_ref, dqkv_ref, gh_ref, w_ref, gains_ref, gt_ref):
+    step = pl.program_id(0)
+    D = tok_ref.shape[-1]
+
+    @pl.when(step * G >= place_ref[0])
+    def _():
+        gt_ref[...] = jnp.zeros_like(gt_ref)
+
+    @pl.when(step * G < place_ref[0])
+    def _():
+        x = tok_ref[...].reshape(G * L, D).astype(f32)
+        scale = inverse_rms(x)
+        xs = x * scale
+        g = nt(dqkv_ref[...], w_ref[...]) * gains_ref[0:1, :]
+        dot = jnp.mean(g * xs, axis=-1, keepdims=True)
+        gt_ref[...] = (gh_ref[...].astype(f32) + scale * (g - xs * dot)).astype(bf16).reshape(G, L, D)
+
+
+def call_token_gradient(place, tokens, dqkv, gh, w, gains):
+    S, L, D = tokens.shape
+    G = GROUP
+    rows = functools.partial(row_spec, G, L)
+    return pl.pallas_call(
+        functools.partial(token_gradient, G, L),
+        out_shape=sds((S, L, D), bf16),
+        grid_spec=pltpu.PrefetchScalarGridSpec(
+            num_scalar_prefetch=1,
+            grid=(S // G,),
+            in_specs=[series_spec(G, tokens.shape), rows(3 * INNER), rows(D), whole(w.shape), whole(gains.shape)],
+            out_specs=series_spec(G, tokens.shape, True),
+        ),
+        compiler_params=params(),
+        cost_estimate=cost(S * L, D * 3 * INNER * 2, S * L * 5000),
+        name="token_gradient",
+    )(place, tokens, dqkv, gh, w, gains)
 
 
 def tree(values):
@@ -598,7 +623,7 @@
 
 def finish(n_f, n_r, place_ref, *refs):
     packs = [refs[i * n_r : (i + 1) * n_r] for i in range(3)]
-    gq, gk, gv, go, gg, gu, gd, gs = refs[3 * n_r :]
+    gq, gk, gv, go, gg, gu, gd, ga, gf, gb = refs[3 * n_r :]
     core = place_ref[1]
     ds, is_, fh = gq.shape[0], go.shape[0], gd.shape[0] // 2
     half = go.shape[1] // 2
@@ -612,7 +637,12 @@
     gq[...] = one[:, :INNER]
     gk[...] = jnp.concatenate([one[:, INNER:CUT], two[:, : 2 * INNER - CUT]], axis=1)
     gv[...] = two[:, 2 * INNER - CUT : 3 * INNER - CUT]
-    gs[...] = two[:, 3 * INNER - CUT :]
+    small = jnp.transpose(two[:, 3 * INNER - CUT :])
+    ga[...] = small[0]
+    gf[...] = small[1]
+    n_b = BUCKETS // n_f
+    heads = jnp.concatenate([small[2:3], small[3:4]], axis=0)
+    gb[...] = heads[:, : n_b * PAIRS]
     chunks = [halves(packs[0]), halves(packs[1])]
     for which, ref in enumerate((gg, gu)):
         wide = [jnp.concatenate([c[which][:ds], c[which][ds : 2 * ds]], axis=1) for c in chunks]
@@ -649,48 +679,92 @@
     def over_rep(value, distance):
         return lax.ppermute(value, "rep", [(i, i ^ distance) for i in range(n_r)])
 
-    def gather(pack):
-        near = jnp.stack([pack] + [over_fsdp(pack, 2 * k) for k in range(1, n_z)])
-        far = over_fsdp(near, 1)
-        return near, far, over_rep(near, 1), over_rep(far, 1)
-
-    def scatter(keep, send):
-        got = over_rep(send, 1)
+    def along_z(pack):
+        return [pack] + [over_fsdp(pack, 2 * k) for k in range(1, n_z)]
+
+    def halved(keep, got):
         away = (keep[1].astype(f32) + got[1].astype(f32)).astype(bf16)
-        here = keep[0].astype(f32) + got[0].astype(f32) + over_fsdp(away, 1).astype(f32)
-        own = here[0]
-        for k in range(1, n_z):
-            own = own + over_fsdp(here[k].astype(bf16), 2 * k).astype(f32)
-        own = own.astype(bf16)
+        return keep[0].astype(f32) + got[0].astype(f32), away
+
+    def joined(here, got):
+        here = here + got.astype(f32)
+        return here[0], [here[k].astype(bf16) for k in range(1, n_z)]
+
+    def to_z(pieces):
+        return [over_fsdp(piece, 2 * (k + 1)) for k, piece in enumerate(pieces)]
+
+    def summed(own, got):
+        for value in got:
+            own = own + value.astype(f32)
+        return own.astype(bf16)
+
+    def replicas(own):
         return [own] + [over_rep(own, m) for m in range(1, n_r)]
+
+    together = lax.optimization_barrier
 
     def body(tokens, counts, attn_gain, wq, wk, wv, wo, rel_bias, ffn_gain, wg, wu, wd, cotangent):
         S, L, D = tokens.shape
         r, f = lax.axis_index("rep"), lax.axis_index("fsdp")
         place = jnp.stack([counts[0, 0], r % 2, f % 2, f // 2]).astype(jnp.int32)
         pack_a, pack_0, pack_1 = call_prepare(place, n_f, attn_gain, wq, wk, wv, wo, rel_bias, ffn_gain, wg, wu, wd)
-        qkv, probs, mixed, w_all, gains = call_attention_forward(place, tokens, gather(pack_a))
+        near_a = jnp.stack(along_z(pack_a))
+        near_a, pack_0 = together((near_a, pack_0))
+        far_a, near_ac, z_0 = over_fsdp(near_a, 1), over_rep(near_a, 1), along_z(pack_0)
+        far_a, near_ac, z_0, pack_1 = together((far_a, near_ac, z_0, pack_1))
+        far_ac, near_0 = over_rep(far_a, 1), jnp.stack(z_0)
+        far_ac, near_0 = together((far_ac, near_0))
+
+        far_0, near_0c, z_1 = over_fsdp(near_0, 1), over_rep(near_0, 1), along_z(pack_1)
+        qkv, probs, mixed, w_all, gains = call_attention_forward(place, tokens, (near_a, far_a, near_ac, far_ac))
+        qkv, probs, mixed, w_all, gains, far_0, near_0c, z_1 = together(
+            (qkv, probs, mixed, w_all, gains, far_0, near_0c, z_1)
+        )
+        far_0c, near_1 = over_rep(far_0, 1), jnp.stack(z_1)
+        far_0c, near_1 = together((far_0c, near_1))
+
+        far_1, near_1c = over_fsdp(near_1, 1), over_rep(near_1, 1)
         hidden, part, gpart, wo_all, keep_0, send_0 = call_ffn_half(
-            True, place, gather(pack_0), gains, (tokens, cotangent, mixed), S, L, D
+            True, place, (near_0, far_0, near_0c, far_0c), gains, (tokens, cotangent, mixed), S, L, D
         )
-        sums_0 = scatter(keep_0, send_0)
+        hidden, part, gpart, wo_all, keep_0, send_0, far_1, near_1c = together(
+            (hidden, part, gpart, wo_all, keep_0, send_0, far_1, near_1c)
+        )
+        far_1c = over_rep(far_1, 1)
+
+        got_0 = over_rep(send_0, 1)
         layer_out, gh, gm, keep_1, send_1, gf = call_ffn_half(
-            False, place, gather(pack_1), gains, (hidden, cotangent, mixed, part, gpart, wo_all), S, L, D
+            False, place, (near_1, far_1, near_1c, far_1c), gains, (hidden, cotangent, mixed, part, gpart, wo_all), S, L, D
         )
-        sums_1 = scatter(keep_1, send_1)
-        grad_tokens, keep_2, send_2 = call_attention_backward(
-            place, n_z, tokens, qkv, probs, gm, gh, w_all, gains, gf
+        layer_out, gh, gm, keep_1, send_1, gf, got_0 = together((layer_out, gh, gm, keep_1, send_1, gf, got_0))
+        here_0, away_0 = halved(keep_0, got_0)
+        away_0, gm = together((away_0, gm))
+
+        got_0, got_1 = over_fsdp(away_0, 1), over_rep(send_1, 1)
+        dqkv, keep_2, send_2 = call_attention_backward(place, n_z, tokens, qkv, probs, gm, w_all, gains, gf)
+        dqkv, keep_2, send_2, got_0, got_1 = together((dqkv, keep_2, send_2, got_0, got_1))
+        own_0, z_0 = joined(here_0, got_0)
+        here_1, away_1 = halved(keep_1, got_1)
+        dqkv, z_0, away_1 = together((dqkv, z_0, away_1))
+
+        z_0, got_1, got_2 = to_z(z_0), over_fsdp(away_1, 1), over_rep(send_2, 1)
+        grad_tokens = call_token_gradient(place, tokens, dqkv, gh, w_all, gains)
+        grad_tokens, z_0, got_1, got_2 = together((grad_tokens, z_0, got_1, got_2))
+        here_2, away_2 = halved(keep_2, got_2)
+        own_1, z_1 = joined(here_1, got_1)
+        sum_0 = summed(own_0, z_0)
+
+        own_2, z_2 = joined(here_2, over_fsdp(away_2, 1))
+        sum_1 = summed(own_1, to_z(z_1))
+        sum_2 = summed(own_2, to_z(z_2))
+        n_b = BUCKETS // n_f
+        gq, gk, gv, go, gg, gu, gd, grad_attn_gain, grad_ffn_gain, grad_bias = call_finish(
+            place, n_f, n_r, [replicas(value) for value in (sum_0, sum_1, sum_2)],
+            (wq.shape, wk.shape, wv.shape, wo.shape, wg.shape, wu.shape, wd.shape,
+             attn_gain.shape, ffn_gain.shape, (2, n_b * PAIRS)),
         )
-        sums_2 = scatter(keep_2, send_2)
-        ds, n_b = wq.shape[0], BUCKETS // n_f
-        gq, gk, gv, go, gg, gu, gd, small = call_finish(
-            place, n_f, n_r, (sums_0, sums_1, sums_2),
-            (wq.shape, wk.shape, wv.shape, wo.shape, wg.shape, wu.shape, wd.shape, (ds, PAIR)),
-        )
-        grad_bias = small[: n_b * PAIRS, ::HDIM].reshape(-1)
-        gain_rows = small[n_b * PAIRS : n_b * PAIRS + 2].reshape(2, PAIR // ds, ds)
-        gain_rows = lax.dynamic_index_in_dim(gain_rows, f % (PAIR // ds), axis=1, keepdims=False)
-        return (layer_out, grad_tokens, gain_rows[0], gq, gk, gv, go, grad_bias, gain_rows[1], gg, gu, gd)
+        grad_bias = grad_bias.T.reshape(-1)
+        return (layer_out, grad_tokens, grad_attn_gain, gq, gk, gv, go, grad_bias, grad_ffn_gain, gg, gu, gd)
 
     rows, cols, flat = P(("rep", "fsdp"), None, None), P("fsdp", None), P("fsdp")
     return jax.shard_map(

time: 213 us -> 191 us (0.90)
  starting transfers between devices: 61.9 us -> 38.2 us
  Pallas kernels: 85.4 us -> 104 us
  waiting for transfers between devices: 49.5 us -> 38.5 us
  other arithmetic: 6.35 us -> 3.53 us
  local copies, waits for them, and re-layouts: 6.66 us -> 4.52 us
    ppermute x24, starting transfers between devices: 43.3 us -> 30.5 us  [over_fsdp(): return lax.ppermute(value, 'fsdp', [(i, i ^ distance) for i in range(n_f)])]
    pallas_call x0 -> x1, Pallas kernels: none -> 12 us  [call_token_gradient(): pl.pallas_call(functools.partial(token_gradient, G, L), out_shape=sds((S,...]
    ppermute x18, starting transfers between devices: 18.6 us -> 7.76 us  [over_rep(): return lax.ppermute(value, 'rep', [(i, i ^ distance) for i in range(n_r)])]
    ppermute x24, waiting for transfers between devices: 39 us -> 31.3 us  [over_fsdp(): return lax.ppermute(value, 'fsdp', [(i, i ^ distance) for i in range(n_f)])]
    pallas_call x2, Pallas kernels: 47.4 us -> 54.3 us  [call_ffn_half(): pl.pallas_call(functools.partial(ffn_half, G, L, CH, n_z, first), out_sha...]
    ppermute x18, waiting for transfers between devices: 10.5 us -> 7.24 us  [over_rep(): return lax.ppermute(value, 'rep', [(i, i ^ distance) for i in range(n_r)])]
    pallas_call x1, Pallas kernels: 20.3 us -> 18 us  [call_attention_backward(): pl.pallas_call(functools.partial(attention_backward, G, L, n_z), out_shap...]
  transfers between devices with their start and end apart: 42 -> 42, of which waited for: 14 -> 12; matrix products, arithmetic and copies ran while one was open for 3% -> 1% of each run, Pallas kernels for 17% -> 52%
where the time goes in v2:
time: 191 us; the launch traced here: 190 us
  Pallas kernels  104 us (54%)
  waiting for transfers between devices  38.5 us (20%)
  starting transfers between devices  38.2 us (20%)
  local copies, waits for them, and re-layouts  4.52 us (2%)
  other arithmetic  3.53 us (2%)
    pallas_call x2, Pallas kernels, call_ffn_half(): pl.pallas_call(functools.partial(ffn_half, G, L, CH, n_z, first), out_sha...  54.3 us
    ppermute x24, waiting for transfers between devices, over_fsdp(): return lax.ppermute(value, 'fsdp', [(i, i ^ distance) for i in range(n_f)])  31.3 us
    ppermute x24, starting transfers between devices, over_fsdp(): return lax.ppermute(value, 'fsdp', [(i, i ^ distance) for i in range(n_f)])  30.5 us
    pallas_call x1, Pallas kernels, call_attention_backward(): pl.pallas_call(functools.partial(attention_backward, G, L, n_z), out_shap...  18 us
    pallas_call x1, Pallas kernels, call_attention_forward(): pl.pallas_call(functools.partial(attention_forward, G, L, n_z), out_shape...  14.7 us
    pallas_call x1, Pallas kernels, call_token_gradient(): pl.pallas_call(functools.partial(token_gradient, G, L), out_shape=sds((S,...  12 us
    ppermute x18, starting transfers between devices, over_rep(): return lax.ppermute(value, 'rep', [(i, i ^ distance) for i in range(n_r)])  7.76 us
    ppermute x18, waiting for transfers between devices, over_rep(): return lax.ppermute(value, 'rep', [(i, i ^ distance) for i in range(n_r)])  7.24 us
  transfers between devices with their start and end apart: 42, of which 12 were waited for; matrix products, arithmetic and copies ran while one was open for 1% of the time, Pallas kernels for 52%

profile of v2, /device:TPU:0, one launch (start us, length us, event | category | flops | bytes accessed | tf_op | source)
XLA Modules:
  0.0 190.3 jit_solution(935040497718373927)
XLA Ops:
  2.0 2.2 %prepare.1 = (bf16[64,640]{1,0:T(8,128)(2,1)}, bf16[240,256]{1,0:T(8,128)(2,1)}, bf16[192,256]{1,0:T(8,128)(2,1)}) custom-call(s32[4]{0:T(128)} %pad_add_fusion.place_ref, f32[24]{0:T(128)} %bias_ref.1, f32[64,384]{1,0:T(8,128)} %wq.1, f32[64,384]{1,0:T(8,128)} %wk.1, f32[64,384]{1,0:T(8,128)} %wv.1, f32[48,512]{1,0:T(8,128)} %wo.1, f32[64,1024]{1,0:T(8,128)} %wg.1, ...), custom_call_target="tpu_custom_call" | custom-call | tf_op jit(solution)/shard_map/prepare/pallas_call | solution.py:150
  4.2 5.0 %collective-permute-start.2 = (bf16[64,640]{1,0:T(8,128)(2,1)}, bf16[64,640]{1,0:T(8,128)(2,1)S(1)}, u32[]{:S(2)}, u32[]{:S(2)}) collective-permute-start(bf16[64,640]{1,0:T(8,128)(2,1)} %get-tuple-element.102), channel_id=1, source_target_pairs={{0,6},{1,7},{2,4},{3,5},{4,2},{5,3},{6,0},{7,1},{8,14},{9,15},{10,... | collective-permute-start | bytes 245768 | tf_op jit(solution)/shard_map/ppermute | solution.py:677
  9.9 2.6 %collective-permute-done.2 = bf16[64,640]{1,0:T(8,128)(2,1)S(1)} collective-permute-done((bf16[64,640]{1,0:T(8,128)(2,1)}, bf16[64,640]{1,0:T(8,128)(2,1)S(1)}, u32[]{:S(2)}, u32[]{:S(2)}) %collective-permute-start.2) | collective-permute-done | bytes 81952 | tf_op jit(solution)/shard_map/ppermute | solution.py:677
  12.5 3.8 %collective-permute-done.1 = bf16[64,640]{1,0:T(8,128)(2,1)S(1)} collective-permute-done((bf16[64,640]{1,0:T(8,128)(2,1)}, bf16[64,640]{1,0:T(8,128)(2,1)S(1)}, u32[]{:S(2)}, u32[]{:S(2)}) %collective-permute-start.1) | collective-permute-done | bytes 81952 | tf_op jit(solution)/shard_map/ppermute | solution.py:677
  17.3 1.6 collective-permute-start.3
  18.9 2.7 %collective-permute-start.7 = (bf16[240,256]{1,0:T(8,128)(2,1)}, bf16[240,256]{1,0:T(8,128)(2,1)S(1)}, u32[]{:S(2)}, u32[]{:S(2)}) collective-permute-start(bf16[240,256]{1,0:T(8,128)(2,1)} %get-tuple-element.109), channel_id=1, source_target_pairs={{0,6},{1,7},{2,4},{3,5},{4,2},{5,3},{6,0},{7,1},{8,14},{9,15},{10,... | collective-permute-start | bytes 368648 | tf_op jit(solution)/shard_map/ppermute | solution.py:677
  21.6 1.7 collective-permute-start.5
  23.3 3.9 %collective-permute-done.7 = bf16[240,256]{1,0:T(8,128)(2,1)S(1)} collective-permute-done((bf16[240,256]{1,0:T(8,128)(2,1)}, bf16[240,256]{1,0:T(8,128)(2,1)S(1)}, u32[]{:S(2)}, u32[]{:S(2)}) %collective-permute-start.7) | collective-permute-done | bytes 122912 | tf_op jit(solution)/shard_map/ppermute | solution.py:677
  27.2 5.5 %collective-permute-done.6 = bf16[240,256]{1,0:T(8,128)(2,1)S(1)} collective-permute-done((bf16[240,256]{1,0:T(8,128)(2,1)}, bf16[240,256]{1,0:T(8,128)(2,1)S(1)}, u32[]{:S(2)}, u32[]{:S(2)}) %collective-permute-start.6) | collective-permute-done | bytes 122912 | tf_op jit(solution)/shard_map/ppermute | solution.py:677
  32.8 1.6 collective-permute-start.13
  34.4 2.9 %collective-permute-start.11 = (bf16[192,256]{1,0:T(8,128)(2,1)}, bf16[192,256]{1,0:T(8,128)(2,1)S(1)}, u32[]{:S(2)}, u32[]{:S(2)}) collective-permute-start(bf16[192,256]{1,0:T(8,128)(2,1)} %get-tuple-element.124), channel_id=1, source_target_pairs={{0,2},{1,3},{2,0},{3,1},{4,6},{5,7},{6,4},{7,5},{8,10},{9,11},{10,... | collective-permute-start | bytes 294920 | tf_op jit(solution)/shard_map/ppermute | solution.py:677
  39.0 14.7 %attention_forward.1 = (bf16[3072,1152]{1,0:T(8,128)(2,1)}, bf16[48,3,64,128]{3,2,1,0:T(8,128)(2,1)}, bf16[3072,384]{1,0:T(8,128)(2,1)}, bf16[512,1152]{1,0:T(8,128)(2,1)}, f32[8,512]{1,0:T(8,128)}) custom-call(s32[4]{0:T(128)} %pad_add_fusion.place_ref, s32[64,128]{1,0:T(8,128)} %constant.38.clone.idx_ref, bf16[48,64,512]{2,1,0:T(8,128)(2,1)} %tok_ref.5, ...), custom_call_target="tpu_custom_call" | custom-call | flops 14495514624 | bytes 15360000 | tf_op jit(solution)/shard_map/attention_forward/pallas_call | solution.py:254
  54.0 1.7 collective-permute-done.14.refs_6_
  55.8 1.5 collective-permute-start.15
  57.3 25.5 %ffn_first.1 = (f32[3072,512]{1,0:T(8,128)}, bf16[3072,512]{1,0:T(8,128)(2,1)}, bf16[3072,512]{1,0:T(8,128)(2,1)}, bf16[384,512]{1,0:T(8,128)(2,1)}, bf16[2,4,19...) custom-call(s32[4]{0:T(128)} %pad_add_fusion.place_ref, bf16[48,64,512]{2,1,0:T(8,128)(2,1)} %tok_ref.5, ...), custom_call_target="tpu_custom_call" | custom-call | flops 19327352832 | bytes 27648000 | tf_op jit(solution)/shard_map/ffn_first/pallas_call | solution.py:469
  83.5 1.2 collective-permute-done.17.refs_8_
  85.5 28.7 %ffn_second.1 = (bf16[48,64,512]{2,1,0:T(8,128)(2,1)}, bf16[3072,512]{1,0:T(8,128)(2,1)}, bf16[3072,384]{1,0:T(8,128)(2,1)}, bf16[2,4,240,256]{3,2,1,0:T(8,128)(...) custom-call(s32[4]{0:T(128)} %pad_add_fusion.place_ref, f32[3072,512]{1,0:T(8,128)} %get-tuple-element.137.refs_0_, ...), custom_call_target="tpu_custom_call" | custom-call | flops 19327352832 | bytes 27648000 | tf_op jit(solution)/shard_map/ffn_second/pallas_call | solution.py:469
  115.0 18.0 %attention_backward.1 = (bf16[3072,1152]{1,0:T(8,128)(2,1)}, bf16[2,4,64,640]{3,2,1,0:T(8,128)(2,1)}, bf16[2,4,64,640]{3,2,1,0:T(8,128)(2,1)}) custom-call(s32[4]{0:T(128)} %pad_add_fusion.place_ref, s32[64,128]{1,0:T(8,128)} %constant.38.clone.idx_ref, bf16[48,64,512]{2,1,0:T(8,128)(2,1)} %tok_ref.5, bf16[3072,1152]{1,0:T(8,128)(2,1)} %get-tuple-element.151.qkv_ref, ...), custom_call_target="tpu_custom_call" | custom-call | flops 14495514624 | bytes 18432000 | tf_op jit(solution)/shard_map/attention_backward/pallas_call | solution.py:561
  134.5 4.3 %collective-permute-start.23 = (bf16[192,256]{1,0:T(8,128)(2,1)S(1)}, bf16[192,256]{1,0:T(8,128)(2,1)S(1)}, u32[]{:S(2)}, u32[]{:S(2)}) collective-permute-start(bf16[192,256]{1,0:T(8,128)(2,1)S(1)} %get-tuple-element.172), channel_id=1, source_target_pairs={{0,6},{1,7},{2,4},{3,5},{4,2},{5,3},{6,0},{7,1},{8,14},{9,15},{10,... | collective-permute-start | bytes 294920 | tf_op jit(solution)/shard_map/ppermute | solution.py:677
  138.8 1.4 collective-permute-start.24
  140.2 12.0 %token_gradient.1 = bf16[48,64,512]{2,1,0:T(8,128)(2,1)} custom-call(s32[4]{0:T(128)} %pad_add_fusion.place_ref, bf16[48,64,512]{2,1,0:T(8,128)(2,1)} %tok_ref.5, bf16[3072,1152]{1,0:T(8,128)(2,1)} %get-tuple-element.168.dqkv_ref, bf16[3072,512]{1,0:T(8,128)(2,1)} %get-tuple-element.169.gh_ref, bf16[512,1152]{1,0:T(8,128)(2,1)} %get-tuple-element.157.w_ref, ...), custom_call_target="tpu_custom_call" | custom-call | flops 7247757312 | bytes 15360000 | tf_op jit(solution)/shard_map/token_gradient/pallas_call | solution.py:603
  152.4 2.1 %collective-permute-start.27 = (bf16[192,256]{1,0:T(8,128)(2,1)S(1)}, bf16[192,256]{1,0:T(8,128)(2,1)S(1)}, u32[]{:S(2)}, u32[]{:S(2)}) collective-permute-start(bf16[192,256]{1,0:T(8,128)(2,1)S(1)} %fusion.10.refs_0_), channel_id=1, source_target_pairs={{0,16},{8,24},{16,0},{24,8},{1,17},{9,25},{17,1},{25,9},{2,18},{10... | collective-permute-start | bytes 294920 | tf_op jit(solution)/shard_map/ppermute | solution.py:680
  155.0 1.2 collective-permute-start.31
  156.2 7.8 %collective-permute-done.35 = bf16[4,64,640]{2,1,0:T(8,128)(2,1)S(1)} collective-permute-done((bf16[4,64,640]{2,1,0:T(8,128)(2,1)S(1)}, bf16[4,64,640]{2,1,0:T(8,128)(2,1)S(1)}, u32[]{:S(2)}, u32[]{:S(2)}) %collective-permute-start.35) | collective-permute-done | bytes 327712 | tf_op jit(solution)/shard_map/ppermute | solution.py:677
  164.2 1.9 collective-permute-start.36
  166.0 2.6 %collective-permute-start.38 = (bf16[64,640]{1,0:T(8,128)(2,1)S(1)}, bf16[64,640]{1,0:T(8,128)(2,1)S(1)}, u32[]{:S(2)}, u32[]{:S(2)}) collective-permute-start(bf16[64,640]{1,0:T(8,128)(2,1)S(1)} %get-tuple-element.205), channel_id=1, source_target_pairs={{0,6},{1,7},{2,4},{3,5},{4,2},{5,3},{6,0},{7,1},{8,14},{9,15},{10,... | collective-permute-start | bytes 245768 | tf_op jit(solution)/shard_map/ppermute | solution.py:677
  168.6 4.4 %collective-permute-done.30 = bf16[240,256]{1,0:T(8,128)(2,1)S(1)} collective-permute-done((bf16[240,256]{1,0:T(8,128)(2,1)S(1)}, bf16[240,256]{1,0:T(8,128)(2,1)S(1)}, u32[]{:S(2)}, u32[]{:S(2)}) %collective-permute-start.30) | collective-permute-done | bytes 122912 | tf_op jit(solution)/shard_map/ppermute | solution.py:677
  174.2 1.1 collective-permute-start.33
  175.3 3.2 %collective-permute-done.37 = bf16[64,640]{1,0:T(8,128)(2,1)S(1)} collective-permute-done((bf16[64,640]{1,0:T(8,128)(2,1)S(1)}, bf16[64,640]{1,0:T(8,128)(2,1)S(1)}, u32[]{:S(2)}, u32[]{:S(2)}) %collective-permute-start.37) | collective-permute-done | bytes 81952 | tf_op jit(solution)/shard_map/ppermute | solution.py:677
  181.5 1.2 collective-permute-done.41.refs_11_
  182.8 2.4 %collective-permute-done.40.refs_10_ = bf16[64,640]{1,0:T(8,128)(2,1)S(1)} collective-permute-done((bf16[64,640]{1,0:T(8,128)(2,1)S(1)}, bf16[64,640]{1,0:T(8,128)(2,1)S(1)}, u32[]{:S(2)}, u32[]{:S(2)}) %collective-permute-start.40) | collective-permute-done | bytes 81952 | tf_op jit(solution)/shard_map/ppermute | solution.py:680
  186.4 2.5 %finish.1 = (f32[64,384]{1,0:T(8,128)}, f32[64,384]{1,0:T(8,128)}, f32[64,384]{1,0:T(8,128)}, f32[48,512]{1,0:T(8,128)}, f32[64,1024]{1,0:T(8,128)}, /*index=5*/...) custom-call(s32[4]{0:T(128)} %pad_add_fusion.place_ref, ...), custom_call_target="tpu_custom_call" | custom-call | tf_op jit(solution)/shard_map/finish/pallas_call | solution.py:663
  (135 shorter events, 15.5 us)
Async XLA Ops:
  4.2 8.3 %collective-permute-start.2 = (bf16[64,640]{1,0:T(8,128)(2,1)}, bf16[64,640]{1,0:T(8,128)(2,1)S(1)}, u32[]{:S(2)}, u32[]{:S(2)}) collective-permute-start(bf16[64,640]{1,0:T(8,128)(2,1)} %get-tuple-element.102), channel_id=1, source_target_pairs={{0,6},{1,7},{2,4},{3,5},{4,2},{5,3},{6,0},{7,1},{8,14},{9,15},{10,... | collective-permute-start | bytes 245768 | tf_op jit(solution)/shard_map/ppermute | solution.py:677
  9.2 7.1 %collective-permute-start.1 = (bf16[64,640]{1,0:T(8,128)(2,1)}, bf16[64,640]{1,0:T(8,128)(2,1)S(1)}, u32[]{:S(2)}, u32[]{:S(2)}) collective-permute-start(bf16[64,640]{1,0:T(8,128)(2,1)} %get-tuple-element.102), channel_id=1, source_target_pairs={{0,4},{1,5},{2,6},{3,7},{4,0},{5,1},{6,2},{7,3},{8,12},{9,13},{10,... | collective-permute-start | bytes 245768 | tf_op jit(solution)/shard_map/ppermute | solution.py:677
  17.3 15.5 %collective-permute-start.4 = (bf16[4,64,640]{2,1,0:T(8,128)(2,1)S(1)}, bf16[4,64,640]{2,1,0:T(8,128)(2,1)S(1)}, u32[]{:S(2)}, u32[]{:S(2)}) collective-permute-start(bf16[4,64,640]{2,1,0:T(8,128)(2,1)S(1)} %pad_maximum_fusion.2.z_ref), channel_id=1, source_target_pairs={{0,8},{8,0},{16,24},{24,16},{1,9},{9,1},{17,25},{25,17},{2,10},{10... | collective-permute-start | bytes 983048 | tf_op jit(solution)/shard_map/ppermute | solution.py:680
  17.3 15.4 %collective-permute-start.3 = (bf16[4,64,640]{2,1,0:T(8,128)(2,1)S(1)}, bf16[4,64,640]{2,1,0:T(8,128)(2,1)S(1)}, u32[]{:S(2)}, u32[]{:S(2)}) collective-permute-start(bf16[4,64,640]{2,1,0:T(8,128)(2,1)S(1)} %pad_maximum_fusion.2.z_ref), channel_id=1, source_target_pairs={{0,1},{1,0},{2,3},{3,2},{4,5},{5,4},{6,7},{7,6},{8,9},{9,8},{10,11... | collective-permute-start | bytes 983048 | tf_op jit(solution)/shard_map/ppermute | solution.py:677
  18.9 8.3 %collective-permute-start.7 = (bf16[240,256]{1,0:T(8,128)(2,1)}, bf16[240,256]{1,0:T(8,128)(2,1)S(1)}, u32[]{:S(2)}, u32[]{:S(2)}) collective-permute-start(bf16[240,256]{1,0:T(8,128)(2,1)} %get-tuple-element.109), channel_id=1, source_target_pairs={{0,6},{1,7},{2,4},{3,5},{4,2},{5,3},{6,0},{7,1},{8,14},{9,15},{10,... | collective-permute-start | bytes 368648 | tf_op jit(solution)/shard_map/ppermute | solution.py:677
  21.6 11.1 %collective-permute-start.6 = (bf16[240,256]{1,0:T(8,128)(2,1)}, bf16[240,256]{1,0:T(8,128)(2,1)S(1)}, u32[]{:S(2)}, u32[]{:S(2)}) collective-permute-start(bf16[240,256]{1,0:T(8,128)(2,1)} %get-tuple-element.109), channel_id=1, source_target_pairs={{0,4},{1,5},{2,6},{3,7},{4,0},{5,1},{6,2},{7,3},{8,12},{9,13},{10,... | collective-permute-start | bytes 368648 | tf_op jit(solution)/shard_map/ppermute | solution.py:677
  21.6 11.1 %collective-permute-start.5 = (bf16[240,256]{1,0:T(8,128)(2,1)}, bf16[240,256]{1,0:T(8,128)(2,1)S(1)}, u32[]{:S(2)}, u32[]{:S(2)}) collective-permute-start(bf16[240,256]{1,0:T(8,128)(2,1)} %get-tuple-element.109), channel_id=1, source_target_pairs={{0,2},{1,3},{2,0},{3,1},{4,6},{5,7},{6,4},{7,5},{8,10},{9,11},{10,... | collective-permute-start | bytes 368648 | tf_op jit(solution)/shard_map/ppermute | solution.py:677
  32.8 20.9 %collective-permute-start.13 = (bf16[192,256]{1,0:T(8,128)(2,1)}, bf16[192,256]{1,0:T(8,128)(2,1)S(1)}, u32[]{:S(2)}, u32[]{:S(2)}) collective-permute-start(bf16[192,256]{1,0:T(8,128)(2,1)} %get-tuple-element.124), channel_id=1, source_target_pairs={{0,6},{1,7},{2,4},{3,5},{4,2},{5,3},{6,0},{7,1},{8,14},{9,15},{10,... | collective-permute-start | bytes 294920 | tf_op jit(solution)/shard_map/ppermute | solution.py:677
  34.4 19.3 %collective-permute-start.12 = (bf16[192,256]{1,0:T(8,128)(2,1)}, bf16[192,256]{1,0:T(8,128)(2,1)S(1)}, u32[]{:S(2)}, u32[]{:S(2)}) collective-permute-start(bf16[192,256]{1,0:T(8,128)(2,1)} %get-tuple-element.124), channel_id=1, source_target_pairs={{0,4},{1,5},{2,6},{3,7},{4,0},{5,1},{6,2},{7,3},{8,12},{9,13},{10,... | collective-permute-start | bytes 294920 | tf_op jit(solution)/shard_map/ppermute | solution.py:677
  34.4 19.3 %collective-permute-start.11 = (bf16[192,256]{1,0:T(8,128)(2,1)}, bf16[192,256]{1,0:T(8,128)(2,1)S(1)}, u32[]{:S(2)}, u32[]{:S(2)}) collective-permute-start(bf16[192,256]{1,0:T(8,128)(2,1)} %get-tuple-element.124), channel_id=1, source_target_pairs={{0,2},{1,3},{2,0},{3,1},{4,6},{5,7},{6,4},{7,5},{8,10},{9,11},{10,... | collective-permute-start | bytes 294920 | tf_op jit(solution)/shard_map/ppermute | solution.py:677
  38.3 15.4 %collective-permute-start.10 = (bf16[4,240,256]{2,1,0:T(8,128)(2,1)S(1)}, bf16[4,240,256]{2,1,0:T(8,128)(2,1)S(1)}, u32[]{:S(2)}, u32[]{:S(2)}) collective-permute-start(bf16[4,240,256]{2,1,0:T(8,128)(2,1)S(1)} %pad_maximum_fusion.refs_3_), channel_id=1, source_target_pairs={{0,8},{8,0},{16,24},{24,16},{1,9},{9,1},{17,25},{25,17},{2,10},{10... | collective-permute-start | bytes 1474568 | tf_op jit(solution)/shard_map/ppermute | solution.py:680
  38.4 15.4 %collective-permute-start.9 = (bf16[4,240,256]{2,1,0:T(8,128)(2,1)S(1)}, bf16[4,240,256]{2,1,0:T(8,128)(2,1)S(1)}, u32[]{:S(2)}, u32[]{:S(2)}) collective-permute-start(bf16[4,240,256]{2,1,0:T(8,128)(2,1)S(1)} %pad_maximum_fusion.refs_3_), channel_id=1, source_target_pairs={{0,1},{1,0},{2,3},{3,2},{4,5},{5,4},{6,7},{7,6},{8,9},{9,8},{10,11... | collective-permute-start | bytes 1474568 | tf_op jit(solution)/shard_map/ppermute | solution.py:677
  55.7 27.2 %collective-permute-start.16 = (bf16[4,192,256]{2,1,0:T(8,128)(2,1)S(1)}, bf16[4,192,256]{2,1,0:T(8,128)(2,1)S(1)}, u32[]{:S(2)}, u32[]{:S(2)}) collective-permute-start(bf16[4,192,256]{2,1,0:T(8,128)(2,1)S(1)} %pad_maximum_fusion.1.refs_5_), channel_id=1, source_target_pairs={{0,8},{8,0},{16,24},{24,16},{1,9},{9,1},{17,25},{25,17},{2,10},{10... | collective-permute-start | bytes 1179656 | tf_op jit(solution)/shard_map/ppermute | solution.py:680
  55.8 27.1 %collective-permute-start.15 = (bf16[4,192,256]{2,1,0:T(8,128)(2,1)S(1)}, bf16[4,192,256]{2,1,0:T(8,128)(2,1)S(1)}, u32[]{:S(2)}, u32[]{:S(2)}) collective-permute-start(bf16[4,192,256]{2,1,0:T(8,128)(2,1)S(1)} %pad_maximum_fusion.1.refs_5_), channel_id=1, source_target_pairs={{0,1},{1,0},{2,3},{3,2},{4,5},{5,4},{6,7},{7,6},{8,9},{9,8},{10,11... | collective-permute-start | bytes 1179656 | tf_op jit(solution)/shard_map/ppermute | solution.py:677
  83.1 31.2 %collective-permute-start.18 = (bf16[2,4,192,256]{3,2,1,0:T(8,128)(2,1)}, bf16[2,4,192,256]{3,2,1,0:T(8,128)(2,1)S(1)}, u32[]{:S(2)}, u32[]{:S(2)}) collective-permute-start(bf16[2,4,192,256]{3,2,1,0:T(8,128)(2,1)} %get-tuple-element.149), channel_id=1, source_target_pairs={{0,8},{8,0},{16,24},{24,16},{1,9},{9,1},{17,25},{25,17},{2,10},{10... | collective-permute-start | bytes 2359304 | tf_op jit(solution)/shard_map/ppermute | solution.py:680
  114.4 18.7 %collective-permute-start.19 = (bf16[4,192,256]{2,1,0:T(8,128)(2,1)S(1)}, bf16[4,192,256]{2,1,0:T(8,128)(2,1)S(1)}, u32[]{:S(2)}, u32[]{:S(2)}) collective-permute-start(bf16[4,192,256]{2,1,0:T(8,128)(2,1)S(1)} %fusion.1), channel_id=1, source_target_pairs={{0,1},{1,0},{2,3},{3,2},{4,5},{5,4},{6,7},{7,6},{8,9},{9,8},{10,11... | collective-permute-start | bytes 1179656 | tf_op jit(solution)/shard_map/ppermute | solution.py:677
  115.0 18.0 %collective-permute-start.20 = (bf16[2,4,240,256]{3,2,1,0:T(8,128)(2,1)}, bf16[2,4,240,256]{3,2,1,0:T(8,128)(2,1)S(1)}, u32[]{:S(2)}, u32[]{:S(2)}) collective-permute-start(bf16[2,4,240,256]{3,2,1,0:T(8,128)(2,1)} %get-tuple-element.163), channel_id=1, source_target_pairs={{0,8},{8,0},{16,24},{24,16},{1,9},{9,1},{17,25},{25,17},{2,10},{10... | collective-permute-start | bytes 2949128 | tf_op jit(solution)/shard_map/ppermute | solution.py:680
  134.3 17.9 %collective-permute-start.21 = (bf16[192,256]{1,0:T(8,128)(2,1)S(1)}, bf16[192,256]{1,0:T(8,128)(2,1)S(1)}, u32[]{:S(2)}, u32[]{:S(2)}) collective-permute-start(bf16[192,256]{1,0:T(8,128)(2,1)S(1)} %get-tuple-element.170), channel_id=1, source_target_pairs={{0,2},{1,3},{2,0},{3,1},{4,6},{5,7},{6,4},{7,5},{8,10},{9,11},{10,... | collective-permute-start | bytes 294920 | tf_op jit(solution)/shard_map/ppermute | solution.py:677
  134.4 17.8 %collective-permute-start.22 = (bf16[192,256]{1,0:T(8,128)(2,1)S(1)}, bf16[192,256]{1,0:T(8,128)(2,1)S(1)}, u32[]{:S(2)}, u32[]{:S(2)}) collective-permute-start(bf16[192,256]{1,0:T(8,128)(2,1)S(1)} %get-tuple-element.171), channel_id=1, source_target_pairs={{0,4},{1,5},{2,6},{3,7},{4,0},{5,1},{6,2},{7,3},{8,12},{9,13},{10,... | collective-permute-start | bytes 294920 | tf_op jit(solution)/shard_map/ppermute | solution.py:677
  134.5 17.7 %collective-permute-start.23 = (bf16[192,256]{1,0:T(8,128)(2,1)S(1)}, bf16[192,256]{1,0:T(8,128)(2,1)S(1)}, u32[]{:S(2)}, u32[]{:S(2)}) collective-permute-start(bf16[192,256]{1,0:T(8,128)(2,1)S(1)} %get-tuple-element.172), channel_id=1, source_target_pairs={{0,6},{1,7},{2,4},{3,5},{4,2},{5,3},{6,0},{7,1},{8,14},{9,15},{10,... | collective-permute-start | bytes 294920 | tf_op jit(solution)/shard_map/ppermute | solution.py:677
  138.8 13.4 %collective-permute-start.24 = (bf16[4,240,256]{2,1,0:T(8,128)(2,1)S(1)}, bf16[4,240,256]{2,1,0:T(8,128)(2,1)S(1)}, u32[]{:S(2)}, u32[]{:S(2)}) collective-permute-start(bf16[4,240,256]{2,1,0:T(8,128)(2,1)S(1)} %fusion), channel_id=1, source_target_pairs={{0,1},{1,0},{2,3},{3,2},{4,5},{5,4},{6,7},{7,6},{8,9},{9,8},{10,11... | collective-permute-start | bytes 1474568 | tf_op jit(solution)/shard_map/ppermute | solution.py:677
  140.2 12.0 %collective-permute-start.25 = (bf16[2,4,64,640]{3,2,1,0:T(8,128)(2,1)S(1)}, bf16[2,4,64,640]{3,2,1,0:T(8,128)(2,1)S(1)}, u32[]{:S(2)}, u32[]{:S(2)}) collective-permute-start(bf16[2,4,64,640]{3,2,1,0:T(8,128)(2,1)S(1)} %copy-done.19), channel_id=1, source_target_pairs={{0,8},{8,0},{16,24},{24,16},{1,9},{9,1},{17,25},{25,17},{2,10},{10... | collective-permute-start | bytes 1966088 | tf_op jit(solution)/shard_map/ppermute | solution.py:680
  152.3 20.8 %collective-permute-start.28 = (bf16[192,256]{1,0:T(8,128)(2,1)S(1)}, bf16[192,256]{1,0:T(8,128)(2,1)S(1)}, u32[]{:S(2)}, u32[]{:S(2)}) collective-permute-start(bf16[192,256]{1,0:T(8,128)(2,1)S(1)} %fusion.10.refs_0_), channel_id=1, source_target_pairs={{0,24},{8,16},{16,8},{24,0},{1,25},{9,17},{17,9},{25,1},{2,26},{10... | collective-permute-start | bytes 294920 | tf_op jit(solution)/shard_map/ppermute | solution.py:680
  152.4 26.2 %collective-permute-start.27 = (bf16[192,256]{1,0:T(8,128)(2,1)S(1)}, bf16[192,256]{1,0:T(8,128)(2,1)S(1)}, u32[]{:S(2)}, u32[]{:S(2)}) collective-permute-start(bf16[192,256]{1,0:T(8,128)(2,1)S(1)} %fusion.10.refs_0_), channel_id=1, source_target_pairs={{0,16},{8,24},{16,0},{24,8},{1,17},{9,25},{17,1},{25,9},{2,18},{10... | collective-permute-start | bytes 294920 | tf_op jit(solution)/shard_map/ppermute | solution.py:680
  154.6 9.4 %collective-permute-start.35 = (bf16[4,64,640]{2,1,0:T(8,128)(2,1)S(1)}, bf16[4,64,640]{2,1,0:T(8,128)(2,1)S(1)}, u32[]{:S(2)}, u32[]{:S(2)}) collective-permute-start(bf16[4,64,640]{2,1,0:T(8,128)(2,1)S(1)} %fusion.2), channel_id=1, source_target_pairs={{0,1},{1,0},{2,3},{3,2},{4,5},{5,4},{6,7},{7,6},{8,9},{9,8},{10,11... | collective-permute-start | bytes 983048 | tf_op jit(solution)/shard_map/ppermute | solution.py:677
  154.9 9.2 %collective-permute-start.29 = (bf16[240,256]{1,0:T(8,128)(2,1)S(1)}, bf16[240,256]{1,0:T(8,128)(2,1)S(1)}, u32[]{:S(2)}, u32[]{:S(2)}) collective-permute-start(bf16[240,256]{1,0:T(8,128)(2,1)S(1)} %get-tuple-element.198), channel_id=1, source_target_pairs={{0,2},{1,3},{2,0},{3,1},{4,6},{5,7},{6,4},{7,5},{8,10},{9,11},{10,... | collective-permute-start | bytes 368648 | tf_op jit(solution)/shard_map/ppermute | solution.py:677
  155.0 11.1 %collective-permute-start.31 = (bf16[240,256]{1,0:T(8,128)(2,1)S(1)}, bf16[240,256]{1,0:T(8,128)(2,1)S(1)}, u32[]{:S(2)}, u32[]{:S(2)}) collective-permute-start(bf16[240,256]{1,0:T(8,128)(2,1)S(1)} %get-tuple-element.199), channel_id=1, source_target_pairs={{0,6},{1,7},{2,4},{3,5},{4,2},{5,3},{6,0},{7,1},{8,14},{9,15},{10,... | collective-permute-start | bytes 368648 | tf_op jit(solution)/shard_map/ppermute | solution.py:677
  164.0 9.0 %collective-permute-start.30 = (bf16[240,256]{1,0:T(8,128)(2,1)S(1)}, bf16[240,256]{1,0:T(8,128)(2,1)S(1)}, u32[]{:S(2)}, u32[]{:S(2)}) collective-permute-start(bf16[240,256]{1,0:T(8,128)(2,1)S(1)} %get-tuple-element.200), channel_id=1, source_target_pairs={{0,4},{1,5},{2,6},{3,7},{4,0},{5,1},{6,2},{7,3},{8,12},{9,13},{10,... | collective-permute-start | bytes 368648 | tf_op jit(solution)/shard_map/ppermute | solution.py:677
  164.2 9.0 %collective-permute-start.36 = (bf16[64,640]{1,0:T(8,128)(2,1)S(1)}, bf16[64,640]{1,0:T(8,128)(2,1)S(1)}, u32[]{:S(2)}, u32[]{:S(2)}) collective-permute-start(bf16[64,640]{1,0:T(8,128)(2,1)S(1)} %get-tuple-element.204), channel_id=1, source_target_pairs={{0,2},{1,3},{2,0},{3,1},{4,6},{5,7},{6,4},{7,5},{8,10},{9,11},{10,... | collective-permute-start | bytes 245768 | tf_op jit(solution)/shard_map/ppermute | solution.py:677
  166.0 8.1 %collective-permute-start.38 = (bf16[64,640]{1,0:T(8,128)(2,1)S(1)}, bf16[64,640]{1,0:T(8,128)(2,1)S(1)}, u32[]{:S(2)}, u32[]{:S(2)}) collective-permute-start(bf16[64,640]{1,0:T(8,128)(2,1)S(1)} %get-tuple-element.205), channel_id=1, source_target_pairs={{0,6},{1,7},{2,4},{3,5},{4,2},{5,3},{6,0},{7,1},{8,14},{9,15},{10,... | collective-permute-start | bytes 245768 | tf_op jit(solution)/shard_map/ppermute | solution.py:677
  173.2 7.6 %collective-permute-start.34 = (bf16[240,256]{1,0:T(8,128)(2,1)S(1)}, bf16[240,256]{1,0:T(8,128)(2,1)S(1)}, u32[]{:S(2)}, u32[]{:S(2)}) collective-permute-start(bf16[240,256]{1,0:T(8,128)(2,1)S(1)} %fusion.6.refs_4_), channel_id=1, source_target_pairs={{0,24},{8,16},{16,8},{24,0},{1,25},{9,17},{17,9},{25,1},{2,26},{10... | collective-permute-start | bytes 368648 | tf_op jit(solution)/shard_map/ppermute | solution.py:680
  174.2 7.3 %collective-permute-start.33 = (bf16[240,256]{1,0:T(8,128)(2,1)S(1)}, bf16[240,256]{1,0:T(8,128)(2,1)S(1)}, u32[]{:S(2)}, u32[]{:S(2)}) collective-permute-start(bf16[240,256]{1,0:T(8,128)(2,1)S(1)} %fusion.6.refs_4_), channel_id=1, source_target_pairs={{0,16},{8,24},{16,0},{24,8},{1,17},{9,25},{17,1},{25,9},{2,18},{10... | collective-permute-start | bytes 368648 | tf_op jit(solution)/shard_map/ppermute | solution.py:680
  (39 other events, 292.9 us)

commit v3 on v2

--- a/solution.py
+++ b/solution.py
@@ -2,7 +2,6 @@
 
 import jax
 import jax.numpy as jnp
-import numpy as np
 from jax import lax
 from jax.experimental import pallas as pl
 from jax.experimental.pallas import tpu as pltpu
@@ -15,11 +14,15 @@
 CUT = 640
 GROUP = 8
 EPS = 1e-6
-VMEM_LIMIT = 56 * 1024 * 1024
+VMEM_LIMIT = 18 * 1024 * 1024
 bf16, f32 = jnp.bfloat16, jnp.float32
 sds = jax.ShapeDtypeStruct
 
 
+def in_hbm(value):
+    return pltpu.with_memory_space_constraint(value, pltpu.HBM)
+
+
 def nn(a, b):
     return jnp.dot(a, b, preferred_element_type=f32)
 
@@ -32,28 +35,25 @@
     return lax.dot_general(a, b, (((0,), (0,)), ((), ())), preferred_element_type=f32)
 
 
-def distance_bucket(distance, half_count, exact_count):
-    if distance < exact_count:
-        return distance
-    reached = 0
-    for higher in range(1, half_count - exact_count):
-        if distance ** (
-            half_count - exact_count
-        ) * exact_count**higher >= 128**higher * exact_count ** (half_count - exact_count):
-            reached = higher
-    return exact_count + reached
+def bucket_edges():
+    half = BUCKETS // 2
+    exact = half // 2
+    power = half - exact
+    return [
+        min(m for m in range(exact, 129) if m**power * exact**k >= 128**k * exact**power) for k in range(1, power)
+    ]
 
 
 def bucket_table(length):
     half = BUCKETS // 2
-    ids = np.array(
-        [
-            [(half if j > i else 0) + distance_bucket(abs(j - i), half, half // 2) for i in range(length)]
-            for j in range(length)
-        ],
-        dtype=np.int32,
-    )
-    return np.concatenate([ids, ids], axis=1)
+    exact = half // 2
+    shape = (length, PAIR)
+    apart = lax.broadcasted_iota(jnp.int32, shape, 0) - lax.broadcasted_iota(jnp.int32, shape, 1) % HDIM
+    distance = jnp.abs(apart)
+    bucket = jnp.minimum(distance, exact)
+    for edge in bucket_edges():
+        bucket = bucket + (distance >= edge).astype(jnp.int32)
+    return bucket + jnp.where(apart > 0, half, 0)
 
 
 def lane_low(shape):
@@ -101,10 +101,9 @@
     )
 
 
-def prepare(n_f, place_ref, bias_ref, wq, wk, wv, wo, wg, wu, wd, ga, gf, a_ref, p0_ref, p1_ref):
+def prepare_attention(n_f, place_ref, bias_ref, wq, wk, wv, ga, gf, a_ref):
     core = place_ref[1]
-    ds, is_, fh = wq.shape[0], wo.shape[0], wd.shape[0] // 2
-    half = wo.shape[1] // 2
+    ds = wq.shape[0]
     joined = jnp.concatenate([wq[...], wk[...], wv[...]], axis=1)
     row = lax.broadcasted_iota(jnp.int32, (ds, PAIR), 0)
     low = lane_low((1, PAIR))
@@ -124,6 +123,17 @@
         else:
             a_ref[:, : 3 * INNER - CUT] = joined[:, CUT:].astype(bf16)
             a_ref[:, 3 * INNER - CUT :] = small.astype(bf16)
+
+    for c in range(2):
+        pl.when(core == c)(functools.partial(write, c))
+
+
+def prepare_ffn(n_f, place_ref, wo, wg, wu, wd, p0_ref, p1_ref):
+    core = place_ref[1]
+    ds, is_, fh = wg.shape[0], wo.shape[0], wd.shape[0] // 2
+    half = wo.shape[1] // 2
+
+    def write(c):
         cols = slice(c * half, (c + 1) * half)
         for chunk, ref in enumerate((p0_ref, p1_ref)):
             g = interleaved((wg, wu)[c][...], n_f, chunk).astype(bf16)
@@ -144,24 +154,32 @@
     return -(-rows // 16) * 16
 
 
-def call_prepare(place, n_f, attn_gain, wq, wk, wv, wo, rel_bias, ffn_gain, wg, wu, wd):
-    ds, fh, half = wq.shape[0], wd.shape[0] // 2, wo.shape[1] // 2
+def call_prepare_attention(place, n_f, attn_gain, wq, wk, wv, rel_bias, ffn_gain):
     vm, sm = pl.BlockSpec(memory_space=pltpu.VMEM), pl.BlockSpec(memory_space=pltpu.SMEM)
     return pl.pallas_call(
-        functools.partial(prepare, n_f),
-        out_shape=(
-            sds((ds, CUT), bf16),
-            sds((2 * ds + fh + padded(wo.shape[0]), half), bf16),
-            sds((2 * ds + fh, half), bf16),
-        ),
-        in_specs=[sm, sm] + [vm] * 9,
-        out_specs=[vm] * 3,
-        name="prepare",
-    )(place, rel_bias, wq, wk, wv, wo, wg, wu, wd, attn_gain.reshape(1, -1), ffn_gain.reshape(1, -1))
-
-
-def attention_forward(G, L, n_z, place_ref, idx_ref, tok_ref, z_ref, x_ref, zc_ref, xc_ref,
-                      qkv_ref, probs_ref, mixed_ref, w_ref, gains_ref, table_ref, st_ref, small_ref):
+        functools.partial(prepare_attention, n_f),
+        out_shape=sds((wq.shape[0], CUT), bf16),
+        in_specs=[sm, sm] + [vm] * 5,
+        out_specs=vm,
+        name="prepare_attention",
+    )(place, rel_bias, wq, wk, wv, attn_gain.reshape(1, -1), ffn_gain.reshape(1, -1))
+
+
+def call_prepare_ffn(place, n_f, wo, wg, wu, wd):
+    ds, fh, half = wg.shape[0], wd.shape[0] // 2, wo.shape[1] // 2
+    vm, sm = pl.BlockSpec(memory_space=pltpu.VMEM), pl.BlockSpec(memory_space=pltpu.SMEM)
+    return pl.pallas_call(
+        functools.partial(prepare_ffn, n_f),
+        out_shape=(sds((2 * ds + fh + padded(wo.shape[0]), half), bf16), sds((2 * ds + fh, half), bf16)),
+        in_specs=[sm] + [vm] * 4,
+        out_specs=[vm] * 2,
+        name="prepare_ffn",
+    )(place, wo, wg, wu, wd)
+
+
+def attention_forward(G, L, n_z, place_ref, tok_ref, *refs):
+    pieces, refs = refs[:4], refs[4:]
+    all_qkv, all_probs, mixed_ref, w_ref, gains_ref, table_ref, st_ref, small_ref = refs
     step = pl.program_id(0)
     place = Place(place_ref, n_z)
     D = tok_ref.shape[-1]
@@ -171,18 +189,18 @@
 
     def assemble(c):
         for xx, k, f in place.shards():
-            here, there = ((z_ref, zc_ref), (x_ref, xc_ref))[xx]
-            one, two = (here, there) if c == 0 else (there, here)
-            w_ref[at(f, ds), :CUT] = one[k]
-            w_ref[at(f, ds), CUT:] = two[k, :, :rest]
-            small_ref[at(f, ds), :] = two[k, :, rest:].astype(f32)
+            one, two = pieces[xx].at[k], pieces[2 + xx].at[k]
+            one, two = (one, two) if c == 0 else (two, one)
+            w_ref[at(f, ds), :CUT] = one[...]
+            w_ref[at(f, ds), CUT:] = two[:, :rest]
+            small_ref[at(f, ds), :] = two[:, rest:].astype(f32)
 
     @pl.when(step == 0)
     def _():
         for c in range(2):
             pl.when(place.core == c)(functools.partial(assemble, c))
         n_b = BUCKETS // n_f
-        ids = idx_ref[...]
+        ids = bucket_table(L)
         for p in range(PAIRS):
             total = jnp.zeros(ids.shape, f32)
             for b in range(BUCKETS):
@@ -202,6 +220,8 @@
 
     @pl.when(step * G < place.count)
     def _():
+        mixed, qkv_ref = group_rows(mixed_ref, step, G * L), group_rows(all_qkv, step, G * L)
+        probs_ref = all_probs.at[pl.ds(step * G, G)]
         x = tok_ref[...].reshape(G * L, D).astype(f32)
         normed = (x * inverse_rms(x) * gains_ref[0:1, :]).astype(bf16)
         qkv_ref[...] = nn(normed, w_ref[...]).astype(bf16)
@@ -220,7 +240,7 @@
             rows = pl.ds(s * L, L)
             for p in range(PAIRS):
                 v = qkv_ref[rows, pl.ds(2 * INNER + p * PAIR, PAIR)]
-                mixed_ref[rows, pl.ds(p * PAIR, PAIR)] = join_heads(tn(probs_ref[s, p], v)).astype(bf16)
+                mixed[rows, pl.ds(p * PAIR, PAIR)] = join_heads(tn(probs_ref[s, p], v)).astype(bf16)
 
 
 def params():
@@ -228,7 +248,7 @@
 
 
 def whole(shape):
-    return pl.BlockSpec(shape, lambda i, *_: (0,) * len(shape), pipeline_mode=pl.Buffered(1))
+    return pl.BlockSpec(memory_space=pltpu.VMEM)
 
 
 def live_group(i, place, G):
@@ -242,6 +262,10 @@
 
 def row_spec(G, L, width):
     return pl.BlockSpec((G * L, width), lambda i, c: (live_group(i, c, G), 0))
+
+
+def group_rows(ref, step, rows):
+    return ref.at[pl.ds(pl.multiple_of(step * rows, rows), rows), :]
 
 
 def cost(rows, per_row, nbytes, exps=0):
@@ -263,11 +287,11 @@
         grid_spec=pltpu.PrefetchScalarGridSpec(
             num_scalar_prefetch=1,
             grid=(S // G,),
-            in_specs=[whole((L, PAIR)), series_spec(G, tokens.shape)] + [whole(piece.shape) for piece in pieces],
+            in_specs=[series_spec(G, tokens.shape)] + [whole(piece.shape) for piece in pieces],
             out_specs=[
-                row_spec(G, L, 3 * INNER),
-                series_spec(G, (S, PAIRS, L, PAIR)),
-                row_spec(G, L, INNER),
+                whole((S * L, 3 * INNER)),
+                whole((S, PAIRS, L, PAIR)),
+                whole((S * L, INNER)),
                 whole((D, 3 * INNER)),
                 whole((8, D)),
             ],
@@ -280,7 +304,7 @@
         compiler_params=params(),
         cost_estimate=cost(S * L, D * 3 * INNER * 4, S * L * 5000),
         name="attention_forward",
-    )(place, jnp.asarray(bucket_table(L)), tokens, *pieces)
+    )(place, in_hbm(tokens), *pieces)
 
 
 def gelu_parts(v):
@@ -292,26 +316,25 @@
 
 
 def put_weights(place, first, n_z, pieces, wg, wu, wd, wo):
-    z_ref, x_ref, zc_ref, xc_ref = pieces
     n_f = 2 * n_z
     D, FW = wg.shape
     ds, fh, half = D // n_f, FW // n_f, FW // 2
 
     def assemble(c):
         for xx, k, f in place.shards():
-            here, there = ((z_ref, zc_ref), (x_ref, xc_ref))[xx]
+            here, there = pieces[xx].at[k], pieces[2 + xx].at[k]
             for which, piece in enumerate((here, there) if c == 0 else (there, here)):
                 gated = (wg, wu)[which]
-                gated[at(f, ds), :half] = piece[k, :ds, :]
-                gated[at(f, ds), half:] = piece[k, ds : 2 * ds, :]
+                gated[at(f, ds), :half] = piece[:ds, :]
+                gated[at(f, ds), half:] = piece[ds : 2 * ds, :]
                 cols = slice(which * half, (which + 1) * half)
-                wd[at(f, fh), cols] = piece[k, 2 * ds : 2 * ds + fh, :]
+                wd[at(f, fh), cols] = piece[2 * ds : 2 * ds + fh, :]
                 if first:
                     is_ = INNER // n_f
                     if is_ % 16 == 0:
-                        wo[at(f, is_), cols] = piece[k, 2 * ds + fh : 2 * ds + fh + is_, :]
+                        wo[at(f, is_), cols] = piece[2 * ds + fh : 2 * ds + fh + is_, :]
                     else:
-                        wo[f, :, cols] = piece[k, 2 * ds + fh :, :]
+                        wo[f, :, cols] = piece[2 * ds + fh :, :]
 
     for c in range(2):
         pl.when(place.core == c)(functools.partial(assemble, c))
@@ -342,12 +365,13 @@
 
 
 def ffn_half(G, L, CH, n_z, first, place_ref, *refs):
+    pieces, refs = refs[:4], refs[4:]
     if first:
-        (tok_ref, ct_ref, mixed_ref, z_ref, x_ref, zc_ref, xc_ref, gains_ref,
+        (tok_ref, ct_ref, mixed_ref, gains_ref,
          hid_ref, part_ref, gpart_ref, wo_out, keep, send,
          ag, au, ad, wg, wu, wd, n2, gb, gate, up, ga, act, ggr, gur, acc, gn, spread) = refs
     else:
-        (hid_ref, ct_ref, mixed_ref, part_ref, gpart_ref, z_ref, x_ref, zc_ref, xc_ref, gains_ref, wo_in,
+        (hid_ref, ct_ref, mixed_ref, part_ref, gpart_ref, gains_ref, wo_in,
          out_ref, gh_ref, gm_ref, keep, send, gf_ref,
          ag, au, ad, wg, wu, wd, n2, gb, gate, up, ga, act, ggr, gur, acc, gn, ao, spread) = refs
     step = pl.program_id(0)
@@ -359,11 +383,17 @@
     is_ = INNER // n_f
     place = Place(place_ref, n_z)
     count = place.count
+    group = jnp.minimum(step, (count + G - 1) // G - 1)
+    hid_ref, mixed_ref, part_ref, gpart_ref = (
+        group_rows(ref, group, R) for ref in (hid_ref, mixed_ref, part_ref, gpart_ref)
+    )
+    if not first:
+        gm_ref, gh_ref = group_rows(gm_ref, group, R), group_rows(gh_ref, group, R)
 
     @pl.when(step == 0)
     def _():
         wo = (wo_out if is_ % 16 == 0 else spread) if first else None
-        put_weights(place, first, n_z, (z_ref, x_ref, zc_ref, xc_ref), wg, wu, wd, wo)
+        put_weights(place, first, n_z, pieces, wg, wu, wd, wo)
         if first and is_ % 16:
             wo_out[...] = jnp.concatenate([spread[f, :is_, :].astype(f32) for f in range(n_f)], axis=0).astype(bf16)
         for ref in (ag, au, ad) if first else (ag, au, ad, ao, gf_ref):
@@ -441,23 +471,24 @@
     FW = D
     ds, fh, half, is_ = D // n_f, FW // n_f, FW // 2, INNER // n_f
     series = series_spec(G, (S, L, D))
-    piece_specs = [whole(piece.shape) for piece in pieces] + [whole(gains.shape)]
+    piece_specs = [whole(piece.shape) for piece in pieces]
     rows = functools.partial(row_spec, G, L)
     extra = 0 if first else padded(is_)
     pack = (2, n_z, 2 * ds + fh + extra, half)
     if first:
-        in_specs = [series, series, rows(INNER)] + piece_specs
+        tokens, ct, mixed = arrays
+        in_specs = piece_specs + [series, series, whole(mixed.shape), whole(gains.shape)]
         out_shape = [sds((S * L, D), f32), sds((S * L, D), bf16), sds((S * L, D), bf16), sds((INNER, D), bf16),
                      sds(pack, bf16), sds(pack, bf16)]
-        out_specs = [rows(D), rows(D), rows(D), whole((INNER, D)), whole(pack), whole(pack)]
-        operands = arrays + tuple(pieces) + (gains,)
+        out_specs = [whole(shape.shape) for shape in out_shape]
+        operands = tuple(pieces) + (in_hbm(tokens), in_hbm(ct), mixed, gains)
     else:
-        *arrays, wo = arrays
-        in_specs = [rows(D), series, rows(INNER), rows(D), rows(D)] + piece_specs + [whole(wo.shape)]
-        out_shape = [sds((S, L, D), bf16), sds((S * L, D), bf16), sds((S * L, INNER), bf16),
+        hidden, ct, *arrays, wo = arrays
+        in_specs = piece_specs + [whole(hidden.shape), series] + [whole(a.shape) for a in (*arrays, gains, wo)]
+        out_shape = [pltpu.HBM((S, L, D), bf16), sds((S * L, D), bf16), sds((S * L, INNER), bf16),
                      sds(pack, bf16), sds(pack, bf16), sds((8, D), f32)]
-        out_specs = [series_spec(G, (S, L, D), True), rows(D), rows(INNER), whole(pack), whole(pack), whole((8, D))]
-        operands = tuple(arrays) + tuple(pieces) + (gains, wo)
+        out_specs = [series_spec(G, (S, L, D), True)] + [whole(pack)] * 5
+        operands = tuple(pieces) + (hidden, in_hbm(ct), *arrays, gains, wo)
     vm = pltpu.VMEM
     scratch = (
         [vm((D, FW), f32)] * 2 + [vm((FW, D), f32)]
@@ -478,7 +509,7 @@
     )(place, *operands)
 
 
-def attention_backward(G, L, n_z, place_ref, idx_ref, tok_ref, qkv_ref, probs_ref, gm_ref, w_ref, gains_ref, gf_ref,
+def attention_backward(G, L, n_z, place_ref, tok_ref, qkv_ref, probs_ref, gm_ref, w_ref, gains_ref, gf_ref,
                        dqkv, keep, send, aw, ab, dp_ref, ds_ref, small):
     step = pl.program_id(0)
     last = pl.num_programs(0) - 1
@@ -486,6 +517,9 @@
     D = tok_ref.shape[-1]
     place = Place(place_ref, n_z)
     count = place.count
+    group = jnp.minimum(step, (count + G - 1) // G - 1)
+    gm_ref, dqkv, qkv_ref = (group_rows(ref, group, R) for ref in (gm_ref, dqkv, qkv_ref))
+    probs_ref = probs_ref.at[pl.ds(group * G, G)]
 
     @pl.when(step == 0)
     def _():
@@ -523,9 +557,8 @@
     def _():
         n_f = 2 * n_z
         ds, n_b, rest = D // n_f, BUCKETS // n_f, 3 * INNER - CUT
-        ids = idx_ref[...]
+        ids = bucket_table(L)
         low = lane_low((1, PAIR))
-        lane = lax.broadcasted_iota(jnp.int32, (1, PAIR), 1)
         small[...] = jnp.zeros_like(small)
         for p in range(PAIRS):
             t = ab[p]
@@ -533,8 +566,9 @@
                 by_lane = jnp.sum(jnp.where(ids == b, t, 0.0), axis=0, keepdims=True)
                 one = jnp.sum(jnp.where(low, by_lane, 0.0), axis=1, keepdims=True)
                 two = jnp.sum(jnp.where(low, 0.0, by_lane), axis=1, keepdims=True)
-                row = b // n_b * ds + (b % n_b) * PAIRS + p
-                small[row : row + 1, :] = jnp.where(lane == 2, one, two)
+                row = b // n_b * ds + (b % n_b) * HEADS + 2 * p
+                small[row : row + 1, :] = jnp.broadcast_to(one, (1, PAIR))
+                small[row + 1 : row + 2, :] = jnp.broadcast_to(two, (1, PAIR))
         gain = jnp.transpose(gains_ref[...])[:, 0:1]
         one = jnp.sum(aw[...] * w_ref[...].astype(f32), axis=1, keepdims=True) / gain
         two = jnp.sum(jnp.transpose(gf_ref[...]), axis=1, keepdims=True)
@@ -543,10 +577,11 @@
 
         def write(c):
             for xx, k, f in place.shards():
-                one, two = (keep, send) if c == 0 else (send, keep)
-                one[xx, k] = aw[at(f, ds), :CUT].astype(bf16)
-                two[xx, k, :, :rest] = aw[at(f, ds), CUT:].astype(bf16)
-                two[xx, k, :, rest:] = small[at(f, ds), :].astype(bf16)
+                one, two = keep.at[xx, k], send.at[xx, k]
+                one, two = (one, two) if c == 0 else (two, one)
+                one[...] = aw[at(f, ds), :CUT].astype(bf16)
+                two[:, :rest] = aw[at(f, ds), CUT:].astype(bf16)
+                two[:, rest:] = small[at(f, ds), :].astype(bf16)
 
         for c in range(2):
             pl.when(place.core == c)(functools.partial(write, c))
@@ -555,7 +590,6 @@
 def call_attention_backward(place, n_z, tokens, qkv, probs, gm, w, gains, gf):
     S, L, D = tokens.shape
     G = GROUP
-    rows = functools.partial(row_spec, G, L)
     pack = (2, n_z, D // (2 * n_z), CUT)
     vm = pltpu.VMEM
     return pl.pallas_call(
@@ -564,9 +598,9 @@
         grid_spec=pltpu.PrefetchScalarGridSpec(
             num_scalar_prefetch=1,
             grid=(S // G,),
-            in_specs=[whole((L, PAIR)), series_spec(G, tokens.shape), rows(3 * INNER), series_spec(G, probs.shape),
-                      rows(INNER), whole(w.shape), whole(gains.shape), whole(gf.shape)],
-            out_specs=[rows(3 * INNER), whole(pack), whole(pack)],
+            in_specs=[series_spec(G, tokens.shape), whole(qkv.shape), whole(probs.shape),
+                      whole(gm.shape), whole(w.shape), whole(gains.shape), whole(gf.shape)],
+            out_specs=[whole(pack)] * 3,
             scratch_shapes=[
                 vm(w.shape, f32), vm((PAIRS, L, PAIR), f32),
                 vm((G, PAIRS, L, PAIR), f32), vm((G, PAIRS, L, PAIR), bf16), vm((D, PAIR), f32),
@@ -575,12 +609,16 @@
         compiler_params=params(),
         cost_estimate=cost(S * L, D * 3 * INNER * 4, S * L * 6000),
         name="attention_backward",
-    )(place, jnp.asarray(bucket_table(L)), tokens, qkv, probs, gm, w, gains, gf)
-
-
-def token_gradient(G, L, place_ref, tok_ref, dqkv_ref, gh_ref, w_ref, gains_ref, gt_ref):
-    step = pl.program_id(0)
+    )(place, in_hbm(tokens), qkv, probs, gm, w, gains, gf)
+
+
+def token_gradient(G, L, first_step, place_ref, tok_ref, dqkv_ref, gh_ref, w_ref, gains_ref, *refs):
+    gt_ref, done_ref = refs[-2:]
+    done_ref[...] = gains_ref[...]
+    step = pl.program_id(0) + first_step
     D = tok_ref.shape[-1]
+    group = jnp.minimum(step, (place_ref[0] + G - 1) // G - 1)
+    dqkv_ref, gh_ref = group_rows(dqkv_ref, group, G * L), group_rows(gh_ref, group, G * L)
 
     @pl.when(step * G >= place_ref[0])
     def _():
@@ -596,41 +634,45 @@
         gt_ref[...] = (gh_ref[...].astype(f32) + scale * (g - xs * dot)).astype(bf16).reshape(G, L, D)
 
 
-def call_token_gradient(place, tokens, dqkv, gh, w, gains):
+def call_token_gradient(place, tokens, dqkv, gh, w, gains, part, earlier=None):
     S, L, D = tokens.shape
     G = GROUP
-    rows = functools.partial(row_spec, G, L)
+    steps = S // G // 2 if part == 0 else S // G - S // G // 2
+    shift = part * (S // G // 2)
+
+    def rows(width):
+        return pl.BlockSpec((G * L, width), lambda i, c: (live_group(i + shift, c, G), 0))
+
+    def series(every):
+        return pl.BlockSpec((G, L, D), lambda i, c: (i + shift if every else live_group(i + shift, c, G), 0, 0))
+
+    more = [] if earlier is None else [earlier]
     return pl.pallas_call(
-        functools.partial(token_gradient, G, L),
-        out_shape=sds((S, L, D), bf16),
+        functools.partial(token_gradient, G, L, shift),
+        out_shape=(pltpu.HBM((S, L, D), bf16), sds(gains.shape, f32)),
         grid_spec=pltpu.PrefetchScalarGridSpec(
             num_scalar_prefetch=1,
-            grid=(S // G,),
-            in_specs=[series_spec(G, tokens.shape), rows(3 * INNER), rows(D), whole(w.shape), whole(gains.shape)],
-            out_specs=series_spec(G, tokens.shape, True),
+            grid=(steps,),
+            in_specs=[series(False), whole(dqkv.shape), whole(gh.shape), whole(w.shape), whole(gains.shape)]
+            + [pl.BlockSpec(memory_space=pl.ANY)] * len(more),
+            out_specs=(series(True), whole(gains.shape)),
         ),
+        input_output_aliases={6: 0} if more else {},
         compiler_params=params(),
-        cost_estimate=cost(S * L, D * 3 * INNER * 2, S * L * 5000),
+        cost_estimate=cost(S * L // 2, D * 3 * INNER * 2, S * L * 2500),
         name="token_gradient",
-    )(place, tokens, dqkv, gh, w, gains)
-
-
-def tree(values):
-    while len(values) > 1:
-        values = [a + b for a, b in zip(values[0::2], values[1::2])]
-    return values[0]
-
-
-def finish(n_f, n_r, place_ref, *refs):
-    packs = [refs[i * n_r : (i + 1) * n_r] for i in range(3)]
-    gq, gk, gv, go, gg, gu, gd, ga, gf, gb = refs[3 * n_r :]
+    )(place, in_hbm(tokens), dqkv, gh, w, gains, *more)
+
+
+def finish(n_f, place_ref, *refs):
+    packs = [refs[2 * i : 2 * i + 2] for i in range(3)]
+    gq, gk, gv, go, gg, gu, gd, ga, gf, gb = refs[7:]
     core = place_ref[1]
     ds, is_, fh = gq.shape[0], go.shape[0], gd.shape[0] // 2
     half = go.shape[1] // 2
 
     def halves(pack):
-        here = tree([ref[...].astype(f32) for ref in pack[0::2]])
-        there = tree([ref[...].astype(f32) for ref in pack[1::2]])
+        here, there = pack[0][...].astype(f32), pack[1][...].astype(f32)
         return jnp.where(core == 0, here, there), jnp.where(core == 0, there, here)
 
     one, two = halves(packs[2])
@@ -640,9 +682,7 @@
     small = jnp.transpose(two[:, 3 * INNER - CUT :])
     ga[...] = small[0]
     gf[...] = small[1]
-    n_b = BUCKETS // n_f
-    heads = jnp.concatenate([small[2:3], small[3:4]], axis=0)
-    gb[...] = heads[:, : n_b * PAIRS]
+    gb[...] = small[2, : BUCKETS // n_f * HEADS]
     chunks = [halves(packs[0]), halves(packs[1])]
     for which, ref in enumerate((gg, gu)):
         wide = [jnp.concatenate([c[which][:ds], c[which][ds : 2 * ds]], axis=1) for c in chunks]
@@ -657,16 +697,16 @@
         go[:, which * half : (which + 1) * half] = chunks[1][which][2 * ds + fh : 2 * ds + fh + is_]
 
 
-def call_finish(place, n_f, n_r, packs, shapes):
+def call_finish(place, n_f, packs, shapes, after):
     vm, sm = pl.BlockSpec(memory_space=pltpu.VMEM), pl.BlockSpec(memory_space=pltpu.SMEM)
     flat = [piece for pack in packs for piece in pack]
     return pl.pallas_call(
-        functools.partial(finish, n_f, n_r),
+        functools.partial(finish, n_f),
         out_shape=tuple(sds(shape, f32) for shape in shapes),
-        in_specs=[sm] + [vm] * len(flat),
+        in_specs=[sm] + [vm] * len(flat) + [pl.BlockSpec(memory_space=pl.ANY)],
         out_specs=[vm] * len(shapes),
         name="finish",
-    )(place, *flat)
+    )(place, *flat, after)
 
 
 def solution(mesh):
@@ -699,27 +739,32 @@
         return own.astype(bf16)
 
     def replicas(own):
-        return [own] + [over_rep(own, m) for m in range(1, n_r)]
+        distance = 2
+        while distance < n_r:
+            own = (own.astype(f32) + over_rep(own, distance).astype(f32)).astype(bf16)
+            distance *= 2
+        return own, over_rep(own, 1)
 
     together = lax.optimization_barrier
 
     def body(tokens, counts, attn_gain, wq, wk, wv, wo, rel_bias, ffn_gain, wg, wu, wd, cotangent):
         S, L, D = tokens.shape
         r, f = lax.axis_index("rep"), lax.axis_index("fsdp")
-        place = jnp.stack([counts[0, 0], r % 2, f % 2, f // 2]).astype(jnp.int32)
-        pack_a, pack_0, pack_1 = call_prepare(place, n_f, attn_gain, wq, wk, wv, wo, rel_bias, ffn_gain, wg, wu, wd)
-        near_a = jnp.stack(along_z(pack_a))
-        near_a, pack_0 = together((near_a, pack_0))
-        far_a, near_ac, z_0 = over_fsdp(near_a, 1), over_rep(near_a, 1), along_z(pack_0)
+        place = in_hbm(jnp.stack([counts[0, 0], r % 2, f % 2, f // 2]).astype(jnp.int32))
+        pack_a = call_prepare_attention(place, n_f, attn_gain, wq, wk, wv, rel_bias, ffn_gain)
+        pack_0, pack_1 = call_prepare_ffn(place, n_f, wo, wg, wu, wd)
+
+        z_a, pack_0, pack_1 = together((along_z(pack_a), pack_0, pack_1))
+        near_a = jnp.stack(z_a)
+        z_0 = along_z(pack_0)
+        far_a, near_ac = over_fsdp(near_a, 1), over_rep(near_a, 1)
         far_a, near_ac, z_0, pack_1 = together((far_a, near_ac, z_0, pack_1))
         far_ac, near_0 = over_rep(far_a, 1), jnp.stack(z_0)
         far_ac, near_0 = together((far_ac, near_0))
 
         far_0, near_0c, z_1 = over_fsdp(near_0, 1), over_rep(near_0, 1), along_z(pack_1)
         qkv, probs, mixed, w_all, gains = call_attention_forward(place, tokens, (near_a, far_a, near_ac, far_ac))
-        qkv, probs, mixed, w_all, gains, far_0, near_0c, z_1 = together(
-            (qkv, probs, mixed, w_all, gains, far_0, near_0c, z_1)
-        )
+        gains, far_0, near_0c, z_1 = together((gains, far_0, near_0c, z_1))
         far_0c, near_1 = over_rep(far_0, 1), jnp.stack(z_1)
         far_0c, near_1 = together((far_0c, near_1))
 
@@ -727,43 +772,42 @@
         hidden, part, gpart, wo_all, keep_0, send_0 = call_ffn_half(
             True, place, (near_0, far_0, near_0c, far_0c), gains, (tokens, cotangent, mixed), S, L, D
         )
-        hidden, part, gpart, wo_all, keep_0, send_0, far_1, near_1c = together(
-            (hidden, part, gpart, wo_all, keep_0, send_0, far_1, near_1c)
-        )
+        wo_all, keep_0, send_0, far_1, near_1c = together((wo_all, keep_0, send_0, far_1, near_1c))
+
         far_1c = over_rep(far_1, 1)
-
         got_0 = over_rep(send_0, 1)
         layer_out, gh, gm, keep_1, send_1, gf = call_ffn_half(
             False, place, (near_1, far_1, near_1c, far_1c), gains, (hidden, cotangent, mixed, part, gpart, wo_all), S, L, D
         )
-        layer_out, gh, gm, keep_1, send_1, gf, got_0 = together((layer_out, gh, gm, keep_1, send_1, gf, got_0))
+        keep_1, send_1, gf, got_0 = together((keep_1, send_1, gf, got_0))
         here_0, away_0 = halved(keep_0, got_0)
-        away_0, gm = together((away_0, gm))
+        away_0, gf = together((away_0, gf))
 
         got_0, got_1 = over_fsdp(away_0, 1), over_rep(send_1, 1)
         dqkv, keep_2, send_2 = call_attention_backward(place, n_z, tokens, qkv, probs, gm, w_all, gains, gf)
-        dqkv, keep_2, send_2, got_0, got_1 = together((dqkv, keep_2, send_2, got_0, got_1))
+        keep_2, send_2, got_0, got_1 = together((keep_2, send_2, got_0, got_1))
         own_0, z_0 = joined(here_0, got_0)
         here_1, away_1 = halved(keep_1, got_1)
-        dqkv, z_0, away_1 = together((dqkv, z_0, away_1))
+        gains, z_0, away_1 = together((gains, z_0, away_1))
 
         z_0, got_1, got_2 = to_z(z_0), over_fsdp(away_1, 1), over_rep(send_2, 1)
-        grad_tokens = call_token_gradient(place, tokens, dqkv, gh, w_all, gains)
-        grad_tokens, z_0, got_1, got_2 = together((grad_tokens, z_0, got_1, got_2))
+        half_tokens, done = call_token_gradient(place, tokens, dqkv, gh, w_all, gains, 0)
+        done, z_0, got_1, got_2 = together((done, z_0, got_1, got_2))
+        sum_0 = summed(own_0, z_0)
         here_2, away_2 = halved(keep_2, got_2)
         own_1, z_1 = joined(here_1, got_1)
-        sum_0 = summed(own_0, z_0)
-
-        own_2, z_2 = joined(here_2, over_fsdp(away_2, 1))
-        sum_1 = summed(own_1, to_z(z_1))
+        done, away_2, z_1, sum_0 = together((done, away_2, z_1, sum_0))
+        got_2, z_1 = over_fsdp(away_2, 1), to_z(z_1)
+        grad_tokens, done = call_token_gradient(place, tokens, dqkv, gh, w_all, done, 1, half_tokens)
+        done, got_2, z_1 = together((done, got_2, z_1))
+        own_2, z_2 = joined(here_2, got_2)
+        sum_1 = summed(own_1, z_1)
         sum_2 = summed(own_2, to_z(z_2))
-        n_b = BUCKETS // n_f
         gq, gk, gv, go, gg, gu, gd, grad_attn_gain, grad_ffn_gain, grad_bias = call_finish(
-            place, n_f, n_r, [replicas(value) for value in (sum_0, sum_1, sum_2)],
+            place, n_f, [replicas(value) for value in (sum_0, sum_1, sum_2)],
             (wq.shape, wk.shape, wv.shape, wo.shape, wg.shape, wu.shape, wd.shape,
-             attn_gain.shape, ffn_gain.shape, (2, n_b * PAIRS)),
+             attn_gain.shape, ffn_gain.shape, rel_bias.shape), done,
         )
-        grad_bias = grad_bias.T.reshape(-1)
         return (layer_out, grad_tokens, grad_attn_gain, gq, gk, gv, go, grad_bias, grad_ffn_gain, gg, gu, gd)
 
     rows, cols, flat = P(("rep", "fsdp"), None, None), P("fsdp", None), P("fsdp")

time: 191 us -> 169 us (0.88)
  Pallas kernels: 104 us -> 37.8 us
  starting transfers between devices: 38.2 us -> 71.3 us
  waiting for transfers between devices: 38.5 us -> 52.9 us
  local copies, waits for them, and re-layouts: 4.52 us -> 1.32 us
    pallas_call x2, Pallas kernels: 54.3 us -> 14.7 us  [call_ffn_half(): pl.pallas_call(functools.partial(ffn_half, G, L, CH, n_z, first), out_sha...]
    ppermute x24, starting transfers between devices: 30.5 us -> 49.6 us  [over_fsdp(): return lax.ppermute(value, 'fsdp', [(i, i ^ distance) for i in range(n_f)])]
    ppermute x18 -> x15, starting transfers between devices: 7.76 us -> 21.7 us  [over_rep(): return lax.ppermute(value, 'rep', [(i, i ^ distance) for i in range(n_r)])]
    ppermute x24, waiting for transfers between devices: 31.3 us -> 45.1 us  [over_fsdp(): return lax.ppermute(value, 'fsdp', [(i, i ^ distance) for i in range(n_f)])]
    pallas_call x1, Pallas kernels: 18 us -> 5.37 us  [call_attention_backward(): pl.pallas_call(functools.partial(attention_backward, G, L, n_z), out_shap...]
    pallas_call x1, Pallas kernels: 14.7 us -> 3.97 us  [call_attention_forward(): pl.pallas_call(functools.partial(attention_forward, G, L, n_z), out_shape...]
    pallas_call x3 -> x5, Pallas kernels: 16.7 us -> 13.8 us  [the longest x2 7.82 us: call_token_gradient(): pl.pallas_call(functools.partial(token_gradient, G, L, shift), out_shape=...]
    ppermute x18 -> x15, waiting for transfers between devices: 7.24 us -> 7.83 us  [over_rep(): return lax.ppermute(value, 'rep', [(i, i ^ distance) for i in range(n_r)])]
  transfers between devices with their start and end apart: 42 -> 39, of which waited for: 12 -> 19; matrix products, arithmetic and copies ran while one was open for 1% -> 1% of each run, Pallas kernels for 52% -> 20%
where the time goes in v3:
time: 169 us
  starting transfers between devices  71.3 us (42%)
  waiting for transfers between devices  52.9 us (31%)
  Pallas kernels  37.8 us (22%)
  other arithmetic  3.5 us (2%)
    ppermute x24, starting transfers between devices, over_fsdp(): return lax.ppermute(value, 'fsdp', [(i, i ^ distance) for i in range(n_f)])  49.6 us
    ppermute x24, waiting for transfers between devices, over_fsdp(): return lax.ppermute(value, 'fsdp', [(i, i ^ distance) for i in range(n_f)])  45.1 us
    ppermute x15, starting transfers between devices, over_rep(): return lax.ppermute(value, 'rep', [(i, i ^ distance) for i in range(n_r)])  21.7 us
    pallas_call x2, Pallas kernels, call_ffn_half(): pl.pallas_call(functools.partial(ffn_half, G, L, CH, n_z, first), out_sha...  14.7 us
    ppermute x15, waiting for transfers between devices, over_rep(): return lax.ppermute(value, 'rep', [(i, i ^ distance) for i in range(n_r)])  7.83 us
    pallas_call x2, Pallas kernels, call_token_gradient(): pl.pallas_call(functools.partial(token_gradient, G, L, shift), out_shape=...  7.82 us
    pallas_call x1, Pallas kernels, call_attention_backward(): pl.pallas_call(functools.partial(attention_backward, G, L, n_z), out_shap...  5.37 us
    pallas_call x1, Pallas kernels, call_attention_forward(): pl.pallas_call(functools.partial(attention_forward, G, L, n_z), out_shape...  3.97 us
  transfers between devices with their start and end apart: 39, of which 19 were waited for; matrix products, arithmetic and copies ran while one was open for 1% of the time, Pallas kernels for 20%

profile of v3, /device:TPU:0, one launch (start us, length us, event | category | flops | bytes accessed | tf_op | source)
XLA Modules:
  0.0 168.5 jit_solution(18226456298682910675)
XLA Ops:
  1.9 1.7 %prepare_attention.1 = bf16[64,640]{1,0:T(8,128)(2,1)} custom-call(s32[4]{0:T(128)} %pad_add_fusion.place_ref, f32[24]{0:T(128)} %bias_ref.1, f32[64,384]{1,0:T(8,128)} %wq.1, f32[64,384]{1,0:T(8,128)} %wk.1, f32[64,384]{1,0:T(8,128)} %wv.1, f32[1,64]{1,0:T(1,128)} %bitcast.94, f32[1,64]{1,0:T(1,128)} %bitcast.95), custom_call_target="tpu_custom_call" | custom-call | tf_op jit(solution)/shard_map/prepare_attention/pallas_call | solution.py:159
  3.6 5.0 %collective-permute-start.2 = (bf16[64,640]{1,0:T(8,128)(2,1)}, bf16[64,640]{1,0:T(8,128)(2,1)S(1)}, u32[]{:S(2)}, u32[]{:S(2)}) collective-permute-start(bf16[64,640]{1,0:T(8,128)(2,1)} %prepare_attention.1), channel_id=1, source_target_pairs={{0,6},{1,7},{2,4},{3,5},{4,2},{5,3},{6,0},{7,1},{8,14},{9,15},{10,... | collective-permute-start | bytes 245768 | tf_op jit(solution)/shard_map/ppermute | solution.py:717
  9.2 2.0 %prepare_ffn.1 = (bf16[240,256]{1,0:T(8,128)(2,1)}, bf16[192,256]{1,0:T(8,128)(2,1)}) custom-call(s32[4]{0:T(128)} %pad_add_fusion.place_ref, f32[48,512]{1,0:T(8,128)} %wo.1, f32[64,1024]{1,0:T(8,128)} %wg.1, f32[64,1024]{1,0:T(8,128)} %wu.1, f32[128,512]{1,0:T(8,128)} %wd.1), custom_call_target="tpu_custom_call" | custom-call | tf_op jit(solution)/shard_map/prepare_ffn/pallas_call | solution.py:171
  11.9 3.8 %collective-permute-done.1 = bf16[64,640]{1,0:T(8,128)(2,1)S(1)} collective-permute-done((bf16[64,640]{1,0:T(8,128)(2,1)}, bf16[64,640]{1,0:T(8,128)(2,1)S(1)}, u32[]{:S(2)}, u32[]{:S(2)}) %collective-permute-start.1) | collective-permute-done | bytes 81952 | tf_op jit(solution)/shard_map/ppermute | solution.py:717
  18.3 2.6 %collective-permute-start.7 = (bf16[240,256]{1,0:T(8,128)(2,1)}, bf16[240,256]{1,0:T(8,128)(2,1)S(1)}, u32[]{:S(2)}, u32[]{:S(2)}) collective-permute-start(bf16[240,256]{1,0:T(8,128)(2,1)} %get-tuple-element.119), channel_id=1, source_target_pairs={{0,6},{1,7},{2,4},{3,5},{4,2},{5,3},{6,0},{7,1},{8,14},{9,15},{10,... | collective-permute-start | bytes 368648 | tf_op jit(solution)/shard_map/ppermute | solution.py:717
  20.9 1.8 %collective-permute-start.5 = (bf16[240,256]{1,0:T(8,128)(2,1)}, bf16[240,256]{1,0:T(8,128)(2,1)S(1)}, u32[]{:S(2)}, u32[]{:S(2)}) collective-permute-start(bf16[240,256]{1,0:T(8,128)(2,1)} %get-tuple-element.119), channel_id=1, source_target_pairs={{0,2},{1,3},{2,0},{3,1},{4,6},{5,7},{6,4},{7,5},{8,10},{9,11},{10,... | collective-permute-start | bytes 368648 | tf_op jit(solution)/shard_map/ppermute | solution.py:717
  22.7 3.9 %collective-permute-done.7 = bf16[240,256]{1,0:T(8,128)(2,1)S(1)} collective-permute-done((bf16[240,256]{1,0:T(8,128)(2,1)}, bf16[240,256]{1,0:T(8,128)(2,1)S(1)}, u32[]{:S(2)}, u32[]{:S(2)}) %collective-permute-start.7) | collective-permute-done | bytes 122912 | tf_op jit(solution)/shard_map/ppermute | solution.py:717
  26.6 5.5 %collective-permute-done.6 = bf16[240,256]{1,0:T(8,128)(2,1)S(1)} collective-permute-done((bf16[240,256]{1,0:T(8,128)(2,1)}, bf16[240,256]{1,0:T(8,128)(2,1)S(1)}, u32[]{:S(2)}, u32[]{:S(2)}) %collective-permute-start.6) | collective-permute-done | bytes 122912 | tf_op jit(solution)/shard_map/ppermute | solution.py:717
  33.8 2.9 %collective-permute-start.11 = (bf16[192,256]{1,0:T(8,128)(2,1)}, bf16[192,256]{1,0:T(8,128)(2,1)S(1)}, u32[]{:S(2)}, u32[]{:S(2)}) collective-permute-start(bf16[192,256]{1,0:T(8,128)(2,1)} %get-tuple-element.128), channel_id=1, source_target_pairs={{0,2},{1,3},{2,0},{3,1},{4,6},{5,7},{6,4},{7,5},{8,10},{9,11},{10,... | collective-permute-start | bytes 294920 | tf_op jit(solution)/shard_map/ppermute | solution.py:717
  38.3 4.0 %attention_forward.1 = (bf16[3072,1152]{1,0:T(8,128)(2,1)S(1)}, bf16[48,3,64,128]{3,2,1,0:T(8,128)(2,1)S(1)}, bf16[3072,384]{1,0:T(8,128)(2,1)S(1)}, bf16[512,1152]{1,0:T(8,128)(2,1)S(1)}, f32[8,512]{1,0:T(8,128)S(1)}) custom-call(s32[4]{0:T(128)} %pad_add_fusion.place_ref, bf16[48,64,512]{2,1,0:T(8,128)(2,1)} %tok_ref.7, ...), custom_call_target="tpu_custom_call" | custom-call | flops 14495514624 | bytes 15360000 | tf_op jit(solution)/shard_map/attention_forward/pallas_call | solution.py:278
  43.7 7.7 %collective-permute-done.9.refs_1_ = bf16[4,240,256]{2,1,0:T(8,128)(2,1)S(1)} collective-permute-done((bf16[4,240,256]{2,1,0:T(8,128)(2,1)S(1)}, bf16[4,240,256]{2,1,0:T(8,128)(2,1)S(1)}, u32[]{:S(2)}, u32[]{:S(2)}) %collective-permute-start.9) | collective-permute-done | bytes 491552 | tf_op jit(solution)/shard_map/ppermute | solution.py:717
  51.4 1.8 %collective-permute-done.14.refs_3_ = bf16[4,240,256]{2,1,0:T(8,128)(2,1)S(1)} collective-permute-done((bf16[4,240,256]{2,1,0:T(8,128)(2,1)S(1)}, bf16[4,240,256]{2,1,0:T(8,128)(2,1)S(1)}, u32[]{:S(2)}, u32[]{:S(2)}) %collective-permute-start.14) | collective-permute-done | bytes 491552 | tf_op jit(solution)/shard_map/ppermute | solution.py:720
  54.3 6.0 %ffn_first.1 = (f32[3072,512]{1,0:T(8,128)S(1)}, bf16[3072,512]{1,0:T(8,128)(2,1)S(1)}, bf16[3072,512]{1,0:T(8,128)(2,1)S(1)}, bf16[384,512]{1,0:T(8,128)(2,1)S(...) custom-call(s32[4]{0:T(128)} %pad_add_fusion.place_ref, ...), custom_call_target="tpu_custom_call" | custom-call | flops 19327352832 | bytes 27648000 | tf_op jit(solution)/shard_map/ffn_first/pallas_call | solution.py:500
  60.3 4.5 %collective-permute-done.15.refs_1_ = bf16[4,192,256]{2,1,0:T(8,128)(2,1)S(1)} collective-permute-done((bf16[4,192,256]{2,1,0:T(8,128)(2,1)S(1)}, bf16[4,192,256]{2,1,0:T(8,128)(2,1)S(1)}, u32[]{:S(2)}, u32[]{:S(2)}) %collective-permute-start.15) | collective-permute-done | bytes 393248 | tf_op jit(solution)/shard_map/ppermute | solution.py:717
  64.8 12.0 %collective-permute-start.17 = (bf16[4,192,256]{2,1,0:T(8,128)(2,1)S(1)}, bf16[4,192,256]{2,1,0:T(8,128)(2,1)S(1)}, u32[]{:S(2)}, u32[]{:S(2)}) collective-permute-start(bf16[4,192,256]{2,1,0:T(8,128)(2,1)S(1)} %collective-permute-done.15.refs_1_), channel_id=1, source_target_pairs={{0,8},{8,0},{16,24},{24,16},{1,9},{9,1},{17,25},{25,17},{2,10},{10... | collective-permute-start | bytes 1179656 | tf_op jit(solution)/shard_map/ppermute | solution.py:720
  78.1 8.7 %ffn_second.1 = (bf16[48,64,512]{2,1,0:T(8,128)(2,1)}, bf16[3072,512]{1,0:T(8,128)(2,1)S(1)}, bf16[3072,384]{1,0:T(8,128)(2,1)S(1)}, bf16[2,4,240,256]{3,2,1,0:T...) custom-call(s32[4]{0:T(128)} %pad_add_fusion.place_ref, ...), custom_call_target="tpu_custom_call" | custom-call | flops 19327352832 | bytes 27648000 | tf_op jit(solution)/shard_map/ffn_second/pallas_call | solution.py:500
  86.9 18.6 %collective-permute-start.19 = (bf16[4,192,256]{2,1,0:T(8,128)(2,1)S(1)}, bf16[4,192,256]{2,1,0:T(8,128)(2,1)S(1)}, u32[]{:S(2)}, u32[]{:S(2)}) collective-permute-start(bf16[4,192,256]{2,1,0:T(8,128)(2,1)S(1)} %fusion.1), channel_id=1, source_target_pairs={{0,1},{1,0},{2,3},{3,2},{4,5},{5,4},{6,7},{7,6},{8,9},{9,8},{10,11... | collective-permute-start | bytes 1179656 | tf_op jit(solution)/shard_map/ppermute | solution.py:717
  105.5 5.4 %attention_backward.1 = (bf16[3072,1152]{1,0:T(8,128)(2,1)S(1)}, bf16[2,4,64,640]{3,2,1,0:T(8,128)(2,1)S(1)}, bf16[2,4,64,640]{3,2,1,0:T(8,128)(2,1)S(1)}) custom-call(s32[4]{0:T(128)} %pad_add_fusion.place_ref, bf16[48,64,512]{2,1,0:T(8,128)(2,1)} %tok_ref.7, bf16[3072,1152]{1,0:T(8,128)(2,1)S(1)} %get-tuple-element.147.qkv_ref, ...), custom_call_target="tpu_custom_call" | custom-call | flops 14495514624 | bytes 18432000 | tf_op jit(solution)/shard_map/attention_backward/pallas_call | solution.py:595
  110.9 4.6 %collective-permute-done.19 = bf16[4,192,256]{2,1,0:T(8,128)(2,1)S(1)} collective-permute-done((bf16[4,192,256]{2,1,0:T(8,128)(2,1)S(1)}, bf16[4,192,256]{2,1,0:T(8,128)(2,1)S(1)}, u32[]{:S(2)}, u32[]{:S(2)}) %collective-permute-start.19) | collective-permute-done | bytes 393248 | tf_op jit(solution)/shard_map/ppermute | solution.py:717
  115.6 5.7 %collective-permute-start.25 = (bf16[2,4,64,640]{3,2,1,0:T(8,128)(2,1)S(1)}, bf16[2,4,64,640]{3,2,1,0:T(8,128)(2,1)S(1)}, u32[]{:S(2)}, u32[]{:S(2)}) collective-permute-start(bf16[2,4,64,640]{3,2,1,0:T(8,128)(2,1)S(1)} %get-tuple-element.174), channel_id=1, source_target_pairs={{0,8},{8,0},{16,24},{24,16},{1,9},{9,1},{17,25},{25,17},{2,10},{10... | collective-permute-start | bytes 1966088 | tf_op jit(solution)/shard_map/ppermute | solution.py:720
  121.9 4.3 %collective-permute-start.23 = (bf16[192,256]{1,0:T(8,128)(2,1)S(1)}, bf16[192,256]{1,0:T(8,128)(2,1)S(1)}, u32[]{:S(2)}, u32[]{:S(2)}) collective-permute-start(bf16[192,256]{1,0:T(8,128)(2,1)S(1)} %get-tuple-element.172), channel_id=1, source_target_pairs={{0,6},{1,7},{2,4},{3,5},{4,2},{5,3},{6,0},{7,1},{8,14},{9,15},{10,... | collective-permute-start | bytes 294920 | tf_op jit(solution)/shard_map/ppermute | solution.py:717
  126.1 4.4 %token_gradient.2 = (bf16[48,64,512]{2,1,0:T(8,128)(2,1)}, f32[8,512]{1,0:T(8,128)S(1)}) custom-call(s32[4]{0:T(128)} %pad_add_fusion.place_ref, bf16[48,64,512]{2,1,0:T(8,128)(2,1)} %tok_ref.7, bf16[3072,1152]{1,0:T(8,128)(2,1)S(1)} %get-tuple-element.159.dqkv_ref, bf16[3072,512]{1,0:T(8,128)(2,1)S(1)} %get-tuple-element.160.gh_ref, ...), custom_call_target="tpu_custom_call" | custom-call | flops 3623878656 | bytes 7680000 | tf_op jit(solution)/shard_map/token_gradient/pallas_call | solution.py:650
  130.6 2.0 %collective-permute-done.22 = bf16[192,256]{1,0:T(8,128)(2,1)S(1)} collective-permute-done((bf16[192,256]{1,0:T(8,128)(2,1)S(1)}, bf16[192,256]{1,0:T(8,128)(2,1)S(1)}, u32[]{:S(2)}, u32[]{:S(2)}) %collective-permute-start.22) | collective-permute-done | bytes 98336 | tf_op jit(solution)/shard_map/ppermute | solution.py:717
  132.5 2.2 %collective-permute-done.24 = bf16[4,240,256]{2,1,0:T(8,128)(2,1)S(1)} collective-permute-done((bf16[4,240,256]{2,1,0:T(8,128)(2,1)S(1)}, bf16[4,240,256]{2,1,0:T(8,128)(2,1)S(1)}, u32[]{:S(2)}, u32[]{:S(2)}) %collective-permute-start.24) | collective-permute-done | bytes 491552 | tf_op jit(solution)/shard_map/ppermute | solution.py:717
  135.1 1.6 collective-permute-start.26
  137.1 4.0 %collective-permute-start.31 = (bf16[240,256]{1,0:T(8,128)(2,1)S(1)}, bf16[240,256]{1,0:T(8,128)(2,1)S(1)}, u32[]{:S(2)}, u32[]{:S(2)}) collective-permute-start(bf16[240,256]{1,0:T(8,128)(2,1)S(1)} %get-tuple-element.190), channel_id=1, source_target_pairs={{0,6},{1,7},{2,4},{3,5},{4,2},{5,3},{6,0},{7,1},{8,14},{9,15},{10,... | collective-permute-start | bytes 368648 | tf_op jit(solution)/shard_map/ppermute | solution.py:717
  142.0 3.4 %token_gradient.3 = (bf16[48,64,512]{2,1,0:T(8,128)(2,1)}, f32[8,512]{1,0:T(8,128)S(1)}) custom-call(s32[4]{0:T(128)} %pad_add_fusion.place_ref, bf16[48,64,512]{2,1,0:T(8,128)(2,1)} %tok_ref.7, bf16[3072,1152]{1,0:T(8,128)(2,1)S(1)} %get-tuple-element.159.dqkv_ref, ...), custom_call_target="tpu_custom_call", output_to_operand_aliasing={{0}: (6, {})} | custom-call | flops 3623878656 | bytes 7680000 | tf_op jit(solution)/shard_map/token_gradient/pallas_call | solution.py:650
  145.8 2.5 %collective-permute-done.30 = bf16[240,256]{1,0:T(8,128)(2,1)S(1)} collective-permute-done((bf16[240,256]{1,0:T(8,128)(2,1)S(1)}, bf16[240,256]{1,0:T(8,128)(2,1)S(1)}, u32[]{:S(2)}, u32[]{:S(2)}) %collective-permute-start.30) | collective-permute-done | bytes 122912 | tf_op jit(solution)/shard_map/ppermute | solution.py:717
  154.6 2.1 %collective-permute-done.36 = bf16[64,640]{1,0:T(8,128)(2,1)S(1)} collective-permute-done((bf16[64,640]{1,0:T(8,128)(2,1)S(1)}, bf16[64,640]{1,0:T(8,128)(2,1)S(1)}, u32[]{:S(2)}, u32[]{:S(2)}) %collective-permute-start.36) | collective-permute-done | bytes 81952 | tf_op jit(solution)/shard_map/ppermute | solution.py:717
  156.7 2.3 %collective-permute-done.35 = bf16[64,640]{1,0:T(8,128)(2,1)S(1)} collective-permute-done((bf16[64,640]{1,0:T(8,128)(2,1)S(1)}, bf16[64,640]{1,0:T(8,128)(2,1)S(1)}, u32[]{:S(2)}, u32[]{:S(2)}) %collective-permute-start.35) | collective-permute-done | bytes 81952 | tf_op jit(solution)/shard_map/ppermute | solution.py:717
  160.1 3.5 %collective-permute-done.37 = bf16[64,640]{1,0:T(8,128)(2,1)S(1)} collective-permute-done((bf16[64,640]{1,0:T(8,128)(2,1)S(1)}, bf16[64,640]{1,0:T(8,128)(2,1)S(1)}, u32[]{:S(2)}, u32[]{:S(2)}) %collective-permute-start.37) | collective-permute-done | bytes 81952 | tf_op jit(solution)/shard_map/ppermute | solution.py:720
  166.2 2.3 %finish.1 = (f32[64,384]{1,0:T(8,128)}, f32[64,384]{1,0:T(8,128)}, f32[64,384]{1,0:T(8,128)}, f32[48,512]{1,0:T(8,128)}, f32[64,1024]{1,0:T(8,128)}, /*index=5*/...) custom-call(s32[4]{0:T(128)} %pad_add_fusion.place_ref, bf16[192,256]{1,0:T(8,128)(2,1)} %copy-done.2, ...), custom_call_target="tpu_custom_call" | custom-call | tf_op jit(solution)/shard_map/finish/pallas_call | solution.py:703
  (90 shorter events, 24.2 us)
Async XLA Ops:
  3.6 8.3 %collective-permute-start.2 = (bf16[64,640]{1,0:T(8,128)(2,1)}, bf16[64,640]{1,0:T(8,128)(2,1)S(1)}, u32[]{:S(2)}, u32[]{:S(2)}) collective-permute-start(bf16[64,640]{1,0:T(8,128)(2,1)} %prepare_attention.1), channel_id=1, source_target_pairs={{0,6},{1,7},{2,4},{3,5},{4,2},{5,3},{6,0},{7,1},{8,14},{9,15},{10,... | collective-permute-start | bytes 245768 | tf_op jit(solution)/shard_map/ppermute | solution.py:717
  8.6 7.1 %collective-permute-start.1 = (bf16[64,640]{1,0:T(8,128)(2,1)}, bf16[64,640]{1,0:T(8,128)(2,1)S(1)}, u32[]{:S(2)}, u32[]{:S(2)}) collective-permute-start(bf16[64,640]{1,0:T(8,128)(2,1)} %prepare_attention.1), channel_id=1, source_target_pairs={{0,4},{1,5},{2,6},{3,7},{4,0},{5,1},{6,2},{7,3},{8,12},{9,13},{10,... | collective-permute-start | bytes 245768 | tf_op jit(solution)/shard_map/ppermute | solution.py:717
  8.6 7.1 %collective-permute-start = (bf16[64,640]{1,0:T(8,128)(2,1)}, bf16[64,640]{1,0:T(8,128)(2,1)S(1)}, u32[]{:S(2)}, u32[]{:S(2)}) collective-permute-start(bf16[64,640]{1,0:T(8,128)(2,1)} %prepare_attention.1), channel_id=1, source_target_pairs={{0,2},{1,3},{2,0},{3,1},{4,6},{5,7},{6,4},{7,5},{8,10},{9,11},{10,... | collective-permute-start | bytes 245768 | tf_op jit(solution)/shard_map/ppermute | solution.py:717
  16.7 15.5 %collective-permute-start.4 = (bf16[4,64,640]{2,1,0:T(8,128)(2,1)S(1)}, bf16[4,64,640]{2,1,0:T(8,128)(2,1)S(1)}, u32[]{:S(2)}, u32[]{:S(2)}) collective-permute-start(bf16[4,64,640]{2,1,0:T(8,128)(2,1)S(1)} %pad_maximum_fusion.2.refs_0_), channel_id=1, source_target_pairs={{0,8},{8,0},{16,24},{24,16},{1,9},{9,1},{17,25},{25,17},{2,10},{10... | collective-permute-start | bytes 983048 | tf_op jit(solution)/shard_map/ppermute | solution.py:720
  16.7 15.4 %collective-permute-start.3 = (bf16[4,64,640]{2,1,0:T(8,128)(2,1)S(1)}, bf16[4,64,640]{2,1,0:T(8,128)(2,1)S(1)}, u32[]{:S(2)}, u32[]{:S(2)}) collective-permute-start(bf16[4,64,640]{2,1,0:T(8,128)(2,1)S(1)} %pad_maximum_fusion.2.refs_0_), channel_id=1, source_target_pairs={{0,1},{1,0},{2,3},{3,2},{4,5},{5,4},{6,7},{7,6},{8,9},{9,8},{10,11... | collective-permute-start | bytes 983048 | tf_op jit(solution)/shard_map/ppermute | solution.py:717
  18.3 8.3 %collective-permute-start.7 = (bf16[240,256]{1,0:T(8,128)(2,1)}, bf16[240,256]{1,0:T(8,128)(2,1)S(1)}, u32[]{:S(2)}, u32[]{:S(2)}) collective-permute-start(bf16[240,256]{1,0:T(8,128)(2,1)} %get-tuple-element.119), channel_id=1, source_target_pairs={{0,6},{1,7},{2,4},{3,5},{4,2},{5,3},{6,0},{7,1},{8,14},{9,15},{10,... | collective-permute-start | bytes 368648 | tf_op jit(solution)/shard_map/ppermute | solution.py:717
  20.9 11.2 %collective-permute-start.6 = (bf16[240,256]{1,0:T(8,128)(2,1)}, bf16[240,256]{1,0:T(8,128)(2,1)S(1)}, u32[]{:S(2)}, u32[]{:S(2)}) collective-permute-start(bf16[240,256]{1,0:T(8,128)(2,1)} %get-tuple-element.119), channel_id=1, source_target_pairs={{0,4},{1,5},{2,6},{3,7},{4,0},{5,1},{6,2},{7,3},{8,12},{9,13},{10,... | collective-permute-start | bytes 368648 | tf_op jit(solution)/shard_map/ppermute | solution.py:717
  20.9 11.2 %collective-permute-start.5 = (bf16[240,256]{1,0:T(8,128)(2,1)}, bf16[240,256]{1,0:T(8,128)(2,1)S(1)}, u32[]{:S(2)}, u32[]{:S(2)}) collective-permute-start(bf16[240,256]{1,0:T(8,128)(2,1)} %get-tuple-element.119), channel_id=1, source_target_pairs={{0,2},{1,3},{2,0},{3,1},{4,6},{5,7},{6,4},{7,5},{8,10},{9,11},{10,... | collective-permute-start | bytes 368648 | tf_op jit(solution)/shard_map/ppermute | solution.py:717
  32.2 10.1 %collective-permute-start.13 = (bf16[192,256]{1,0:T(8,128)(2,1)}, bf16[192,256]{1,0:T(8,128)(2,1)S(1)}, u32[]{:S(2)}, u32[]{:S(2)}) collective-permute-start(bf16[192,256]{1,0:T(8,128)(2,1)} %get-tuple-element.128), channel_id=1, source_target_pairs={{0,6},{1,7},{2,4},{3,5},{4,2},{5,3},{6,0},{7,1},{8,14},{9,15},{10,... | collective-permute-start | bytes 294920 | tf_op jit(solution)/shard_map/ppermute | solution.py:717
  33.8 9.9 %collective-permute-start.12 = (bf16[192,256]{1,0:T(8,128)(2,1)}, bf16[192,256]{1,0:T(8,128)(2,1)S(1)}, u32[]{:S(2)}, u32[]{:S(2)}) collective-permute-start(bf16[192,256]{1,0:T(8,128)(2,1)} %get-tuple-element.128), channel_id=1, source_target_pairs={{0,4},{1,5},{2,6},{3,7},{4,0},{5,1},{6,2},{7,3},{8,12},{9,13},{10,... | collective-permute-start | bytes 294920 | tf_op jit(solution)/shard_map/ppermute | solution.py:717
  33.8 9.9 %collective-permute-start.11 = (bf16[192,256]{1,0:T(8,128)(2,1)}, bf16[192,256]{1,0:T(8,128)(2,1)S(1)}, u32[]{:S(2)}, u32[]{:S(2)}) collective-permute-start(bf16[192,256]{1,0:T(8,128)(2,1)} %get-tuple-element.128), channel_id=1, source_target_pairs={{0,2},{1,3},{2,0},{3,1},{4,6},{5,7},{6,4},{7,5},{8,10},{9,11},{10,... | collective-permute-start | bytes 294920 | tf_op jit(solution)/shard_map/ppermute | solution.py:717
  37.7 13.6 %collective-permute-start.9 = (bf16[4,240,256]{2,1,0:T(8,128)(2,1)S(1)}, bf16[4,240,256]{2,1,0:T(8,128)(2,1)S(1)}, u32[]{:S(2)}, u32[]{:S(2)}) collective-permute-start(bf16[4,240,256]{2,1,0:T(8,128)(2,1)S(1)} %pad_maximum_fusion.refs_0_), channel_id=1, source_target_pairs={{0,1},{1,0},{2,3},{3,2},{4,5},{5,4},{6,7},{7,6},{8,9},{9,8},{10,11... | collective-permute-start | bytes 1474568 | tf_op jit(solution)/shard_map/ppermute | solution.py:717
  53.2 7.0 %collective-permute-start.16 = (bf16[4,192,256]{2,1,0:T(8,128)(2,1)S(1)}, bf16[4,192,256]{2,1,0:T(8,128)(2,1)S(1)}, u32[]{:S(2)}, u32[]{:S(2)}) collective-permute-start(bf16[4,192,256]{2,1,0:T(8,128)(2,1)S(1)} %pad_maximum_fusion.1.refs_0_), channel_id=1, source_target_pairs={{0,8},{8,0},{16,24},{24,16},{1,9},{9,1},{17,25},{25,17},{2,10},{10... | collective-permute-start | bytes 1179656 | tf_op jit(solution)/shard_map/ppermute | solution.py:720
  53.4 11.4 %collective-permute-start.15 = (bf16[4,192,256]{2,1,0:T(8,128)(2,1)S(1)}, bf16[4,192,256]{2,1,0:T(8,128)(2,1)S(1)}, u32[]{:S(2)}, u32[]{:S(2)}) collective-permute-start(bf16[4,192,256]{2,1,0:T(8,128)(2,1)S(1)} %pad_maximum_fusion.1.refs_0_), channel_id=1, source_target_pairs={{0,1},{1,0},{2,3},{3,2},{4,5},{5,4},{6,7},{7,6},{8,9},{9,8},{10,11... | collective-permute-start | bytes 1179656 | tf_op jit(solution)/shard_map/ppermute | solution.py:717
  64.8 13.3 %collective-permute-start.17 = (bf16[4,192,256]{2,1,0:T(8,128)(2,1)S(1)}, bf16[4,192,256]{2,1,0:T(8,128)(2,1)S(1)}, u32[]{:S(2)}, u32[]{:S(2)}) collective-permute-start(bf16[4,192,256]{2,1,0:T(8,128)(2,1)S(1)} %collective-permute-done.15.refs_1_), channel_id=1, source_target_pairs={{0,8},{8,0},{16,24},{24,16},{1,9},{9,1},{17,25},{25,17},{2,10},{10... | collective-permute-start | bytes 1179656 | tf_op jit(solution)/shard_map/ppermute | solution.py:720
  76.7 10.0 %collective-permute-start.18 = (bf16[2,4,192,256]{3,2,1,0:T(8,128)(2,1)S(1)}, bf16[2,4,192,256]{3,2,1,0:T(8,128)(2,1)S(1)}, u32[]{:S(2)}, u32[]{:S(2)}) collective-permute-start(bf16[2,4,192,256]{3,2,1,0:T(8,128)(2,1)S(1)} %get-tuple-element.155), channel_id=1, source_target_pairs={{0,8},{8,0},{16,24},{24,16},{1,9},{9,1},{17,25},{25,17},{2,10},{10... | collective-permute-start | bytes 2359304 | tf_op jit(solution)/shard_map/ppermute | solution.py:720
  86.9 28.6 %collective-permute-start.19 = (bf16[4,192,256]{2,1,0:T(8,128)(2,1)S(1)}, bf16[4,192,256]{2,1,0:T(8,128)(2,1)S(1)}, u32[]{:S(2)}, u32[]{:S(2)}) collective-permute-start(bf16[4,192,256]{2,1,0:T(8,128)(2,1)S(1)} %fusion.1), channel_id=1, source_target_pairs={{0,1},{1,0},{2,3},{3,2},{4,5},{5,4},{6,7},{7,6},{8,9},{9,8},{10,11... | collective-permute-start | bytes 1179656 | tf_op jit(solution)/shard_map/ppermute | solution.py:717
  105.5 10.0 %collective-permute-start.20 = (bf16[2,4,240,256]{3,2,1,0:T(8,128)(2,1)S(1)}, bf16[2,4,240,256]{3,2,1,0:T(8,128)(2,1)S(1)}, u32[]{:S(2)}, u32[]{:S(2)}) collective-permute-start(bf16[2,4,240,256]{3,2,1,0:T(8,128)(2,1)S(1)} %get-tuple-element.164), channel_id=1, source_target_pairs={{0,8},{8,0},{16,24},{24,16},{1,9},{9,1},{17,25},{25,17},{2,10},{10... | collective-permute-start | bytes 2949128 | tf_op jit(solution)/shard_map/ppermute | solution.py:720
  115.6 19.1 %collective-permute-start.25 = (bf16[2,4,64,640]{3,2,1,0:T(8,128)(2,1)S(1)}, bf16[2,4,64,640]{3,2,1,0:T(8,128)(2,1)S(1)}, u32[]{:S(2)}, u32[]{:S(2)}) collective-permute-start(bf16[2,4,64,640]{3,2,1,0:T(8,128)(2,1)S(1)} %get-tuple-element.174), channel_id=1, source_target_pairs={{0,8},{8,0},{16,24},{24,16},{1,9},{9,1},{17,25},{25,17},{2,10},{10... | collective-permute-start | bytes 1966088 | tf_op jit(solution)/shard_map/ppermute | solution.py:720
  121.5 13.2 %collective-permute-start.24 = (bf16[4,240,256]{2,1,0:T(8,128)(2,1)S(1)}, bf16[4,240,256]{2,1,0:T(8,128)(2,1)S(1)}, u32[]{:S(2)}, u32[]{:S(2)}) collective-permute-start(bf16[4,240,256]{2,1,0:T(8,128)(2,1)S(1)} %fusion), channel_id=1, source_target_pairs={{0,1},{1,0},{2,3},{3,2},{4,5},{5,4},{6,7},{7,6},{8,9},{9,8},{10,11... | collective-permute-start | bytes 1474568 | tf_op jit(solution)/shard_map/ppermute | solution.py:717
  121.8 8.8 %collective-permute-start.21 = (bf16[192,256]{1,0:T(8,128)(2,1)S(1)}, bf16[192,256]{1,0:T(8,128)(2,1)S(1)}, u32[]{:S(2)}, u32[]{:S(2)}) collective-permute-start(bf16[192,256]{1,0:T(8,128)(2,1)S(1)} %get-tuple-element.170), channel_id=1, source_target_pairs={{0,2},{1,3},{2,0},{3,1},{4,6},{5,7},{6,4},{7,5},{8,10},{9,11},{10,... | collective-permute-start | bytes 294920 | tf_op jit(solution)/shard_map/ppermute | solution.py:717
  121.8 10.8 %collective-permute-start.22 = (bf16[192,256]{1,0:T(8,128)(2,1)S(1)}, bf16[192,256]{1,0:T(8,128)(2,1)S(1)}, u32[]{:S(2)}, u32[]{:S(2)}) collective-permute-start(bf16[192,256]{1,0:T(8,128)(2,1)S(1)} %get-tuple-element.171), channel_id=1, source_target_pairs={{0,4},{1,5},{2,6},{3,7},{4,0},{5,1},{6,2},{7,3},{8,12},{9,13},{10,... | collective-permute-start | bytes 294920 | tf_op jit(solution)/shard_map/ppermute | solution.py:717
  121.9 10.7 %collective-permute-start.23 = (bf16[192,256]{1,0:T(8,128)(2,1)S(1)}, bf16[192,256]{1,0:T(8,128)(2,1)S(1)}, u32[]{:S(2)}, u32[]{:S(2)}) collective-permute-start(bf16[192,256]{1,0:T(8,128)(2,1)S(1)} %get-tuple-element.172), channel_id=1, source_target_pairs={{0,6},{1,7},{2,4},{3,5},{4,2},{5,3},{6,0},{7,1},{8,14},{9,15},{10,... | collective-permute-start | bytes 294920 | tf_op jit(solution)/shard_map/ppermute | solution.py:717
  135.1 10.3 %collective-permute-start.26 = (bf16[192,256]{1,0:T(8,128)(2,1)S(1)}, bf16[192,256]{1,0:T(8,128)(2,1)S(1)}, u32[]{:S(2)}, u32[]{:S(2)}) collective-permute-start(bf16[192,256]{1,0:T(8,128)(2,1)S(1)} %fusion.10), channel_id=1, source_target_pairs={{0,16},{8,24},{16,0},{24,8},{1,17},{9,25},{17,1},{25,9},{2,18},{10... | collective-permute-start | bytes 294920 | tf_op jit(solution)/shard_map/ppermute | solution.py:720
  136.7 9.1 %collective-permute-start.29 = (bf16[240,256]{1,0:T(8,128)(2,1)S(1)}, bf16[240,256]{1,0:T(8,128)(2,1)S(1)}, u32[]{:S(2)}, u32[]{:S(2)}) collective-permute-start(bf16[240,256]{1,0:T(8,128)(2,1)S(1)} %get-tuple-element.188), channel_id=1, source_target_pairs={{0,2},{1,3},{2,0},{3,1},{4,6},{5,7},{6,4},{7,5},{8,10},{9,11},{10,... | collective-permute-start | bytes 368648 | tf_op jit(solution)/shard_map/ppermute | solution.py:717
  136.7 11.6 %collective-permute-start.30 = (bf16[240,256]{1,0:T(8,128)(2,1)S(1)}, bf16[240,256]{1,0:T(8,128)(2,1)S(1)}, u32[]{:S(2)}, u32[]{:S(2)}) collective-permute-start(bf16[240,256]{1,0:T(8,128)(2,1)S(1)} %get-tuple-element.189), channel_id=1, source_target_pairs={{0,4},{1,5},{2,6},{3,7},{4,0},{5,1},{6,2},{7,3},{8,12},{9,13},{10,... | collective-permute-start | bytes 368648 | tf_op jit(solution)/shard_map/ppermute | solution.py:717
  137.1 11.2 %collective-permute-start.31 = (bf16[240,256]{1,0:T(8,128)(2,1)S(1)}, bf16[240,256]{1,0:T(8,128)(2,1)S(1)}, u32[]{:S(2)}, u32[]{:S(2)}) collective-permute-start(bf16[240,256]{1,0:T(8,128)(2,1)S(1)} %get-tuple-element.190), channel_id=1, source_target_pairs={{0,6},{1,7},{2,4},{3,5},{4,2},{5,3},{6,0},{7,1},{8,14},{9,15},{10,... | collective-permute-start | bytes 368648 | tf_op jit(solution)/shard_map/ppermute | solution.py:717
  141.1 7.7 %collective-permute-start.28 = (bf16[4,64,640]{2,1,0:T(8,128)(2,1)S(1)}, bf16[4,64,640]{2,1,0:T(8,128)(2,1)S(1)}, u32[]{:S(2)}, u32[]{:S(2)}) collective-permute-start(bf16[4,64,640]{2,1,0:T(8,128)(2,1)S(1)} %fusion.2), channel_id=1, source_target_pairs={{0,1},{1,0},{2,3},{3,2},{4,5},{5,4},{6,7},{7,6},{8,9},{9,8},{10,11... | collective-permute-start | bytes 983048 | tf_op jit(solution)/shard_map/ppermute | solution.py:717
  145.4 18.3 %collective-permute-start.27 = (bf16[192,256]{1,0:T(8,128)(2,1)S(1)}, bf16[192,256]{1,0:T(8,128)(2,1)S(1)}, u32[]{:S(2)}, u32[]{:S(2)}) collective-permute-start(bf16[192,256]{1,0:T(8,128)(2,1)S(1)} %add_convert_fusion.4.refs_0_), channel_id=1, source_target_pairs={{0,8},{8,0},{16,24},{24,16},{1,9},{9,1},{17,25},{25,17},{2,10},{10... | collective-permute-start | bytes 294920 | tf_op jit(solution)/shard_map/ppermute | solution.py:720
  150.4 6.2 %collective-permute-start.36 = (bf16[64,640]{1,0:T(8,128)(2,1)S(1)}, bf16[64,640]{1,0:T(8,128)(2,1)S(1)}, u32[]{:S(2)}, u32[]{:S(2)}) collective-permute-start(bf16[64,640]{1,0:T(8,128)(2,1)S(1)} %get-tuple-element.219), channel_id=1, source_target_pairs={{0,6},{1,7},{2,4},{3,5},{4,2},{5,3},{6,0},{7,1},{8,14},{9,15},{10,... | collective-permute-start | bytes 245768 | tf_op jit(solution)/shard_map/ppermute | solution.py:717
  151.9 7.1 %collective-permute-start.35 = (bf16[64,640]{1,0:T(8,128)(2,1)S(1)}, bf16[64,640]{1,0:T(8,128)(2,1)S(1)}, u32[]{:S(2)}, u32[]{:S(2)}) collective-permute-start(bf16[64,640]{1,0:T(8,128)(2,1)S(1)} %get-tuple-element.220), channel_id=1, source_target_pairs={{0,4},{1,5},{2,6},{3,7},{4,0},{5,1},{6,2},{7,3},{8,12},{9,13},{10,... | collective-permute-start | bytes 245768 | tf_op jit(solution)/shard_map/ppermute | solution.py:717
  152.5 7.4 %collective-permute-start.32 = (bf16[240,256]{1,0:T(8,128)(2,1)S(1)}, bf16[240,256]{1,0:T(8,128)(2,1)S(1)}, u32[]{:S(2)}, u32[]{:S(2)}) collective-permute-start(bf16[240,256]{1,0:T(8,128)(2,1)S(1)} %fusion.6), channel_id=1, source_target_pairs={{0,16},{8,24},{16,0},{24,8},{1,17},{9,25},{17,1},{25,9},{2,18},{10... | collective-permute-start | bytes 368648 | tf_op jit(solution)/shard_map/ppermute | solution.py:720
  (15 other events, 75.6 us)

commit v4 on v3

--- a/solution.py
+++ b/solution.py
@@ -14,7 +14,6 @@
 CUT = 640
 GROUP = 8
 EPS = 1e-6
-VMEM_LIMIT = 18 * 1024 * 1024
 bf16, f32 = jnp.bfloat16, jnp.float32
 sds = jax.ShapeDtypeStruct
 
@@ -150,6 +149,10 @@
         pl.when(core == c)(functools.partial(write, c))
 
 
+def small_params():
+    return pltpu.CompilerParams(vmem_limit_bytes=12 * 1024 * 1024)
+
+
 def padded(rows):
     return -(-rows // 16) * 16
 
@@ -179,7 +182,7 @@
 
 def attention_forward(G, L, n_z, place_ref, tok_ref, *refs):
     pieces, refs = refs[:4], refs[4:]
-    all_qkv, all_probs, mixed_ref, w_ref, gains_ref, table_ref, st_ref, small_ref = refs
+    all_qkv, probs_ref, mixed_ref, w_ref, gains_ref, table_ref, st_ref, small_ref = refs
     step = pl.program_id(0)
     place = Place(place_ref, n_z)
     D = tok_ref.shape[-1]
@@ -221,7 +224,6 @@
     @pl.when(step * G < place.count)
     def _():
         mixed, qkv_ref = group_rows(mixed_ref, step, G * L), group_rows(all_qkv, step, G * L)
-        probs_ref = all_probs.at[pl.ds(step * G, G)]
         x = tok_ref[...].reshape(G * L, D).astype(f32)
         normed = (x * inverse_rms(x) * gains_ref[0:1, :]).astype(bf16)
         qkv_ref[...] = nn(normed, w_ref[...]).astype(bf16)
@@ -243,8 +245,11 @@
                 mixed[rows, pl.ds(p * PAIR, PAIR)] = join_heads(tn(probs_ref[s, p], v)).astype(bf16)
 
 
-def params():
-    return pltpu.CompilerParams(dimension_semantics=("arbitrary",), vmem_limit_bytes=VMEM_LIMIT)
+MIB_FORWARD, MIB_FFN, MIB_BACKWARD, MIB_TOKENS, MIB_RESULT = 12, 18, 14, 10, 10
+
+
+def params(mib):
+    return pltpu.CompilerParams(dimension_semantics=("arbitrary",), vmem_limit_bytes=mib * 1024 * 1024)
 
 
 def whole(shape):
@@ -279,7 +284,7 @@
         functools.partial(attention_forward, G, L, n_z),
         out_shape=(
             sds((S * L, 3 * INNER), bf16),
-            sds((S, PAIRS, L, PAIR), bf16),
+            pltpu.HBM((S, PAIRS, L, PAIR), bf16),
             sds((S * L, INNER), bf16),
             sds((D, 3 * INNER), bf16),
             sds((8, D), f32),
@@ -290,7 +295,7 @@
             in_specs=[series_spec(G, tokens.shape)] + [whole(piece.shape) for piece in pieces],
             out_specs=[
                 whole((S * L, 3 * INNER)),
-                whole((S, PAIRS, L, PAIR)),
+                series_spec(G, (S, PAIRS, L, PAIR)),
                 whole((S * L, INNER)),
                 whole((D, 3 * INNER)),
                 whole((8, D)),
@@ -301,7 +306,7 @@
                 pltpu.VMEM((D, PAIR), f32),
             ],
         ),
-        compiler_params=params(),
+        compiler_params=params(MIB_FORWARD),
         cost_estimate=cost(S * L, D * 3 * INNER * 4, S * L * 5000),
         name="attention_forward",
     )(place, in_hbm(tokens), *pieces)
@@ -315,43 +320,42 @@
     return v * half, half + (0.5 * v) * (1.0 - t * t) * (c + (3 * c * 0.044715) * v2)
 
 
-def put_weights(place, first, n_z, pieces, wg, wu, wd, wo):
-    n_f = 2 * n_z
-    D, FW = wg.shape
-    ds, fh, half = D // n_f, FW // n_f, FW // 2
+def put_weights(place, pieces, wgu, wd, wo=None):
+    FW, D = wd.shape
 
     def assemble(c):
-        for xx, k, f in place.shards():
-            here, there = pieces[xx].at[k], pieces[2 + xx].at[k]
+        for f, here, there in pieces:
             for which, piece in enumerate((here, there) if c == 0 else (there, here)):
-                gated = (wg, wu)[which]
-                gated[at(f, ds), :half] = piece[:ds, :]
-                gated[at(f, ds), half:] = piece[ds : 2 * ds, :]
+                n_f = len(pieces)
+                ds, fh, half, is_ = D // n_f, FW // n_f, FW // 2, INNER // n_f
+                for part in range(2):
+                    start = (2 * part + which) * half
+                    wgu[at(f, ds), start : start + half] = piece[part * ds : (part + 1) * ds, :]
                 cols = slice(which * half, (which + 1) * half)
                 wd[at(f, fh), cols] = piece[2 * ds : 2 * ds + fh, :]
-                if first:
-                    is_ = INNER // n_f
-                    if is_ % 16 == 0:
-                        wo[at(f, is_), cols] = piece[2 * ds + fh : 2 * ds + fh + is_, :]
-                    else:
-                        wo[f, :, cols] = piece[2 * ds + fh :, :]
+                if wo is None:
+                    continue
+                if is_ % 16 == 0:
+                    wo[at(f, is_), cols] = piece[2 * ds + fh : 2 * ds + fh + is_, :]
+                else:
+                    wo[f, :, cols] = piece[2 * ds + fh :, :]
 
     for c in range(2):
         pl.when(place.core == c)(functools.partial(assemble, c))
 
 
-def put_grads(place, n_z, keep, send, ag, au, ad, ao=None):
+def put_grads(place, n_z, keep, send, agu, ad, ao=None):
     n_f = 2 * n_z
-    D, FW = ag.shape
+    FW, D = ad.shape
     ds, fh, half = D // n_f, FW // n_f, FW // 2
 
     def write(c):
         for xx, k, f in place.shards():
             for which, ref in enumerate((keep, send) if c == 0 else (send, keep)):
-                gated = (ag, au)[which]
+                for part in range(2):
+                    start = (2 * part + which) * half
+                    ref[xx, k, part * ds : (part + 1) * ds, :] = agu[at(f, ds), start : start + half].astype(bf16)
                 cols = slice(which * half, (which + 1) * half)
-                ref[xx, k, :ds, :] = gated[at(f, ds), :half].astype(bf16)
-                ref[xx, k, ds : 2 * ds, :] = gated[at(f, ds), half:].astype(bf16)
                 ref[xx, k, 2 * ds : 2 * ds + fh, :] = ad[at(f, fh), cols].astype(bf16)
                 if ao is not None:
                     is_ = INNER // n_f
@@ -364,46 +368,39 @@
         pl.when(place.core == c)(functools.partial(write, c))
 
 
-def ffn_half(G, L, CH, n_z, first, place_ref, *refs):
+def ffn_half(G, L, n_z, first, place_ref, *refs):
+    n_f = 2 * n_z
+    place = Place(place_ref, n_z)
     pieces, refs = refs[:4], refs[4:]
+    pieces = [(f, pieces[xx].at[k], pieces[2 + xx].at[k]) for xx, k, f in place.shards()]
     if first:
         (tok_ref, ct_ref, mixed_ref, gains_ref,
-         hid_ref, part_ref, gpart_ref, wo_out, keep, send,
-         ag, au, ad, wg, wu, wd, n2, gb, gate, up, ga, act, ggr, gur, acc, gn, spread) = refs
+         hid_ref, act, gpart_ref, wd, wo_out, keep, send,
+         agu, ad, wgu, n2, gb, gu, ga, low, gn, spread) = refs
     else:
-        (hid_ref, ct_ref, mixed_ref, part_ref, gpart_ref, gains_ref, wo_in,
-         out_ref, gh_ref, gm_ref, keep, send, gf_ref,
-         ag, au, ad, wg, wu, wd, n2, gb, gate, up, ga, act, ggr, gur, acc, gn, ao, spread) = refs
+        (hid_ref, ct_ref, mixed_ref, gpart_ref, gains_ref, wo_in,
+         gh_ref, gm_ref, act, wd, keep, send, gf_ref,
+         agu, ad, wgu, n2, gb, gu, ga, low, gn, ao, spread) = refs
     step = pl.program_id(0)
     last = pl.num_programs(0) - 1
     R = G * L
-    D = ct_ref.shape[-1]
-    FW = wg.shape[1]
-    n_f = 2 * n_z
+    FW, D = wd.shape
+    CH = FW // 2
     is_ = INNER // n_f
-    place = Place(place_ref, n_z)
     count = place.count
     group = jnp.minimum(step, (count + G - 1) // G - 1)
-    hid_ref, mixed_ref, part_ref, gpart_ref = (
-        group_rows(ref, group, R) for ref in (hid_ref, mixed_ref, part_ref, gpart_ref)
-    )
+    hid_ref, mixed_ref, act, gpart_ref = (group_rows(ref, group, R) for ref in (hid_ref, mixed_ref, act, gpart_ref))
     if not first:
         gm_ref, gh_ref = group_rows(gm_ref, group, R), group_rows(gh_ref, group, R)
 
     @pl.when(step == 0)
     def _():
         wo = (wo_out if is_ % 16 == 0 else spread) if first else None
-        put_weights(place, first, n_z, pieces, wg, wu, wd, wo)
+        put_weights(place, pieces, wgu, wd, wo)
         if first and is_ % 16:
             wo_out[...] = jnp.concatenate([spread[f, :is_, :].astype(f32) for f in range(n_f)], axis=0).astype(bf16)
-        for ref in (ag, au, ad) if first else (ag, au, ad, ao, gf_ref):
+        for ref in (agu, ad) if first else (agu, ad, ao, gf_ref):
             ref[...] = jnp.zeros_like(ref)
-
-    if not first:
-
-        @pl.when(step * G >= count)
-        def _():
-            out_ref[...] = jnp.zeros_like(out_ref)
 
     @pl.when(step * G < count)
     def _():
@@ -413,35 +410,30 @@
         n2[...] = (h * inverse_rms(h) * gains_ref[1:2, :]).astype(bf16)
         live = (step * G + lax.broadcasted_iota(jnp.int32, (R, 1), 0) // L) < count
         gb[...] = jnp.where(live, ct_ref[...].reshape(R, D), jnp.zeros((), bf16))
-        for c in range(FW // CH):
-            cols = pl.ds(c * CH, CH)
-            gate[...] = nn(n2[...], wg[:, cols])
-            up[...] = nn(n2[...], wu[:, cols])
-            ga[...] = nt(gb[...], wd[cols, :])
+        for c in range(2):
+            cols, both = pl.ds(c * CH, CH), pl.ds(2 * c * CH, 2 * CH)
+            gu[c] = nn(n2[...], wgu[:, both])
+            ga[c] = nt(gb[...], wd[cols, :])
+        for c in range(2):
+            cols, both = pl.ds(c * CH, CH), pl.ds(2 * c * CH, 2 * CH)
             for r in range(0, R, L):
                 rows = pl.ds(r, L)
-                u = up[rows, :]
-                a = ga[rows, :]
-                g, dg = gelu_parts(gate[rows, :])
-                act[rows, :] = (g * u).astype(bf16)
-                ggr[rows, :] = (a * u * dg).astype(bf16)
-                gur[rows, :] = (a * g).astype(bf16)
+                u = gu[c, rows, CH:]
+                a = ga[c, rows, :]
+                g, dg = gelu_parts(gu[c, rows, :CH])
+                act[rows, cols] = (g * u).astype(bf16)
+                low[c, rows, :CH] = (a * u * dg).astype(bf16)
+                low[c, rows, CH:] = (a * g).astype(bf16)
             if c == 0:
-                acc[...] = nn(act[...], wd[cols, :])
-                gn[...] = nt(ggr[...], wg[:, cols]) + nt(gur[...], wu[:, cols])
+                gn[...] = nt(low[c], wgu[:, both])
             else:
-                acc[...] += nn(act[...], wd[cols, :])
-                gn[...] += nt(ggr[...], wg[:, cols]) + nt(gur[...], wu[:, cols])
-            ad[cols, :] += tn(act[...], gb[...])
-            ag[:, cols] += tn(n2[...], ggr[...])
-            au[:, cols] += tn(n2[...], gur[...])
+                gn[...] += nt(low[c], wgu[:, both])
+            ad[cols, :] += tn(act[:, cols], gb[...])
+            agu[:, both] += tn(n2[...], low[c])
         if first:
-            part_ref[...] = acc[...].astype(bf16)
             gpart_ref[...] = gn[...].astype(bf16)
         else:
             h = hid_ref[...]
-            out = h + part_ref[...].astype(f32) + acc[...]
-            out_ref[...] = jnp.where(live, out, 0.0).astype(bf16).reshape(G, L, D)
             scale = inverse_rms(h)
             hs = h * scale
             g2 = gn[...] + gpart_ref[...].astype(f32)
@@ -456,56 +448,90 @@
     @pl.when(step == last)
     def _():
         if first:
-            put_grads(place, n_z, keep, send, ag, au, ad)
+            put_grads(place, n_z, keep, send, agu, ad)
         elif is_ % 16 == 0:
-            put_grads(place, n_z, keep, send, ag, au, ad, ao)
+            put_grads(place, n_z, keep, send, agu, ad, ao)
         else:
             for f in range(n_f):
                 spread[f, :is_, :] = ao[f * is_ : (f + 1) * is_, :]
-            put_grads(place, n_z, keep, send, ag, au, ad, spread)
-
-
-def call_ffn_half(first, place, pieces, gains, arrays, S, L, D, CH=256):
-    G, n_z = GROUP, pieces[0].shape[0]
+            put_grads(place, n_z, keep, send, agu, ad, spread)
+
+
+def call_ffn_half(first, place, n_z, pieces, gains, arrays, S, L, D):
+    G = GROUP
     R, n_f = G * L, 2 * n_z
     FW = D
-    ds, fh, half, is_ = D // n_f, FW // n_f, FW // 2, INNER // n_f
+    CH = FW // 2
+    ds, fh, is_ = D // n_f, FW // n_f, INNER // n_f
     series = series_spec(G, (S, L, D))
-    piece_specs = [whole(piece.shape) for piece in pieces]
-    rows = functools.partial(row_spec, G, L)
-    extra = 0 if first else padded(is_)
-    pack = (2, n_z, 2 * ds + fh + extra, half)
+    pack = (2, n_z, 2 * ds + fh + (0 if first else padded(is_)), CH)
+    packs, act, wd = [sds(pack, bf16)] * 2, sds((S * L, FW), bf16), sds((FW, D), bf16)
     if first:
         tokens, ct, mixed = arrays
-        in_specs = piece_specs + [series, series, whole(mixed.shape), whole(gains.shape)]
-        out_shape = [sds((S * L, D), f32), sds((S * L, D), bf16), sds((S * L, D), bf16), sds((INNER, D), bf16),
-                     sds(pack, bf16), sds(pack, bf16)]
-        out_specs = [whole(shape.shape) for shape in out_shape]
-        operands = tuple(pieces) + (in_hbm(tokens), in_hbm(ct), mixed, gains)
+        operands = (*pieces, in_hbm(tokens), in_hbm(ct), mixed, gains)
+        out_shape = [sds((S * L, D), f32), act, sds((S * L, D), bf16), wd, sds((INNER, D), bf16)] + packs
     else:
-        hidden, ct, *arrays, wo = arrays
-        in_specs = piece_specs + [whole(hidden.shape), series] + [whole(a.shape) for a in (*arrays, gains, wo)]
-        out_shape = [pltpu.HBM((S, L, D), bf16), sds((S * L, D), bf16), sds((S * L, INNER), bf16),
-                     sds(pack, bf16), sds(pack, bf16), sds((8, D), f32)]
-        out_specs = [series_spec(G, (S, L, D), True)] + [whole(pack)] * 5
-        operands = tuple(pieces) + (hidden, in_hbm(ct), *arrays, gains, wo)
+        hidden, ct, *arrays = arrays
+        operands = (*pieces, hidden, in_hbm(ct), *arrays)
+        out_shape = [sds((S * L, D), bf16), sds((S * L, INNER), bf16), act, wd] + packs + [sds((8, D), f32)]
     vm = pltpu.VMEM
-    scratch = (
-        [vm((D, FW), f32)] * 2 + [vm((FW, D), f32)]
-        + [vm((D, FW), bf16)] * 2 + [vm((FW, D), bf16)]
-        + [vm((R, D), bf16)] * 2 + [vm((R, CH), f32)] * 3 + [vm((R, CH), bf16)] * 3 + [vm((R, D), f32)] * 2
-        + ([] if first else [vm((INNER, D), f32)])
-        + [vm((n_f, padded(is_), D) if is_ % 16 else (1, 16, 128), bf16 if first else f32)]
-    )
+    scratch = [
+        vm((D, 2 * FW), f32), vm((FW, D), f32), vm((D, 2 * FW), bf16), vm((R, D), bf16), vm((R, D), bf16),
+        vm((2, R, 2 * CH), f32), vm((2, R, CH), f32), vm((2, R, 2 * CH), bf16), vm((R, D), f32),
+    ]
+    scratch += [] if first else [vm((INNER, D), f32)]
+    scratch += [vm((n_f, padded(is_), D) if is_ % 16 else (1, 16, 128), bf16 if first else f32)]
     return pl.pallas_call(
-        functools.partial(ffn_half, G, L, CH, n_z, first),
+        functools.partial(ffn_half, G, L, n_z, first),
         out_shape=tuple(out_shape),
         grid_spec=pltpu.PrefetchScalarGridSpec(
-            num_scalar_prefetch=1, grid=(S // G,), in_specs=in_specs, out_specs=out_specs, scratch_shapes=scratch
+            num_scalar_prefetch=1,
+            grid=(S // G,),
+            in_specs=[series if len(a.shape) == 3 and a.shape[0] == S else whole(a.shape) for a in operands],
+            out_specs=[whole(shape.shape) for shape in out_shape],
+            scratch_shapes=scratch,
         ),
-        compiler_params=params(),
-        cost_estimate=cost(S * L, 12 * D * FW, S * L * 9000),
+        compiler_params=params(MIB_FFN),
+        cost_estimate=cost(S * L, 9 * D * FW, S * L * 9000),
         name="ffn_first" if first else "ffn_second",
+    )(place, *operands)
+
+
+def layer_result(G, L, place_ref, hid_ref, act_0, act_1, wd_0, wd_1, gains_ref, out_ref, done_ref):
+    step = pl.program_id(0)
+    count = place_ref[0]
+    R = G * L
+    D = hid_ref.shape[-1]
+    done_ref[...] = gains_ref[...]
+    group = jnp.minimum(step, (count + G - 1) // G - 1)
+    hid_ref, act_0, act_1 = (group_rows(ref, group, R) for ref in (hid_ref, act_0, act_1))
+
+    @pl.when(step * G >= count)
+    def _():
+        out_ref[...] = jnp.zeros_like(out_ref)
+
+    @pl.when(step * G < count)
+    def _():
+        live = (step * G + lax.broadcasted_iota(jnp.int32, (R, 1), 0) // L) < count
+        out = hid_ref[...] + nn(act_0[...], wd_0[...]) + nn(act_1[...], wd_1[...])
+        out_ref[...] = jnp.where(live, out, 0.0).astype(bf16).reshape(G, L, D)
+
+
+def call_layer_result(place, hidden, act_0, act_1, wd_0, wd_1, gains, S, L):
+    G, D = GROUP, hidden.shape[-1]
+    operands = (hidden, act_0, act_1, wd_0, wd_1, gains)
+    return pl.pallas_call(
+        functools.partial(layer_result, G, L),
+        out_shape=(pltpu.HBM((S, L, D), bf16), sds(gains.shape, f32)),
+        grid_spec=pltpu.PrefetchScalarGridSpec(
+            num_scalar_prefetch=1,
+            grid=(S // G,),
+            in_specs=[whole(a.shape) for a in operands],
+            out_specs=(series_spec(G, (S, L, D), True), whole(gains.shape)),
+        ),
+        compiler_params=params(MIB_RESULT),
+        cost_estimate=cost(S * L, 2 * D * act_0.shape[-1], S * L * 6000),
+        name="layer_result",
     )(place, *operands)
 
 
@@ -519,7 +545,6 @@
     count = place.count
     group = jnp.minimum(step, (count + G - 1) // G - 1)
     gm_ref, dqkv, qkv_ref = (group_rows(ref, group, R) for ref in (gm_ref, dqkv, qkv_ref))
-    probs_ref = probs_ref.at[pl.ds(group * G, G)]
 
     @pl.when(step == 0)
     def _():
@@ -598,7 +623,7 @@
         grid_spec=pltpu.PrefetchScalarGridSpec(
             num_scalar_prefetch=1,
             grid=(S // G,),
-            in_specs=[series_spec(G, tokens.shape), whole(qkv.shape), whole(probs.shape),
+            in_specs=[series_spec(G, tokens.shape), whole(qkv.shape), series_spec(G, probs.shape),
                       whole(gm.shape), whole(w.shape), whole(gains.shape), whole(gf.shape)],
             out_specs=[whole(pack)] * 3,
             scratch_shapes=[
@@ -606,10 +631,10 @@
                 vm((G, PAIRS, L, PAIR), f32), vm((G, PAIRS, L, PAIR), bf16), vm((D, PAIR), f32),
             ],
         ),
-        compiler_params=params(),
+        compiler_params=params(MIB_BACKWARD),
         cost_estimate=cost(S * L, D * 3 * INNER * 4, S * L * 6000),
         name="attention_backward",
-    )(place, in_hbm(tokens), qkv, probs, gm, w, gains, gf)
+    )(place, in_hbm(tokens), qkv, in_hbm(probs), gm, w, gains, gf)
 
 
 def token_gradient(G, L, first_step, place_ref, tok_ref, dqkv_ref, gh_ref, w_ref, gains_ref, *refs):
@@ -658,7 +683,7 @@
             out_specs=(series(True), whole(gains.shape)),
         ),
         input_output_aliases={6: 0} if more else {},
-        compiler_params=params(),
+        compiler_params=params(MIB_TOKENS),
         cost_estimate=cost(S * L // 2, D * 3 * INNER * 2, S * L * 2500),
         name="token_gradient",
     )(place, in_hbm(tokens), dqkv, gh, w, gains, *more)
@@ -703,8 +728,9 @@
     return pl.pallas_call(
         functools.partial(finish, n_f),
         out_shape=tuple(sds(shape, f32) for shape in shapes),
-        in_specs=[sm] + [vm] * len(flat) + [pl.BlockSpec(memory_space=pl.ANY)],
+        in_specs=[sm] + [vm] * len(flat) + [vm],
         out_specs=[vm] * len(shapes),
+        compiler_params=small_params(),
         name="finish",
     )(place, *flat, after)
 
@@ -754,9 +780,9 @@
         pack_a = call_prepare_attention(place, n_f, attn_gain, wq, wk, wv, rel_bias, ffn_gain)
         pack_0, pack_1 = call_prepare_ffn(place, n_f, wo, wg, wu, wd)
 
-        z_a, pack_0, pack_1 = together((along_z(pack_a), pack_0, pack_1))
+        z_0 = along_z(pack_0)
+        z_a, pack_1 = together((along_z(pack_a), pack_1))
         near_a = jnp.stack(z_a)
-        z_0 = along_z(pack_0)
         far_a, near_ac = over_fsdp(near_a, 1), over_rep(near_a, 1)
         far_a, near_ac, z_0, pack_1 = together((far_a, near_ac, z_0, pack_1))
         far_ac, near_0 = over_rep(far_a, 1), jnp.stack(z_0)
@@ -769,15 +795,14 @@
         far_0c, near_1 = together((far_0c, near_1))
 
         far_1, near_1c = over_fsdp(near_1, 1), over_rep(near_1, 1)
-        hidden, part, gpart, wo_all, keep_0, send_0 = call_ffn_half(
-            True, place, (near_0, far_0, near_0c, far_0c), gains, (tokens, cotangent, mixed), S, L, D
+        hidden, act_0, gpart, wd_0, wo_all, keep_0, send_0 = call_ffn_half(
+            True, place, n_z, (near_0, far_0, near_0c, far_0c), gains, (tokens, cotangent, mixed), S, L, D
         )
         wo_all, keep_0, send_0, far_1, near_1c = together((wo_all, keep_0, send_0, far_1, near_1c))
 
-        far_1c = over_rep(far_1, 1)
-        got_0 = over_rep(send_0, 1)
-        layer_out, gh, gm, keep_1, send_1, gf = call_ffn_half(
-            False, place, (near_1, far_1, near_1c, far_1c), gains, (hidden, cotangent, mixed, part, gpart, wo_all), S, L, D
+        far_1c, got_0 = over_rep(far_1, 1), over_rep(send_0, 1)
+        gh, gm, act_1, wd_1, keep_1, send_1, gf = call_ffn_half(
+            False, place, n_z, (near_1, far_1, near_1c, far_1c), None, (hidden, cotangent, mixed, gpart, gains, wo_all), S, L, D
         )
         keep_1, send_1, gf, got_0 = together((keep_1, send_1, gf, got_0))
         here_0, away_0 = halved(keep_0, got_0)
@@ -802,7 +827,11 @@
         done, got_2, z_1 = together((done, got_2, z_1))
         own_2, z_2 = joined(here_2, got_2)
         sum_1 = summed(own_1, z_1)
-        sum_2 = summed(own_2, to_z(z_2))
+        done, z_2, sum_1 = together((done, z_2, sum_1))
+        z_2 = to_z(z_2)
+        layer_out, done = call_layer_result(place, hidden, act_0, act_1, wd_0, wd_1, done, S, L)
+        done, z_2 = together((done, z_2))
+        sum_2 = summed(own_2, z_2)
         gq, gk, gv, go, gg, gu, gd, grad_attn_gain, grad_ffn_gain, grad_bias = call_finish(
             place, n_f, [replicas(value) for value in (sum_0, sum_1, sum_2)],
             (wq.shape, wk.shape, wv.shape, wo.shape, wg.shape, wu.shape, wd.shape,

time: 169 us -> 163 us (0.964)
  waiting for transfers between devices: 52.9 us -> 33.3 us
  Pallas kernels: 37.8 us -> 50.3 us
  starting transfers between devices: 71.3 us -> 74.3 us
    ppermute x24, waiting for transfers between devices: 45.1 us -> 26.7 us  [over_fsdp(): return lax.ppermute(value, 'fsdp', [(i, i ^ distance) for i in range(n_f)])]
    pallas_call x2 -> x3, Pallas kernels: 14.7 us -> 22.6 us  [the longest x2 18 us: call_ffn_half(): pl.pallas_call(functools.partial(ffn_half, G, L, n_z, first), out_shape=t...]
    ppermute x24, starting transfers between devices: 49.6 us -> 52.5 us  [over_fsdp(): return lax.ppermute(value, 'fsdp', [(i, i ^ distance) for i in range(n_f)])]
    pallas_call x1, Pallas kernels: 3.97 us -> 6.49 us  [call_attention_forward(): pl.pallas_call(functools.partial(attention_forward, G, L, n_z), out_shape...]
    pallas_call x1, Pallas kernels: 5.37 us -> 7.48 us  [call_attention_backward(): pl.pallas_call(functools.partial(attention_backward, G, L, n_z), out_shap...]
  transfers between devices with their start and end apart: 39 -> 39, of which waited for: 19 -> 14; matrix products, arithmetic and copies ran while one was open for 1% -> 1% of each run, Pallas kernels for 20% -> 29%
where the time goes in v4:
time: 163 us
  starting transfers between devices  74.3 us (46%)
  Pallas kernels  50.3 us (31%)
  waiting for transfers between devices  33.3 us (20%)
  other arithmetic  3.6 us (2%)
    ppermute x24, starting transfers between devices, over_fsdp(): return lax.ppermute(value, 'fsdp', [(i, i ^ distance) for i in range(n_f)])  52.5 us
    ppermute x24, waiting for transfers between devices, over_fsdp(): return lax.ppermute(value, 'fsdp', [(i, i ^ distance) for i in range(n_f)])  26.7 us
    ppermute x15, starting transfers between devices, over_rep(): return lax.ppermute(value, 'rep', [(i, i ^ distance) for i in range(n_r)])  21.8 us
    pallas_call x2, Pallas kernels, call_ffn_half(): pl.pallas_call(functools.partial(ffn_half, G, L, n_z, first), out_shape=t...  18 us
    pallas_call x2, Pallas kernels, call_token_gradient(): pl.pallas_call(functools.partial(token_gradient, G, L, shift), out_shape=...  8.28 us
    pallas_call x1, Pallas kernels, call_attention_backward(): pl.pallas_call(functools.partial(attention_backward, G, L, n_z), out_shap...  7.48 us
    ppermute x15, waiting for transfers between devices, over_rep(): return lax.ppermute(value, 'rep', [(i, i ^ distance) for i in range(n_r)])  6.6 us
    pallas_call x1, Pallas kernels, call_attention_forward(): pl.pallas_call(functools.partial(attention_forward, G, L, n_z), out_shape...  6.49 us
  transfers between devices with their start and end apart: 39, of which 14 were waited for; matrix products, arithmetic and copies ran while one was open for 1% of the time, Pallas kernels for 29%

profile of v4, /device:TPU:0, one launch (start us, length us, event | category | flops | bytes accessed | tf_op | source)
XLA Modules:
  0.0 163.2 jit_solution(9901940498572341377)
XLA Ops:
  2.0 1.7 %prepare_attention.1 = bf16[64,640]{1,0:T(8,128)(2,1)} custom-call(s32[4]{0:T(128)} %pad_add_fusion.place_ref, f32[24]{0:T(128)} %bias_ref.1, f32[64,384]{1,0:T(8,128)} %wq.1, f32[64,384]{1,0:T(8,128)} %wk.1, f32[64,384]{1,0:T(8,128)} %wv.1, f32[1,64]{1,0:T(1,128)} %bitcast.94, f32[1,64]{1,0:T(1,128)} %bitcast.95), custom_call_target="tpu_custom_call" | custom-call | tf_op jit(solution)/shard_map/prepare_attention/pallas_call | solution.py:162
  3.7 5.0 %collective-permute-start.2 = (bf16[64,640]{1,0:T(8,128)(2,1)}, bf16[64,640]{1,0:T(8,128)(2,1)S(1)}, u32[]{:S(2)}, u32[]{:S(2)}) collective-permute-start(bf16[64,640]{1,0:T(8,128)(2,1)} %prepare_attention.1), channel_id=1, source_target_pairs={{0,6},{1,7},{2,4},{3,5},{4,2},{5,3},{6,0},{7,1},{8,14},{9,15},{10,... | collective-permute-start | bytes 245768 | tf_op jit(solution)/shard_map/ppermute | solution.py:743
  9.3 2.0 %prepare_ffn.1 = (bf16[240,256]{1,0:T(8,128)(2,1)}, bf16[192,256]{1,0:T(8,128)(2,1)}) custom-call(s32[4]{0:T(128)} %pad_add_fusion.place_ref, f32[48,512]{1,0:T(8,128)} %wo.1, f32[64,1024]{1,0:T(8,128)} %wg.1, f32[64,1024]{1,0:T(8,128)} %wu.1, f32[128,512]{1,0:T(8,128)} %wd.1), custom_call_target="tpu_custom_call" | custom-call | tf_op jit(solution)/shard_map/prepare_ffn/pallas_call | solution.py:174
  12.0 3.8 %collective-permute-done.1 = bf16[64,640]{1,0:T(8,128)(2,1)S(1)} collective-permute-done((bf16[64,640]{1,0:T(8,128)(2,1)}, bf16[64,640]{1,0:T(8,128)(2,1)S(1)}, u32[]{:S(2)}, u32[]{:S(2)}) %collective-permute-start.1) | collective-permute-done | bytes 81952 | tf_op jit(solution)/shard_map/ppermute | solution.py:743
  18.4 2.6 %collective-permute-start.7 = (bf16[240,256]{1,0:T(8,128)(2,1)}, bf16[240,256]{1,0:T(8,128)(2,1)S(1)}, u32[]{:S(2)}, u32[]{:S(2)}) collective-permute-start(bf16[240,256]{1,0:T(8,128)(2,1)} %get-tuple-element.129), channel_id=1, source_target_pairs={{0,6},{1,7},{2,4},{3,5},{4,2},{5,3},{6,0},{7,1},{8,14},{9,15},{10,... | collective-permute-start | bytes 368648 | tf_op jit(solution)/shard_map/ppermute | solution.py:743
  21.0 1.8 %collective-permute-start.5 = (bf16[240,256]{1,0:T(8,128)(2,1)}, bf16[240,256]{1,0:T(8,128)(2,1)S(1)}, u32[]{:S(2)}, u32[]{:S(2)}) collective-permute-start(bf16[240,256]{1,0:T(8,128)(2,1)} %get-tuple-element.129), channel_id=1, source_target_pairs={{0,2},{1,3},{2,0},{3,1},{4,6},{5,7},{6,4},{7,5},{8,10},{9,11},{10,... | collective-permute-start | bytes 368648 | tf_op jit(solution)/shard_map/ppermute | solution.py:743
  22.8 3.9 %collective-permute-done.7 = bf16[240,256]{1,0:T(8,128)(2,1)S(1)} collective-permute-done((bf16[240,256]{1,0:T(8,128)(2,1)}, bf16[240,256]{1,0:T(8,128)(2,1)S(1)}, u32[]{:S(2)}, u32[]{:S(2)}) %collective-permute-start.7) | collective-permute-done | bytes 122912 | tf_op jit(solution)/shard_map/ppermute | solution.py:743
  26.7 5.5 %collective-permute-done.6 = bf16[240,256]{1,0:T(8,128)(2,1)S(1)} collective-permute-done((bf16[240,256]{1,0:T(8,128)(2,1)}, bf16[240,256]{1,0:T(8,128)(2,1)S(1)}, u32[]{:S(2)}, u32[]{:S(2)}) %collective-permute-start.6) | collective-permute-done | bytes 122912 | tf_op jit(solution)/shard_map/ppermute | solution.py:743
  33.9 2.9 %collective-permute-start.11 = (bf16[192,256]{1,0:T(8,128)(2,1)}, bf16[192,256]{1,0:T(8,128)(2,1)S(1)}, u32[]{:S(2)}, u32[]{:S(2)}) collective-permute-start(bf16[192,256]{1,0:T(8,128)(2,1)} %get-tuple-element.140), channel_id=1, source_target_pairs={{0,2},{1,3},{2,0},{3,1},{4,6},{5,7},{6,4},{7,5},{8,10},{9,11},{10,... | collective-permute-start | bytes 294920 | tf_op jit(solution)/shard_map/ppermute | solution.py:743
  38.4 6.5 %attention_forward.1 = (bf16[3072,1152]{1,0:T(8,128)(2,1)S(1)}, bf16[48,3,64,128]{3,2,1,0:T(8,128)(2,1)}, bf16[3072,384]{1,0:T(8,128)(2,1)S(1)}, bf16[512,1152]{1,0:T(8,128)(2,1)S(1)}, f32[8,512]{1,0:T(8,128)S(1)}) custom-call(s32[4]{0:T(128)} %pad_add_fusion.place_ref, bf16[48,64,512]{2,1,0:T(8,128)(2,1)} %tok_ref.7, ...), custom_call_target="tpu_custom_call" | custom-call | flops 14495514624 | bytes 15360000 | tf_op jit(solution)/shard_map/attention_forward/pallas_call | solution.py:283
  44.9 6.5 %collective-permute-done.9.refs_1_ = bf16[4,240,256]{2,1,0:T(8,128)(2,1)S(1)} collective-permute-done((bf16[4,240,256]{2,1,0:T(8,128)(2,1)S(1)}, bf16[4,240,256]{2,1,0:T(8,128)(2,1)S(1)}, u32[]{:S(2)}, u32[]{:S(2)}) %collective-permute-start.9) | collective-permute-done | bytes 491552 | tf_op jit(solution)/shard_map/ppermute | solution.py:743
  51.5 1.8 %collective-permute-done.14.refs_3_ = bf16[4,240,256]{2,1,0:T(8,128)(2,1)S(1)} collective-permute-done((bf16[4,240,256]{2,1,0:T(8,128)(2,1)S(1)}, bf16[4,240,256]{2,1,0:T(8,128)(2,1)S(1)}, u32[]{:S(2)}, u32[]{:S(2)}) %collective-permute-start.14) | collective-permute-done | bytes 491552 | tf_op jit(solution)/shard_map/ppermute | solution.py:746
  53.5 1.7 %collective-permute-start.15 = (bf16[4,192,256]{2,1,0:T(8,128)(2,1)S(1)}, bf16[4,192,256]{2,1,0:T(8,128)(2,1)S(1)}, u32[]{:S(2)}, u32[]{:S(2)}) collective-permute-start(bf16[4,192,256]{2,1,0:T(8,128)(2,1)S(1)} %pad_maximum_fusion.1.refs_0_), channel_id=1, source_target_pairs={{0,1},{1,0},{2,3},{3,2},{4,5},{5,4},{6,7},{7,6},{8,9},{9,8},{10,11... | collective-permute-start | bytes 1179656 | tf_op jit(solution)/shard_map/ppermute | solution.py:743
  55.2 8.7 %ffn_first.1 = (f32[3072,512]{1,0:T(8,128)S(1)}, bf16[3072,512]{1,0:T(8,128)(2,1)S(1)}, bf16[3072,512]{1,0:T(8,128)(2,1)S(1)}, bf16[512,512]{1,0:T(8,128)(2,1)S(...) custom-call(s32[4]{0:T(128)} %pad_add_fusion.place_ref, ...), custom_call_target="tpu_custom_call" | custom-call | flops 14495514624 | bytes 27648000 | tf_op jit(solution)/shard_map/ffn_first/pallas_call | solution.py:484
  66.6 9.3 %ffn_second.1 = (bf16[3072,512]{1,0:T(8,128)(2,1)S(1)}, bf16[3072,384]{1,0:T(8,128)(2,1)S(1)}, bf16[3072,512]{1,0:T(8,128)(2,1)S(1)}, bf16[512,512]{1,0:T(8,128)...) custom-call(s32[4]{0:T(128)} %pad_add_fusion.place_ref, ...), custom_call_target="tpu_custom_call" | custom-call | flops 14495514624 | bytes 27648000 | tf_op jit(solution)/shard_map/ffn_second/pallas_call | solution.py:484
  76.0 11.2 %collective-permute-start.19 = (bf16[4,192,256]{2,1,0:T(8,128)(2,1)S(1)}, bf16[4,192,256]{2,1,0:T(8,128)(2,1)S(1)}, u32[]{:S(2)}, u32[]{:S(2)}) collective-permute-start(bf16[4,192,256]{2,1,0:T(8,128)(2,1)S(1)} %fusion.1), channel_id=1, source_target_pairs={{0,1},{1,0},{2,3},{3,2},{4,5},{5,4},{6,7},{7,6},{8,9},{9,8},{10,11... | collective-permute-start | bytes 1179656 | tf_op jit(solution)/shard_map/ppermute | solution.py:743
  87.2 13.3 %collective-permute-start.20 = (bf16[2,4,240,256]{3,2,1,0:T(8,128)(2,1)S(1)}, bf16[2,4,240,256]{3,2,1,0:T(8,128)(2,1)S(1)}, u32[]{:S(2)}, u32[]{:S(2)}) collective-permute-start(bf16[2,4,240,256]{3,2,1,0:T(8,128)(2,1)S(1)} %get-tuple-element.177), channel_id=1, source_target_pairs={{0,8},{8,0},{16,24},{24,16},{1,9},{9,1},{17,25},{25,17},{2,10},{10... | collective-permute-start | bytes 2949128 | tf_op jit(solution)/shard_map/ppermute | solution.py:746
  100.5 7.5 %attention_backward.1 = (bf16[3072,1152]{1,0:T(8,128)(2,1)S(1)}, bf16[2,4,64,640]{3,2,1,0:T(8,128)(2,1)S(1)}, bf16[2,4,64,640]{3,2,1,0:T(8,128)(2,1)S(1)}) custom-call(s32[4]{0:T(128)} %pad_add_fusion.place_ref, bf16[48,64,512]{2,1,0:T(8,128)(2,1)} %tok_ref.7, bf16[3072,1152]{1,0:T(8,128)(2,1)S(1)} %get-tuple-element.160.qkv_ref, ...), custom_call_target="tpu_custom_call" | custom-call | flops 14495514624 | bytes 18432000 | tf_op jit(solution)/shard_map/attention_backward/pallas_call | solution.py:620
  108.4 8.2 %collective-permute-start.24 = (bf16[4,240,256]{2,1,0:T(8,128)(2,1)S(1)}, bf16[4,240,256]{2,1,0:T(8,128)(2,1)S(1)}, u32[]{:S(2)}, u32[]{:S(2)}) collective-permute-start(bf16[4,240,256]{2,1,0:T(8,128)(2,1)S(1)} %fusion), channel_id=1, source_target_pairs={{0,1},{1,0},{2,3},{3,2},{4,5},{5,4},{6,7},{7,6},{8,9},{9,8},{10,11... | collective-permute-start | bytes 1474568 | tf_op jit(solution)/shard_map/ppermute | solution.py:743
  118.0 3.0 %collective-permute-start.23 = (bf16[192,256]{1,0:T(8,128)(2,1)S(1)}, bf16[192,256]{1,0:T(8,128)(2,1)S(1)}, u32[]{:S(2)}, u32[]{:S(2)}) collective-permute-start(bf16[192,256]{1,0:T(8,128)(2,1)S(1)} %get-tuple-element.185), channel_id=1, source_target_pairs={{0,6},{1,7},{2,4},{3,5},{4,2},{5,3},{6,0},{7,1},{8,14},{9,15},{10,... | collective-permute-start | bytes 294920 | tf_op jit(solution)/shard_map/ppermute | solution.py:743
  121.0 4.9 %token_gradient.2 = (bf16[48,64,512]{2,1,0:T(8,128)(2,1)}, f32[8,512]{1,0:T(8,128)S(1)}) custom-call(s32[4]{0:T(128)} %pad_add_fusion.place_ref, bf16[48,64,512]{2,1,0:T(8,128)(2,1)} %tok_ref.7, bf16[3072,1152]{1,0:T(8,128)(2,1)S(1)} %get-tuple-element.172.dqkv_ref, bf16[3072,512]{1,0:T(8,128)(2,1)S(1)} %get-tuple-element.173.gh_ref, ...), custom_call_target="tpu_custom_call" | custom-call | flops 3623878656 | bytes 7680000 | tf_op jit(solution)/shard_map/token_gradient/pallas_call | solution.py:675
  125.9 1.8 %collective-permute-done.22 = bf16[192,256]{1,0:T(8,128)(2,1)S(1)} collective-permute-done((bf16[192,256]{1,0:T(8,128)(2,1)S(1)}, bf16[192,256]{1,0:T(8,128)(2,1)S(1)}, u32[]{:S(2)}, u32[]{:S(2)}) %collective-permute-start.22) | collective-permute-done | bytes 98336 | tf_op jit(solution)/shard_map/ppermute | solution.py:743
  128.4 3.9 %collective-permute-start.30 = (bf16[192,256]{1,0:T(8,128)(2,1)S(1)}, bf16[192,256]{1,0:T(8,128)(2,1)S(1)}, u32[]{:S(2)}, u32[]{:S(2)}) collective-permute-start(bf16[192,256]{1,0:T(8,128)(2,1)S(1)} %fusion.10), channel_id=1, source_target_pairs={{0,16},{8,24},{16,0},{24,8},{1,17},{9,25},{17,1},{25,9},{2,18},{10... | collective-permute-start | bytes 294920 | tf_op jit(solution)/shard_map/ppermute | solution.py:746
  133.0 3.7 %collective-permute-start.29 = (bf16[240,256]{1,0:T(8,128)(2,1)S(1)}, bf16[240,256]{1,0:T(8,128)(2,1)S(1)}, u32[]{:S(2)}, u32[]{:S(2)}) collective-permute-start(bf16[240,256]{1,0:T(8,128)(2,1)S(1)} %get-tuple-element.201), channel_id=1, source_target_pairs={{0,6},{1,7},{2,4},{3,5},{4,2},{5,3},{6,0},{7,1},{8,14},{9,15},{10,... | collective-permute-start | bytes 368648 | tf_op jit(solution)/shard_map/ppermute | solution.py:743
  138.2 3.4 %token_gradient.3 = (bf16[48,64,512]{2,1,0:T(8,128)(2,1)}, f32[8,512]{1,0:T(8,128)S(1)}) custom-call(s32[4]{0:T(128)} %pad_add_fusion.place_ref, bf16[48,64,512]{2,1,0:T(8,128)(2,1)} %tok_ref.7, bf16[3072,1152]{1,0:T(8,128)(2,1)S(1)} %get-tuple-element.172.dqkv_ref, ...), custom_call_target="tpu_custom_call", output_to_operand_aliasing={{0}: (6, {})} | custom-call | flops 3623878656 | bytes 7680000 | tf_op jit(solution)/shard_map/token_gradient/pallas_call | solution.py:675
  141.7 2.8 %collective-permute-done.28 = bf16[240,256]{1,0:T(8,128)(2,1)S(1)} collective-permute-done((bf16[240,256]{1,0:T(8,128)(2,1)S(1)}, bf16[240,256]{1,0:T(8,128)(2,1)S(1)}, u32[]{:S(2)}, u32[]{:S(2)}) %collective-permute-start.28) | collective-permute-done | bytes 122912 | tf_op jit(solution)/shard_map/ppermute | solution.py:743
  145.1 1.6 collective-permute-start.34
  146.8 2.8 %collective-permute-start.36 = (bf16[64,640]{1,0:T(8,128)(2,1)S(1)}, bf16[64,640]{1,0:T(8,128)(2,1)S(1)}, u32[]{:S(2)}, u32[]{:S(2)}) collective-permute-start(bf16[64,640]{1,0:T(8,128)(2,1)S(1)} %get-tuple-element.215), channel_id=1, source_target_pairs={{0,6},{1,7},{2,4},{3,5},{4,2},{5,3},{6,0},{7,1},{8,14},{9,15},{10,... | collective-permute-start | bytes 245768 | tf_op jit(solution)/shard_map/ppermute | solution.py:743
  149.9 4.6 %layer_result.1 = (bf16[48,64,512]{2,1,0:T(8,128)(2,1)}, f32[8,512]{1,0:T(8,128)S(1)}) custom-call(s32[4]{0:T(128)} %pad_add_fusion.place_ref, f32[3072,512]{1,0:T(8,128)S(1)} %get-tuple-element.147.refs_4_.hid_ref, bf16[3072,512]{1,0:T(8,128)(2,1)S(1)} %get-tuple-element.148.act_0, bf16[3072,512]{1,0:T(8,128)(2,1)S(1)} %get-tuple-element.157.act_1, ...), custom_call_target="tpu_custom_call" | custom-call | flops 3221225472 | bytes 18432000 | tf_op jit(solution)/shard_map/layer_result/pallas_call | solution.py:523
  154.6 3.1 %collective-permute-start.37 = (bf16[64,640]{1,0:T(8,128)(2,1)S(1)}, bf16[64,640]{1,0:T(8,128)(2,1)S(1)}, u32[]{:S(2)}, u32[]{:S(2)}) collective-permute-start(bf16[64,640]{1,0:T(8,128)(2,1)S(1)} %fusion.14), channel_id=1, source_target_pairs={{0,16},{8,24},{16,0},{24,8},{1,17},{9,25},{17,1},{25,9},{2,18},{10... | collective-permute-start | bytes 245768 | tf_op jit(solution)/shard_map/ppermute | solution.py:746
  157.8 2.3 %collective-permute-done.37 = bf16[64,640]{1,0:T(8,128)(2,1)S(1)} collective-permute-done((bf16[64,640]{1,0:T(8,128)(2,1)S(1)}, bf16[64,640]{1,0:T(8,128)(2,1)S(1)}, u32[]{:S(2)}, u32[]{:S(2)}) %collective-permute-start.37) | collective-permute-done | bytes 81952 | tf_op jit(solution)/shard_map/ppermute | solution.py:746
  161.4 1.8 %finish.1 = (f32[64,384]{1,0:T(8,128)}, f32[64,384]{1,0:T(8,128)}, f32[64,384]{1,0:T(8,128)}, f32[48,512]{1,0:T(8,128)}, f32[64,1024]{1,0:T(8,128)}, /*index=5*/...) custom-call(s32[4]{0:T(128)} %pad_add_fusion.place_ref, ...), custom_call_target="tpu_custom_call" | custom-call | tf_op jit(solution)/shard_map/finish/pallas_call | solution.py:728
  (77 shorter events, 18.0 us)
Async XLA Ops:
  3.7 8.3 %collective-permute-start.2 = (bf16[64,640]{1,0:T(8,128)(2,1)}, bf16[64,640]{1,0:T(8,128)(2,1)S(1)}, u32[]{:S(2)}, u32[]{:S(2)}) collective-permute-start(bf16[64,640]{1,0:T(8,128)(2,1)} %prepare_attention.1), channel_id=1, source_target_pairs={{0,6},{1,7},{2,4},{3,5},{4,2},{5,3},{6,0},{7,1},{8,14},{9,15},{10,... | collective-permute-start | bytes 245768 | tf_op jit(solution)/shard_map/ppermute | solution.py:743
  8.7 7.1 %collective-permute-start.1 = (bf16[64,640]{1,0:T(8,128)(2,1)}, bf16[64,640]{1,0:T(8,128)(2,1)S(1)}, u32[]{:S(2)}, u32[]{:S(2)}) collective-permute-start(bf16[64,640]{1,0:T(8,128)(2,1)} %prepare_attention.1), channel_id=1, source_target_pairs={{0,4},{1,5},{2,6},{3,7},{4,0},{5,1},{6,2},{7,3},{8,12},{9,13},{10,... | collective-permute-start | bytes 245768 | tf_op jit(solution)/shard_map/ppermute | solution.py:743
  16.8 15.5 %collective-permute-start.4 = (bf16[4,64,640]{2,1,0:T(8,128)(2,1)S(1)}, bf16[4,64,640]{2,1,0:T(8,128)(2,1)S(1)}, u32[]{:S(2)}, u32[]{:S(2)}) collective-permute-start(bf16[4,64,640]{2,1,0:T(8,128)(2,1)S(1)} %pad_maximum_fusion.2.refs_0_), channel_id=1, source_target_pairs={{0,8},{8,0},{16,24},{24,16},{1,9},{9,1},{17,25},{25,17},{2,10},{10... | collective-permute-start | bytes 983048 | tf_op jit(solution)/shard_map/ppermute | solution.py:746
  16.8 15.4 %collective-permute-start.3 = (bf16[4,64,640]{2,1,0:T(8,128)(2,1)S(1)}, bf16[4,64,640]{2,1,0:T(8,128)(2,1)S(1)}, u32[]{:S(2)}, u32[]{:S(2)}) collective-permute-start(bf16[4,64,640]{2,1,0:T(8,128)(2,1)S(1)} %pad_maximum_fusion.2.refs_0_), channel_id=1, source_target_pairs={{0,1},{1,0},{2,3},{3,2},{4,5},{5,4},{6,7},{7,6},{8,9},{9,8},{10,11... | collective-permute-start | bytes 983048 | tf_op jit(solution)/shard_map/ppermute | solution.py:743
  18.4 8.3 %collective-permute-start.7 = (bf16[240,256]{1,0:T(8,128)(2,1)}, bf16[240,256]{1,0:T(8,128)(2,1)S(1)}, u32[]{:S(2)}, u32[]{:S(2)}) collective-permute-start(bf16[240,256]{1,0:T(8,128)(2,1)} %get-tuple-element.129), channel_id=1, source_target_pairs={{0,6},{1,7},{2,4},{3,5},{4,2},{5,3},{6,0},{7,1},{8,14},{9,15},{10,... | collective-permute-start | bytes 368648 | tf_op jit(solution)/shard_map/ppermute | solution.py:743
  21.0 11.2 %collective-permute-start.6 = (bf16[240,256]{1,0:T(8,128)(2,1)}, bf16[240,256]{1,0:T(8,128)(2,1)S(1)}, u32[]{:S(2)}, u32[]{:S(2)}) collective-permute-start(bf16[240,256]{1,0:T(8,128)(2,1)} %get-tuple-element.129), channel_id=1, source_target_pairs={{0,4},{1,5},{2,6},{3,7},{4,0},{5,1},{6,2},{7,3},{8,12},{9,13},{10,... | collective-permute-start | bytes 368648 | tf_op jit(solution)/shard_map/ppermute | solution.py:743
  21.0 11.2 %collective-permute-start.5 = (bf16[240,256]{1,0:T(8,128)(2,1)}, bf16[240,256]{1,0:T(8,128)(2,1)S(1)}, u32[]{:S(2)}, u32[]{:S(2)}) collective-permute-start(bf16[240,256]{1,0:T(8,128)(2,1)} %get-tuple-element.129), channel_id=1, source_target_pairs={{0,2},{1,3},{2,0},{3,1},{4,6},{5,7},{6,4},{7,5},{8,10},{9,11},{10,... | collective-permute-start | bytes 368648 | tf_op jit(solution)/shard_map/ppermute | solution.py:743
  32.3 12.6 %collective-permute-start.13 = (bf16[192,256]{1,0:T(8,128)(2,1)}, bf16[192,256]{1,0:T(8,128)(2,1)S(1)}, u32[]{:S(2)}, u32[]{:S(2)}) collective-permute-start(bf16[192,256]{1,0:T(8,128)(2,1)} %get-tuple-element.140), channel_id=1, source_target_pairs={{0,6},{1,7},{2,4},{3,5},{4,2},{5,3},{6,0},{7,1},{8,14},{9,15},{10,... | collective-permute-start | bytes 294920 | tf_op jit(solution)/shard_map/ppermute | solution.py:743
  33.9 11.1 %collective-permute-start.12 = (bf16[192,256]{1,0:T(8,128)(2,1)}, bf16[192,256]{1,0:T(8,128)(2,1)S(1)}, u32[]{:S(2)}, u32[]{:S(2)}) collective-permute-start(bf16[192,256]{1,0:T(8,128)(2,1)} %get-tuple-element.140), channel_id=1, source_target_pairs={{0,4},{1,5},{2,6},{3,7},{4,0},{5,1},{6,2},{7,3},{8,12},{9,13},{10,... | collective-permute-start | bytes 294920 | tf_op jit(solution)/shard_map/ppermute | solution.py:743
  33.9 11.1 %collective-permute-start.11 = (bf16[192,256]{1,0:T(8,128)(2,1)}, bf16[192,256]{1,0:T(8,128)(2,1)S(1)}, u32[]{:S(2)}, u32[]{:S(2)}) collective-permute-start(bf16[192,256]{1,0:T(8,128)(2,1)} %get-tuple-element.140), channel_id=1, source_target_pairs={{0,2},{1,3},{2,0},{3,1},{4,6},{5,7},{6,4},{7,5},{8,10},{9,11},{10,... | collective-permute-start | bytes 294920 | tf_op jit(solution)/shard_map/ppermute | solution.py:743
  37.8 7.2 %collective-permute-start.10 = (bf16[4,240,256]{2,1,0:T(8,128)(2,1)S(1)}, bf16[4,240,256]{2,1,0:T(8,128)(2,1)S(1)}, u32[]{:S(2)}, u32[]{:S(2)}) collective-permute-start(bf16[4,240,256]{2,1,0:T(8,128)(2,1)S(1)} %pad_maximum_fusion.refs_0_), channel_id=1, source_target_pairs={{0,8},{8,0},{16,24},{24,16},{1,9},{9,1},{17,25},{25,17},{2,10},{10... | collective-permute-start | bytes 1474568 | tf_op jit(solution)/shard_map/ppermute | solution.py:746
  37.8 13.6 %collective-permute-start.9 = (bf16[4,240,256]{2,1,0:T(8,128)(2,1)S(1)}, bf16[4,240,256]{2,1,0:T(8,128)(2,1)S(1)}, u32[]{:S(2)}, u32[]{:S(2)}) collective-permute-start(bf16[4,240,256]{2,1,0:T(8,128)(2,1)S(1)} %pad_maximum_fusion.refs_0_), channel_id=1, source_target_pairs={{0,1},{1,0},{2,3},{3,2},{4,5},{5,4},{6,7},{7,6},{8,9},{9,8},{10,11... | collective-permute-start | bytes 1474568 | tf_op jit(solution)/shard_map/ppermute | solution.py:743
  53.3 10.6 %collective-permute-start.16 = (bf16[4,192,256]{2,1,0:T(8,128)(2,1)S(1)}, bf16[4,192,256]{2,1,0:T(8,128)(2,1)S(1)}, u32[]{:S(2)}, u32[]{:S(2)}) collective-permute-start(bf16[4,192,256]{2,1,0:T(8,128)(2,1)S(1)} %pad_maximum_fusion.1.refs_0_), channel_id=1, source_target_pairs={{0,8},{8,0},{16,24},{24,16},{1,9},{9,1},{17,25},{25,17},{2,10},{10... | collective-permute-start | bytes 1179656 | tf_op jit(solution)/shard_map/ppermute | solution.py:746
  53.5 11.4 %collective-permute-start.15 = (bf16[4,192,256]{2,1,0:T(8,128)(2,1)S(1)}, bf16[4,192,256]{2,1,0:T(8,128)(2,1)S(1)}, u32[]{:S(2)}, u32[]{:S(2)}) collective-permute-start(bf16[4,192,256]{2,1,0:T(8,128)(2,1)S(1)} %pad_maximum_fusion.1.refs_0_), channel_id=1, source_target_pairs={{0,1},{1,0},{2,3},{3,2},{4,5},{5,4},{6,7},{7,6},{8,9},{9,8},{10,11... | collective-permute-start | bytes 1179656 | tf_op jit(solution)/shard_map/ppermute | solution.py:743
  64.9 11.0 %collective-permute-start.18 = (bf16[2,4,192,256]{3,2,1,0:T(8,128)(2,1)S(1)}, bf16[2,4,192,256]{3,2,1,0:T(8,128)(2,1)S(1)}, u32[]{:S(2)}, u32[]{:S(2)}) collective-permute-start(bf16[2,4,192,256]{3,2,1,0:T(8,128)(2,1)S(1)} %get-tuple-element.168), channel_id=1, source_target_pairs={{0,8},{8,0},{16,24},{24,16},{1,9},{9,1},{17,25},{25,17},{2,10},{10... | collective-permute-start | bytes 2359304 | tf_op jit(solution)/shard_map/ppermute | solution.py:746
  76.0 32.0 %collective-permute-start.19 = (bf16[4,192,256]{2,1,0:T(8,128)(2,1)S(1)}, bf16[4,192,256]{2,1,0:T(8,128)(2,1)S(1)}, u32[]{:S(2)}, u32[]{:S(2)}) collective-permute-start(bf16[4,192,256]{2,1,0:T(8,128)(2,1)S(1)} %fusion.1), channel_id=1, source_target_pairs={{0,1},{1,0},{2,3},{3,2},{4,5},{5,4},{6,7},{7,6},{8,9},{9,8},{10,11... | collective-permute-start | bytes 1179656 | tf_op jit(solution)/shard_map/ppermute | solution.py:743
  87.2 20.8 %collective-permute-start.20 = (bf16[2,4,240,256]{3,2,1,0:T(8,128)(2,1)S(1)}, bf16[2,4,240,256]{3,2,1,0:T(8,128)(2,1)S(1)}, u32[]{:S(2)}, u32[]{:S(2)}) collective-permute-start(bf16[2,4,240,256]{3,2,1,0:T(8,128)(2,1)S(1)} %get-tuple-element.177), channel_id=1, source_target_pairs={{0,8},{8,0},{16,24},{24,16},{1,9},{9,1},{17,25},{25,17},{2,10},{10... | collective-permute-start | bytes 2949128 | tf_op jit(solution)/shard_map/ppermute | solution.py:746
  108.2 19.9 %collective-permute-start.25 = (bf16[2,4,64,640]{3,2,1,0:T(8,128)(2,1)S(1)}, bf16[2,4,64,640]{3,2,1,0:T(8,128)(2,1)S(1)}, u32[]{:S(2)}, u32[]{:S(2)}) collective-permute-start(bf16[2,4,64,640]{3,2,1,0:T(8,128)(2,1)S(1)} %get-tuple-element.187), channel_id=1, source_target_pairs={{0,8},{8,0},{16,24},{24,16},{1,9},{9,1},{17,25},{25,17},{2,10},{10... | collective-permute-start | bytes 1966088 | tf_op jit(solution)/shard_map/ppermute | solution.py:746
  108.4 19.6 %collective-permute-start.24 = (bf16[4,240,256]{2,1,0:T(8,128)(2,1)S(1)}, bf16[4,240,256]{2,1,0:T(8,128)(2,1)S(1)}, u32[]{:S(2)}, u32[]{:S(2)}) collective-permute-start(bf16[4,240,256]{2,1,0:T(8,128)(2,1)S(1)} %fusion), channel_id=1, source_target_pairs={{0,1},{1,0},{2,3},{3,2},{4,5},{5,4},{6,7},{7,6},{8,9},{9,8},{10,11... | collective-permute-start | bytes 1474568 | tf_op jit(solution)/shard_map/ppermute | solution.py:743
  116.6 9.3 %collective-permute-start.21 = (bf16[192,256]{1,0:T(8,128)(2,1)S(1)}, bf16[192,256]{1,0:T(8,128)(2,1)S(1)}, u32[]{:S(2)}, u32[]{:S(2)}) collective-permute-start(bf16[192,256]{1,0:T(8,128)(2,1)S(1)} %get-tuple-element.183), channel_id=1, source_target_pairs={{0,2},{1,3},{2,0},{3,1},{4,6},{5,7},{6,4},{7,5},{8,10},{9,11},{10,... | collective-permute-start | bytes 294920 | tf_op jit(solution)/shard_map/ppermute | solution.py:743
  117.0 10.6 %collective-permute-start.22 = (bf16[192,256]{1,0:T(8,128)(2,1)S(1)}, bf16[192,256]{1,0:T(8,128)(2,1)S(1)}, u32[]{:S(2)}, u32[]{:S(2)}) collective-permute-start(bf16[192,256]{1,0:T(8,128)(2,1)S(1)} %get-tuple-element.184), channel_id=1, source_target_pairs={{0,4},{1,5},{2,6},{3,7},{4,0},{5,1},{6,2},{7,3},{8,12},{9,13},{10,... | collective-permute-start | bytes 294920 | tf_op jit(solution)/shard_map/ppermute | solution.py:743
  118.0 9.7 %collective-permute-start.23 = (bf16[192,256]{1,0:T(8,128)(2,1)S(1)}, bf16[192,256]{1,0:T(8,128)(2,1)S(1)}, u32[]{:S(2)}, u32[]{:S(2)}) collective-permute-start(bf16[192,256]{1,0:T(8,128)(2,1)S(1)} %get-tuple-element.185), channel_id=1, source_target_pairs={{0,6},{1,7},{2,4},{3,5},{4,2},{5,3},{6,0},{7,1},{8,14},{9,15},{10,... | collective-permute-start | bytes 294920 | tf_op jit(solution)/shard_map/ppermute | solution.py:743
  128.4 13.2 %collective-permute-start.30 = (bf16[192,256]{1,0:T(8,128)(2,1)S(1)}, bf16[192,256]{1,0:T(8,128)(2,1)S(1)}, u32[]{:S(2)}, u32[]{:S(2)}) collective-permute-start(bf16[192,256]{1,0:T(8,128)(2,1)S(1)} %fusion.10), channel_id=1, source_target_pairs={{0,16},{8,24},{16,0},{24,8},{1,17},{9,25},{17,1},{25,9},{2,18},{10... | collective-permute-start | bytes 294920 | tf_op jit(solution)/shard_map/ppermute | solution.py:746
  132.3 9.4 %collective-permute-start.27 = (bf16[240,256]{1,0:T(8,128)(2,1)S(1)}, bf16[240,256]{1,0:T(8,128)(2,1)S(1)}, u32[]{:S(2)}, u32[]{:S(2)}) collective-permute-start(bf16[240,256]{1,0:T(8,128)(2,1)S(1)} %get-tuple-element.199), channel_id=1, source_target_pairs={{0,2},{1,3},{2,0},{3,1},{4,6},{5,7},{6,4},{7,5},{8,10},{9,11},{10,... | collective-permute-start | bytes 368648 | tf_op jit(solution)/shard_map/ppermute | solution.py:743
  132.9 11.6 %collective-permute-start.28 = (bf16[240,256]{1,0:T(8,128)(2,1)S(1)}, bf16[240,256]{1,0:T(8,128)(2,1)S(1)}, u32[]{:S(2)}, u32[]{:S(2)}) collective-permute-start(bf16[240,256]{1,0:T(8,128)(2,1)S(1)} %get-tuple-element.200), channel_id=1, source_target_pairs={{0,4},{1,5},{2,6},{3,7},{4,0},{5,1},{6,2},{7,3},{8,12},{9,13},{10,... | collective-permute-start | bytes 368648 | tf_op jit(solution)/shard_map/ppermute | solution.py:743
  133.0 11.5 %collective-permute-start.29 = (bf16[240,256]{1,0:T(8,128)(2,1)S(1)}, bf16[240,256]{1,0:T(8,128)(2,1)S(1)}, u32[]{:S(2)}, u32[]{:S(2)}) collective-permute-start(bf16[240,256]{1,0:T(8,128)(2,1)S(1)} %get-tuple-element.201), channel_id=1, source_target_pairs={{0,6},{1,7},{2,4},{3,5},{4,2},{5,3},{6,0},{7,1},{8,14},{9,15},{10,... | collective-permute-start | bytes 368648 | tf_op jit(solution)/shard_map/ppermute | solution.py:743
  136.7 8.2 %collective-permute-start.26 = (bf16[4,64,640]{2,1,0:T(8,128)(2,1)S(1)}, bf16[4,64,640]{2,1,0:T(8,128)(2,1)S(1)}, u32[]{:S(2)}, u32[]{:S(2)}) collective-permute-start(bf16[4,64,640]{2,1,0:T(8,128)(2,1)S(1)} %fusion.2), channel_id=1, source_target_pairs={{0,1},{1,0},{2,3},{3,2},{4,5},{5,4},{6,7},{7,6},{8,9},{9,8},{10,11... | collective-permute-start | bytes 983048 | tf_op jit(solution)/shard_map/ppermute | solution.py:743
  141.6 18.6 %collective-permute-start.31 = (bf16[192,256]{1,0:T(8,128)(2,1)S(1)}, bf16[192,256]{1,0:T(8,128)(2,1)S(1)}, u32[]{:S(2)}, u32[]{:S(2)}) collective-permute-start(bf16[192,256]{1,0:T(8,128)(2,1)S(1)} %add_convert_fusion.4.refs_0_), channel_id=1, source_target_pairs={{0,8},{8,0},{16,24},{24,16},{1,9},{9,1},{17,25},{25,17},{2,10},{10... | collective-permute-start | bytes 294920 | tf_op jit(solution)/shard_map/ppermute | solution.py:746
  145.1 9.4 %collective-permute-start.34 = (bf16[64,640]{1,0:T(8,128)(2,1)S(1)}, bf16[64,640]{1,0:T(8,128)(2,1)S(1)}, u32[]{:S(2)}, u32[]{:S(2)}) collective-permute-start(bf16[64,640]{1,0:T(8,128)(2,1)S(1)} %get-tuple-element.213), channel_id=1, source_target_pairs={{0,2},{1,3},{2,0},{3,1},{4,6},{5,7},{6,4},{7,5},{8,10},{9,11},{10,... | collective-permute-start | bytes 245768 | tf_op jit(solution)/shard_map/ppermute | solution.py:743
  146.7 7.8 %collective-permute-start.35 = (bf16[64,640]{1,0:T(8,128)(2,1)S(1)}, bf16[64,640]{1,0:T(8,128)(2,1)S(1)}, u32[]{:S(2)}, u32[]{:S(2)}) collective-permute-start(bf16[64,640]{1,0:T(8,128)(2,1)S(1)} %get-tuple-element.214), channel_id=1, source_target_pairs={{0,4},{1,5},{2,6},{3,7},{4,0},{5,1},{6,2},{7,3},{8,12},{9,13},{10,... | collective-permute-start | bytes 245768 | tf_op jit(solution)/shard_map/ppermute | solution.py:743
  146.8 7.7 %collective-permute-start.36 = (bf16[64,640]{1,0:T(8,128)(2,1)S(1)}, bf16[64,640]{1,0:T(8,128)(2,1)S(1)}, u32[]{:S(2)}, u32[]{:S(2)}) collective-permute-start(bf16[64,640]{1,0:T(8,128)(2,1)S(1)} %get-tuple-element.215), channel_id=1, source_target_pairs={{0,6},{1,7},{2,4},{3,5},{4,2},{5,3},{6,0},{7,1},{8,14},{9,15},{10,... | collective-permute-start | bytes 245768 | tf_op jit(solution)/shard_map/ppermute | solution.py:743
  149.6 8.1 %collective-permute-start.32 = (bf16[240,256]{1,0:T(8,128)(2,1)S(1)}, bf16[240,256]{1,0:T(8,128)(2,1)S(1)}, u32[]{:S(2)}, u32[]{:S(2)}) collective-permute-start(bf16[240,256]{1,0:T(8,128)(2,1)S(1)} %fusion.6), channel_id=1, source_target_pairs={{0,16},{8,24},{16,0},{24,8},{1,17},{9,25},{17,1},{25,9},{2,18},{10... | collective-permute-start | bytes 368648 | tf_op jit(solution)/shard_map/ppermute | solution.py:746
  (8 other events, 40.5 us)

commit v5 on v4

--- a/solution.py
+++ b/solution.py
@@ -180,9 +180,32 @@
     )(place, wo, wg, wu, wd)
 
 
-def attention_forward(G, L, n_z, place_ref, tok_ref, *refs):
+def keep_close(G, tok_ref, ct_ref, tok_out, ct_out, done_ref):
+    series = pl.ds(pl.program_id(0) * G, G)
+    tok_out[series] = tok_ref[...]
+    ct_out[series] = ct_ref[...]
+    done_ref[...] = jnp.zeros_like(done_ref)
+
+
+def call_keep_close(tokens, ct):
+    S, L, D = tokens.shape
+    G = GROUP
+    block = pl.BlockSpec((G, L, D), lambda i: (i, 0, 0))
+    return pl.pallas_call(
+        functools.partial(keep_close, G),
+        out_shape=(sds(tokens.shape, bf16), sds(ct.shape, bf16), sds((8, PAIR), f32)),
+        grid=(S // G,),
+        in_specs=[block, block],
+        out_specs=[whole(tokens.shape), whole(ct.shape), whole((8, PAIR))],
+        compiler_params=params(MIB_TOKENS),
+        cost_estimate=cost(S * L, 1, 8 * S * L * D),
+        name="keep_close",
+    )(in_hbm(tokens), in_hbm(ct))
+
+
+def attention_forward(G, L, n_z, place_ref, tok_ref, after_ref, *refs):
     pieces, refs = refs[:4], refs[4:]
-    all_qkv, probs_ref, mixed_ref, w_ref, gains_ref, table_ref, st_ref, small_ref = refs
+    all_qkv, all_probs, mixed_ref, w_ref, gains_ref, table_ref, st_ref, small_ref = refs
     step = pl.program_id(0)
     place = Place(place_ref, n_z)
     D = tok_ref.shape[-1]
@@ -224,7 +247,8 @@
     @pl.when(step * G < place.count)
     def _():
         mixed, qkv_ref = group_rows(mixed_ref, step, G * L), group_rows(all_qkv, step, G * L)
-        x = tok_ref[...].reshape(G * L, D).astype(f32)
+        probs_ref = all_probs.at[pl.ds(step * G, G)]
+        x = tok_ref[pl.ds(step * G, G)].reshape(G * L, D).astype(f32)
         normed = (x * inverse_rms(x) * gains_ref[0:1, :]).astype(bf16)
         qkv_ref[...] = nn(normed, w_ref[...]).astype(bf16)
         for s in range(G):
@@ -245,7 +269,7 @@
                 mixed[rows, pl.ds(p * PAIR, PAIR)] = join_heads(tn(probs_ref[s, p], v)).astype(bf16)
 
 
-MIB_FORWARD, MIB_FFN, MIB_BACKWARD, MIB_TOKENS, MIB_RESULT = 12, 18, 14, 10, 10
+MIB_FORWARD, MIB_FFN, MIB_BACKWARD, MIB_TOKENS, MIB_RESULT = 8, 14, 10, 6, 6
 
 
 def params(mib):
@@ -277,14 +301,14 @@
     return pl.CostEstimate(flops=2 * rows * per_row, bytes_accessed=nbytes, transcendentals=exps)
 
 
-def call_attention_forward(place, tokens, pieces):
+def call_attention_forward(place, tokens, after, pieces):
     S, L, D = tokens.shape
     G, n_z = GROUP, pieces[0].shape[0]
     return pl.pallas_call(
         functools.partial(attention_forward, G, L, n_z),
         out_shape=(
             sds((S * L, 3 * INNER), bf16),
-            pltpu.HBM((S, PAIRS, L, PAIR), bf16),
+            sds((S, PAIRS, L, PAIR), bf16),
             sds((S * L, INNER), bf16),
             sds((D, 3 * INNER), bf16),
             sds((8, D), f32),
@@ -292,10 +316,10 @@
         grid_spec=pltpu.PrefetchScalarGridSpec(
             num_scalar_prefetch=1,
             grid=(S // G,),
-            in_specs=[series_spec(G, tokens.shape)] + [whole(piece.shape) for piece in pieces],
+            in_specs=[whole(tokens.shape), whole(after.shape)] + [whole(piece.shape) for piece in pieces],
             out_specs=[
                 whole((S * L, 3 * INNER)),
-                series_spec(G, (S, PAIRS, L, PAIR)),
+                whole((S, PAIRS, L, PAIR)),
                 whole((S * L, INNER)),
                 whole((D, 3 * INNER)),
                 whole((8, D)),
@@ -309,7 +333,7 @@
         compiler_params=params(MIB_FORWARD),
         cost_estimate=cost(S * L, D * 3 * INNER * 4, S * L * 5000),
         name="attention_forward",
-    )(place, in_hbm(tokens), *pieces)
+    )(place, tokens, after, *pieces)
 
 
 def gelu_parts(v):
@@ -368,21 +392,24 @@
         pl.when(place.core == c)(functools.partial(write, c))
 
 
-def ffn_half(G, L, n_z, first, place_ref, *refs):
+def ffn_half(G, L, n_z, stage, shift, place_ref, *refs):
     n_f = 2 * n_z
     place = Place(place_ref, n_z)
-    pieces, refs = refs[:4], refs[4:]
-    pieces = [(f, pieces[xx].at[k], pieces[2 + xx].at[k]) for xx, k, f in place.shards()]
-    if first:
+    first, begins, ends = stage == 0, stage < 2, stage != 1
+    if begins:
+        pieces, refs = refs[:4], refs[4:]
+        pieces = [(f, pieces[xx].at[k], pieces[2 + xx].at[k]) for xx, k, f in place.shards()]
+    if stage == 0:
         (tok_ref, ct_ref, mixed_ref, gains_ref,
          hid_ref, act, gpart_ref, wd, wo_out, keep, send,
          agu, ad, wgu, n2, gb, gu, ga, low, gn, spread) = refs
+    elif stage == 1:
+        hid_ref, ct_ref, gains_ref, wo_in, _, _ = refs[:6]
+        gpart_ref, mixed_ref, act, agu, ad, ao, gf_ref, wd, wgu, n2, gb, gu, ga, low, gn = refs[6:]
     else:
-        (hid_ref, ct_ref, mixed_ref, gpart_ref, gains_ref, wo_in,
-         gh_ref, gm_ref, act, wd, keep, send, gf_ref,
-         agu, ad, wgu, n2, gb, gu, ga, low, gn, ao, spread) = refs
-    step = pl.program_id(0)
-    last = pl.num_programs(0) - 1
+        hid_ref, ct_ref, gains_ref, wo_in, wd, wgu = refs[:6]
+        gpart_ref, mixed_ref, act, agu, ad, ao, gf_ref, keep, send, n2, gb, gu, ga, low, gn, spread = refs[13:]
+    step = pl.program_id(0) + shift
     R = G * L
     FW, D = wd.shape
     CH = FW // 2
@@ -390,26 +417,28 @@
     count = place.count
     group = jnp.minimum(step, (count + G - 1) // G - 1)
     hid_ref, mixed_ref, act, gpart_ref = (group_rows(ref, group, R) for ref in (hid_ref, mixed_ref, act, gpart_ref))
-    if not first:
-        gm_ref, gh_ref = group_rows(gm_ref, group, R), group_rows(gh_ref, group, R)
-
-    @pl.when(step == 0)
-    def _():
-        wo = (wo_out if is_ % 16 == 0 else spread) if first else None
-        put_weights(place, pieces, wgu, wd, wo)
-        if first and is_ % 16:
-            wo_out[...] = jnp.concatenate([spread[f, :is_, :].astype(f32) for f in range(n_f)], axis=0).astype(bf16)
-        for ref in (agu, ad) if first else (agu, ad, ao, gf_ref):
-            ref[...] = jnp.zeros_like(ref)
+
+    if begins:
+
+        @pl.when(step == 0)
+        def _():
+            wo = (wo_out if is_ % 16 == 0 else spread) if first else None
+            put_weights(place, pieces, wgu, wd, wo)
+            if first and is_ % 16:
+                wo_out[...] = jnp.concatenate([spread[f, :is_, :].astype(f32) for f in range(n_f)], axis=0).astype(bf16)
+            for ref in (agu, ad) if first else (agu, ad, ao, gf_ref):
+                ref[...] = jnp.zeros_like(ref)
 
     @pl.when(step * G < count)
     def _():
         if first:
-            hid_ref[...] = tok_ref[...].reshape(R, D).astype(f32) + nn(mixed_ref[...], wo_out[...])
-        h = hid_ref[...]
+            h = tok_ref[pl.ds(group * G, G)].reshape(R, D).astype(f32) + nn(mixed_ref[...], wo_out[...])
+            hid_ref[...] = h.astype(bf16)
+        else:
+            h = hid_ref[...].astype(f32)
         n2[...] = (h * inverse_rms(h) * gains_ref[1:2, :]).astype(bf16)
         live = (step * G + lax.broadcasted_iota(jnp.int32, (R, 1), 0) // L) < count
-        gb[...] = jnp.where(live, ct_ref[...].reshape(R, D), jnp.zeros((), bf16))
+        gb[...] = jnp.where(live, ct_ref[pl.ds(group * G, G)].reshape(R, D), jnp.zeros((), bf16))
         for c in range(2):
             cols, both = pl.ds(c * CH, CH), pl.ds(2 * c * CH, 2 * CH)
             gu[c] = nn(n2[...], wgu[:, both])
@@ -433,7 +462,7 @@
         if first:
             gpart_ref[...] = gn[...].astype(bf16)
         else:
-            h = hid_ref[...]
+            h = hid_ref[...].astype(f32)
             scale = inverse_rms(h)
             hs = h * scale
             g2 = gn[...] + gpart_ref[...].astype(f32)
@@ -441,59 +470,67 @@
             g2 = g2 * gains_ref[1:2, :]
             dot = jnp.mean(g2 * hs, axis=-1, keepdims=True)
             gh = (gb[...].astype(f32) + scale * (g2 - hs * dot)).astype(bf16)
-            gh_ref[...] = gh
+            gpart_ref[...] = gh
             ao[...] += tn(mixed_ref[...], gh)
-            gm_ref[...] = nt(gh, wo_in[...]).astype(bf16)
-
-    @pl.when(step == last)
-    def _():
-        if first:
-            put_grads(place, n_z, keep, send, agu, ad)
-        elif is_ % 16 == 0:
-            put_grads(place, n_z, keep, send, agu, ad, ao)
-        else:
-            for f in range(n_f):
-                spread[f, :is_, :] = ao[f * is_ : (f + 1) * is_, :]
-            put_grads(place, n_z, keep, send, agu, ad, spread)
-
-
-def call_ffn_half(first, place, n_z, pieces, gains, arrays, S, L, D):
+            mixed_ref[...] = nt(gh, wo_in[...]).astype(bf16)
+
+    if ends:
+
+        @pl.when(pl.program_id(0) == pl.num_programs(0) - 1)
+        def _():
+            if first:
+                put_grads(place, n_z, keep, send, agu, ad)
+            elif is_ % 16 == 0:
+                put_grads(place, n_z, keep, send, agu, ad, ao)
+            else:
+                for f in range(n_f):
+                    spread[f, :is_, :] = ao[f * is_ : (f + 1) * is_, :]
+                put_grads(place, n_z, keep, send, agu, ad, spread)
+
+
+def call_ffn_half(stage, place, n_z, operands, S, L, D):
     G = GROUP
     R, n_f = G * L, 2 * n_z
     FW = D
     CH = FW // 2
     ds, fh, is_ = D // n_f, FW // n_f, INNER // n_f
-    series = series_spec(G, (S, L, D))
-    pack = (2, n_z, 2 * ds + fh + (0 if first else padded(is_)), CH)
-    packs, act, wd = [sds(pack, bf16)] * 2, sds((S * L, FW), bf16), sds((FW, D), bf16)
-    if first:
-        tokens, ct, mixed = arrays
-        operands = (*pieces, in_hbm(tokens), in_hbm(ct), mixed, gains)
-        out_shape = [sds((S * L, D), f32), act, sds((S * L, D), bf16), wd, sds((INNER, D), bf16)] + packs
-    else:
-        hidden, ct, *arrays = arrays
-        operands = (*pieces, hidden, in_hbm(ct), *arrays)
-        out_shape = [sds((S * L, D), bf16), sds((S * L, INNER), bf16), act, wd] + packs + [sds((8, D), f32)]
+    pack = (2, n_z, 2 * ds + fh + (padded(is_) if stage else 0), CH)
+    packs, act = [sds(pack, bf16)] * 2, sds((S * L, FW), bf16)
+    wd, wgu, rows = sds((FW, D), bf16), sds((D, 2 * FW), bf16), sds((S * L, D), bf16)
+    agu, ad = sds((D, 2 * FW), f32), sds((FW, D), f32)
+    running = [rows, sds((S * L, INNER), bf16), act, agu, ad, sds((INNER, D), f32), sds((8, D), f32)]
     vm = pltpu.VMEM
-    scratch = [
-        vm((D, 2 * FW), f32), vm((FW, D), f32), vm((D, 2 * FW), bf16), vm((R, D), bf16), vm((R, D), bf16),
+    work = [
+        vm((R, D), bf16), vm((R, D), bf16),
         vm((2, R, 2 * CH), f32), vm((2, R, CH), f32), vm((2, R, 2 * CH), bf16), vm((R, D), f32),
     ]
-    scratch += [] if first else [vm((INNER, D), f32)]
-    scratch += [vm((n_f, padded(is_), D) if is_ % 16 else (1, 16, 128), bf16 if first else f32)]
+    spread = [vm((n_f, padded(is_), D) if is_ % 16 else (1, 16, 128), f32 if stage else bf16)]
+    half = S // G // 2
+    steps, shift = ((S // G, 0), (half, 0), (S // G - half, half))[stage]
+    if stage == 0:
+        out_shape = [rows, act, rows, wd, sds((INNER, D), bf16)] + packs
+        scratch = [vm(agu.shape, f32), vm(ad.shape, f32), vm(wgu.shape, bf16)] + work + spread
+        aliases = {}
+    elif stage == 1:
+        out_shape, scratch = running + [wd, wgu], work
+        aliases = {9: 0, 10: 1}
+    else:
+        out_shape, scratch = running + packs, work + spread
+        aliases = {7 + i: i for i in range(7)}
     return pl.pallas_call(
-        functools.partial(ffn_half, G, L, n_z, first),
+        functools.partial(ffn_half, G, L, n_z, stage, shift),
         out_shape=tuple(out_shape),
         grid_spec=pltpu.PrefetchScalarGridSpec(
             num_scalar_prefetch=1,
-            grid=(S // G,),
-            in_specs=[series if len(a.shape) == 3 and a.shape[0] == S else whole(a.shape) for a in operands],
+            grid=(steps,),
+            in_specs=[whole(a.shape) for a in operands],
             out_specs=[whole(shape.shape) for shape in out_shape],
             scratch_shapes=scratch,
         ),
+        input_output_aliases=aliases,
         compiler_params=params(MIB_FFN),
-        cost_estimate=cost(S * L, 9 * D * FW, S * L * 9000),
-        name="ffn_first" if first else "ffn_second",
+        cost_estimate=cost(steps * R, 9 * D * FW, S * L * 9000),
+        name=("ffn_first", "ffn_second", "ffn_third")[stage],
     )(place, *operands)
 
 
@@ -513,7 +550,7 @@
     @pl.when(step * G < count)
     def _():
         live = (step * G + lax.broadcasted_iota(jnp.int32, (R, 1), 0) // L) < count
-        out = hid_ref[...] + nn(act_0[...], wd_0[...]) + nn(act_1[...], wd_1[...])
+        out = hid_ref[...].astype(f32) + nn(act_0[...], wd_0[...]) + nn(act_1[...], wd_1[...])
         out_ref[...] = jnp.where(live, out, 0.0).astype(bf16).reshape(G, L, D)
 
 
@@ -535,7 +572,7 @@
     )(place, *operands)
 
 
-def attention_backward(G, L, n_z, place_ref, tok_ref, qkv_ref, probs_ref, gm_ref, w_ref, gains_ref, gf_ref,
+def attention_backward(G, L, n_z, place_ref, tok_ref, _, probs_ref, gm_ref, w_ref, gains_ref, gf_ref,
                        dqkv, keep, send, aw, ab, dp_ref, ds_ref, small):
     step = pl.program_id(0)
     last = pl.num_programs(0) - 1
@@ -544,7 +581,8 @@
     place = Place(place_ref, n_z)
     count = place.count
     group = jnp.minimum(step, (count + G - 1) // G - 1)
-    gm_ref, dqkv, qkv_ref = (group_rows(ref, group, R) for ref in (gm_ref, dqkv, qkv_ref))
+    probs_ref = probs_ref.at[pl.ds(group * G, G)]
+    gm_ref, dqkv = group_rows(gm_ref, group, R), group_rows(dqkv, group, R)
 
     @pl.when(step == 0)
     def _():
@@ -558,7 +596,7 @@
             for s in range(G):
                 rows = pl.ds(s * L, L)
                 dm = split_heads(gm_ref[rows, pl.ds(p * PAIR, PAIR)])
-                dp_ref[s, p] = nt(qkv_ref[rows, cols[p][2]], dm)
+                dp_ref[s, p] = nt(dqkv[rows, cols[p][2]], dm)
                 dqkv[rows, cols[p][2]] = nn(probs_ref[s, p], dm).astype(bf16)
         for p in range(PAIRS):
             total = ab[p]
@@ -573,9 +611,10 @@
             for s in range(G):
                 rows = pl.ds(s * L, L)
                 low = ds_ref[s, p]
-                dqkv[rows, cols[p][1]] = nn(low, split_heads(qkv_ref[rows, cols[p][0]])).astype(bf16)
-                dqkv[rows, cols[p][0]] = join_heads(tn(low, qkv_ref[rows, cols[p][1]])).astype(bf16)
-        x = tok_ref[...].reshape(R, D).astype(f32)
+                q, k = dqkv[rows, cols[p][0]], dqkv[rows, cols[p][1]]
+                dqkv[rows, cols[p][1]] = nn(low, split_heads(q)).astype(bf16)
+                dqkv[rows, cols[p][0]] = join_heads(tn(low, k)).astype(bf16)
+        x = tok_ref[pl.ds(group * G, G)].reshape(R, D).astype(f32)
         aw[...] += tn((x * inverse_rms(x) * gains_ref[0:1, :]).astype(bf16), dqkv[...])
 
     @pl.when(step == last)
@@ -623,7 +662,7 @@
         grid_spec=pltpu.PrefetchScalarGridSpec(
             num_scalar_prefetch=1,
             grid=(S // G,),
-            in_specs=[series_spec(G, tokens.shape), whole(qkv.shape), series_spec(G, probs.shape),
+            in_specs=[whole(tokens.shape), whole(qkv.shape), whole(probs.shape),
                       whole(gm.shape), whole(w.shape), whole(gains.shape), whole(gf.shape)],
             out_specs=[whole(pack)] * 3,
             scratch_shapes=[
@@ -631,10 +670,11 @@
                 vm((G, PAIRS, L, PAIR), f32), vm((G, PAIRS, L, PAIR), bf16), vm((D, PAIR), f32),
             ],
         ),
+        input_output_aliases={2: 0},
         compiler_params=params(MIB_BACKWARD),
         cost_estimate=cost(S * L, D * 3 * INNER * 4, S * L * 6000),
         name="attention_backward",
-    )(place, in_hbm(tokens), qkv, in_hbm(probs), gm, w, gains, gf)
+    )(place, tokens, qkv, probs, gm, w, gains, gf)
 
 
 def token_gradient(G, L, first_step, place_ref, tok_ref, dqkv_ref, gh_ref, w_ref, gains_ref, *refs):
@@ -651,7 +691,7 @@
 
     @pl.when(step * G < place_ref[0])
     def _():
-        x = tok_ref[...].reshape(G * L, D).astype(f32)
+        x = tok_ref[pl.ds(group * G, G)].reshape(G * L, D).astype(f32)
         scale = inverse_rms(x)
         xs = x * scale
         g = nt(dqkv_ref[...], w_ref[...]) * gains_ref[0:1, :]
@@ -678,7 +718,7 @@
         grid_spec=pltpu.PrefetchScalarGridSpec(
             num_scalar_prefetch=1,
             grid=(steps,),
-            in_specs=[series(False), whole(dqkv.shape), whole(gh.shape), whole(w.shape), whole(gains.shape)]
+            in_specs=[whole(tokens.shape), whole(dqkv.shape), whole(gh.shape), whole(w.shape), whole(gains.shape)]
             + [pl.BlockSpec(memory_space=pl.ANY)] * len(more),
             out_specs=(series(True), whole(gains.shape)),
         ),
@@ -686,7 +726,7 @@
         compiler_params=params(MIB_TOKENS),
         cost_estimate=cost(S * L // 2, D * 3 * INNER * 2, S * L * 2500),
         name="token_gradient",
-    )(place, in_hbm(tokens), dqkv, gh, w, gains, *more)
+    )(place, tokens, dqkv, gh, w, gains, *more)
 
 
 def finish(n_f, place_ref, *refs):
@@ -784,50 +824,55 @@
         z_a, pack_1 = together((along_z(pack_a), pack_1))
         near_a = jnp.stack(z_a)
         far_a, near_ac = over_fsdp(near_a, 1), over_rep(near_a, 1)
-        far_a, near_ac, z_0, pack_1 = together((far_a, near_ac, z_0, pack_1))
+        tokens, cotangent, done = call_keep_close(tokens, cotangent)
+        done, far_a, near_ac, z_0, pack_1 = together((done, far_a, near_ac, z_0, pack_1))
         far_ac, near_0 = over_rep(far_a, 1), jnp.stack(z_0)
         far_ac, near_0 = together((far_ac, near_0))
 
         far_0, near_0c, z_1 = over_fsdp(near_0, 1), over_rep(near_0, 1), along_z(pack_1)
-        qkv, probs, mixed, w_all, gains = call_attention_forward(place, tokens, (near_a, far_a, near_ac, far_ac))
+        qkv, probs, mixed, w_all, gains = call_attention_forward(place, tokens, done, (near_a, far_a, near_ac, far_ac))
         gains, far_0, near_0c, z_1 = together((gains, far_0, near_0c, z_1))
         far_0c, near_1 = over_rep(far_0, 1), jnp.stack(z_1)
         far_0c, near_1 = together((far_0c, near_1))
 
         far_1, near_1c = over_fsdp(near_1, 1), over_rep(near_1, 1)
         hidden, act_0, gpart, wd_0, wo_all, keep_0, send_0 = call_ffn_half(
-            True, place, n_z, (near_0, far_0, near_0c, far_0c), gains, (tokens, cotangent, mixed), S, L, D
+            0, place, n_z, (near_0, far_0, near_0c, far_0c, tokens, cotangent, mixed, gains), S, L, D
         )
         wo_all, keep_0, send_0, far_1, near_1c = together((wo_all, keep_0, send_0, far_1, near_1c))
 
         far_1c, got_0 = over_rep(far_1, 1), over_rep(send_0, 1)
-        gh, gm, act_1, wd_1, keep_1, send_1, gf = call_ffn_half(
-            False, place, n_z, (near_1, far_1, near_1c, far_1c), None, (hidden, cotangent, mixed, gpart, gains, wo_all), S, L, D
+        *running, gf, wd_1, wgu = call_ffn_half(
+            1, place, n_z, (near_1, far_1, near_1c, far_1c, hidden, cotangent, gains, wo_all, gpart, mixed), S, L, D
+        )
+        gf, got_0 = together((gf, got_0))
+        here_0, away_0 = halved(keep_0, got_0)
+        away_0, gf = together((away_0, gf))
+        got_0 = over_fsdp(away_0, 1)
+        gh, gm, act_1, _, _, _, gf, keep_1, send_1 = call_ffn_half(
+            2, place, n_z, (hidden, cotangent, gains, wo_all, wd_1, wgu, *running, gf), S, L, D
         )
         keep_1, send_1, gf, got_0 = together((keep_1, send_1, gf, got_0))
-        here_0, away_0 = halved(keep_0, got_0)
-        away_0, gf = together((away_0, gf))
-
-        got_0, got_1 = over_fsdp(away_0, 1), over_rep(send_1, 1)
+        own_0, z_0 = joined(here_0, got_0)
+        z_0, got_1 = to_z(z_0), over_rep(send_1, 1)
+        here_1, away_1 = halved(keep_1, got_1)
+        gf, away_1 = together((gf, away_1))
+        got_1 = over_fsdp(away_1, 1)
         dqkv, keep_2, send_2 = call_attention_backward(place, n_z, tokens, qkv, probs, gm, w_all, gains, gf)
-        keep_2, send_2, got_0, got_1 = together((keep_2, send_2, got_0, got_1))
-        own_0, z_0 = joined(here_0, got_0)
-        here_1, away_1 = halved(keep_1, got_1)
-        gains, z_0, away_1 = together((gains, z_0, away_1))
-
-        z_0, got_1, got_2 = to_z(z_0), over_fsdp(away_1, 1), over_rep(send_2, 1)
+        keep_2, send_2, z_0, got_1 = together((keep_2, send_2, z_0, got_1))
+        sum_0 = summed(own_0, z_0)
+        own_1, z_1 = joined(here_1, got_1)
+
+        z_1, got_2 = to_z(z_1), over_rep(send_2, 1)
+        here_2, away_2 = halved(keep_2, got_2)
+        gains, away_2, sum_0 = together((gains, away_2, sum_0))
+        got_2 = over_fsdp(away_2, 1)
         half_tokens, done = call_token_gradient(place, tokens, dqkv, gh, w_all, gains, 0)
-        done, z_0, got_1, got_2 = together((done, z_0, got_1, got_2))
-        sum_0 = summed(own_0, z_0)
-        here_2, away_2 = halved(keep_2, got_2)
-        own_1, z_1 = joined(here_1, got_1)
-        done, away_2, z_1, sum_0 = together((done, away_2, z_1, sum_0))
-        got_2, z_1 = over_fsdp(away_2, 1), to_z(z_1)
         grad_tokens, done = call_token_gradient(place, tokens, dqkv, gh, w_all, done, 1, half_tokens)
         done, got_2, z_1 = together((done, got_2, z_1))
+        sum_1 = summed(own_1, z_1)
         own_2, z_2 = joined(here_2, got_2)
-        sum_1 = summed(own_1, z_1)
-        done, z_2, sum_1 = together((done, z_2, sum_1))
+        done, z_2 = together((done, z_2))
         z_2 = to_z(z_2)
         layer_out, done = call_layer_result(place, hidden, act_0, act_1, wd_0, wd_1, done, S, L)
         done, z_2 = together((done, z_2))

time: 163 us -> 152 us (0.933)
  starting transfers between devices: 74.3 us -> 49.8 us
  Pallas kernels: 50.3 us -> 70 us
  waiting for transfers between devices: 33.3 us -> 29.2 us
    ppermute x24, starting transfers between devices: 52.5 us -> 34.4 us  [over_fsdp(): return lax.ppermute(value, 'fsdp', [(i, i ^ distance) for i in range(n_f)])]
    pallas_call x2 -> x4, Pallas kernels: 18 us -> 33.3 us  [the longest x3 29.1 us: call_ffn_half(): pl.pallas_call(functools.partial(ffn_half, G, L, n_z, stage, shift), out_...]
    ppermute x15, starting transfers between devices: 21.8 us -> 15.4 us  [over_rep(): return lax.ppermute(value, 'rep', [(i, i ^ distance) for i in range(n_r)])]
    ppermute x24, waiting for transfers between devices: 26.7 us -> 21.9 us  [over_fsdp(): return lax.ppermute(value, 'fsdp', [(i, i ^ distance) for i in range(n_f)])]
    pallas_call x1, Pallas kernels: 7.48 us -> 9.85 us  [call_attention_backward(): pl.pallas_call(functools.partial(attention_backward, G, L, n_z), out_shap...]
  transfers between devices with their start and end apart: 39 -> 39, of which waited for: 14 -> 10; matrix products, arithmetic and copies ran while one was open for 1% -> 1% of each run, Pallas kernels for 29% -> 43%
where the time goes in v5:
time: 152 us; the launch traced here: 153 us
  Pallas kernels  70 us (46%)
  starting transfers between devices  49.8 us (33%)
  waiting for transfers between devices  29.2 us (19%)
  other arithmetic  2.69 us (2%)
  between operations  1.66 us (1%)
    ppermute x24, starting transfers between devices, over_fsdp(): return lax.ppermute(value, 'fsdp', [(i, i ^ distance) for i in range(n_f)])  34.4 us
    pallas_call x3, Pallas kernels, call_ffn_half(): pl.pallas_call(functools.partial(ffn_half, G, L, n_z, stage, shift), out_...  29.1 us
    ppermute x24, waiting for transfers between devices, over_fsdp(): return lax.ppermute(value, 'fsdp', [(i, i ^ distance) for i in range(n_f)])  21.9 us
    ppermute x15, starting transfers between devices, over_rep(): return lax.ppermute(value, 'rep', [(i, i ^ distance) for i in range(n_r)])  15.4 us
    pallas_call x1, Pallas kernels, call_attention_backward(): pl.pallas_call(functools.partial(attention_backward, G, L, n_z), out_shap...  9.85 us
    pallas_call x2, Pallas kernels, call_token_gradient(): pl.pallas_call(functools.partial(token_gradient, G, L, shift), out_shape=...  8.19 us
    pallas_call x1, Pallas kernels, call_attention_forward(): pl.pallas_call(functools.partial(attention_forward, G, L, n_z), out_shape...  7.86 us
    ppermute x15, waiting for transfers between devices, over_rep(): return lax.ppermute(value, 'rep', [(i, i ^ distance) for i in range(n_r)])  7.25 us
  transfers between devices with their start and end apart: 39, of which 10 were waited for; matrix products, arithmetic and copies ran while one was open for 1% of the time, Pallas kernels for 43%

profile of v5, /device:TPU:0, one launch (start us, length us, event | category | flops | bytes accessed | tf_op | source)
XLA Modules:
  0.0 153.4 jit_solution(3271505876848733208)
XLA Ops:
  2.0 1.7 %prepare_attention.1 = bf16[64,640]{1,0:T(8,128)(2,1)} custom-call(s32[4]{0:T(128)} %pad_add_fusion.place_ref, f32[24]{0:T(128)} %bias_ref.1, f32[64,384]{1,0:T(8,128)} %wq.1, f32[64,384]{1,0:T(8,128)} %wk.1, f32[64,384]{1,0:T(8,128)} %wv.1, f32[1,64]{1,0:T(1,128)} %bitcast.94, f32[1,64]{1,0:T(1,128)} %bitcast.95), custom_call_target="tpu_custom_call" | custom-call | tf_op jit(solution)/shard_map/prepare_attention/pallas_call | solution.py:162
  3.7 5.0 %collective-permute-start.2 = (bf16[64,640]{1,0:T(8,128)(2,1)}, bf16[64,640]{1,0:T(8,128)(2,1)S(1)}, u32[]{:S(2)}, u32[]{:S(2)}) collective-permute-start(bf16[64,640]{1,0:T(8,128)(2,1)} %prepare_attention.1), channel_id=1, source_target_pairs={{0,6},{1,7},{2,4},{3,5},{4,2},{5,3},{6,0},{7,1},{8,14},{9,15},{10,... | collective-permute-start | bytes 245768 | tf_op jit(solution)/shard_map/ppermute | solution.py:783
  9.3 2.0 %prepare_ffn.1 = (bf16[240,256]{1,0:T(8,128)(2,1)}, bf16[192,256]{1,0:T(8,128)(2,1)}) custom-call(s32[4]{0:T(128)} %pad_add_fusion.place_ref, f32[48,512]{1,0:T(8,128)} %wo.1, f32[64,1024]{1,0:T(8,128)} %wg.1, f32[64,1024]{1,0:T(8,128)} %wu.1, f32[128,512]{1,0:T(8,128)} %wd.1), custom_call_target="tpu_custom_call" | custom-call | tf_op jit(solution)/shard_map/prepare_ffn/pallas_call | solution.py:174
  12.0 3.8 %collective-permute-done.1 = bf16[64,640]{1,0:T(8,128)(2,1)S(1)} collective-permute-done((bf16[64,640]{1,0:T(8,128)(2,1)}, bf16[64,640]{1,0:T(8,128)(2,1)S(1)}, u32[]{:S(2)}, u32[]{:S(2)}) %collective-permute-start.1) | collective-permute-done | bytes 81952 | tf_op jit(solution)/shard_map/ppermute | solution.py:783
  18.4 2.6 %collective-permute-start.7 = (bf16[240,256]{1,0:T(8,128)(2,1)}, bf16[240,256]{1,0:T(8,128)(2,1)S(1)}, u32[]{:S(2)}, u32[]{:S(2)}) collective-permute-start(bf16[240,256]{1,0:T(8,128)(2,1)} %get-tuple-element.133), channel_id=1, source_target_pairs={{0,6},{1,7},{2,4},{3,5},{4,2},{5,3},{6,0},{7,1},{8,14},{9,15},{10,... | collective-permute-start | bytes 368648 | tf_op jit(solution)/shard_map/ppermute | solution.py:783
  21.0 1.8 %collective-permute-start.5 = (bf16[240,256]{1,0:T(8,128)(2,1)}, bf16[240,256]{1,0:T(8,128)(2,1)S(1)}, u32[]{:S(2)}, u32[]{:S(2)}) collective-permute-start(bf16[240,256]{1,0:T(8,128)(2,1)} %get-tuple-element.133), channel_id=1, source_target_pairs={{0,2},{1,3},{2,0},{3,1},{4,6},{5,7},{6,4},{7,5},{8,10},{9,11},{10,... | collective-permute-start | bytes 368648 | tf_op jit(solution)/shard_map/ppermute | solution.py:783
  22.8 4.3 %keep_close.1 = (bf16[48,64,512]{2,1,0:T(8,128)(2,1)S(1)}, bf16[48,64,512]{2,1,0:T(8,128)(2,1)S(1)}, f32[8,128]{1,0:T(8,128)S(1)}) custom-call(bf16[48,64,512]{2,1,0:T(8,128)(2,1)} %tok_ref.1, bf16[48,64,512]{2,1,0:T(8,128)(2,1)} %ct_ref.1), custom_call_target="tpu_custom_call" | custom-call | flops 6144 | bytes 12582912 | tf_op jit(solution)/shard_map/keep_close/pallas_call | solution.py:194
  27.1 5.1 %collective-permute-done.6 = bf16[240,256]{1,0:T(8,128)(2,1)S(1)} collective-permute-done((bf16[240,256]{1,0:T(8,128)(2,1)}, bf16[240,256]{1,0:T(8,128)(2,1)S(1)}, u32[]{:S(2)}, u32[]{:S(2)}) %collective-permute-start.6) | collective-permute-done | bytes 122912 | tf_op jit(solution)/shard_map/ppermute | solution.py:783
  32.3 1.6 %collective-permute-start.13 = (bf16[192,256]{1,0:T(8,128)(2,1)S(1)}, bf16[192,256]{1,0:T(8,128)(2,1)S(1)}, u32[]{:S(2)}, u32[]{:S(2)}) collective-permute-start(bf16[192,256]{1,0:T(8,128)(2,1)S(1)} %copy-done.1), channel_id=1, source_target_pairs={{0,6},{1,7},{2,4},{3,5},{4,2},{5,3},{6,0},{7,1},{8,14},{9,15},{10,... | collective-permute-start | bytes 294920 | tf_op jit(solution)/shard_map/ppermute | solution.py:783
  33.9 2.9 %collective-permute-start.11 = (bf16[192,256]{1,0:T(8,128)(2,1)S(1)}, bf16[192,256]{1,0:T(8,128)(2,1)S(1)}, u32[]{:S(2)}, u32[]{:S(2)}) collective-permute-start(bf16[192,256]{1,0:T(8,128)(2,1)S(1)} %copy-done.1), channel_id=1, source_target_pairs={{0,2},{1,3},{2,0},{3,1},{4,6},{5,7},{6,4},{7,5},{8,10},{9,11},{10,... | collective-permute-start | bytes 294920 | tf_op jit(solution)/shard_map/ppermute | solution.py:783
  37.5 7.9 %attention_forward.1 = (bf16[3072,1152]{1,0:T(8,128)(2,1)S(1)}, bf16[48,3,64,128]{3,2,1,0:T(8,128)(2,1)S(1)}, bf16[3072,384]{1,0:T(8,128)(2,1)S(1)}, bf16[512,1152]{1,0:T(8,128)(2,1)S(1)}, f32[8,512]{1,0:T(8,128)S(1)}) custom-call(s32[4]{0:T(128)} %pad_add_fusion.place_ref, bf16[48,64,512]{2,1,0:T(8,128)(2,1)S(1)} %get-tuple-element.138.tok_ref.refs_4_, ...), custom_call_target="tpu_custom_call" | custom-call | flops 14495514624 | bytes 15360000 | tf_op jit(solution)/shard_map/attention_forward/pallas_call | solution.py:307
  45.4 5.1 %collective-permute-done.9.refs_1_ = bf16[4,240,256]{2,1,0:T(8,128)(2,1)S(1)} collective-permute-done((bf16[4,240,256]{2,1,0:T(8,128)(2,1)S(1)}, bf16[4,240,256]{2,1,0:T(8,128)(2,1)S(1)}, u32[]{:S(2)}, u32[]{:S(2)}) %collective-permute-start.9) | collective-permute-done | bytes 491552 | tf_op jit(solution)/shard_map/ppermute | solution.py:783
  50.6 1.8 %collective-permute-done.14.refs_3_ = bf16[4,240,256]{2,1,0:T(8,128)(2,1)S(1)} collective-permute-done((bf16[4,240,256]{2,1,0:T(8,128)(2,1)S(1)}, bf16[4,240,256]{2,1,0:T(8,128)(2,1)S(1)}, u32[]{:S(2)}, u32[]{:S(2)}) %collective-permute-start.14) | collective-permute-done | bytes 491552 | tf_op jit(solution)/shard_map/ppermute | solution.py:786
  53.1 13.5 %ffn_first.1 = (bf16[3072,512]{1,0:T(8,128)(2,1)S(1)}, bf16[3072,512]{1,0:T(8,128)(2,1)S(1)}, bf16[3072,512]{1,0:T(8,128)(2,1)S(1)}, bf16[512,512]{1,0:T(8,128)(...) custom-call(s32[4]{0:T(128)} %pad_add_fusion.place_ref, ...), custom_call_target="tpu_custom_call" | custom-call | flops 14495514624 | bytes 27648000 | tf_op jit(solution)/shard_map/ffn_first/pallas_call | solution.py:520
  66.6 6.2 %collective-permute-start.17 = (bf16[4,192,256]{2,1,0:T(8,128)(2,1)S(1)}, bf16[4,192,256]{2,1,0:T(8,128)(2,1)S(1)}, u32[]{:S(2)}, u32[]{:S(2)}) collective-permute-start(bf16[4,192,256]{2,1,0:T(8,128)(2,1)S(1)} %collective-permute-done.15.refs_1_), channel_id=1, source_target_pairs={{0,8},{8,0},{16,24},{24,16},{1,9},{9,1},{17,25},{25,17},{2,10},{10... | collective-permute-start | bytes 1179656 | tf_op jit(solution)/shard_map/ppermute | solution.py:786
  74.1 11.1 %ffn_second.1 = (bf16[3072,512]{1,0:T(8,128)(2,1)S(1)}, bf16[3072,384]{1,0:T(8,128)(2,1)S(1)}, bf16[3072,512]{1,0:T(8,128)(2,1)S(1)}, f32[512,1024]{1,0:T(8,128)...) custom-call(s32[4]{0:T(128)} %pad_add_fusion.place_ref, ...), custom_call_target="tpu_custom_call", output_to_operand_aliasing={{0}: (9, {}), {1}: (10, {})} | custom-call | flops 7247757312 | bytes 27648000 | tf_op jit(solution)/shard_map/ffn_second/pallas_call | solution.py:520
  85.4 1.8 %collective-permute-start.19 = (bf16[4,192,256]{2,1,0:T(8,128)(2,1)S(1)}, bf16[4,192,256]{2,1,0:T(8,128)(2,1)S(1)}, u32[]{:S(2)}, u32[]{:S(2)}) collective-permute-start(bf16[4,192,256]{2,1,0:T(8,128)(2,1)S(1)} %fusion.1), channel_id=1, source_target_pairs={{0,1},{1,0},{2,3},{3,2},{4,5},{5,4},{6,7},{7,6},{8,9},{9,8},{10,11... | collective-permute-start | bytes 1179656 | tf_op jit(solution)/shard_map/ppermute | solution.py:783
  87.2 4.5 %ffn_third.1 = (bf16[3072,512]{1,0:T(8,128)(2,1)S(1)}, bf16[3072,384]{1,0:T(8,128)(2,1)S(1)}, bf16[3072,512]{1,0:T(8,128)(2,1)S(1)}, f32[512,1024]{1,0:T(8,128)S...) custom-call(s32[4]{0:T(128)} %pad_add_fusion.place_ref, ...), custom_call_target="tpu_custom_call", output_to_operand_aliasing={{0}: (7, {}), {1}: (8, {}), {2}: (9, {}), {3}: (10, {}), {4... | custom-call | flops 7247757312 | bytes 27648000 | tf_op jit(solution)/shard_map/ffn_third/pallas_call | solution.py:520
  91.7 5.1 %collective-permute-done.19 = bf16[4,192,256]{2,1,0:T(8,128)(2,1)S(1)} collective-permute-done((bf16[4,192,256]{2,1,0:T(8,128)(2,1)S(1)}, bf16[4,192,256]{2,1,0:T(8,128)(2,1)S(1)}, u32[]{:S(2)}, u32[]{:S(2)}) %collective-permute-start.19) | collective-permute-done | bytes 393248 | tf_op jit(solution)/shard_map/ppermute | solution.py:783
  100.0 2.9 %collective-permute-start.21 = (bf16[192,256]{1,0:T(8,128)(2,1)S(1)}, bf16[192,256]{1,0:T(8,128)(2,1)S(1)}, u32[]{:S(2)}, u32[]{:S(2)}) collective-permute-start(bf16[192,256]{1,0:T(8,128)(2,1)S(1)} %get-tuple-element.247), channel_id=1, source_target_pairs={{0,2},{1,3},{2,0},{3,1},{4,6},{5,7},{6,4},{7,5},{8,10},{9,11},{10,... | collective-permute-start | bytes 294920 | tf_op jit(solution)/shard_map/ppermute | solution.py:783
  103.6 9.9 %attention_backward.1 = (bf16[3072,1152]{1,0:T(8,128)(2,1)S(1)}, bf16[2,4,64,640]{3,2,1,0:T(8,128)(2,1)S(1)}, bf16[2,4,64,640]{3,2,1,0:T(8,128)(2,1)S(1)}) custom-call(s32[4]{0:T(128)} %pad_add_fusion.place_ref, bf16[48,64,512]{2,1,0:T(8,128)(2,1)S(1)} %get-tuple-element.138.tok_ref.refs_4_, ...), custom_call_target="tpu_custom_call", output_to_operand_aliasing={{0}: (2, {})} | custom-call | flops 14495514624 | bytes 18432000 | tf_op jit(solution)/shard_map/attention_backward/pallas_call | solution.py:659
  113.5 1.9 %collective-permute-done.24 = bf16[4,240,256]{2,1,0:T(8,128)(2,1)S(1)} collective-permute-done((bf16[4,240,256]{2,1,0:T(8,128)(2,1)S(1)}, bf16[4,240,256]{2,1,0:T(8,128)(2,1)S(1)}, u32[]{:S(2)}, u32[]{:S(2)}) %collective-permute-start.24) | collective-permute-done | bytes 491552 | tf_op jit(solution)/shard_map/ppermute | solution.py:783
  117.0 2.3 %collective-permute-start.29 = (bf16[240,256]{1,0:T(8,128)(2,1)S(1)}, bf16[240,256]{1,0:T(8,128)(2,1)S(1)}, u32[]{:S(2)}, u32[]{:S(2)}) collective-permute-start(bf16[240,256]{1,0:T(8,128)(2,1)S(1)} %get-tuple-element.242), channel_id=1, source_target_pairs={{0,6},{1,7},{2,4},{3,5},{4,2},{5,3},{6,0},{7,1},{8,14},{9,15},{10,... | collective-permute-start | bytes 368648 | tf_op jit(solution)/shard_map/ppermute | solution.py:783
  119.3 2.1 %collective-permute-start.27 = (bf16[240,256]{1,0:T(8,128)(2,1)S(1)}, bf16[240,256]{1,0:T(8,128)(2,1)S(1)}, u32[]{:S(2)}, u32[]{:S(2)}) collective-permute-start(bf16[240,256]{1,0:T(8,128)(2,1)S(1)} %get-tuple-element.244), channel_id=1, source_target_pairs={{0,2},{1,3},{2,0},{3,1},{4,6},{5,7},{6,4},{7,5},{8,10},{9,11},{10,... | collective-permute-start | bytes 368648 | tf_op jit(solution)/shard_map/ppermute | solution.py:783
  121.6 2.5 %collective-permute-start.30 = (bf16[192,256]{1,0:T(8,128)(2,1)S(1)}, bf16[192,256]{1,0:T(8,128)(2,1)S(1)}, u32[]{:S(2)}, u32[]{:S(2)}) collective-permute-start(bf16[192,256]{1,0:T(8,128)(2,1)S(1)} %fusion.10), channel_id=1, source_target_pairs={{0,16},{8,24},{16,0},{24,8},{1,17},{9,25},{17,1},{25,9},{2,18},{10... | collective-permute-start | bytes 294920 | tf_op jit(solution)/shard_map/ppermute | solution.py:786
  125.6 4.8 %token_gradient.2 = (bf16[48,64,512]{2,1,0:T(8,128)(2,1)}, f32[8,512]{1,0:T(8,128)S(1)}) custom-call(s32[4]{0:T(128)} %pad_add_fusion.place_ref, bf16[48,64,512]{2,1,0:T(8,128)(2,1)S(1)} %get-tuple-element.138.tok_ref.refs_4_, bf16[3072,1152]{1,0:T(8,128)(2,1)S(1)} %get-tuple-element.192.dqkv_ref, bf16[3072,512]{1,0:T(8,128)(2,1)S(1)} %get-tuple-element.193.gh_ref, ...), custom_call_target="tpu_custom_call" | custom-call | flops 3623878656 | bytes 7680000 | tf_op jit(solution)/shard_map/token_gradient/pallas_call | solution.py:715
  130.4 3.4 %token_gradient.3 = (bf16[48,64,512]{2,1,0:T(8,128)(2,1)}, f32[8,512]{1,0:T(8,128)S(1)}) custom-call(s32[4]{0:T(128)} %pad_add_fusion.place_ref, bf16[48,64,512]{2,1,0:T(8,128)(2,1)S(1)} %get-tuple-element.138.tok_ref.refs_4_, bf16[3072,1152]{1,0:T(8,128)(2,1)S(1)} %get-tuple-element.192.dqkv_ref, ...), custom_call_target="tpu_custom_call", output_to_operand_aliasing={{0}: (6, {})} | custom-call | flops 3623878656 | bytes 7680000 | tf_op jit(solution)/shard_map/token_gradient/pallas_call | solution.py:715
  134.6 1.7 %collective-permute-start.35 = (bf16[64,640]{1,0:T(8,128)(2,1)S(1)}, bf16[64,640]{1,0:T(8,128)(2,1)S(1)}, u32[]{:S(2)}, u32[]{:S(2)}) collective-permute-start(bf16[64,640]{1,0:T(8,128)(2,1)S(1)} %get-tuple-element.220), channel_id=1, source_target_pairs={{0,4},{1,5},{2,6},{3,7},{4,0},{5,1},{6,2},{7,3},{8,12},{9,13},{10,... | collective-permute-start | bytes 245768 | tf_op jit(solution)/shard_map/ppermute | solution.py:783
  136.3 2.7 %collective-permute-start.36 = (bf16[64,640]{1,0:T(8,128)(2,1)S(1)}, bf16[64,640]{1,0:T(8,128)(2,1)S(1)}, u32[]{:S(2)}, u32[]{:S(2)}) collective-permute-start(bf16[64,640]{1,0:T(8,128)(2,1)S(1)} %get-tuple-element.221), channel_id=1, source_target_pairs={{0,6},{1,7},{2,4},{3,5},{4,2},{5,3},{6,0},{7,1},{8,14},{9,15},{10,... | collective-permute-start | bytes 245768 | tf_op jit(solution)/shard_map/ppermute | solution.py:783
  140.4 5.3 %layer_result.1 = (bf16[48,64,512]{2,1,0:T(8,128)(2,1)}, f32[8,512]{1,0:T(8,128)S(1)}) custom-call(s32[4]{0:T(128)} %pad_add_fusion.place_ref, bf16[3072,512]{1,0:T(8,128)(2,1)S(1)} %get-tuple-element.154.refs_4_.refs_0_.hid_ref, bf16[3072,512]{1,0:T(8,128)(2,1)S(1)} %get-tuple-element.155.act_0, bf16[3072,512]{1,0:T(8,128)(2,1)S(1)} %get-tuple-element.178.act_1, ...), custom_call_target="tpu_custom_call" | custom-call | flops 3221225472 | bytes 18432000 | tf_op jit(solution)/shard_map/layer_result/pallas_call | solution.py:560
  147.4 2.9 %collective-permute-done.37 = bf16[64,640]{1,0:T(8,128)(2,1)S(1)} collective-permute-done((bf16[64,640]{1,0:T(8,128)(2,1)S(1)}, bf16[64,640]{1,0:T(8,128)(2,1)S(1)}, u32[]{:S(2)}, u32[]{:S(2)}) %collective-permute-start.37) | collective-permute-done | bytes 81952 | tf_op jit(solution)/shard_map/ppermute | solution.py:786
  151.6 1.8 %finish.1 = (f32[64,384]{1,0:T(8,128)}, f32[64,384]{1,0:T(8,128)}, f32[64,384]{1,0:T(8,128)}, f32[48,512]{1,0:T(8,128)}, f32[64,1024]{1,0:T(8,128)}, /*index=5*/...) custom-call(s32[4]{0:T(128)} %pad_add_fusion.place_ref, ...), custom_call_target="tpu_custom_call" | custom-call | tf_op jit(solution)/shard_map/finish/pallas_call | solution.py:768
  (81 shorter events, 19.7 us)
Async XLA Ops:
  3.7 8.3 %collective-permute-start.2 = (bf16[64,640]{1,0:T(8,128)(2,1)}, bf16[64,640]{1,0:T(8,128)(2,1)S(1)}, u32[]{:S(2)}, u32[]{:S(2)}) collective-permute-start(bf16[64,640]{1,0:T(8,128)(2,1)} %prepare_attention.1), channel_id=1, source_target_pairs={{0,6},{1,7},{2,4},{3,5},{4,2},{5,3},{6,0},{7,1},{8,14},{9,15},{10,... | collective-permute-start | bytes 245768 | tf_op jit(solution)/shard_map/ppermute | solution.py:783
  8.7 7.1 %collective-permute-start.1 = (bf16[64,640]{1,0:T(8,128)(2,1)}, bf16[64,640]{1,0:T(8,128)(2,1)S(1)}, u32[]{:S(2)}, u32[]{:S(2)}) collective-permute-start(bf16[64,640]{1,0:T(8,128)(2,1)} %prepare_attention.1), channel_id=1, source_target_pairs={{0,4},{1,5},{2,6},{3,7},{4,0},{5,1},{6,2},{7,3},{8,12},{9,13},{10,... | collective-permute-start | bytes 245768 | tf_op jit(solution)/shard_map/ppermute | solution.py:783
  8.7 7.1 %collective-permute-start = (bf16[64,640]{1,0:T(8,128)(2,1)}, bf16[64,640]{1,0:T(8,128)(2,1)S(1)}, u32[]{:S(2)}, u32[]{:S(2)}) collective-permute-start(bf16[64,640]{1,0:T(8,128)(2,1)} %prepare_attention.1), channel_id=1, source_target_pairs={{0,2},{1,3},{2,0},{3,1},{4,6},{5,7},{6,4},{7,5},{8,10},{9,11},{10,... | collective-permute-start | bytes 245768 | tf_op jit(solution)/shard_map/ppermute | solution.py:783
  16.8 15.5 %collective-permute-start.4 = (bf16[4,64,640]{2,1,0:T(8,128)(2,1)S(1)}, bf16[4,64,640]{2,1,0:T(8,128)(2,1)S(1)}, u32[]{:S(2)}, u32[]{:S(2)}) collective-permute-start(bf16[4,64,640]{2,1,0:T(8,128)(2,1)S(1)} %pad_maximum_fusion.2.refs_0_), channel_id=1, source_target_pairs={{0,8},{8,0},{16,24},{24,16},{1,9},{9,1},{17,25},{25,17},{2,10},{10... | collective-permute-start | bytes 983048 | tf_op jit(solution)/shard_map/ppermute | solution.py:786
  16.8 15.4 %collective-permute-start.3 = (bf16[4,64,640]{2,1,0:T(8,128)(2,1)S(1)}, bf16[4,64,640]{2,1,0:T(8,128)(2,1)S(1)}, u32[]{:S(2)}, u32[]{:S(2)}) collective-permute-start(bf16[4,64,640]{2,1,0:T(8,128)(2,1)S(1)} %pad_maximum_fusion.2.refs_0_), channel_id=1, source_target_pairs={{0,1},{1,0},{2,3},{3,2},{4,5},{5,4},{6,7},{7,6},{8,9},{9,8},{10,11... | collective-permute-start | bytes 983048 | tf_op jit(solution)/shard_map/ppermute | solution.py:783
  18.4 8.7 %collective-permute-start.7 = (bf16[240,256]{1,0:T(8,128)(2,1)}, bf16[240,256]{1,0:T(8,128)(2,1)S(1)}, u32[]{:S(2)}, u32[]{:S(2)}) collective-permute-start(bf16[240,256]{1,0:T(8,128)(2,1)} %get-tuple-element.133), channel_id=1, source_target_pairs={{0,6},{1,7},{2,4},{3,5},{4,2},{5,3},{6,0},{7,1},{8,14},{9,15},{10,... | collective-permute-start | bytes 368648 | tf_op jit(solution)/shard_map/ppermute | solution.py:783
  21.0 11.2 %collective-permute-start.6 = (bf16[240,256]{1,0:T(8,128)(2,1)}, bf16[240,256]{1,0:T(8,128)(2,1)S(1)}, u32[]{:S(2)}, u32[]{:S(2)}) collective-permute-start(bf16[240,256]{1,0:T(8,128)(2,1)} %get-tuple-element.133), channel_id=1, source_target_pairs={{0,4},{1,5},{2,6},{3,7},{4,0},{5,1},{6,2},{7,3},{8,12},{9,13},{10,... | collective-permute-start | bytes 368648 | tf_op jit(solution)/shard_map/ppermute | solution.py:783
  21.0 11.2 %collective-permute-start.5 = (bf16[240,256]{1,0:T(8,128)(2,1)}, bf16[240,256]{1,0:T(8,128)(2,1)S(1)}, u32[]{:S(2)}, u32[]{:S(2)}) collective-permute-start(bf16[240,256]{1,0:T(8,128)(2,1)} %get-tuple-element.133), channel_id=1, source_target_pairs={{0,2},{1,3},{2,0},{3,1},{4,6},{5,7},{6,4},{7,5},{8,10},{9,11},{10,... | collective-permute-start | bytes 368648 | tf_op jit(solution)/shard_map/ppermute | solution.py:783
  32.3 13.1 %collective-permute-start.13 = (bf16[192,256]{1,0:T(8,128)(2,1)S(1)}, bf16[192,256]{1,0:T(8,128)(2,1)S(1)}, u32[]{:S(2)}, u32[]{:S(2)}) collective-permute-start(bf16[192,256]{1,0:T(8,128)(2,1)S(1)} %copy-done.1), channel_id=1, source_target_pairs={{0,6},{1,7},{2,4},{3,5},{4,2},{5,3},{6,0},{7,1},{8,14},{9,15},{10,... | collective-permute-start | bytes 294920 | tf_op jit(solution)/shard_map/ppermute | solution.py:783
  33.9 11.5 %collective-permute-start.12 = (bf16[192,256]{1,0:T(8,128)(2,1)S(1)}, bf16[192,256]{1,0:T(8,128)(2,1)S(1)}, u32[]{:S(2)}, u32[]{:S(2)}) collective-permute-start(bf16[192,256]{1,0:T(8,128)(2,1)S(1)} %copy-done.1), channel_id=1, source_target_pairs={{0,4},{1,5},{2,6},{3,7},{4,0},{5,1},{6,2},{7,3},{8,12},{9,13},{10,... | collective-permute-start | bytes 294920 | tf_op jit(solution)/shard_map/ppermute | solution.py:783
  33.9 11.5 %collective-permute-start.11 = (bf16[192,256]{1,0:T(8,128)(2,1)S(1)}, bf16[192,256]{1,0:T(8,128)(2,1)S(1)}, u32[]{:S(2)}, u32[]{:S(2)}) collective-permute-start(bf16[192,256]{1,0:T(8,128)(2,1)S(1)} %copy-done.1), channel_id=1, source_target_pairs={{0,2},{1,3},{2,0},{3,1},{4,6},{5,7},{6,4},{7,5},{8,10},{9,11},{10,... | collective-permute-start | bytes 294920 | tf_op jit(solution)/shard_map/ppermute | solution.py:783
  36.9 8.6 %collective-permute-start.10 = (bf16[4,240,256]{2,1,0:T(8,128)(2,1)S(1)}, bf16[4,240,256]{2,1,0:T(8,128)(2,1)S(1)}, u32[]{:S(2)}, u32[]{:S(2)}) collective-permute-start(bf16[4,240,256]{2,1,0:T(8,128)(2,1)S(1)} %pad_maximum_fusion.refs_0_), channel_id=1, source_target_pairs={{0,8},{8,0},{16,24},{24,16},{1,9},{9,1},{17,25},{25,17},{2,10},{10... | collective-permute-start | bytes 1474568 | tf_op jit(solution)/shard_map/ppermute | solution.py:786
  36.9 13.6 %collective-permute-start.9 = (bf16[4,240,256]{2,1,0:T(8,128)(2,1)S(1)}, bf16[4,240,256]{2,1,0:T(8,128)(2,1)S(1)}, u32[]{:S(2)}, u32[]{:S(2)}) collective-permute-start(bf16[4,240,256]{2,1,0:T(8,128)(2,1)S(1)} %pad_maximum_fusion.refs_0_), channel_id=1, source_target_pairs={{0,1},{1,0},{2,3},{3,2},{4,5},{5,4},{6,7},{7,6},{8,9},{9,8},{10,11... | collective-permute-start | bytes 1474568 | tf_op jit(solution)/shard_map/ppermute | solution.py:783
  52.4 14.2 %collective-permute-start.16 = (bf16[4,192,256]{2,1,0:T(8,128)(2,1)S(1)}, bf16[4,192,256]{2,1,0:T(8,128)(2,1)S(1)}, u32[]{:S(2)}, u32[]{:S(2)}) collective-permute-start(bf16[4,192,256]{2,1,0:T(8,128)(2,1)S(1)} %pad_maximum_fusion.1.refs_0_), channel_id=1, source_target_pairs={{0,8},{8,0},{16,24},{24,16},{1,9},{9,1},{17,25},{25,17},{2,10},{10... | collective-permute-start | bytes 1179656 | tf_op jit(solution)/shard_map/ppermute | solution.py:786
  52.6 14.0 %collective-permute-start.15 = (bf16[4,192,256]{2,1,0:T(8,128)(2,1)S(1)}, bf16[4,192,256]{2,1,0:T(8,128)(2,1)S(1)}, u32[]{:S(2)}, u32[]{:S(2)}) collective-permute-start(bf16[4,192,256]{2,1,0:T(8,128)(2,1)S(1)} %pad_maximum_fusion.1.refs_0_), channel_id=1, source_target_pairs={{0,1},{1,0},{2,3},{3,2},{4,5},{5,4},{6,7},{7,6},{8,9},{9,8},{10,11... | collective-permute-start | bytes 1179656 | tf_op jit(solution)/shard_map/ppermute | solution.py:783
  66.6 7.5 %collective-permute-start.17 = (bf16[4,192,256]{2,1,0:T(8,128)(2,1)S(1)}, bf16[4,192,256]{2,1,0:T(8,128)(2,1)S(1)}, u32[]{:S(2)}, u32[]{:S(2)}) collective-permute-start(bf16[4,192,256]{2,1,0:T(8,128)(2,1)S(1)} %collective-permute-done.15.refs_1_), channel_id=1, source_target_pairs={{0,8},{8,0},{16,24},{24,16},{1,9},{9,1},{17,25},{25,17},{2,10},{10... | collective-permute-start | bytes 1179656 | tf_op jit(solution)/shard_map/ppermute | solution.py:786
  72.8 12.5 %collective-permute-start.18 = (bf16[2,4,192,256]{3,2,1,0:T(8,128)(2,1)S(1)}, bf16[2,4,192,256]{3,2,1,0:T(8,128)(2,1)S(1)}, u32[]{:S(2)}, u32[]{:S(2)}) collective-permute-start(bf16[2,4,192,256]{3,2,1,0:T(8,128)(2,1)S(1)} %get-tuple-element.174), channel_id=1, source_target_pairs={{0,8},{8,0},{16,24},{24,16},{1,9},{9,1},{17,25},{25,17},{2,10},{10... | collective-permute-start | bytes 2359304 | tf_op jit(solution)/shard_map/ppermute | solution.py:786
  85.4 11.5 %collective-permute-start.19 = (bf16[4,192,256]{2,1,0:T(8,128)(2,1)S(1)}, bf16[4,192,256]{2,1,0:T(8,128)(2,1)S(1)}, u32[]{:S(2)}, u32[]{:S(2)}) collective-permute-start(bf16[4,192,256]{2,1,0:T(8,128)(2,1)S(1)} %fusion.1), channel_id=1, source_target_pairs={{0,1},{1,0},{2,3},{3,2},{4,5},{5,4},{6,7},{7,6},{8,9},{9,8},{10,11... | collective-permute-start | bytes 1179656 | tf_op jit(solution)/shard_map/ppermute | solution.py:783
  98.5 15.0 %collective-permute-start.23 = (bf16[192,256]{1,0:T(8,128)(2,1)S(1)}, bf16[192,256]{1,0:T(8,128)(2,1)S(1)}, u32[]{:S(2)}, u32[]{:S(2)}) collective-permute-start(bf16[192,256]{1,0:T(8,128)(2,1)S(1)} %get-tuple-element.245), channel_id=1, source_target_pairs={{0,6},{1,7},{2,4},{3,5},{4,2},{5,3},{6,0},{7,1},{8,14},{9,15},{10,... | collective-permute-start | bytes 294920 | tf_op jit(solution)/shard_map/ppermute | solution.py:783
  100.0 13.5 %collective-permute-start.22 = (bf16[192,256]{1,0:T(8,128)(2,1)S(1)}, bf16[192,256]{1,0:T(8,128)(2,1)S(1)}, u32[]{:S(2)}, u32[]{:S(2)}) collective-permute-start(bf16[192,256]{1,0:T(8,128)(2,1)S(1)} %get-tuple-element.246), channel_id=1, source_target_pairs={{0,4},{1,5},{2,6},{3,7},{4,0},{5,1},{6,2},{7,3},{8,12},{9,13},{10,... | collective-permute-start | bytes 294920 | tf_op jit(solution)/shard_map/ppermute | solution.py:783
  100.0 13.5 %collective-permute-start.21 = (bf16[192,256]{1,0:T(8,128)(2,1)S(1)}, bf16[192,256]{1,0:T(8,128)(2,1)S(1)}, u32[]{:S(2)}, u32[]{:S(2)}) collective-permute-start(bf16[192,256]{1,0:T(8,128)(2,1)S(1)} %get-tuple-element.247), channel_id=1, source_target_pairs={{0,2},{1,3},{2,0},{3,1},{4,6},{5,7},{6,4},{7,5},{8,10},{9,11},{10,... | collective-permute-start | bytes 294920 | tf_op jit(solution)/shard_map/ppermute | solution.py:783
  103.0 12.4 %collective-permute-start.24 = (bf16[4,240,256]{2,1,0:T(8,128)(2,1)S(1)}, bf16[4,240,256]{2,1,0:T(8,128)(2,1)S(1)}, u32[]{:S(2)}, u32[]{:S(2)}) collective-permute-start(bf16[4,240,256]{2,1,0:T(8,128)(2,1)S(1)} %fusion), channel_id=1, source_target_pairs={{0,1},{1,0},{2,3},{3,2},{4,5},{5,4},{6,7},{7,6},{8,9},{9,8},{10,11... | collective-permute-start | bytes 1474568 | tf_op jit(solution)/shard_map/ppermute | solution.py:783
  117.0 17.4 %collective-permute-start.29 = (bf16[240,256]{1,0:T(8,128)(2,1)S(1)}, bf16[240,256]{1,0:T(8,128)(2,1)S(1)}, u32[]{:S(2)}, u32[]{:S(2)}) collective-permute-start(bf16[240,256]{1,0:T(8,128)(2,1)S(1)} %get-tuple-element.242), channel_id=1, source_target_pairs={{0,6},{1,7},{2,4},{3,5},{4,2},{5,3},{6,0},{7,1},{8,14},{9,15},{10,... | collective-permute-start | bytes 368648 | tf_op jit(solution)/shard_map/ppermute | solution.py:783
  119.3 15.0 %collective-permute-start.28 = (bf16[240,256]{1,0:T(8,128)(2,1)S(1)}, bf16[240,256]{1,0:T(8,128)(2,1)S(1)}, u32[]{:S(2)}, u32[]{:S(2)}) collective-permute-start(bf16[240,256]{1,0:T(8,128)(2,1)S(1)} %get-tuple-element.243), channel_id=1, source_target_pairs={{0,4},{1,5},{2,6},{3,7},{4,0},{5,1},{6,2},{7,3},{8,12},{9,13},{10,... | collective-permute-start | bytes 368648 | tf_op jit(solution)/shard_map/ppermute | solution.py:783
  119.3 15.0 %collective-permute-start.27 = (bf16[240,256]{1,0:T(8,128)(2,1)S(1)}, bf16[240,256]{1,0:T(8,128)(2,1)S(1)}, u32[]{:S(2)}, u32[]{:S(2)}) collective-permute-start(bf16[240,256]{1,0:T(8,128)(2,1)S(1)} %get-tuple-element.244), channel_id=1, source_target_pairs={{0,2},{1,3},{2,0},{3,1},{4,6},{5,7},{6,4},{7,5},{8,10},{9,11},{10,... | collective-permute-start | bytes 368648 | tf_op jit(solution)/shard_map/ppermute | solution.py:783
  121.6 12.2 %collective-permute-start.30 = (bf16[192,256]{1,0:T(8,128)(2,1)S(1)}, bf16[192,256]{1,0:T(8,128)(2,1)S(1)}, u32[]{:S(2)}, u32[]{:S(2)}) collective-permute-start(bf16[192,256]{1,0:T(8,128)(2,1)S(1)} %fusion.10), channel_id=1, source_target_pairs={{0,16},{8,24},{16,0},{24,8},{1,17},{9,25},{17,1},{25,9},{2,18},{10... | collective-permute-start | bytes 294920 | tf_op jit(solution)/shard_map/ppermute | solution.py:786
  124.1 10.3 %collective-permute-start.26 = (bf16[4,64,640]{2,1,0:T(8,128)(2,1)S(1)}, bf16[4,64,640]{2,1,0:T(8,128)(2,1)S(1)}, u32[]{:S(2)}, u32[]{:S(2)}) collective-permute-start(bf16[4,64,640]{2,1,0:T(8,128)(2,1)S(1)} %fusion.2), channel_id=1, source_target_pairs={{0,1},{1,0},{2,3},{3,2},{4,5},{5,4},{6,7},{7,6},{8,9},{9,8},{10,11... | collective-permute-start | bytes 983048 | tf_op jit(solution)/shard_map/ppermute | solution.py:783
  133.8 16.6 %collective-permute-start.31 = (bf16[192,256]{1,0:T(8,128)(2,1)S(1)}, bf16[192,256]{1,0:T(8,128)(2,1)S(1)}, u32[]{:S(2)}, u32[]{:S(2)}) collective-permute-start(bf16[192,256]{1,0:T(8,128)(2,1)S(1)} %add_convert_fusion.4.refs_0_), channel_id=1, source_target_pairs={{0,8},{8,0},{16,24},{24,16},{1,9},{9,1},{17,25},{25,17},{2,10},{10... | collective-permute-start | bytes 294920 | tf_op jit(solution)/shard_map/ppermute | solution.py:786
  134.5 11.2 %collective-permute-start.34 = (bf16[64,640]{1,0:T(8,128)(2,1)S(1)}, bf16[64,640]{1,0:T(8,128)(2,1)S(1)}, u32[]{:S(2)}, u32[]{:S(2)}) collective-permute-start(bf16[64,640]{1,0:T(8,128)(2,1)S(1)} %get-tuple-element.219), channel_id=1, source_target_pairs={{0,2},{1,3},{2,0},{3,1},{4,6},{5,7},{6,4},{7,5},{8,10},{9,11},{10,... | collective-permute-start | bytes 245768 | tf_op jit(solution)/shard_map/ppermute | solution.py:783
  134.6 11.1 %collective-permute-start.35 = (bf16[64,640]{1,0:T(8,128)(2,1)S(1)}, bf16[64,640]{1,0:T(8,128)(2,1)S(1)}, u32[]{:S(2)}, u32[]{:S(2)}) collective-permute-start(bf16[64,640]{1,0:T(8,128)(2,1)S(1)} %get-tuple-element.220), channel_id=1, source_target_pairs={{0,4},{1,5},{2,6},{3,7},{4,0},{5,1},{6,2},{7,3},{8,12},{9,13},{10,... | collective-permute-start | bytes 245768 | tf_op jit(solution)/shard_map/ppermute | solution.py:783
  136.3 9.4 %collective-permute-start.36 = (bf16[64,640]{1,0:T(8,128)(2,1)S(1)}, bf16[64,640]{1,0:T(8,128)(2,1)S(1)}, u32[]{:S(2)}, u32[]{:S(2)}) collective-permute-start(bf16[64,640]{1,0:T(8,128)(2,1)S(1)} %get-tuple-element.221), channel_id=1, source_target_pairs={{0,6},{1,7},{2,4},{3,5},{4,2},{5,3},{6,0},{7,1},{8,14},{9,15},{10,... | collective-permute-start | bytes 245768 | tf_op jit(solution)/shard_map/ppermute | solution.py:783
  139.1 8.2 %collective-permute-start.32 = (bf16[240,256]{1,0:T(8,128)(2,1)S(1)}, bf16[240,256]{1,0:T(8,128)(2,1)S(1)}, u32[]{:S(2)}, u32[]{:S(2)}) collective-permute-start(bf16[240,256]{1,0:T(8,128)(2,1)S(1)} %fusion.6), channel_id=1, source_target_pairs={{0,16},{8,24},{16,0},{24,8},{1,17},{9,25},{17,1},{25,9},{2,18},{10... | collective-permute-start | bytes 368648 | tf_op jit(solution)/shard_map/ppermute | solution.py:786
  (9 other events, 61.1 us)

commit v6 on v5

--- a/solution.py
+++ b/solution.py
@@ -180,27 +180,29 @@
     )(place, wo, wg, wu, wd)
 
 
-def keep_close(G, tok_ref, ct_ref, tok_out, ct_out, done_ref):
-    series = pl.ds(pl.program_id(0) * G, G)
-    tok_out[series] = tok_ref[...]
-    ct_out[series] = ct_ref[...]
+def keep_close(G, L, place_ref, tok_ref, ct_ref, tok_out, ct_out, done_ref):
+    step = pl.program_id(0)
+    R, D = G * L, tok_ref.shape[-1]
+    live = (step * G + lax.broadcasted_iota(jnp.int32, (R, 1), 0) // L) < place_ref[0]
+    group_rows(tok_out, step, R)[...] = tok_ref[...].reshape(R, D)
+    group_rows(ct_out, step, R)[...] = jnp.where(live, ct_ref[...].reshape(R, D), jnp.zeros((), bf16))
     done_ref[...] = jnp.zeros_like(done_ref)
 
 
-def call_keep_close(tokens, ct):
+def call_keep_close(place, tokens, ct):
     S, L, D = tokens.shape
     G = GROUP
-    block = pl.BlockSpec((G, L, D), lambda i: (i, 0, 0))
+    block = pl.BlockSpec((G, L, D), lambda i, c: (i, 0, 0))
     return pl.pallas_call(
-        functools.partial(keep_close, G),
-        out_shape=(sds(tokens.shape, bf16), sds(ct.shape, bf16), sds((8, PAIR), f32)),
-        grid=(S // G,),
-        in_specs=[block, block],
-        out_specs=[whole(tokens.shape), whole(ct.shape), whole((8, PAIR))],
+        functools.partial(keep_close, G, L),
+        out_shape=(sds((S * L, D), bf16), sds((S * L, D), bf16), sds((8, PAIR), f32)),
+        grid_spec=pltpu.PrefetchScalarGridSpec(
+            num_scalar_prefetch=1, grid=(S // G,), in_specs=[block, block], out_specs=[whole(None)] * 3
+        ),
         compiler_params=params(MIB_TOKENS),
         cost_estimate=cost(S * L, 1, 8 * S * L * D),
         name="keep_close",
-    )(in_hbm(tokens), in_hbm(ct))
+    )(place, in_hbm(tokens), in_hbm(ct))
 
 
 def attention_forward(G, L, n_z, place_ref, tok_ref, after_ref, *refs):
@@ -248,7 +250,7 @@
     def _():
         mixed, qkv_ref = group_rows(mixed_ref, step, G * L), group_rows(all_qkv, step, G * L)
         probs_ref = all_probs.at[pl.ds(step * G, G)]
-        x = tok_ref[pl.ds(step * G, G)].reshape(G * L, D).astype(f32)
+        x = group_rows(tok_ref, step, G * L)[...].astype(f32)
         normed = (x * inverse_rms(x) * gains_ref[0:1, :]).astype(bf16)
         qkv_ref[...] = nn(normed, w_ref[...]).astype(bf16)
         for s in range(G):
@@ -301,8 +303,7 @@
     return pl.CostEstimate(flops=2 * rows * per_row, bytes_accessed=nbytes, transcendentals=exps)
 
 
-def call_attention_forward(place, tokens, after, pieces):
-    S, L, D = tokens.shape
+def call_attention_forward(place, tokens, after, pieces, S, L, D):
     G, n_z = GROUP, pieces[0].shape[0]
     return pl.pallas_call(
         functools.partial(attention_forward, G, L, n_z),
@@ -401,14 +402,14 @@
         pieces = [(f, pieces[xx].at[k], pieces[2 + xx].at[k]) for xx, k, f in place.shards()]
     if stage == 0:
         (tok_ref, ct_ref, mixed_ref, gains_ref,
-         hid_ref, act, gpart_ref, wd, wo_out, keep, send,
-         agu, ad, wgu, n2, gb, gu, ga, low, gn, spread) = refs
+         hid_ref, act_ref, gpart_ref, wd, wo_out, keep, send,
+         agu, ad, wgu, n2, n2_next, gu, ga, low, gn, spread) = refs
     elif stage == 1:
         hid_ref, ct_ref, gains_ref, wo_in, _, _ = refs[:6]
-        gpart_ref, mixed_ref, act, agu, ad, ao, gf_ref, wd, wgu, n2, gb, gu, ga, low, gn = refs[6:]
+        gpart_ref, mixed_ref, act_ref, agu, ad, ao, gf_ref, wd, wgu, n2, n2_next, gu, ga, low, gn = refs[6:]
     else:
         hid_ref, ct_ref, gains_ref, wo_in, wd, wgu = refs[:6]
-        gpart_ref, mixed_ref, act, agu, ad, ao, gf_ref, keep, send, n2, gb, gu, ga, low, gn, spread = refs[13:]
+        gpart_ref, mixed_ref, act_ref, agu, ad, ao, gf_ref, keep, send, n2, n2_next, gu, ga, low, gn, spread = refs[13:]
     step = pl.program_id(0) + shift
     R = G * L
     FW, D = wd.shape
@@ -416,7 +417,14 @@
     is_ = INNER // n_f
     count = place.count
     group = jnp.minimum(step, (count + G - 1) // G - 1)
-    hid_ref, mixed_ref, act, gpart_ref = (group_rows(ref, group, R) for ref in (hid_ref, mixed_ref, act, gpart_ref))
+
+    def normalise(group, into):
+        if first:
+            h = group_rows(tok_ref, group, R)[...].astype(f32) + nn(group_rows(mixed_ref, group, R)[...], wo_out[...])
+            group_rows(hid_ref, group, R)[...] = h.astype(bf16)
+        else:
+            h = group_rows(hid_ref, group, R)[...].astype(f32)
+        into[...] = (h * inverse_rms(h) * gains_ref[1:2, :]).astype(bf16)
 
     if begins:
 
@@ -431,14 +439,8 @@
 
     @pl.when(step * G < count)
     def _():
-        if first:
-            h = tok_ref[pl.ds(group * G, G)].reshape(R, D).astype(f32) + nn(mixed_ref[...], wo_out[...])
-            hid_ref[...] = h.astype(bf16)
-        else:
-            h = hid_ref[...].astype(f32)
-        n2[...] = (h * inverse_rms(h) * gains_ref[1:2, :]).astype(bf16)
-        live = (step * G + lax.broadcasted_iota(jnp.int32, (R, 1), 0) // L) < count
-        gb[...] = jnp.where(live, ct_ref[pl.ds(group * G, G)].reshape(R, D), jnp.zeros((), bf16))
+        normalise(group, n2)
+        gb, act, gpart, hid = (group_rows(ref, group, R) for ref in (ct_ref, act_ref, gpart_ref, hid_ref))
         for c in range(2):
             cols, both = pl.ds(c * CH, CH), pl.ds(2 * c * CH, 2 * CH)
             gu[c] = nn(n2[...], wgu[:, both])
@@ -460,19 +462,20 @@
             ad[cols, :] += tn(act[:, cols], gb[...])
             agu[:, both] += tn(n2[...], low[c])
         if first:
-            gpart_ref[...] = gn[...].astype(bf16)
+            gpart[...] = gn[...].astype(bf16)
         else:
-            h = hid_ref[...].astype(f32)
+            mixed = group_rows(mixed_ref, group, R)
+            h = hid[...].astype(f32)
             scale = inverse_rms(h)
             hs = h * scale
-            g2 = gn[...] + gpart_ref[...].astype(f32)
+            g2 = gn[...] + gpart[...].astype(f32)
             gf_ref[...] += row_sums(g2 * hs)
             g2 = g2 * gains_ref[1:2, :]
             dot = jnp.mean(g2 * hs, axis=-1, keepdims=True)
             gh = (gb[...].astype(f32) + scale * (g2 - hs * dot)).astype(bf16)
-            gpart_ref[...] = gh
-            ao[...] += tn(mixed_ref[...], gh)
-            mixed_ref[...] = nt(gh, wo_in[...]).astype(bf16)
+            gpart[...] = gh
+            ao[...] += tn(mixed[...], gh)
+            mixed[...] = nt(gh, wo_in[...]).astype(bf16)
 
     if ends:
 
@@ -534,8 +537,9 @@
     )(place, *operands)
 
 
-def layer_result(G, L, place_ref, hid_ref, act_0, act_1, wd_0, wd_1, gains_ref, out_ref, done_ref):
-    step = pl.program_id(0)
+def layer_result(G, L, shift, place_ref, hid_ref, act_0, act_1, wd_0, wd_1, gains_ref, *refs):
+    out_ref, done_ref = refs[-2:]
+    step = pl.program_id(0) + shift
     count = place_ref[0]
     R = G * L
     D = hid_ref.shape[-1]
@@ -554,22 +558,26 @@
         out_ref[...] = jnp.where(live, out, 0.0).astype(bf16).reshape(G, L, D)
 
 
-def call_layer_result(place, hidden, act_0, act_1, wd_0, wd_1, gains, S, L):
+def call_layer_result(place, hidden, act_0, act_1, wd_0, wd_1, gains, S, L, earlier=None):
     G, D = GROUP, hidden.shape[-1]
     operands = (hidden, act_0, act_1, wd_0, wd_1, gains)
+    half = S // G // 2
+    steps, shift = (half, 0) if earlier is None else (S // G - half, half)
+    more = () if earlier is None else (earlier,)
     return pl.pallas_call(
-        functools.partial(layer_result, G, L),
+        functools.partial(layer_result, G, L, shift),
         out_shape=(pltpu.HBM((S, L, D), bf16), sds(gains.shape, f32)),
         grid_spec=pltpu.PrefetchScalarGridSpec(
             num_scalar_prefetch=1,
-            grid=(S // G,),
-            in_specs=[whole(a.shape) for a in operands],
-            out_specs=(series_spec(G, (S, L, D), True), whole(gains.shape)),
+            grid=(steps,),
+            in_specs=[whole(a.shape) for a in operands] + [pl.BlockSpec(memory_space=pl.ANY)] * len(more),
+            out_specs=(pl.BlockSpec((G, L, D), lambda i, c: (i + shift, 0, 0)), whole(gains.shape)),
         ),
+        input_output_aliases={7: 0} if more else {},
         compiler_params=params(MIB_RESULT),
-        cost_estimate=cost(S * L, 2 * D * act_0.shape[-1], S * L * 6000),
+        cost_estimate=cost(S * L // 2, 2 * D * act_0.shape[-1], S * L * 3000),
         name="layer_result",
-    )(place, *operands)
+    )(place, *operands, *more)
 
 
 def attention_backward(G, L, n_z, place_ref, tok_ref, _, probs_ref, gm_ref, w_ref, gains_ref, gf_ref,
@@ -614,7 +622,7 @@
                 q, k = dqkv[rows, cols[p][0]], dqkv[rows, cols[p][1]]
                 dqkv[rows, cols[p][1]] = nn(low, split_heads(q)).astype(bf16)
                 dqkv[rows, cols[p][0]] = join_heads(tn(low, k)).astype(bf16)
-        x = tok_ref[pl.ds(group * G, G)].reshape(R, D).astype(f32)
+        x = group_rows(tok_ref, group, R)[...].astype(f32)
         aw[...] += tn((x * inverse_rms(x) * gains_ref[0:1, :]).astype(bf16), dqkv[...])
 
     @pl.when(step == last)
@@ -651,8 +659,7 @@
             pl.when(place.core == c)(functools.partial(write, c))
 
 
-def call_attention_backward(place, n_z, tokens, qkv, probs, gm, w, gains, gf):
-    S, L, D = tokens.shape
+def call_attention_backward(place, n_z, tokens, qkv, probs, gm, w, gains, gf, S, L, D):
     G = GROUP
     pack = (2, n_z, D // (2 * n_z), CUT)
     vm = pltpu.VMEM
@@ -677,13 +684,12 @@
     )(place, tokens, qkv, probs, gm, w, gains, gf)
 
 
-def token_gradient(G, L, first_step, place_ref, tok_ref, dqkv_ref, gh_ref, w_ref, gains_ref, *refs):
-    gt_ref, done_ref = refs[-2:]
+def token_gradient(G, L, place_ref, tok_ref, dqkv_ref, gh_ref, w_ref, gains_ref, gt_ref, done_ref):
+    step = pl.program_id(0)
+    D = tok_ref.shape[-1]
     done_ref[...] = gains_ref[...]
-    step = pl.program_id(0) + first_step
-    D = tok_ref.shape[-1]
     group = jnp.minimum(step, (place_ref[0] + G - 1) // G - 1)
-    dqkv_ref, gh_ref = group_rows(dqkv_ref, group, G * L), group_rows(gh_ref, group, G * L)
+    tok_ref, dqkv_ref, gh_ref = (group_rows(ref, group, G * L) for ref in (tok_ref, dqkv_ref, gh_ref))
 
     @pl.when(step * G >= place_ref[0])
     def _():
@@ -691,42 +697,35 @@
 
     @pl.when(step * G < place_ref[0])
     def _():
-        x = tok_ref[pl.ds(group * G, G)].reshape(G * L, D).astype(f32)
-        scale = inverse_rms(x)
-        xs = x * scale
-        g = nt(dqkv_ref[...], w_ref[...]) * gains_ref[0:1, :]
-        dot = jnp.mean(g * xs, axis=-1, keepdims=True)
-        gt_ref[...] = (gh_ref[...].astype(f32) + scale * (g - xs * dot)).astype(bf16).reshape(G, L, D)
-
-
-def call_token_gradient(place, tokens, dqkv, gh, w, gains, part, earlier=None):
-    S, L, D = tokens.shape
+        half = G * L // 2
+        parts = [pl.ds(i * half, half) for i in range(2)]
+        products = [nt(dqkv_ref[rows, :], w_ref[...]) for rows in parts]
+        for i, rows in enumerate(parts):
+            x = tok_ref[rows, :].astype(f32)
+            scale = inverse_rms(x)
+            xs = x * scale
+            g = products[i] * gains_ref[0:1, :]
+            dot = jnp.mean(g * xs, axis=-1, keepdims=True)
+            gt = gh_ref[rows, :].astype(f32) + scale * (g - xs * dot)
+            gt_ref[pl.ds(i * G // 2, G // 2)] = gt.astype(bf16).reshape(G // 2, L, D)
+
+
+def call_token_gradient(place, tokens, dqkv, gh, w, gains, S, L, D):
     G = GROUP
-    steps = S // G // 2 if part == 0 else S // G - S // G // 2
-    shift = part * (S // G // 2)
-
-    def rows(width):
-        return pl.BlockSpec((G * L, width), lambda i, c: (live_group(i + shift, c, G), 0))
-
-    def series(every):
-        return pl.BlockSpec((G, L, D), lambda i, c: (i + shift if every else live_group(i + shift, c, G), 0, 0))
-
-    more = [] if earlier is None else [earlier]
+    operands = (tokens, dqkv, gh, w, gains)
     return pl.pallas_call(
-        functools.partial(token_gradient, G, L, shift),
+        functools.partial(token_gradient, G, L),
         out_shape=(pltpu.HBM((S, L, D), bf16), sds(gains.shape, f32)),
         grid_spec=pltpu.PrefetchScalarGridSpec(
             num_scalar_prefetch=1,
-            grid=(steps,),
-            in_specs=[whole(tokens.shape), whole(dqkv.shape), whole(gh.shape), whole(w.shape), whole(gains.shape)]
-            + [pl.BlockSpec(memory_space=pl.ANY)] * len(more),
-            out_specs=(series(True), whole(gains.shape)),
+            grid=(S // G,),
+            in_specs=[whole(a.shape) for a in operands],
+            out_specs=(series_spec(G, (S, L, D), True), whole(gains.shape)),
         ),
-        input_output_aliases={6: 0} if more else {},
         compiler_params=params(MIB_TOKENS),
-        cost_estimate=cost(S * L // 2, D * 3 * INNER * 2, S * L * 2500),
+        cost_estimate=cost(S * L, D * 3 * INNER * 2, S * L * 5000),
         name="token_gradient",
-    )(place, tokens, dqkv, gh, w, gains, *more)
+    )(place, *operands)
 
 
 def finish(n_f, place_ref, *refs):
@@ -804,11 +803,12 @@
             own = own + value.astype(f32)
         return own.astype(bf16)
 
-    def replicas(own):
+    def replicas(own, got):
         distance = 2
         while distance < n_r:
-            own = (own.astype(f32) + over_rep(own, distance).astype(f32)).astype(bf16)
+            own = (own.astype(f32) + got.astype(f32)).astype(bf16)
             distance *= 2
+            got = over_rep(own, distance) if distance < n_r else None
         return own, over_rep(own, 1)
 
     together = lax.optimization_barrier
@@ -824,13 +824,13 @@
         z_a, pack_1 = together((along_z(pack_a), pack_1))
         near_a = jnp.stack(z_a)
         far_a, near_ac = over_fsdp(near_a, 1), over_rep(near_a, 1)
-        tokens, cotangent, done = call_keep_close(tokens, cotangent)
+        tokens, cotangent, done = call_keep_close(place, tokens, cotangent)
         done, far_a, near_ac, z_0, pack_1 = together((done, far_a, near_ac, z_0, pack_1))
         far_ac, near_0 = over_rep(far_a, 1), jnp.stack(z_0)
         far_ac, near_0 = together((far_ac, near_0))
 
         far_0, near_0c, z_1 = over_fsdp(near_0, 1), over_rep(near_0, 1), along_z(pack_1)
-        qkv, probs, mixed, w_all, gains = call_attention_forward(place, tokens, done, (near_a, far_a, near_ac, far_ac))
+        qkv, probs, mixed, w_all, gains = call_attention_forward(place, tokens, done, (near_a, far_a, near_ac, far_ac), S, L, D)
         gains, far_0, near_0c, z_1 = together((gains, far_0, near_0c, z_1))
         far_0c, near_1 = over_rep(far_0, 1), jnp.stack(z_1)
         far_0c, near_1 = together((far_0c, near_1))
@@ -858,7 +858,7 @@
         here_1, away_1 = halved(keep_1, got_1)
         gf, away_1 = together((gf, away_1))
         got_1 = over_fsdp(away_1, 1)
-        dqkv, keep_2, send_2 = call_attention_backward(place, n_z, tokens, qkv, probs, gm, w_all, gains, gf)
+        dqkv, keep_2, send_2 = call_attention_backward(place, n_z, tokens, qkv, probs, gm, w_all, gains, gf, S, L, D)
         keep_2, send_2, z_0, got_1 = together((keep_2, send_2, z_0, got_1))
         sum_0 = summed(own_0, z_0)
         own_1, z_1 = joined(here_1, got_1)
@@ -867,18 +867,21 @@
         here_2, away_2 = halved(keep_2, got_2)
         gains, away_2, sum_0 = together((gains, away_2, sum_0))
         got_2 = over_fsdp(away_2, 1)
-        half_tokens, done = call_token_gradient(place, tokens, dqkv, gh, w_all, gains, 0)
-        grad_tokens, done = call_token_gradient(place, tokens, dqkv, gh, w_all, done, 1, half_tokens)
+        grad_tokens, done = call_token_gradient(place, tokens, dqkv, gh, w_all, gains, S, L, D)
         done, got_2, z_1 = together((done, got_2, z_1))
         sum_1 = summed(own_1, z_1)
         own_2, z_2 = joined(here_2, got_2)
         done, z_2 = together((done, z_2))
         z_2 = to_z(z_2)
-        layer_out, done = call_layer_result(place, hidden, act_0, act_1, wd_0, wd_1, done, S, L)
+        half_out, done = call_layer_result(place, hidden, act_0, act_1, wd_0, wd_1, done, S, L)
         done, z_2 = together((done, z_2))
         sum_2 = summed(own_2, z_2)
+        done, sum_2 = together((done, sum_2))
+        got = [over_rep(value, 2) for value in (sum_0, sum_1, sum_2)]
+        layer_out, done = call_layer_result(place, hidden, act_0, act_1, wd_0, wd_1, done, S, L, half_out)
+        done, got = together((done, got))
         gq, gk, gv, go, gg, gu, gd, grad_attn_gain, grad_ffn_gain, grad_bias = call_finish(
-            place, n_f, [replicas(value) for value in (sum_0, sum_1, sum_2)],
+            place, n_f, [replicas(own, y) for own, y in zip((sum_0, sum_1, sum_2), got)],
             (wq.shape, wk.shape, wv.shape, wo.shape, wg.shape, wu.shape, wd.shape,
              attn_gain.shape, ffn_gain.shape, rel_bias.shape), done,
         )

time: 152 us -> 150 us (0.987); the launches traced: 153 us -> 149 us
  Pallas kernels: 70 us -> 47.8 us
  waiting for transfers between devices: 29.2 us -> 42.6 us
  starting transfers between devices: 49.8 us -> 54.4 us
    ppermute x24, waiting for transfers between devices: 21.9 us -> 38.2 us  [over_fsdp(): return lax.ppermute(value, 'fsdp', [(i, i ^ distance) for i in range(n_f)])]
    pallas_call x3, Pallas kernels: 29.1 us -> 16.1 us  [call_ffn_half(): pl.pallas_call(functools.partial(ffn_half, G, L, n_z, stage, shift), out_...]
    ppermute x24, starting transfers between devices: 34.4 us -> 45.1 us  [over_fsdp(): return lax.ppermute(value, 'fsdp', [(i, i ^ distance) for i in range(n_f)])]
    ppermute x15, starting transfers between devices: 15.4 us -> 9.35 us  [over_rep(): return lax.ppermute(value, 'rep', [(i, i ^ distance) for i in range(n_r)])]
    pallas_call x1, Pallas kernels: 9.85 us -> 5.98 us  [call_attention_backward(): pl.pallas_call(functools.partial(attention_backward, G, L, n_z), out_shap...]
    pallas_call x1, Pallas kernels: 7.86 us -> 4.52 us  [call_attention_forward(): pl.pallas_call(functools.partial(attention_forward, G, L, n_z), out_shape...]
    ppermute x15, waiting for transfers between devices: 7.25 us -> 4.44 us  [over_rep(): return lax.ppermute(value, 'rep', [(i, i ^ distance) for i in range(n_r)])]
    pallas_call x4, Pallas kernels: 17.8 us -> 15.7 us  [the longest x2 5.48 us: call_layer_result(): pl.pallas_call(functools.partial(layer_result, G, L, shift), out_shape=(p...]
  transfers between devices with their start and end apart: 39 -> 39, of which waited for: 10 -> 15; matrix products, arithmetic and copies ran while one was open for 1% -> 1% of each run, Pallas kernels for 43% -> 30%
where the time goes in v6:
time: 150 us; the launch traced here: 149 us
  starting transfers between devices  54.4 us (36%)
  Pallas kernels  47.8 us (32%)
  waiting for transfers between devices  42.6 us (28%)
  other arithmetic  2.67 us (2%)
  between operations  1.59 us (1%)
    ppermute x24, starting transfers between devices, over_fsdp(): return lax.ppermute(value, 'fsdp', [(i, i ^ distance) for i in range(n_f)])  45.1 us
    ppermute x24, waiting for transfers between devices, over_fsdp(): return lax.ppermute(value, 'fsdp', [(i, i ^ distance) for i in range(n_f)])  38.2 us
    pallas_call x3, Pallas kernels, call_ffn_half(): pl.pallas_call(functools.partial(ffn_half, G, L, n_z, stage, shift), out_...  16.1 us
    ppermute x15, starting transfers between devices, over_rep(): return lax.ppermute(value, 'rep', [(i, i ^ distance) for i in range(n_r)])  9.35 us
    pallas_call x1, Pallas kernels, call_attention_backward(): pl.pallas_call(functools.partial(attention_backward, G, L, n_z), out_shap...  5.98 us
    pallas_call x2, Pallas kernels, call_layer_result(): pl.pallas_call(functools.partial(layer_result, G, L, shift), out_shape=(p...  5.48 us
    pallas_call x1, Pallas kernels, call_token_gradient(): pl.pallas_call(functools.partial(token_gradient, G, L), out_shape=(pltpu....  5.22 us
    pallas_call x1, Pallas kernels, call_keep_close(): pl.pallas_call(functools.partial(keep_close, G, L), out_shape=(sds((S * L...  5.01 us
  transfers between devices with their start and end apart: 39, of which 15 were waited for; matrix products, arithmetic and copies ran while one was open for 1% of the time, Pallas kernels for 30%

profile of v6, /device:TPU:0, one launch (start us, length us, event | category | flops | bytes accessed | tf_op | source)
XLA Modules:
  0.0 149.2 jit_solution(5828515350496060880)
XLA Ops:
  2.0 1.7 %prepare_attention.1 = bf16[64,640]{1,0:T(8,128)(2,1)} custom-call(s32[4]{0:T(128)} %pad_add_fusion.place_ref, f32[24]{0:T(128)} %bias_ref.1, f32[64,384]{1,0:T(8,128)} %wq.1, f32[64,384]{1,0:T(8,128)} %wk.1, f32[64,384]{1,0:T(8,128)} %wv.1, f32[1,64]{1,0:T(1,128)} %bitcast.94, f32[1,64]{1,0:T(1,128)} %bitcast.95), custom_call_target="tpu_custom_call" | custom-call | tf_op jit(solution)/shard_map/prepare_attention/pallas_call | solution.py:162
  3.7 5.0 %collective-permute-start.2 = (bf16[64,640]{1,0:T(8,128)(2,1)}, bf16[64,640]{1,0:T(8,128)(2,1)S(1)}, u32[]{:S(2)}, u32[]{:S(2)}) collective-permute-start(bf16[64,640]{1,0:T(8,128)(2,1)} %prepare_attention.1), channel_id=1, source_target_pairs={{0,6},{1,7},{2,4},{3,5},{4,2},{5,3},{6,0},{7,1},{8,14},{9,15},{10,... | collective-permute-start | bytes 245768 | tf_op jit(solution)/shard_map/ppermute | solution.py:782
  9.3 2.0 %prepare_ffn.1 = (bf16[240,256]{1,0:T(8,128)(2,1)}, bf16[192,256]{1,0:T(8,128)(2,1)}) custom-call(s32[4]{0:T(128)} %pad_add_fusion.place_ref, f32[48,512]{1,0:T(8,128)} %wo.1, f32[64,1024]{1,0:T(8,128)} %wg.1, f32[64,1024]{1,0:T(8,128)} %wu.1, f32[128,512]{1,0:T(8,128)} %wd.1), custom_call_target="tpu_custom_call" | custom-call | tf_op jit(solution)/shard_map/prepare_ffn/pallas_call | solution.py:174
  12.0 3.8 %collective-permute-done.1 = bf16[64,640]{1,0:T(8,128)(2,1)S(1)} collective-permute-done((bf16[64,640]{1,0:T(8,128)(2,1)}, bf16[64,640]{1,0:T(8,128)(2,1)S(1)}, u32[]{:S(2)}, u32[]{:S(2)}) %collective-permute-start.1) | collective-permute-done | bytes 81952 | tf_op jit(solution)/shard_map/ppermute | solution.py:782
  16.8 1.6 %collective-permute-start.3 = (bf16[4,64,640]{2,1,0:T(8,128)(2,1)S(1)}, bf16[4,64,640]{2,1,0:T(8,128)(2,1)S(1)}, u32[]{:S(2)}, u32[]{:S(2)}) collective-permute-start(bf16[4,64,640]{2,1,0:T(8,128)(2,1)S(1)} %pad_maximum_fusion.2.refs_0_), channel_id=1, source_target_pairs={{0,1},{1,0},{2,3},{3,2},{4,5},{5,4},{6,7},{7,6},{8,9},{9,8},{10,11... | collective-permute-start | bytes 983048 | tf_op jit(solution)/shard_map/ppermute | solution.py:782
  18.4 2.6 %collective-permute-start.7 = (bf16[240,256]{1,0:T(8,128)(2,1)}, bf16[240,256]{1,0:T(8,128)(2,1)S(1)}, u32[]{:S(2)}, u32[]{:S(2)}) collective-permute-start(bf16[240,256]{1,0:T(8,128)(2,1)} %get-tuple-element.139), channel_id=1, source_target_pairs={{0,6},{1,7},{2,4},{3,5},{4,2},{5,3},{6,0},{7,1},{8,14},{9,15},{10,... | collective-permute-start | bytes 368648 | tf_op jit(solution)/shard_map/ppermute | solution.py:782
  21.0 1.8 %collective-permute-start.5 = (bf16[240,256]{1,0:T(8,128)(2,1)}, bf16[240,256]{1,0:T(8,128)(2,1)S(1)}, u32[]{:S(2)}, u32[]{:S(2)}) collective-permute-start(bf16[240,256]{1,0:T(8,128)(2,1)} %get-tuple-element.139), channel_id=1, source_target_pairs={{0,2},{1,3},{2,0},{3,1},{4,6},{5,7},{6,4},{7,5},{8,10},{9,11},{10,... | collective-permute-start | bytes 368648 | tf_op jit(solution)/shard_map/ppermute | solution.py:782
  22.8 5.0 %keep_close.1 = (bf16[3072,512]{1,0:T(8,128)(2,1)S(1)}, bf16[3072,512]{1,0:T(8,128)(2,1)S(1)}, f32[8,128]{1,0:T(8,128)S(1)}) custom-call(s32[4]{0:T(128)} %pad_add_fusion.place_ref, bf16[48,64,512]{2,1,0:T(8,128)(2,1)} %tok_ref.1, bf16[48,64,512]{2,1,0:T(8,128)(2,1)} %ct_ref.1), custom_call_target="tpu_custom_call" | custom-call | flops 6144 | bytes 12582912 | tf_op jit(solution)/shard_map/keep_close/pallas_call | solution.py:196
  27.8 4.4 %collective-permute-done.6 = bf16[240,256]{1,0:T(8,128)(2,1)S(1)} collective-permute-done((bf16[240,256]{1,0:T(8,128)(2,1)}, bf16[240,256]{1,0:T(8,128)(2,1)S(1)}, u32[]{:S(2)}, u32[]{:S(2)}) %collective-permute-start.6) | collective-permute-done | bytes 122912 | tf_op jit(solution)/shard_map/ppermute | solution.py:782
  32.3 1.6 %collective-permute-start.13 = (bf16[192,256]{1,0:T(8,128)(2,1)S(1)}, bf16[192,256]{1,0:T(8,128)(2,1)S(1)}, u32[]{:S(2)}, u32[]{:S(2)}) collective-permute-start(bf16[192,256]{1,0:T(8,128)(2,1)S(1)} %copy-done.1), channel_id=1, source_target_pairs={{0,6},{1,7},{2,4},{3,5},{4,2},{5,3},{6,0},{7,1},{8,14},{9,15},{10,... | collective-permute-start | bytes 294920 | tf_op jit(solution)/shard_map/ppermute | solution.py:782
  33.9 2.9 %collective-permute-start.11 = (bf16[192,256]{1,0:T(8,128)(2,1)S(1)}, bf16[192,256]{1,0:T(8,128)(2,1)S(1)}, u32[]{:S(2)}, u32[]{:S(2)}) collective-permute-start(bf16[192,256]{1,0:T(8,128)(2,1)S(1)} %copy-done.1), channel_id=1, source_target_pairs={{0,2},{1,3},{2,0},{3,1},{4,6},{5,7},{6,4},{7,5},{8,10},{9,11},{10,... | collective-permute-start | bytes 294920 | tf_op jit(solution)/shard_map/ppermute | solution.py:782
  37.5 4.5 %attention_forward.1 = (bf16[3072,1152]{1,0:T(8,128)(2,1)S(1)}, bf16[48,3,64,128]{3,2,1,0:T(8,128)(2,1)S(1)}, bf16[3072,384]{1,0:T(8,128)(2,1)S(1)}, bf16[512,1152]{1,0:T(8,128)(2,1)S(1)}, f32[8,512]{1,0:T(8,128)S(1)}) custom-call(s32[4]{0:T(128)} %pad_add_fusion.place_ref, bf16[3072,512]{1,0:T(8,128)(2,1)S(1)} %get-tuple-element.144.tok_ref.refs_4_, ...), custom_call_target="tpu_custom_call" | custom-call | flops 14495514624 | bytes 15360000 | tf_op jit(solution)/shard_map/attention_forward/pallas_call | solution.py:308
  43.5 7.0 %collective-permute-done.9.refs_1_ = bf16[4,240,256]{2,1,0:T(8,128)(2,1)S(1)} collective-permute-done((bf16[4,240,256]{2,1,0:T(8,128)(2,1)S(1)}, bf16[4,240,256]{2,1,0:T(8,128)(2,1)S(1)}, u32[]{:S(2)}, u32[]{:S(2)}) %collective-permute-start.9) | collective-permute-done | bytes 491552 | tf_op jit(solution)/shard_map/ppermute | solution.py:782
  50.6 1.8 %collective-permute-done.14.refs_3_ = bf16[4,240,256]{2,1,0:T(8,128)(2,1)S(1)} collective-permute-done((bf16[4,240,256]{2,1,0:T(8,128)(2,1)S(1)}, bf16[4,240,256]{2,1,0:T(8,128)(2,1)S(1)}, u32[]{:S(2)}, u32[]{:S(2)}) %collective-permute-start.14) | collective-permute-done | bytes 491552 | tf_op jit(solution)/shard_map/ppermute | solution.py:785
  53.1 7.3 %ffn_first.1 = (bf16[3072,512]{1,0:T(8,128)(2,1)S(1)}, bf16[3072,512]{1,0:T(8,128)(2,1)S(1)}, bf16[3072,512]{1,0:T(8,128)(2,1)S(1)}, bf16[512,512]{1,0:T(8,128)(...) custom-call(s32[4]{0:T(128)} %pad_add_fusion.place_ref, ...), custom_call_target="tpu_custom_call" | custom-call | flops 14495514624 | bytes 27648000 | tf_op jit(solution)/shard_map/ffn_first/pallas_call | solution.py:523
  60.4 3.5 %collective-permute-done.15.refs_1_ = bf16[4,192,256]{2,1,0:T(8,128)(2,1)S(1)} collective-permute-done((bf16[4,192,256]{2,1,0:T(8,128)(2,1)S(1)}, bf16[4,192,256]{2,1,0:T(8,128)(2,1)S(1)}, u32[]{:S(2)}, u32[]{:S(2)}) %collective-permute-start.15) | collective-permute-done | bytes 393248 | tf_op jit(solution)/shard_map/ppermute | solution.py:782
  65.7 7.7 %ffn_second.1 = (bf16[3072,512]{1,0:T(8,128)(2,1)S(1)}, bf16[3072,384]{1,0:T(8,128)(2,1)S(1)}, bf16[3072,512]{1,0:T(8,128)(2,1)S(1)}, f32[512,1024]{1,0:T(8,128)...) custom-call(s32[4]{0:T(128)} %pad_add_fusion.place_ref, ...), custom_call_target="tpu_custom_call", output_to_operand_aliasing={{0}: (9, {}), {1}: (10, {})} | custom-call | flops 7247757312 | bytes 27648000 | tf_op jit(solution)/shard_map/ffn_second/pallas_call | solution.py:523
  73.5 10.2 %collective-permute-start.19 = (bf16[4,192,256]{2,1,0:T(8,128)(2,1)S(1)}, bf16[4,192,256]{2,1,0:T(8,128)(2,1)S(1)}, u32[]{:S(2)}, u32[]{:S(2)}) collective-permute-start(bf16[4,192,256]{2,1,0:T(8,128)(2,1)S(1)} %fusion.1), channel_id=1, source_target_pairs={{0,1},{1,0},{2,3},{3,2},{4,5},{5,4},{6,7},{7,6},{8,9},{9,8},{10,11... | collective-permute-start | bytes 1179656 | tf_op jit(solution)/shard_map/ppermute | solution.py:782
  84.8 8.3 %collective-permute-done.19 = bf16[4,192,256]{2,1,0:T(8,128)(2,1)S(1)} collective-permute-done((bf16[4,192,256]{2,1,0:T(8,128)(2,1)S(1)}, bf16[4,192,256]{2,1,0:T(8,128)(2,1)S(1)}, u32[]{:S(2)}, u32[]{:S(2)}) %collective-permute-start.19) | collective-permute-done | bytes 393248 | tf_op jit(solution)/shard_map/ppermute | solution.py:782
  94.6 4.7 %collective-permute-start.22 = (bf16[192,256]{1,0:T(8,128)(2,1)S(1)}, bf16[192,256]{1,0:T(8,128)(2,1)S(1)}, u32[]{:S(2)}, u32[]{:S(2)}) collective-permute-start(bf16[192,256]{1,0:T(8,128)(2,1)S(1)} %get-tuple-element.258), channel_id=1, source_target_pairs={{0,4},{1,5},{2,6},{3,7},{4,0},{5,1},{6,2},{7,3},{8,12},{9,13},{10,... | collective-permute-start | bytes 294920 | tf_op jit(solution)/shard_map/ppermute | solution.py:782
  100.3 6.0 %attention_backward.1 = (bf16[3072,1152]{1,0:T(8,128)(2,1)S(1)}, bf16[2,4,64,640]{3,2,1,0:T(8,128)(2,1)S(1)}, bf16[2,4,64,640]{3,2,1,0:T(8,128)(2,1)S(1)}) custom-call(s32[4]{0:T(128)} %pad_add_fusion.place_ref, bf16[3072,512]{1,0:T(8,128)(2,1)S(1)} %get-tuple-element.144.tok_ref.refs_4_, ...), custom_call_target="tpu_custom_call", output_to_operand_aliasing={{0}: (2, {})} | custom-call | flops 14495514624 | bytes 18432000 | tf_op jit(solution)/shard_map/attention_backward/pallas_call | solution.py:666
  106.7 5.9 %collective-permute-done.24 = bf16[4,240,256]{2,1,0:T(8,128)(2,1)S(1)} collective-permute-done((bf16[4,240,256]{2,1,0:T(8,128)(2,1)S(1)}, bf16[4,240,256]{2,1,0:T(8,128)(2,1)S(1)}, u32[]{:S(2)}, u32[]{:S(2)}) %collective-permute-start.24) | collective-permute-done | bytes 491552 | tf_op jit(solution)/shard_map/ppermute | solution.py:782
  112.8 2.1 %collective-permute-start.29 = (bf16[240,256]{1,0:T(8,128)(2,1)S(1)}, bf16[240,256]{1,0:T(8,128)(2,1)S(1)}, u32[]{:S(2)}, u32[]{:S(2)}) collective-permute-start(bf16[240,256]{1,0:T(8,128)(2,1)S(1)} %get-tuple-element.254), channel_id=1, source_target_pairs={{0,6},{1,7},{2,4},{3,5},{4,2},{5,3},{6,0},{7,1},{8,14},{9,15},{10,... | collective-permute-start | bytes 368648 | tf_op jit(solution)/shard_map/ppermute | solution.py:782
  114.9 2.8 %collective-permute-start.28 = (bf16[240,256]{1,0:T(8,128)(2,1)S(1)}, bf16[240,256]{1,0:T(8,128)(2,1)S(1)}, u32[]{:S(2)}, u32[]{:S(2)}) collective-permute-start(bf16[240,256]{1,0:T(8,128)(2,1)S(1)} %get-tuple-element.255), channel_id=1, source_target_pairs={{0,4},{1,5},{2,6},{3,7},{4,0},{5,1},{6,2},{7,3},{8,12},{9,13},{10,... | collective-permute-start | bytes 368648 | tf_op jit(solution)/shard_map/ppermute | solution.py:782
  117.9 5.4 %collective-permute-start.33 = (bf16[192,256]{1,0:T(8,128)(2,1)S(1)}, bf16[192,256]{1,0:T(8,128)(2,1)S(1)}, u32[]{:S(2)}, u32[]{:S(2)}) collective-permute-start(bf16[192,256]{1,0:T(8,128)(2,1)S(1)} %fusion.10), channel_id=1, source_target_pairs={{0,16},{8,24},{16,0},{24,8},{1,17},{9,25},{17,1},{25,9},{2,18},{10... | collective-permute-start | bytes 294920 | tf_op jit(solution)/shard_map/ppermute | solution.py:785
  124.7 5.2 %token_gradient.1 = (bf16[48,64,512]{2,1,0:T(8,128)(2,1)}, f32[8,512]{1,0:T(8,128)S(1)}) custom-call(s32[4]{0:T(128)} %pad_add_fusion.place_ref, bf16[3072,512]{1,0:T(8,128)(2,1)S(1)} %get-tuple-element.144.tok_ref.refs_4_, bf16[3072,1152]{1,0:T(8,128)(2,1)S(1)} %get-tuple-element.198.dqkv_ref, bf16[3072,512]{1,0:T(8,128)(2,1)S(1)} %get-tuple-element.199.gh_ref, ...), custom_call_target="tpu_custom_call" | custom-call | flops 7247757312 | bytes 15360000 | tf_op jit(solution)/shard_map/token_gradient/pallas_call | solution.py:716
  130.0 2.3 %collective-permute-done.26 = bf16[4,64,640]{2,1,0:T(8,128)(2,1)S(1)} collective-permute-done((bf16[4,64,640]{2,1,0:T(8,128)(2,1)S(1)}, bf16[4,64,640]{2,1,0:T(8,128)(2,1)S(1)}, u32[]{:S(2)}, u32[]{:S(2)}) %collective-permute-start.26) | collective-permute-done | bytes 327712 | tf_op jit(solution)/shard_map/ppermute | solution.py:782
  133.4 3.5 %collective-permute-start.32 = (bf16[64,640]{1,0:T(8,128)(2,1)S(1)}, bf16[64,640]{1,0:T(8,128)(2,1)S(1)}, u32[]{:S(2)}, u32[]{:S(2)}) collective-permute-start(bf16[64,640]{1,0:T(8,128)(2,1)S(1)} %get-tuple-element.219), channel_id=1, source_target_pairs={{0,6},{1,7},{2,4},{3,5},{4,2},{5,3},{6,0},{7,1},{8,14},{9,15},{10,... | collective-permute-start | bytes 245768 | tf_op jit(solution)/shard_map/ppermute | solution.py:782
  137.3 3.1 %layer_result.2 = (bf16[48,64,512]{2,1,0:T(8,128)(2,1)}, f32[8,512]{1,0:T(8,128)S(1)}) custom-call(s32[4]{0:T(128)} %pad_add_fusion.place_ref, bf16[3072,512]{1,0:T(8,128)(2,1)S(1)} %get-tuple-element.160.refs_4_.refs_0_.hid_ref, bf16[3072,512]{1,0:T(8,128)(2,1)S(1)} %get-tuple-element.161.act_0, bf16[3072,512]{1,0:T(8,128)(2,1)S(1)} %get-tuple-element.184.act_1, ...), custom_call_target="tpu_custom_call" | custom-call | flops 1610612736 | bytes 9216000 | tf_op jit(solution)/shard_map/layer_result/pallas_call | solution.py:567
  140.9 1.9 %collective-permute-start.35 = (bf16[64,640]{1,0:T(8,128)(2,1)S(1)}, bf16[64,640]{1,0:T(8,128)(2,1)S(1)}, u32[]{:S(2)}, u32[]{:S(2)}) collective-permute-start(bf16[64,640]{1,0:T(8,128)(2,1)S(1)} %fusion.14), channel_id=1, source_target_pairs={{0,16},{8,24},{16,0},{24,8},{1,17},{9,25},{17,1},{25,9},{2,18},{10... | collective-permute-start | bytes 245768 | tf_op jit(solution)/shard_map/ppermute | solution.py:785
  142.9 2.4 %layer_result.3 = (bf16[48,64,512]{2,1,0:T(8,128)(2,1)}, f32[8,512]{1,0:T(8,128)S(1)}) custom-call(s32[4]{0:T(128)} %pad_add_fusion.place_ref, bf16[3072,512]{1,0:T(8,128)(2,1)S(1)} %get-tuple-element.160.refs_4_.refs_0_.hid_ref, bf16[3072,512]{1,0:T(8,128)(2,1)S(1)} %get-tuple-element.161.act_0, ...), custom_call_target="tpu_custom_call", output_to_operand_aliasing={{0}: (7, {})} | custom-call | flops 1610612736 | bytes 9216000 | tf_op jit(solution)/shard_map/layer_result/pallas_call | solution.py:567
  147.4 1.8 %finish.1 = (f32[64,384]{1,0:T(8,128)}, f32[64,384]{1,0:T(8,128)}, f32[64,384]{1,0:T(8,128)}, f32[48,512]{1,0:T(8,128)}, f32[64,1024]{1,0:T(8,128)}, /*index=5*/...) custom-call(s32[4]{0:T(128)} %pad_add_fusion.place_ref, ...), custom_call_target="tpu_custom_call" | custom-call | tf_op jit(solution)/shard_map/finish/pallas_call | solution.py:767
  (81 shorter events, 17.9 us)
Async XLA Ops:
  3.7 8.3 %collective-permute-start.2 = (bf16[64,640]{1,0:T(8,128)(2,1)}, bf16[64,640]{1,0:T(8,128)(2,1)S(1)}, u32[]{:S(2)}, u32[]{:S(2)}) collective-permute-start(bf16[64,640]{1,0:T(8,128)(2,1)} %prepare_attention.1), channel_id=1, source_target_pairs={{0,6},{1,7},{2,4},{3,5},{4,2},{5,3},{6,0},{7,1},{8,14},{9,15},{10,... | collective-permute-start | bytes 245768 | tf_op jit(solution)/shard_map/ppermute | solution.py:782
  8.7 7.1 %collective-permute-start.1 = (bf16[64,640]{1,0:T(8,128)(2,1)}, bf16[64,640]{1,0:T(8,128)(2,1)S(1)}, u32[]{:S(2)}, u32[]{:S(2)}) collective-permute-start(bf16[64,640]{1,0:T(8,128)(2,1)} %prepare_attention.1), channel_id=1, source_target_pairs={{0,4},{1,5},{2,6},{3,7},{4,0},{5,1},{6,2},{7,3},{8,12},{9,13},{10,... | collective-permute-start | bytes 245768 | tf_op jit(solution)/shard_map/ppermute | solution.py:782
  8.7 7.1 %collective-permute-start = (bf16[64,640]{1,0:T(8,128)(2,1)}, bf16[64,640]{1,0:T(8,128)(2,1)S(1)}, u32[]{:S(2)}, u32[]{:S(2)}) collective-permute-start(bf16[64,640]{1,0:T(8,128)(2,1)} %prepare_attention.1), channel_id=1, source_target_pairs={{0,2},{1,3},{2,0},{3,1},{4,6},{5,7},{6,4},{7,5},{8,10},{9,11},{10,... | collective-permute-start | bytes 245768 | tf_op jit(solution)/shard_map/ppermute | solution.py:782
  16.8 15.5 %collective-permute-start.4 = (bf16[4,64,640]{2,1,0:T(8,128)(2,1)S(1)}, bf16[4,64,640]{2,1,0:T(8,128)(2,1)S(1)}, u32[]{:S(2)}, u32[]{:S(2)}) collective-permute-start(bf16[4,64,640]{2,1,0:T(8,128)(2,1)S(1)} %pad_maximum_fusion.2.refs_0_), channel_id=1, source_target_pairs={{0,8},{8,0},{16,24},{24,16},{1,9},{9,1},{17,25},{25,17},{2,10},{10... | collective-permute-start | bytes 983048 | tf_op jit(solution)/shard_map/ppermute | solution.py:785
  16.8 15.4 %collective-permute-start.3 = (bf16[4,64,640]{2,1,0:T(8,128)(2,1)S(1)}, bf16[4,64,640]{2,1,0:T(8,128)(2,1)S(1)}, u32[]{:S(2)}, u32[]{:S(2)}) collective-permute-start(bf16[4,64,640]{2,1,0:T(8,128)(2,1)S(1)} %pad_maximum_fusion.2.refs_0_), channel_id=1, source_target_pairs={{0,1},{1,0},{2,3},{3,2},{4,5},{5,4},{6,7},{7,6},{8,9},{9,8},{10,11... | collective-permute-start | bytes 983048 | tf_op jit(solution)/shard_map/ppermute | solution.py:782
  18.4 9.4 %collective-permute-start.7 = (bf16[240,256]{1,0:T(8,128)(2,1)}, bf16[240,256]{1,0:T(8,128)(2,1)S(1)}, u32[]{:S(2)}, u32[]{:S(2)}) collective-permute-start(bf16[240,256]{1,0:T(8,128)(2,1)} %get-tuple-element.139), channel_id=1, source_target_pairs={{0,6},{1,7},{2,4},{3,5},{4,2},{5,3},{6,0},{7,1},{8,14},{9,15},{10,... | collective-permute-start | bytes 368648 | tf_op jit(solution)/shard_map/ppermute | solution.py:782
  21.0 11.2 %collective-permute-start.6 = (bf16[240,256]{1,0:T(8,128)(2,1)}, bf16[240,256]{1,0:T(8,128)(2,1)S(1)}, u32[]{:S(2)}, u32[]{:S(2)}) collective-permute-start(bf16[240,256]{1,0:T(8,128)(2,1)} %get-tuple-element.139), channel_id=1, source_target_pairs={{0,4},{1,5},{2,6},{3,7},{4,0},{5,1},{6,2},{7,3},{8,12},{9,13},{10,... | collective-permute-start | bytes 368648 | tf_op jit(solution)/shard_map/ppermute | solution.py:782
  21.0 11.2 %collective-permute-start.5 = (bf16[240,256]{1,0:T(8,128)(2,1)}, bf16[240,256]{1,0:T(8,128)(2,1)S(1)}, u32[]{:S(2)}, u32[]{:S(2)}) collective-permute-start(bf16[240,256]{1,0:T(8,128)(2,1)} %get-tuple-element.139), channel_id=1, source_target_pairs={{0,2},{1,3},{2,0},{3,1},{4,6},{5,7},{6,4},{7,5},{8,10},{9,11},{10,... | collective-permute-start | bytes 368648 | tf_op jit(solution)/shard_map/ppermute | solution.py:782
  32.3 9.7 %collective-permute-start.13 = (bf16[192,256]{1,0:T(8,128)(2,1)S(1)}, bf16[192,256]{1,0:T(8,128)(2,1)S(1)}, u32[]{:S(2)}, u32[]{:S(2)}) collective-permute-start(bf16[192,256]{1,0:T(8,128)(2,1)S(1)} %copy-done.1), channel_id=1, source_target_pairs={{0,6},{1,7},{2,4},{3,5},{4,2},{5,3},{6,0},{7,1},{8,14},{9,15},{10,... | collective-permute-start | bytes 294920 | tf_op jit(solution)/shard_map/ppermute | solution.py:782
  33.9 9.6 %collective-permute-start.12 = (bf16[192,256]{1,0:T(8,128)(2,1)S(1)}, bf16[192,256]{1,0:T(8,128)(2,1)S(1)}, u32[]{:S(2)}, u32[]{:S(2)}) collective-permute-start(bf16[192,256]{1,0:T(8,128)(2,1)S(1)} %copy-done.1), channel_id=1, source_target_pairs={{0,4},{1,5},{2,6},{3,7},{4,0},{5,1},{6,2},{7,3},{8,12},{9,13},{10,... | collective-permute-start | bytes 294920 | tf_op jit(solution)/shard_map/ppermute | solution.py:782
  33.9 9.6 %collective-permute-start.11 = (bf16[192,256]{1,0:T(8,128)(2,1)S(1)}, bf16[192,256]{1,0:T(8,128)(2,1)S(1)}, u32[]{:S(2)}, u32[]{:S(2)}) collective-permute-start(bf16[192,256]{1,0:T(8,128)(2,1)S(1)} %copy-done.1), channel_id=1, source_target_pairs={{0,2},{1,3},{2,0},{3,1},{4,6},{5,7},{6,4},{7,5},{8,10},{9,11},{10,... | collective-permute-start | bytes 294920 | tf_op jit(solution)/shard_map/ppermute | solution.py:782
  36.9 6.7 %collective-permute-start.10 = (bf16[4,240,256]{2,1,0:T(8,128)(2,1)S(1)}, bf16[4,240,256]{2,1,0:T(8,128)(2,1)S(1)}, u32[]{:S(2)}, u32[]{:S(2)}) collective-permute-start(bf16[4,240,256]{2,1,0:T(8,128)(2,1)S(1)} %pad_maximum_fusion.refs_0_), channel_id=1, source_target_pairs={{0,8},{8,0},{16,24},{24,16},{1,9},{9,1},{17,25},{25,17},{2,10},{10... | collective-permute-start | bytes 1474568 | tf_op jit(solution)/shard_map/ppermute | solution.py:785
  36.9 13.6 %collective-permute-start.9 = (bf16[4,240,256]{2,1,0:T(8,128)(2,1)S(1)}, bf16[4,240,256]{2,1,0:T(8,128)(2,1)S(1)}, u32[]{:S(2)}, u32[]{:S(2)}) collective-permute-start(bf16[4,240,256]{2,1,0:T(8,128)(2,1)S(1)} %pad_maximum_fusion.refs_0_), channel_id=1, source_target_pairs={{0,1},{1,0},{2,3},{3,2},{4,5},{5,4},{6,7},{7,6},{8,9},{9,8},{10,11... | collective-permute-start | bytes 1474568 | tf_op jit(solution)/shard_map/ppermute | solution.py:782
  52.4 8.0 %collective-permute-start.16 = (bf16[4,192,256]{2,1,0:T(8,128)(2,1)S(1)}, bf16[4,192,256]{2,1,0:T(8,128)(2,1)S(1)}, u32[]{:S(2)}, u32[]{:S(2)}) collective-permute-start(bf16[4,192,256]{2,1,0:T(8,128)(2,1)S(1)} %pad_maximum_fusion.1.refs_0_), channel_id=1, source_target_pairs={{0,8},{8,0},{16,24},{24,16},{1,9},{9,1},{17,25},{25,17},{2,10},{10... | collective-permute-start | bytes 1179656 | tf_op jit(solution)/shard_map/ppermute | solution.py:785
  52.6 11.4 %collective-permute-start.15 = (bf16[4,192,256]{2,1,0:T(8,128)(2,1)S(1)}, bf16[4,192,256]{2,1,0:T(8,128)(2,1)S(1)}, u32[]{:S(2)}, u32[]{:S(2)}) collective-permute-start(bf16[4,192,256]{2,1,0:T(8,128)(2,1)S(1)} %pad_maximum_fusion.1.refs_0_), channel_id=1, source_target_pairs={{0,1},{1,0},{2,3},{3,2},{4,5},{5,4},{6,7},{7,6},{8,9},{9,8},{10,11... | collective-permute-start | bytes 1179656 | tf_op jit(solution)/shard_map/ppermute | solution.py:782
  64.0 9.4 %collective-permute-start.18 = (bf16[2,4,192,256]{3,2,1,0:T(8,128)(2,1)S(1)}, bf16[2,4,192,256]{3,2,1,0:T(8,128)(2,1)S(1)}, u32[]{:S(2)}, u32[]{:S(2)}) collective-permute-start(bf16[2,4,192,256]{3,2,1,0:T(8,128)(2,1)S(1)} %get-tuple-element.180), channel_id=1, source_target_pairs={{0,8},{8,0},{16,24},{24,16},{1,9},{9,1},{17,25},{25,17},{2,10},{10... | collective-permute-start | bytes 2359304 | tf_op jit(solution)/shard_map/ppermute | solution.py:785
  73.5 19.6 %collective-permute-start.19 = (bf16[4,192,256]{2,1,0:T(8,128)(2,1)S(1)}, bf16[4,192,256]{2,1,0:T(8,128)(2,1)S(1)}, u32[]{:S(2)}, u32[]{:S(2)}) collective-permute-start(bf16[4,192,256]{2,1,0:T(8,128)(2,1)S(1)} %fusion.1), channel_id=1, source_target_pairs={{0,1},{1,0},{2,3},{3,2},{4,5},{5,4},{6,7},{7,6},{8,9},{9,8},{10,11... | collective-permute-start | bytes 1179656 | tf_op jit(solution)/shard_map/ppermute | solution.py:782
  93.1 6.2 %collective-permute-start.20 = (bf16[2,4,240,256]{3,2,1,0:T(8,128)(2,1)S(1)}, bf16[2,4,240,256]{3,2,1,0:T(8,128)(2,1)S(1)}, u32[]{:S(2)}, u32[]{:S(2)}) collective-permute-start(bf16[2,4,240,256]{3,2,1,0:T(8,128)(2,1)S(1)} %get-tuple-element.196), channel_id=1, source_target_pairs={{0,8},{8,0},{16,24},{24,16},{1,9},{9,1},{17,25},{25,17},{2,10},{10... | collective-permute-start | bytes 2949128 | tf_op jit(solution)/shard_map/ppermute | solution.py:785
  93.3 13.0 %collective-permute-start.23 = (bf16[192,256]{1,0:T(8,128)(2,1)S(1)}, bf16[192,256]{1,0:T(8,128)(2,1)S(1)}, u32[]{:S(2)}, u32[]{:S(2)}) collective-permute-start(bf16[192,256]{1,0:T(8,128)(2,1)S(1)} %get-tuple-element.257), channel_id=1, source_target_pairs={{0,6},{1,7},{2,4},{3,5},{4,2},{5,3},{6,0},{7,1},{8,14},{9,15},{10,... | collective-permute-start | bytes 294920 | tf_op jit(solution)/shard_map/ppermute | solution.py:782
  94.6 12.1 %collective-permute-start.22 = (bf16[192,256]{1,0:T(8,128)(2,1)S(1)}, bf16[192,256]{1,0:T(8,128)(2,1)S(1)}, u32[]{:S(2)}, u32[]{:S(2)}) collective-permute-start(bf16[192,256]{1,0:T(8,128)(2,1)S(1)} %get-tuple-element.258), channel_id=1, source_target_pairs={{0,4},{1,5},{2,6},{3,7},{4,0},{5,1},{6,2},{7,3},{8,12},{9,13},{10,... | collective-permute-start | bytes 294920 | tf_op jit(solution)/shard_map/ppermute | solution.py:782
  99.3 7.4 %collective-permute-start.21 = (bf16[192,256]{1,0:T(8,128)(2,1)S(1)}, bf16[192,256]{1,0:T(8,128)(2,1)S(1)}, u32[]{:S(2)}, u32[]{:S(2)}) collective-permute-start(bf16[192,256]{1,0:T(8,128)(2,1)S(1)} %get-tuple-element.259), channel_id=1, source_target_pairs={{0,2},{1,3},{2,0},{3,1},{4,6},{5,7},{6,4},{7,5},{8,10},{9,11},{10,... | collective-permute-start | bytes 294920 | tf_op jit(solution)/shard_map/ppermute | solution.py:782
  99.5 13.1 %collective-permute-start.24 = (bf16[4,240,256]{2,1,0:T(8,128)(2,1)S(1)}, bf16[4,240,256]{2,1,0:T(8,128)(2,1)S(1)}, u32[]{:S(2)}, u32[]{:S(2)}) collective-permute-start(bf16[4,240,256]{2,1,0:T(8,128)(2,1)S(1)} %fusion), channel_id=1, source_target_pairs={{0,1},{1,0},{2,3},{3,2},{4,5},{5,4},{6,7},{7,6},{8,9},{9,8},{10,11... | collective-permute-start | bytes 1474568 | tf_op jit(solution)/shard_map/ppermute | solution.py:782
  112.6 5.2 %collective-permute-start.25 = (bf16[2,4,64,640]{3,2,1,0:T(8,128)(2,1)S(1)}, bf16[2,4,64,640]{3,2,1,0:T(8,128)(2,1)S(1)}, u32[]{:S(2)}, u32[]{:S(2)}) collective-permute-start(bf16[2,4,64,640]{3,2,1,0:T(8,128)(2,1)S(1)} %get-tuple-element.205), channel_id=1, source_target_pairs={{0,8},{8,0},{16,24},{24,16},{1,9},{9,1},{17,25},{25,17},{2,10},{10... | collective-permute-start | bytes 1966088 | tf_op jit(solution)/shard_map/ppermute | solution.py:785
  112.8 17.2 %collective-permute-start.29 = (bf16[240,256]{1,0:T(8,128)(2,1)S(1)}, bf16[240,256]{1,0:T(8,128)(2,1)S(1)}, u32[]{:S(2)}, u32[]{:S(2)}) collective-permute-start(bf16[240,256]{1,0:T(8,128)(2,1)S(1)} %get-tuple-element.254), channel_id=1, source_target_pairs={{0,6},{1,7},{2,4},{3,5},{4,2},{5,3},{6,0},{7,1},{8,14},{9,15},{10,... | collective-permute-start | bytes 368648 | tf_op jit(solution)/shard_map/ppermute | solution.py:782
  114.9 15.1 %collective-permute-start.28 = (bf16[240,256]{1,0:T(8,128)(2,1)S(1)}, bf16[240,256]{1,0:T(8,128)(2,1)S(1)}, u32[]{:S(2)}, u32[]{:S(2)}) collective-permute-start(bf16[240,256]{1,0:T(8,128)(2,1)S(1)} %get-tuple-element.255), channel_id=1, source_target_pairs={{0,4},{1,5},{2,6},{3,7},{4,0},{5,1},{6,2},{7,3},{8,12},{9,13},{10,... | collective-permute-start | bytes 368648 | tf_op jit(solution)/shard_map/ppermute | solution.py:782
  117.7 12.3 %collective-permute-start.27 = (bf16[240,256]{1,0:T(8,128)(2,1)S(1)}, bf16[240,256]{1,0:T(8,128)(2,1)S(1)}, u32[]{:S(2)}, u32[]{:S(2)}) collective-permute-start(bf16[240,256]{1,0:T(8,128)(2,1)S(1)} %get-tuple-element.256), channel_id=1, source_target_pairs={{0,2},{1,3},{2,0},{3,1},{4,6},{5,7},{6,4},{7,5},{8,10},{9,11},{10,... | collective-permute-start | bytes 368648 | tf_op jit(solution)/shard_map/ppermute | solution.py:782
  117.9 27.4 %collective-permute-start.33 = (bf16[192,256]{1,0:T(8,128)(2,1)S(1)}, bf16[192,256]{1,0:T(8,128)(2,1)S(1)}, u32[]{:S(2)}, u32[]{:S(2)}) collective-permute-start(bf16[192,256]{1,0:T(8,128)(2,1)S(1)} %fusion.10), channel_id=1, source_target_pairs={{0,16},{8,24},{16,0},{24,8},{1,17},{9,25},{17,1},{25,9},{2,18},{10... | collective-permute-start | bytes 294920 | tf_op jit(solution)/shard_map/ppermute | solution.py:785
  123.3 9.0 %collective-permute-start.26 = (bf16[4,64,640]{2,1,0:T(8,128)(2,1)S(1)}, bf16[4,64,640]{2,1,0:T(8,128)(2,1)S(1)}, u32[]{:S(2)}, u32[]{:S(2)}) collective-permute-start(bf16[4,64,640]{2,1,0:T(8,128)(2,1)S(1)} %fusion.2), channel_id=1, source_target_pairs={{0,1},{1,0},{2,3},{3,2},{4,5},{5,4},{6,7},{7,6},{8,9},{9,8},{10,11... | collective-permute-start | bytes 983048 | tf_op jit(solution)/shard_map/ppermute | solution.py:782
  132.4 8.1 %collective-permute-start.30 = (bf16[64,640]{1,0:T(8,128)(2,1)S(1)}, bf16[64,640]{1,0:T(8,128)(2,1)S(1)}, u32[]{:S(2)}, u32[]{:S(2)}) collective-permute-start(bf16[64,640]{1,0:T(8,128)(2,1)S(1)} %get-tuple-element.217), channel_id=1, source_target_pairs={{0,2},{1,3},{2,0},{3,1},{4,6},{5,7},{6,4},{7,5},{8,10},{9,11},{10,... | collective-permute-start | bytes 245768 | tf_op jit(solution)/shard_map/ppermute | solution.py:782
  132.8 8.1 %collective-permute-start.31 = (bf16[64,640]{1,0:T(8,128)(2,1)S(1)}, bf16[64,640]{1,0:T(8,128)(2,1)S(1)}, u32[]{:S(2)}, u32[]{:S(2)}) collective-permute-start(bf16[64,640]{1,0:T(8,128)(2,1)S(1)} %get-tuple-element.218), channel_id=1, source_target_pairs={{0,4},{1,5},{2,6},{3,7},{4,0},{5,1},{6,2},{7,3},{8,12},{9,13},{10,... | collective-permute-start | bytes 245768 | tf_op jit(solution)/shard_map/ppermute | solution.py:782
  133.4 7.5 %collective-permute-start.32 = (bf16[64,640]{1,0:T(8,128)(2,1)S(1)}, bf16[64,640]{1,0:T(8,128)(2,1)S(1)}, u32[]{:S(2)}, u32[]{:S(2)}) collective-permute-start(bf16[64,640]{1,0:T(8,128)(2,1)S(1)} %get-tuple-element.219), channel_id=1, source_target_pairs={{0,6},{1,7},{2,4},{3,5},{4,2},{5,3},{6,0},{7,1},{8,14},{9,15},{10,... | collective-permute-start | bytes 245768 | tf_op jit(solution)/shard_map/ppermute | solution.py:782
  136.9 8.3 %collective-permute-start.34 = (bf16[240,256]{1,0:T(8,128)(2,1)S(1)}, bf16[240,256]{1,0:T(8,128)(2,1)S(1)}, u32[]{:S(2)}, u32[]{:S(2)}) collective-permute-start(bf16[240,256]{1,0:T(8,128)(2,1)S(1)} %fusion.6), channel_id=1, source_target_pairs={{0,16},{8,24},{16,0},{24,8},{1,17},{9,25},{17,1},{25,9},{2,18},{10... | collective-permute-start | bytes 368648 | tf_op jit(solution)/shard_map/ppermute | solution.py:785
  (9 other events, 50.2 us)

commit v7 on v6

--- a/solution.py
+++ b/solution.py
@@ -69,6 +69,11 @@
     return jnp.where(lane_low((rows, PAIR)), both[:rows], both[rows:])
 
 
+def side_by_side(one, two):
+    zero = jnp.zeros_like(one)
+    return jnp.concatenate([jnp.concatenate([one, zero], axis=1), jnp.concatenate([zero, two], axis=1)], axis=0)
+
+
 def row_sums(values):
     rows, width = values.shape
     return jnp.sum(values.reshape(rows // 8, 8, width), axis=0)
@@ -100,8 +105,8 @@
     )
 
 
-def prepare_attention(n_f, place_ref, bias_ref, wq, wk, wv, ga, gf, a_ref):
-    core = place_ref[1]
+def prepare_attention(n_f, bias_ref, wq, wk, wv, ga, gf, a_ref):
+    core = lax.rem(lax.axis_index("rep"), 2)
     ds = wq.shape[0]
     joined = jnp.concatenate([wq[...], wk[...], wv[...]], axis=1)
     row = lax.broadcasted_iota(jnp.int32, (ds, PAIR), 0)
@@ -157,15 +162,15 @@
     return -(-rows // 16) * 16
 
 
-def call_prepare_attention(place, n_f, attn_gain, wq, wk, wv, rel_bias, ffn_gain):
+def call_prepare_attention(n_f, attn_gain, wq, wk, wv, rel_bias, ffn_gain):
     vm, sm = pl.BlockSpec(memory_space=pltpu.VMEM), pl.BlockSpec(memory_space=pltpu.SMEM)
     return pl.pallas_call(
         functools.partial(prepare_attention, n_f),
         out_shape=sds((wq.shape[0], CUT), bf16),
-        in_specs=[sm, sm] + [vm] * 5,
+        in_specs=[sm] + [vm] * 5,
         out_specs=vm,
         name="prepare_attention",
-    )(place, rel_bias, wq, wk, wv, attn_gain.reshape(1, -1), ffn_gain.reshape(1, -1))
+    )(rel_bias, wq, wk, wv, attn_gain.reshape(1, -1), ffn_gain.reshape(1, -1))
 
 
 def call_prepare_ffn(place, n_f, wo, wg, wu, wd):
@@ -253,12 +258,13 @@
         x = group_rows(tok_ref, step, G * L)[...].astype(f32)
         normed = (x * inverse_rms(x) * gains_ref[0:1, :]).astype(bf16)
         qkv_ref[...] = nn(normed, w_ref[...]).astype(bf16)
-        for s in range(G):
-            rows = pl.ds(s * L, L)
+        for s in range(0, G, 2):
             for p in range(PAIRS):
-                q = qkv_ref[rows, pl.ds(p * PAIR, PAIR)]
-                k = qkv_ref[rows, pl.ds(INNER + p * PAIR, PAIR)]
-                st_ref[s, p] = nt(k, split_heads(q))
+                q, k = (
+                    [qkv_ref[pl.ds((s + i) * L, L), pl.ds(b * INNER + p * PAIR, PAIR)] for i in range(2)] for b in range(2)
+                )
+                st = nt(jnp.concatenate(k, axis=1), side_by_side(split_heads(q[0]), split_heads(q[1])))
+                st_ref[s, p], st_ref[s + 1, p] = st[:, :PAIR], st[:, PAIR:]
         for s in range(G):
             for p in range(PAIRS):
                 st = st_ref[s, p] + table_ref[p]
@@ -397,7 +403,15 @@
     n_f = 2 * n_z
     place = Place(place_ref, n_z)
     first, begins, ends = stage == 0, stage < 2, stage != 1
-    if begins:
+    if first:
+        (near, own_far, far, near_c, own_far_c, far_c), refs = refs[:6], refs[6:]
+        here, there = ([near.at[k] for k in range(n_z)] for near in (near, near_c))
+        here, there = (
+            side + [own] + [rest.at[k] for k in range(n_z - 1)]
+            for side, own, rest in ((here, own_far, far), (there, own_far_c, far_c))
+        )
+        pieces = [(f, *pair) for (_, _, f), pair in zip(place.shards(), zip(here, there))]
+    elif begins:
         pieces, refs = refs[:4], refs[4:]
         pieces = [(f, pieces[xx].at[k], pieces[2 + xx].at[k]) for xx, k, f in place.shards()]
     if stage == 0:
@@ -600,8 +614,8 @@
     @pl.when(step * G < count)
     def _():
         cols = [[pl.ds(b * INNER + p * PAIR, PAIR) for b in range(3)] for p in range(PAIRS)]
-        for p in range(PAIRS):
-            for s in range(G):
+        for s in range(G):
+            for p in range(PAIRS):
                 rows = pl.ds(s * L, L)
                 dm = split_heads(gm_ref[rows, pl.ds(p * PAIR, PAIR)])
                 dp_ref[s, p] = nt(dqkv[rows, cols[p][2]], dm)
@@ -615,8 +629,8 @@
                 total = total + ds
                 ds_ref[s, p] = ds.astype(bf16)
             ab[p] = total
-        for p in range(PAIRS):
-            for s in range(G):
+        for s in range(G):
+            for p in range(PAIRS):
                 rows = pl.ds(s * L, L)
                 low = ds_ref[s, p]
                 q, k = dqkv[rows, cols[p][0]], dqkv[rows, cols[p][1]]
@@ -817,27 +831,27 @@
         S, L, D = tokens.shape
         r, f = lax.axis_index("rep"), lax.axis_index("fsdp")
         place = in_hbm(jnp.stack([counts[0, 0], r % 2, f % 2, f // 2]).astype(jnp.int32))
-        pack_a = call_prepare_attention(place, n_f, attn_gain, wq, wk, wv, rel_bias, ffn_gain)
+        pack_a = call_prepare_attention(n_f, attn_gain, wq, wk, wv, rel_bias, ffn_gain)
         pack_0, pack_1 = call_prepare_ffn(place, n_f, wo, wg, wu, wd)
 
         z_0 = along_z(pack_0)
         z_a, pack_1 = together((along_z(pack_a), pack_1))
         near_a = jnp.stack(z_a)
-        far_a, near_ac = over_fsdp(near_a, 1), over_rep(near_a, 1)
+        far_a, own_far_0 = over_fsdp(near_a, 1), over_fsdp(pack_0, 1)
         tokens, cotangent, done = call_keep_close(place, tokens, cotangent)
-        done, far_a, near_ac, z_0, pack_1 = together((done, far_a, near_ac, z_0, pack_1))
-        far_ac, near_0 = over_rep(far_a, 1), jnp.stack(z_0)
+        done, far_a, own_far_0, z_0, pack_1 = together((done, far_a, own_far_0, z_0, pack_1))
+        near_ac, far_ac, near_0 = over_rep(near_a, 1), over_rep(far_a, 1), jnp.stack(z_0)
         far_ac, near_0 = together((far_ac, near_0))
 
-        far_0, near_0c, z_1 = over_fsdp(near_0, 1), over_rep(near_0, 1), along_z(pack_1)
+        far_0, near_0c, z_1 = over_fsdp(near_0[1:], 1), over_rep(near_0, 1), along_z(pack_1)
         qkv, probs, mixed, w_all, gains = call_attention_forward(place, tokens, done, (near_a, far_a, near_ac, far_ac), S, L, D)
-        gains, far_0, near_0c, z_1 = together((gains, far_0, near_0c, z_1))
-        far_0c, near_1 = over_rep(far_0, 1), jnp.stack(z_1)
+        gains, far_0, near_0c, own_far_0, z_1 = together((gains, far_0, near_0c, own_far_0, z_1))
+        own_far_0c, far_0c, near_1 = over_rep(own_far_0, 1), over_rep(far_0, 1), jnp.stack(z_1)
         far_0c, near_1 = together((far_0c, near_1))
 
         far_1, near_1c = over_fsdp(near_1, 1), over_rep(near_1, 1)
         hidden, act_0, gpart, wd_0, wo_all, keep_0, send_0 = call_ffn_half(
-            0, place, n_z, (near_0, far_0, near_0c, far_0c, tokens, cotangent, mixed, gains), S, L, D
+            0, place, n_z, (near_0, own_far_0, far_0, near_0c, own_far_0c, far_0c, tokens, cotangent, mixed, gains), S, L, D
         )
         wo_all, keep_0, send_0, far_1, near_1c = together((wo_all, keep_0, send_0, far_1, near_1c))
 

time: 150 us -> 147 us (0.980)
  Pallas kernels: 47.8 us -> 69.8 us
  waiting for transfers between devices: 42.6 us -> 23.5 us
  starting transfers between devices: 54.4 us -> 48.9 us
    ppermute x24 -> x25, waiting for transfers between devices: 38.2 us -> 19.9 us  [over_fsdp(): return lax.ppermute(value, 'fsdp', [(i, i ^ distance) for i in range(n_f)])]
    pallas_call x3, Pallas kernels: 16.1 us -> 28.5 us  [call_ffn_half(): pl.pallas_call(functools.partial(ffn_half, G, L, n_z, stage, shift), out_...]
    ppermute x24 -> x25, starting transfers between devices: 45.1 us -> 33 us  [over_fsdp(): return lax.ppermute(value, 'fsdp', [(i, i ^ distance) for i in range(n_f)])]
    ppermute x15 -> x16, starting transfers between devices: 9.35 us -> 16 us  [over_rep(): return lax.ppermute(value, 'rep', [(i, i ^ distance) for i in range(n_r)])]
    pallas_call x1, Pallas kernels: 5.98 us -> 9.7 us  [call_attention_backward(): pl.pallas_call(functools.partial(attention_backward, G, L, n_z), out_shap...]
    pallas_call x1, Pallas kernels: 4.52 us -> 7.77 us  [call_attention_forward(): pl.pallas_call(functools.partial(attention_forward, G, L, n_z), out_shape...]
    ppermute x15 -> x16, waiting for transfers between devices: 4.44 us -> 3.68 us  [over_rep(): return lax.ppermute(value, 'rep', [(i, i ^ distance) for i in range(n_r)])]
  transfers between devices with their start and end apart: 39 -> 41, of which waited for: 15 -> 9; matrix products, arithmetic and copies ran while one was open for 1% -> 1% of each run, Pallas kernels for 30% -> 45%
where the time goes in v7:
time: 147 us
  Pallas kernels  69.8 us (47%)
  starting transfers between devices  48.9 us (33%)
  waiting for transfers between devices  23.5 us (16%)
  other arithmetic  2.73 us (2%)
  between operations  1.63 us (1%)
    ppermute x25, starting transfers between devices, over_fsdp(): return lax.ppermute(value, 'fsdp', [(i, i ^ distance) for i in range(n_f)])  33 us
    pallas_call x3, Pallas kernels, call_ffn_half(): pl.pallas_call(functools.partial(ffn_half, G, L, n_z, stage, shift), out_...  28.5 us
    ppermute x25, waiting for transfers between devices, over_fsdp(): return lax.ppermute(value, 'fsdp', [(i, i ^ distance) for i in range(n_f)])  19.9 us
    ppermute x16, starting transfers between devices, over_rep(): return lax.ppermute(value, 'rep', [(i, i ^ distance) for i in range(n_r)])  16 us
    pallas_call x1, Pallas kernels, call_attention_backward(): pl.pallas_call(functools.partial(attention_backward, G, L, n_z), out_shap...  9.7 us
    pallas_call x1, Pallas kernels, call_attention_forward(): pl.pallas_call(functools.partial(attention_forward, G, L, n_z), out_shape...  7.77 us
    pallas_call x2, Pallas kernels, call_layer_result(): pl.pallas_call(functools.partial(layer_result, G, L, shift), out_shape=(p...  6.76 us
    pallas_call x1, Pallas kernels, call_token_gradient(): pl.pallas_call(functools.partial(token_gradient, G, L), out_shape=(pltpu....  6.48 us
  transfers between devices with their start and end apart: 41, of which 9 were waited for; matrix products, arithmetic and copies ran while one was open for 1% of the time, Pallas kernels for 45%

profile of v7, /device:TPU:0, one launch (start us, length us, event | category | flops | bytes accessed | tf_op | source)
XLA Modules:
  0.0 146.7 jit_solution(17675009794684930937)
XLA Ops:
  0.6 1.7 %prepare_attention.1 = bf16[64,640]{1,0:T(8,128)(2,1)} custom-call(f32[24]{0:T(128)} %bias_ref.1, f32[64,384]{1,0:T(8,128)} %wq.1, f32[64,384]{1,0:T(8,128)} %wk.1, f32[64,384]{1,0:T(8,128)} %wv.1, f32[1,64]{1,0:T(1,128)} %bitcast.94, f32[1,64]{1,0:T(1,128)} %bitcast.95), custom_call_target="tpu_custom_call" | custom-call | tf_op jit(solution)/shard_map/prepare_attention/pallas_call | solution.py:167
  2.4 5.0 %collective-permute-start.2 = (bf16[64,640]{1,0:T(8,128)(2,1)}, bf16[64,640]{1,0:T(8,128)(2,1)S(1)}, u32[]{:S(2)}, u32[]{:S(2)}) collective-permute-start(bf16[64,640]{1,0:T(8,128)(2,1)} %prepare_attention.1), channel_id=1, source_target_pairs={{0,6},{1,7},{2,4},{3,5},{4,2},{5,3},{6,0},{7,1},{8,14},{9,15},{10,... | collective-permute-start | bytes 245768 | tf_op jit(solution)/shard_map/ppermute | solution.py:796
  9.3 2.0 %prepare_ffn.1 = (bf16[240,256]{1,0:T(8,128)(2,1)}, bf16[192,256]{1,0:T(8,128)(2,1)}) custom-call(s32[4]{0:T(128)} %pad_add_fusion.place_ref, f32[48,512]{1,0:T(8,128)} %wo.1, f32[64,1024]{1,0:T(8,128)} %wg.1, f32[64,1024]{1,0:T(8,128)} %wu.1, f32[128,512]{1,0:T(8,128)} %wd.1), custom_call_target="tpu_custom_call" | custom-call | tf_op jit(solution)/shard_map/prepare_ffn/pallas_call | solution.py:179
  11.3 3.2 %collective-permute-done.1 = bf16[64,640]{1,0:T(8,128)(2,1)S(1)} collective-permute-done((bf16[64,640]{1,0:T(8,128)(2,1)}, bf16[64,640]{1,0:T(8,128)(2,1)S(1)}, u32[]{:S(2)}, u32[]{:S(2)}) %collective-permute-start.1) | collective-permute-done | bytes 81952 | tf_op jit(solution)/shard_map/ppermute | solution.py:796
  15.4 1.6 %collective-permute-start.3 = (bf16[4,64,640]{2,1,0:T(8,128)(2,1)S(1)}, bf16[4,64,640]{2,1,0:T(8,128)(2,1)S(1)}, u32[]{:S(2)}, u32[]{:S(2)}) collective-permute-start(bf16[4,64,640]{2,1,0:T(8,128)(2,1)S(1)} %pad_maximum_fusion.2.refs_0_), channel_id=1, source_target_pairs={{0,1},{1,0},{2,3},{3,2},{4,5},{5,4},{6,7},{7,6},{8,9},{9,8},{10,11... | collective-permute-start | bytes 983048 | tf_op jit(solution)/shard_map/ppermute | solution.py:796
  17.0 2.6 %collective-permute-start.7 = (bf16[240,256]{1,0:T(8,128)(2,1)}, bf16[240,256]{1,0:T(8,128)(2,1)S(1)}, u32[]{:S(2)}, u32[]{:S(2)}) collective-permute-start(bf16[240,256]{1,0:T(8,128)(2,1)} %get-tuple-element.140), channel_id=1, source_target_pairs={{0,6},{1,7},{2,4},{3,5},{4,2},{5,3},{6,0},{7,1},{8,14},{9,15},{10,... | collective-permute-start | bytes 368648 | tf_op jit(solution)/shard_map/ppermute | solution.py:796
  19.6 1.8 %collective-permute-start.5 = (bf16[240,256]{1,0:T(8,128)(2,1)}, bf16[240,256]{1,0:T(8,128)(2,1)S(1)}, u32[]{:S(2)}, u32[]{:S(2)}) collective-permute-start(bf16[240,256]{1,0:T(8,128)(2,1)} %get-tuple-element.140), channel_id=1, source_target_pairs={{0,2},{1,3},{2,0},{3,1},{4,6},{5,7},{6,4},{7,5},{8,10},{9,11},{10,... | collective-permute-start | bytes 368648 | tf_op jit(solution)/shard_map/ppermute | solution.py:796
  21.9 5.0 %keep_close.1 = (bf16[3072,512]{1,0:T(8,128)(2,1)S(1)}, bf16[3072,512]{1,0:T(8,128)(2,1)S(1)}, f32[8,128]{1,0:T(8,128)S(1)}) custom-call(s32[4]{0:T(128)} %pad_add_fusion.place_ref, bf16[48,64,512]{2,1,0:T(8,128)(2,1)} %tok_ref.1, bf16[48,64,512]{2,1,0:T(8,128)(2,1)} %ct_ref.1), custom_call_target="tpu_custom_call" | custom-call | flops 6144 | bytes 12582912 | tf_op jit(solution)/shard_map/keep_close/pallas_call | solution.py:201
  27.0 3.0 %collective-permute-done.6 = bf16[240,256]{1,0:T(8,128)(2,1)S(1)} collective-permute-done((bf16[240,256]{1,0:T(8,128)(2,1)}, bf16[240,256]{1,0:T(8,128)(2,1)S(1)}, u32[]{:S(2)}, u32[]{:S(2)}) %collective-permute-start.6) | collective-permute-done | bytes 122912 | tf_op jit(solution)/shard_map/ppermute | solution.py:796
  30.6 1.6 %collective-permute-start.14 = (bf16[192,256]{1,0:T(8,128)(2,1)S(1)}, bf16[192,256]{1,0:T(8,128)(2,1)S(1)}, u32[]{:S(2)}, u32[]{:S(2)}) collective-permute-start(bf16[192,256]{1,0:T(8,128)(2,1)S(1)} %copy-done.1), channel_id=1, source_target_pairs={{0,6},{1,7},{2,4},{3,5},{4,2},{5,3},{6,0},{7,1},{8,14},{9,15},{10,... | collective-permute-start | bytes 294920 | tf_op jit(solution)/shard_map/ppermute | solution.py:796
  32.2 2.8 %collective-permute-start.12 = (bf16[192,256]{1,0:T(8,128)(2,1)S(1)}, bf16[192,256]{1,0:T(8,128)(2,1)S(1)}, u32[]{:S(2)}, u32[]{:S(2)}) collective-permute-start(bf16[192,256]{1,0:T(8,128)(2,1)S(1)} %copy-done.1), channel_id=1, source_target_pairs={{0,2},{1,3},{2,0},{3,1},{4,6},{5,7},{6,4},{7,5},{8,10},{9,11},{10,... | collective-permute-start | bytes 294920 | tf_op jit(solution)/shard_map/ppermute | solution.py:796
  35.6 7.8 %attention_forward.1 = (bf16[3072,1152]{1,0:T(8,128)(2,1)S(1)}, bf16[48,3,64,128]{3,2,1,0:T(8,128)(2,1)S(1)}, bf16[3072,384]{1,0:T(8,128)(2,1)S(1)}, bf16[512,1152]{1,0:T(8,128)(2,1)S(1)}, f32[8,512]{1,0:T(8,128)S(1)}) custom-call(s32[4]{0:T(128)} %pad_add_fusion.place_ref, bf16[3072,512]{1,0:T(8,128)(2,1)S(1)} %get-tuple-element.145.tok_ref.refs_6_, ...), custom_call_target="tpu_custom_call" | custom-call | flops 14495514624 | bytes 15360000 | tf_op jit(solution)/shard_map/attention_forward/pallas_call | solution.py:314
  43.4 2.7 %collective-permute-done.10.refs_2_ = bf16[3,240,256]{2,1,0:T(8,128)(2,1)S(1)} collective-permute-done((bf16[3,240,256]{2,1,0:T(8,128)(2,1)S(1)}, bf16[3,240,256]{2,1,0:T(8,128)(2,1)S(1)}, u32[]{:S(2)}, u32[]{:S(2)}) %collective-permute-start.10) | collective-permute-done | bytes 368672 | tf_op jit(solution)/shard_map/ppermute | solution.py:796
  48.7 13.2 %ffn_first.1 = (bf16[3072,512]{1,0:T(8,128)(2,1)S(1)}, bf16[3072,512]{1,0:T(8,128)(2,1)S(1)}, bf16[3072,512]{1,0:T(8,128)(2,1)S(1)}, bf16[512,512]{1,0:T(8,128)(...) custom-call(s32[4]{0:T(128)} %pad_add_fusion.place_ref, ...), custom_call_target="tpu_custom_call" | custom-call | flops 14495514624 | bytes 27648000 | tf_op jit(solution)/shard_map/ffn_first/pallas_call | solution.py:537
  61.9 6.1 %collective-permute-start.19 = (bf16[4,192,256]{2,1,0:T(8,128)(2,1)S(1)}, bf16[4,192,256]{2,1,0:T(8,128)(2,1)S(1)}, u32[]{:S(2)}, u32[]{:S(2)}) collective-permute-start(bf16[4,192,256]{2,1,0:T(8,128)(2,1)S(1)} %collective-permute-done.17.refs_1_), channel_id=1, source_target_pairs={{0,8},{8,0},{16,24},{24,16},{1,9},{9,1},{17,25},{25,17},{2,10},{10... | collective-permute-start | bytes 1179656 | tf_op jit(solution)/shard_map/ppermute | solution.py:799
  68.1 1.3 collective-permute-done.19.refs_3_
  69.4 10.9 %ffn_second.1 = (bf16[3072,512]{1,0:T(8,128)(2,1)S(1)}, bf16[3072,384]{1,0:T(8,128)(2,1)S(1)}, bf16[3072,512]{1,0:T(8,128)(2,1)S(1)}, f32[512,1024]{1,0:T(8,128)...) custom-call(s32[4]{0:T(128)} %pad_add_fusion.place_ref, ...), custom_call_target="tpu_custom_call", output_to_operand_aliasing={{0}: (9, {}), {1}: (10, {})} | custom-call | flops 7247757312 | bytes 27648000 | tf_op jit(solution)/shard_map/ffn_second/pallas_call | solution.py:537
  80.5 4.4 %ffn_third.1 = (bf16[3072,512]{1,0:T(8,128)(2,1)S(1)}, bf16[3072,384]{1,0:T(8,128)(2,1)S(1)}, bf16[3072,512]{1,0:T(8,128)(2,1)S(1)}, f32[512,1024]{1,0:T(8,128)S...) custom-call(s32[4]{0:T(128)} %pad_add_fusion.place_ref, ...), custom_call_target="tpu_custom_call", output_to_operand_aliasing={{0}: (7, {}), {1}: (8, {}), {2}: (9, {}), {3}: (10, {}), {4... | custom-call | flops 7247757312 | bytes 27648000 | tf_op jit(solution)/shard_map/ffn_third/pallas_call | solution.py:537
  84.9 7.0 %collective-permute-done.21 = bf16[4,192,256]{2,1,0:T(8,128)(2,1)S(1)} collective-permute-done((bf16[4,192,256]{2,1,0:T(8,128)(2,1)S(1)}, bf16[4,192,256]{2,1,0:T(8,128)(2,1)S(1)}, u32[]{:S(2)}, u32[]{:S(2)}) %collective-permute-start.21) | collective-permute-done | bytes 393248 | tf_op jit(solution)/shard_map/ppermute | solution.py:796
  92.1 3.3 %collective-permute-start.25 = (bf16[192,256]{1,0:T(8,128)(2,1)S(1)}, bf16[192,256]{1,0:T(8,128)(2,1)S(1)}, u32[]{:S(2)}, u32[]{:S(2)}) collective-permute-start(bf16[192,256]{1,0:T(8,128)(2,1)S(1)} %get-tuple-element.259), channel_id=1, source_target_pairs={{0,6},{1,7},{2,4},{3,5},{4,2},{5,3},{6,0},{7,1},{8,14},{9,15},{10,... | collective-permute-start | bytes 294920 | tf_op jit(solution)/shard_map/ppermute | solution.py:796
  96.7 1.2 collective-permute-start.26
  97.9 9.7 %attention_backward.1 = (bf16[3072,1152]{1,0:T(8,128)(2,1)S(1)}, bf16[2,4,64,640]{3,2,1,0:T(8,128)(2,1)S(1)}, bf16[2,4,64,640]{3,2,1,0:T(8,128)(2,1)S(1)}) custom-call(s32[4]{0:T(128)} %pad_add_fusion.place_ref, bf16[3072,512]{1,0:T(8,128)(2,1)S(1)} %get-tuple-element.145.tok_ref.refs_6_, ...), custom_call_target="tpu_custom_call", output_to_operand_aliasing={{0}: (2, {})} | custom-call | flops 14495514624 | bytes 18432000 | tf_op jit(solution)/shard_map/attention_backward/pallas_call | solution.py:680
  107.6 1.9 %collective-permute-done.26 = bf16[4,240,256]{2,1,0:T(8,128)(2,1)S(1)} collective-permute-done((bf16[4,240,256]{2,1,0:T(8,128)(2,1)S(1)}, bf16[4,240,256]{2,1,0:T(8,128)(2,1)S(1)}, u32[]{:S(2)}, u32[]{:S(2)}) %collective-permute-start.26) | collective-permute-done | bytes 491552 | tf_op jit(solution)/shard_map/ppermute | solution.py:796
  110.9 4.6 %collective-permute-start.31 = (bf16[240,256]{1,0:T(8,128)(2,1)S(1)}, bf16[240,256]{1,0:T(8,128)(2,1)S(1)}, u32[]{:S(2)}, u32[]{:S(2)}) collective-permute-start(bf16[240,256]{1,0:T(8,128)(2,1)S(1)} %get-tuple-element.256), channel_id=1, source_target_pairs={{0,6},{1,7},{2,4},{3,5},{4,2},{5,3},{6,0},{7,1},{8,14},{9,15},{10,... | collective-permute-start | bytes 368648 | tf_op jit(solution)/shard_map/ppermute | solution.py:796
  116.4 3.9 %collective-permute-start.35 = (bf16[192,256]{1,0:T(8,128)(2,1)S(1)}, bf16[192,256]{1,0:T(8,128)(2,1)S(1)}, u32[]{:S(2)}, u32[]{:S(2)}) collective-permute-start(bf16[192,256]{1,0:T(8,128)(2,1)S(1)} %fusion.10), channel_id=1, source_target_pairs={{0,16},{8,24},{16,0},{24,8},{1,17},{9,25},{17,1},{25,9},{2,18},{10... | collective-permute-start | bytes 294920 | tf_op jit(solution)/shard_map/ppermute | solution.py:799
  120.8 6.5 %token_gradient.1 = (bf16[48,64,512]{2,1,0:T(8,128)(2,1)}, f32[8,512]{1,0:T(8,128)S(1)}) custom-call(s32[4]{0:T(128)} %pad_add_fusion.place_ref, bf16[3072,512]{1,0:T(8,128)(2,1)S(1)} %get-tuple-element.145.tok_ref.refs_6_, bf16[3072,1152]{1,0:T(8,128)(2,1)S(1)} %get-tuple-element.200.dqkv_ref, bf16[3072,512]{1,0:T(8,128)(2,1)S(1)} %get-tuple-element.201.gh_ref, ...), custom_call_target="tpu_custom_call" | custom-call | flops 7247757312 | bytes 15360000 | tf_op jit(solution)/shard_map/token_gradient/pallas_call | solution.py:730
  127.3 2.0 %collective-permute-done.28 = bf16[4,64,640]{2,1,0:T(8,128)(2,1)S(1)} collective-permute-done((bf16[4,64,640]{2,1,0:T(8,128)(2,1)S(1)}, bf16[4,64,640]{2,1,0:T(8,128)(2,1)S(1)}, u32[]{:S(2)}, u32[]{:S(2)}) %collective-permute-start.28) | collective-permute-done | bytes 327712 | tf_op jit(solution)/shard_map/ppermute | solution.py:796
  130.4 3.5 %collective-permute-start.34 = (bf16[64,640]{1,0:T(8,128)(2,1)S(1)}, bf16[64,640]{1,0:T(8,128)(2,1)S(1)}, u32[]{:S(2)}, u32[]{:S(2)}) collective-permute-start(bf16[64,640]{1,0:T(8,128)(2,1)S(1)} %get-tuple-element.221), channel_id=1, source_target_pairs={{0,6},{1,7},{2,4},{3,5},{4,2},{5,3},{6,0},{7,1},{8,14},{9,15},{10,... | collective-permute-start | bytes 245768 | tf_op jit(solution)/shard_map/ppermute | solution.py:796
  134.3 3.7 %layer_result.2 = (bf16[48,64,512]{2,1,0:T(8,128)(2,1)}, f32[8,512]{1,0:T(8,128)S(1)}) custom-call(s32[4]{0:T(128)} %pad_add_fusion.place_ref, bf16[3072,512]{1,0:T(8,128)(2,1)S(1)} %get-tuple-element.162.refs_4_.refs_0_.hid_ref, bf16[3072,512]{1,0:T(8,128)(2,1)S(1)} %get-tuple-element.163.act_0, bf16[3072,512]{1,0:T(8,128)(2,1)S(1)} %get-tuple-element.186.act_1, ...), custom_call_target="tpu_custom_call" | custom-call | flops 1610612736 | bytes 9216000 | tf_op jit(solution)/shard_map/layer_result/pallas_call | solution.py:581
  138.1 1.7 %collective-permute-start.37 = (bf16[64,640]{1,0:T(8,128)(2,1)S(1)}, bf16[64,640]{1,0:T(8,128)(2,1)S(1)}, u32[]{:S(2)}, u32[]{:S(2)}) collective-permute-start(bf16[64,640]{1,0:T(8,128)(2,1)S(1)} %fusion.14), channel_id=1, source_target_pairs={{0,16},{8,24},{16,0},{24,8},{1,17},{9,25},{17,1},{25,9},{2,18},{10... | collective-permute-start | bytes 245768 | tf_op jit(solution)/shard_map/ppermute | solution.py:799
  139.8 3.0 %layer_result.3 = (bf16[48,64,512]{2,1,0:T(8,128)(2,1)}, f32[8,512]{1,0:T(8,128)S(1)}) custom-call(s32[4]{0:T(128)} %pad_add_fusion.place_ref, bf16[3072,512]{1,0:T(8,128)(2,1)S(1)} %get-tuple-element.162.refs_4_.refs_0_.hid_ref, bf16[3072,512]{1,0:T(8,128)(2,1)S(1)} %get-tuple-element.163.act_0, ...), custom_call_target="tpu_custom_call", output_to_operand_aliasing={{0}: (7, {})} | custom-call | flops 1610612736 | bytes 9216000 | tf_op jit(solution)/shard_map/layer_result/pallas_call | solution.py:581
  144.9 1.8 %finish.1 = (f32[64,384]{1,0:T(8,128)}, f32[64,384]{1,0:T(8,128)}, f32[64,384]{1,0:T(8,128)}, f32[48,512]{1,0:T(8,128)}, f32[64,1024]{1,0:T(8,128)}, /*index=5*/...) custom-call(s32[4]{0:T(128)} %pad_add_fusion.place_ref, ...), custom_call_target="tpu_custom_call" | custom-call | tf_op jit(solution)/shard_map/finish/pallas_call | solution.py:781
  (86 shorter events, 14.6 us)
Async XLA Ops:
  2.4 8.9 %collective-permute-start.2 = (bf16[64,640]{1,0:T(8,128)(2,1)}, bf16[64,640]{1,0:T(8,128)(2,1)S(1)}, u32[]{:S(2)}, u32[]{:S(2)}) collective-permute-start(bf16[64,640]{1,0:T(8,128)(2,1)} %prepare_attention.1), channel_id=1, source_target_pairs={{0,6},{1,7},{2,4},{3,5},{4,2},{5,3},{6,0},{7,1},{8,14},{9,15},{10,... | collective-permute-start | bytes 245768 | tf_op jit(solution)/shard_map/ppermute | solution.py:796
  7.4 7.1 %collective-permute-start.1 = (bf16[64,640]{1,0:T(8,128)(2,1)}, bf16[64,640]{1,0:T(8,128)(2,1)S(1)}, u32[]{:S(2)}, u32[]{:S(2)}) collective-permute-start(bf16[64,640]{1,0:T(8,128)(2,1)} %prepare_attention.1), channel_id=1, source_target_pairs={{0,4},{1,5},{2,6},{3,7},{4,0},{5,1},{6,2},{7,3},{8,12},{9,13},{10,... | collective-permute-start | bytes 245768 | tf_op jit(solution)/shard_map/ppermute | solution.py:796
  7.4 7.1 %collective-permute-start = (bf16[64,640]{1,0:T(8,128)(2,1)}, bf16[64,640]{1,0:T(8,128)(2,1)S(1)}, u32[]{:S(2)}, u32[]{:S(2)}) collective-permute-start(bf16[64,640]{1,0:T(8,128)(2,1)} %prepare_attention.1), channel_id=1, source_target_pairs={{0,2},{1,3},{2,0},{3,1},{4,6},{5,7},{6,4},{7,5},{8,10},{9,11},{10,... | collective-permute-start | bytes 245768 | tf_op jit(solution)/shard_map/ppermute | solution.py:796
  15.4 14.5 %collective-permute-start.3 = (bf16[4,64,640]{2,1,0:T(8,128)(2,1)S(1)}, bf16[4,64,640]{2,1,0:T(8,128)(2,1)S(1)}, u32[]{:S(2)}, u32[]{:S(2)}) collective-permute-start(bf16[4,64,640]{2,1,0:T(8,128)(2,1)S(1)} %pad_maximum_fusion.2.refs_0_), channel_id=1, source_target_pairs={{0,1},{1,0},{2,3},{3,2},{4,5},{5,4},{6,7},{7,6},{8,9},{9,8},{10,11... | collective-permute-start | bytes 983048 | tf_op jit(solution)/shard_map/ppermute | solution.py:796
  17.0 9.9 %collective-permute-start.7 = (bf16[240,256]{1,0:T(8,128)(2,1)}, bf16[240,256]{1,0:T(8,128)(2,1)S(1)}, u32[]{:S(2)}, u32[]{:S(2)}) collective-permute-start(bf16[240,256]{1,0:T(8,128)(2,1)} %get-tuple-element.140), channel_id=1, source_target_pairs={{0,6},{1,7},{2,4},{3,5},{4,2},{5,3},{6,0},{7,1},{8,14},{9,15},{10,... | collective-permute-start | bytes 368648 | tf_op jit(solution)/shard_map/ppermute | solution.py:796
  19.6 10.4 %collective-permute-start.6 = (bf16[240,256]{1,0:T(8,128)(2,1)}, bf16[240,256]{1,0:T(8,128)(2,1)S(1)}, u32[]{:S(2)}, u32[]{:S(2)}) collective-permute-start(bf16[240,256]{1,0:T(8,128)(2,1)} %get-tuple-element.140), channel_id=1, source_target_pairs={{0,4},{1,5},{2,6},{3,7},{4,0},{5,1},{6,2},{7,3},{8,12},{9,13},{10,... | collective-permute-start | bytes 368648 | tf_op jit(solution)/shard_map/ppermute | solution.py:796
  19.6 10.4 %collective-permute-start.5 = (bf16[240,256]{1,0:T(8,128)(2,1)}, bf16[240,256]{1,0:T(8,128)(2,1)S(1)}, u32[]{:S(2)}, u32[]{:S(2)}) collective-permute-start(bf16[240,256]{1,0:T(8,128)(2,1)} %get-tuple-element.140), channel_id=1, source_target_pairs={{0,2},{1,3},{2,0},{3,1},{4,6},{5,7},{6,4},{7,5},{8,10},{9,11},{10,... | collective-permute-start | bytes 368648 | tf_op jit(solution)/shard_map/ppermute | solution.py:796
  21.4 8.6 %collective-permute-start.4 = (bf16[240,256]{1,0:T(8,128)(2,1)}, bf16[240,256]{1,0:T(8,128)(2,1)S(1)}, u32[]{:S(2)}, u32[]{:S(2)}) collective-permute-start(bf16[240,256]{1,0:T(8,128)(2,1)} %get-tuple-element.140), channel_id=1, source_target_pairs={{0,1},{1,0},{2,3},{3,2},{4,5},{5,4},{6,7},{7,6},{8,9},{9,8},{10,11... | collective-permute-start | bytes 368648 | tf_op jit(solution)/shard_map/ppermute | solution.py:796
  30.6 12.8 %collective-permute-start.14 = (bf16[192,256]{1,0:T(8,128)(2,1)S(1)}, bf16[192,256]{1,0:T(8,128)(2,1)S(1)}, u32[]{:S(2)}, u32[]{:S(2)}) collective-permute-start(bf16[192,256]{1,0:T(8,128)(2,1)S(1)} %copy-done.1), channel_id=1, source_target_pairs={{0,6},{1,7},{2,4},{3,5},{4,2},{5,3},{6,0},{7,1},{8,14},{9,15},{10,... | collective-permute-start | bytes 294920 | tf_op jit(solution)/shard_map/ppermute | solution.py:796
  32.2 11.2 %collective-permute-start.13 = (bf16[192,256]{1,0:T(8,128)(2,1)S(1)}, bf16[192,256]{1,0:T(8,128)(2,1)S(1)}, u32[]{:S(2)}, u32[]{:S(2)}) collective-permute-start(bf16[192,256]{1,0:T(8,128)(2,1)S(1)} %copy-done.1), channel_id=1, source_target_pairs={{0,4},{1,5},{2,6},{3,7},{4,0},{5,1},{6,2},{7,3},{8,12},{9,13},{10,... | collective-permute-start | bytes 294920 | tf_op jit(solution)/shard_map/ppermute | solution.py:796
  32.2 11.3 %collective-permute-start.12 = (bf16[192,256]{1,0:T(8,128)(2,1)S(1)}, bf16[192,256]{1,0:T(8,128)(2,1)S(1)}, u32[]{:S(2)}, u32[]{:S(2)}) collective-permute-start(bf16[192,256]{1,0:T(8,128)(2,1)S(1)} %copy-done.1), channel_id=1, source_target_pairs={{0,2},{1,3},{2,0},{3,1},{4,6},{5,7},{6,4},{7,5},{8,10},{9,11},{10,... | collective-permute-start | bytes 294920 | tf_op jit(solution)/shard_map/ppermute | solution.py:796
  35.1 11.1 %collective-permute-start.11 = (bf16[4,240,256]{2,1,0:T(8,128)(2,1)S(1)}, bf16[4,240,256]{2,1,0:T(8,128)(2,1)S(1)}, u32[]{:S(2)}, u32[]{:S(2)}) collective-permute-start(bf16[4,240,256]{2,1,0:T(8,128)(2,1)S(1)} %pad_maximum_fusion.refs_0_), channel_id=1, source_target_pairs={{0,8},{8,0},{16,24},{24,16},{1,9},{9,1},{17,25},{25,17},{2,10},{10... | collective-permute-start | bytes 1474568 | tf_op jit(solution)/shard_map/ppermute | solution.py:799
  35.2 11.0 %collective-permute-start.10 = (bf16[3,240,256]{2,1,0:T(8,128)(2,1)S(1)}, bf16[3,240,256]{2,1,0:T(8,128)(2,1)S(1)}, u32[]{:S(2)}, u32[]{:S(2)}) collective-permute-start(bf16[3,240,256]{2,1,0:T(8,128)(2,1)S(1)} %slice.84), channel_id=1, source_target_pairs={{0,1},{1,0},{2,3},{3,2},{4,5},{5,4},{6,7},{7,6},{8,9},{9,8},{10,11... | collective-permute-start | bytes 1105928 | tf_op jit(solution)/shard_map/ppermute | solution.py:796
  48.3 13.6 %collective-permute-start.18 = (bf16[4,192,256]{2,1,0:T(8,128)(2,1)S(1)}, bf16[4,192,256]{2,1,0:T(8,128)(2,1)S(1)}, u32[]{:S(2)}, u32[]{:S(2)}) collective-permute-start(bf16[4,192,256]{2,1,0:T(8,128)(2,1)S(1)} %pad_maximum_fusion.1.refs_0_), channel_id=1, source_target_pairs={{0,8},{8,0},{16,24},{24,16},{1,9},{9,1},{17,25},{25,17},{2,10},{10... | collective-permute-start | bytes 1179656 | tf_op jit(solution)/shard_map/ppermute | solution.py:799
  48.7 13.2 %collective-permute-start.17 = (bf16[4,192,256]{2,1,0:T(8,128)(2,1)S(1)}, bf16[4,192,256]{2,1,0:T(8,128)(2,1)S(1)}, u32[]{:S(2)}, u32[]{:S(2)}) collective-permute-start(bf16[4,192,256]{2,1,0:T(8,128)(2,1)S(1)} %pad_maximum_fusion.1.refs_0_), channel_id=1, source_target_pairs={{0,1},{1,0},{2,3},{3,2},{4,5},{5,4},{6,7},{7,6},{8,9},{9,8},{10,11... | collective-permute-start | bytes 1179656 | tf_op jit(solution)/shard_map/ppermute | solution.py:796
  61.9 7.5 %collective-permute-start.19 = (bf16[4,192,256]{2,1,0:T(8,128)(2,1)S(1)}, bf16[4,192,256]{2,1,0:T(8,128)(2,1)S(1)}, u32[]{:S(2)}, u32[]{:S(2)}) collective-permute-start(bf16[4,192,256]{2,1,0:T(8,128)(2,1)S(1)} %collective-permute-done.17.refs_1_), channel_id=1, source_target_pairs={{0,8},{8,0},{16,24},{24,16},{1,9},{9,1},{17,25},{25,17},{2,10},{10... | collective-permute-start | bytes 1179656 | tf_op jit(solution)/shard_map/ppermute | solution.py:799
  68.0 12.3 %collective-permute-start.20 = (bf16[2,4,192,256]{3,2,1,0:T(8,128)(2,1)S(1)}, bf16[2,4,192,256]{3,2,1,0:T(8,128)(2,1)S(1)}, u32[]{:S(2)}, u32[]{:S(2)}) collective-permute-start(bf16[2,4,192,256]{3,2,1,0:T(8,128)(2,1)S(1)} %get-tuple-element.182), channel_id=1, source_target_pairs={{0,8},{8,0},{16,24},{24,16},{1,9},{9,1},{17,25},{25,17},{2,10},{10... | collective-permute-start | bytes 2359304 | tf_op jit(solution)/shard_map/ppermute | solution.py:799
  80.4 11.5 %collective-permute-start.21 = (bf16[4,192,256]{2,1,0:T(8,128)(2,1)S(1)}, bf16[4,192,256]{2,1,0:T(8,128)(2,1)S(1)}, u32[]{:S(2)}, u32[]{:S(2)}) collective-permute-start(bf16[4,192,256]{2,1,0:T(8,128)(2,1)S(1)} %fusion.1), channel_id=1, source_target_pairs={{0,1},{1,0},{2,3},{3,2},{4,5},{5,4},{6,7},{7,6},{8,9},{9,8},{10,11... | collective-permute-start | bytes 1179656 | tf_op jit(solution)/shard_map/ppermute | solution.py:796
  92.1 15.5 %collective-permute-start.25 = (bf16[192,256]{1,0:T(8,128)(2,1)S(1)}, bf16[192,256]{1,0:T(8,128)(2,1)S(1)}, u32[]{:S(2)}, u32[]{:S(2)}) collective-permute-start(bf16[192,256]{1,0:T(8,128)(2,1)S(1)} %get-tuple-element.259), channel_id=1, source_target_pairs={{0,6},{1,7},{2,4},{3,5},{4,2},{5,3},{6,0},{7,1},{8,14},{9,15},{10,... | collective-permute-start | bytes 294920 | tf_op jit(solution)/shard_map/ppermute | solution.py:796
  95.4 12.3 %collective-permute-start.24 = (bf16[192,256]{1,0:T(8,128)(2,1)S(1)}, bf16[192,256]{1,0:T(8,128)(2,1)S(1)}, u32[]{:S(2)}, u32[]{:S(2)}) collective-permute-start(bf16[192,256]{1,0:T(8,128)(2,1)S(1)} %get-tuple-element.260), channel_id=1, source_target_pairs={{0,4},{1,5},{2,6},{3,7},{4,0},{5,1},{6,2},{7,3},{8,12},{9,13},{10,... | collective-permute-start | bytes 294920 | tf_op jit(solution)/shard_map/ppermute | solution.py:796
  95.4 12.3 %collective-permute-start.23 = (bf16[192,256]{1,0:T(8,128)(2,1)S(1)}, bf16[192,256]{1,0:T(8,128)(2,1)S(1)}, u32[]{:S(2)}, u32[]{:S(2)}) collective-permute-start(bf16[192,256]{1,0:T(8,128)(2,1)S(1)} %get-tuple-element.261), channel_id=1, source_target_pairs={{0,2},{1,3},{2,0},{3,1},{4,6},{5,7},{6,4},{7,5},{8,10},{9,11},{10,... | collective-permute-start | bytes 294920 | tf_op jit(solution)/shard_map/ppermute | solution.py:796
  96.7 12.9 %collective-permute-start.26 = (bf16[4,240,256]{2,1,0:T(8,128)(2,1)S(1)}, bf16[4,240,256]{2,1,0:T(8,128)(2,1)S(1)}, u32[]{:S(2)}, u32[]{:S(2)}) collective-permute-start(bf16[4,240,256]{2,1,0:T(8,128)(2,1)S(1)} %fusion), channel_id=1, source_target_pairs={{0,1},{1,0},{2,3},{3,2},{4,5},{5,4},{6,7},{7,6},{8,9},{9,8},{10,11... | collective-permute-start | bytes 1474568 | tf_op jit(solution)/shard_map/ppermute | solution.py:796
  109.5 6.7 %collective-permute-start.27 = (bf16[2,4,64,640]{3,2,1,0:T(8,128)(2,1)S(1)}, bf16[2,4,64,640]{3,2,1,0:T(8,128)(2,1)S(1)}, u32[]{:S(2)}, u32[]{:S(2)}) collective-permute-start(bf16[2,4,64,640]{3,2,1,0:T(8,128)(2,1)S(1)} %get-tuple-element.207), channel_id=1, source_target_pairs={{0,8},{8,0},{16,24},{24,16},{1,9},{9,1},{17,25},{25,17},{2,10},{10... | collective-permute-start | bytes 1966088 | tf_op jit(solution)/shard_map/ppermute | solution.py:799
  110.9 16.3 %collective-permute-start.31 = (bf16[240,256]{1,0:T(8,128)(2,1)S(1)}, bf16[240,256]{1,0:T(8,128)(2,1)S(1)}, u32[]{:S(2)}, u32[]{:S(2)}) collective-permute-start(bf16[240,256]{1,0:T(8,128)(2,1)S(1)} %get-tuple-element.256), channel_id=1, source_target_pairs={{0,6},{1,7},{2,4},{3,5},{4,2},{5,3},{6,0},{7,1},{8,14},{9,15},{10,... | collective-permute-start | bytes 368648 | tf_op jit(solution)/shard_map/ppermute | solution.py:796
  115.6 11.7 %collective-permute-start.30 = (bf16[240,256]{1,0:T(8,128)(2,1)S(1)}, bf16[240,256]{1,0:T(8,128)(2,1)S(1)}, u32[]{:S(2)}, u32[]{:S(2)}) collective-permute-start(bf16[240,256]{1,0:T(8,128)(2,1)S(1)} %get-tuple-element.257), channel_id=1, source_target_pairs={{0,4},{1,5},{2,6},{3,7},{4,0},{5,1},{6,2},{7,3},{8,12},{9,13},{10,... | collective-permute-start | bytes 368648 | tf_op jit(solution)/shard_map/ppermute | solution.py:796
  115.6 11.7 %collective-permute-start.29 = (bf16[240,256]{1,0:T(8,128)(2,1)S(1)}, bf16[240,256]{1,0:T(8,128)(2,1)S(1)}, u32[]{:S(2)}, u32[]{:S(2)}) collective-permute-start(bf16[240,256]{1,0:T(8,128)(2,1)S(1)} %get-tuple-element.258), channel_id=1, source_target_pairs={{0,2},{1,3},{2,0},{3,1},{4,6},{5,7},{6,4},{7,5},{8,10},{9,11},{10,... | collective-permute-start | bytes 368648 | tf_op jit(solution)/shard_map/ppermute | solution.py:796
  116.4 26.5 %collective-permute-start.35 = (bf16[192,256]{1,0:T(8,128)(2,1)S(1)}, bf16[192,256]{1,0:T(8,128)(2,1)S(1)}, u32[]{:S(2)}, u32[]{:S(2)}) collective-permute-start(bf16[192,256]{1,0:T(8,128)(2,1)S(1)} %fusion.10), channel_id=1, source_target_pairs={{0,16},{8,24},{16,0},{24,8},{1,17},{9,25},{17,1},{25,9},{2,18},{10... | collective-permute-start | bytes 294920 | tf_op jit(solution)/shard_map/ppermute | solution.py:799
  120.2 9.0 %collective-permute-start.28 = (bf16[4,64,640]{2,1,0:T(8,128)(2,1)S(1)}, bf16[4,64,640]{2,1,0:T(8,128)(2,1)S(1)}, u32[]{:S(2)}, u32[]{:S(2)}) collective-permute-start(bf16[4,64,640]{2,1,0:T(8,128)(2,1)S(1)} %fusion.2), channel_id=1, source_target_pairs={{0,1},{1,0},{2,3},{3,2},{4,5},{5,4},{6,7},{7,6},{8,9},{9,8},{10,11... | collective-permute-start | bytes 983048 | tf_op jit(solution)/shard_map/ppermute | solution.py:796
  129.4 8.7 %collective-permute-start.32 = (bf16[64,640]{1,0:T(8,128)(2,1)S(1)}, bf16[64,640]{1,0:T(8,128)(2,1)S(1)}, u32[]{:S(2)}, u32[]{:S(2)}) collective-permute-start(bf16[64,640]{1,0:T(8,128)(2,1)S(1)} %get-tuple-element.219), channel_id=1, source_target_pairs={{0,2},{1,3},{2,0},{3,1},{4,6},{5,7},{6,4},{7,5},{8,10},{9,11},{10,... | collective-permute-start | bytes 245768 | tf_op jit(solution)/shard_map/ppermute | solution.py:796
  129.7 8.3 %collective-permute-start.33 = (bf16[64,640]{1,0:T(8,128)(2,1)S(1)}, bf16[64,640]{1,0:T(8,128)(2,1)S(1)}, u32[]{:S(2)}, u32[]{:S(2)}) collective-permute-start(bf16[64,640]{1,0:T(8,128)(2,1)S(1)} %get-tuple-element.220), channel_id=1, source_target_pairs={{0,4},{1,5},{2,6},{3,7},{4,0},{5,1},{6,2},{7,3},{8,12},{9,13},{10,... | collective-permute-start | bytes 245768 | tf_op jit(solution)/shard_map/ppermute | solution.py:796
  130.4 7.7 %collective-permute-start.34 = (bf16[64,640]{1,0:T(8,128)(2,1)S(1)}, bf16[64,640]{1,0:T(8,128)(2,1)S(1)}, u32[]{:S(2)}, u32[]{:S(2)}) collective-permute-start(bf16[64,640]{1,0:T(8,128)(2,1)S(1)} %get-tuple-element.221), channel_id=1, source_target_pairs={{0,6},{1,7},{2,4},{3,5},{4,2},{5,3},{6,0},{7,1},{8,14},{9,15},{10,... | collective-permute-start | bytes 245768 | tf_op jit(solution)/shard_map/ppermute | solution.py:796
  133.9 9.0 %collective-permute-start.36 = (bf16[240,256]{1,0:T(8,128)(2,1)S(1)}, bf16[240,256]{1,0:T(8,128)(2,1)S(1)}, u32[]{:S(2)}, u32[]{:S(2)}) collective-permute-start(bf16[240,256]{1,0:T(8,128)(2,1)S(1)} %fusion.6), channel_id=1, source_target_pairs={{0,16},{8,24},{16,0},{24,8},{1,17},{9,25},{17,1},{25,9},{2,18},{10... | collective-permute-start | bytes 368648 | tf_op jit(solution)/shard_map/ppermute | solution.py:799
  (11 other events, 60.1 us)

commit v8 on v7

--- a/solution.py
+++ b/solution.py
@@ -167,10 +167,11 @@
     return pl.pallas_call(
         functools.partial(prepare_attention, n_f),
         out_shape=sds((wq.shape[0], CUT), bf16),
-        in_specs=[sm] + [vm] * 5,
+        in_specs=[sm] + [pl.BlockSpec()] * 5,
         out_specs=vm,
+        compiler_params=small_params(),
         name="prepare_attention",
-    )(rel_bias, wq, wk, wv, attn_gain.reshape(1, -1), ffn_gain.reshape(1, -1))
+    )(*(in_hbm(a) for a in (rel_bias, wq, wk, wv, attn_gain.reshape(1, -1), ffn_gain.reshape(1, -1))))
 
 
 def call_prepare_ffn(place, n_f, wo, wg, wu, wd):
@@ -179,10 +180,11 @@
     return pl.pallas_call(
         functools.partial(prepare_ffn, n_f),
         out_shape=(sds((2 * ds + fh + padded(wo.shape[0]), half), bf16), sds((2 * ds + fh, half), bf16)),
-        in_specs=[sm] + [vm] * 4,
+        in_specs=[sm] + [pl.BlockSpec()] * 4,
         out_specs=[vm] * 2,
+        compiler_params=small_params(),
         name="prepare_ffn",
-    )(place, wo, wg, wu, wd)
+    )(place, *(in_hbm(a) for a in (wo, wg, wu, wd)))
 
 
 def keep_close(G, L, place_ref, tok_ref, ct_ref, tok_out, ct_out, done_ref):

time: 147 us -> 144 us (0.980)
  Pallas kernels: 69.8 us -> 46.4 us
  waiting for transfers between devices: 23.5 us -> 37.7 us
  starting transfers between devices: 48.9 us -> 56.9 us
    ppermute x25, waiting for transfers between devices: 19.9 us -> 33.5 us  [over_fsdp(): return lax.ppermute(value, 'fsdp', [(i, i ^ distance) for i in range(n_f)])]
    pallas_call x3, Pallas kernels: 28.5 us -> 16.2 us  [call_ffn_half(): pl.pallas_call(functools.partial(ffn_half, G, L, n_z, stage, shift), out_...]
    ppermute x16, starting transfers between devices: 16 us -> 20.5 us  [over_rep(): return lax.ppermute(value, 'rep', [(i, i ^ distance) for i in range(n_r)])]
    pallas_call x1, Pallas kernels: 9.7 us -> 5.91 us  [call_attention_backward(): pl.pallas_call(functools.partial(attention_backward, G, L, n_z), out_shap...]
    ppermute x25, starting transfers between devices: 33 us -> 36.4 us  [over_fsdp(): return lax.ppermute(value, 'fsdp', [(i, i ^ distance) for i in range(n_f)])]
    pallas_call x1, Pallas kernels: 7.77 us -> 4.49 us  [call_attention_forward(): pl.pallas_call(functools.partial(attention_forward, G, L, n_z), out_shape...]
  transfers between devices with their start and end apart: 41 -> 41, of which waited for: 9 -> 13; matrix products, arithmetic and copies ran while one was open for 1% -> 1% of each run, Pallas kernels for 45% -> 30%
where the time goes in v8:
time: 144 us; the launch traced here: 145 us
  starting transfers between devices  56.9 us (40%)
  Pallas kernels  46.4 us (32%)
  waiting for transfers between devices  37.7 us (26%)
  other arithmetic  1.79 us (1%)
  between operations  1.62 us (1%)
    ppermute x25, starting transfers between devices, over_fsdp(): return lax.ppermute(value, 'fsdp', [(i, i ^ distance) for i in range(n_f)])  36.4 us
    ppermute x25, waiting for transfers between devices, over_fsdp(): return lax.ppermute(value, 'fsdp', [(i, i ^ distance) for i in range(n_f)])  33.5 us
    ppermute x16, starting transfers between devices, over_rep(): return lax.ppermute(value, 'rep', [(i, i ^ distance) for i in range(n_r)])  20.5 us
    pallas_call x3, Pallas kernels, call_ffn_half(): pl.pallas_call(functools.partial(ffn_half, G, L, n_z, stage, shift), out_...  16.2 us
    pallas_call x1, Pallas kernels, call_attention_backward(): pl.pallas_call(functools.partial(attention_backward, G, L, n_z), out_shap...  5.91 us
    pallas_call x2, Pallas kernels, call_layer_result(): pl.pallas_call(functools.partial(layer_result, G, L, shift), out_shape=(p...  5.48 us
    pallas_call x1, Pallas kernels, call_token_gradient(): pl.pallas_call(functools.partial(token_gradient, G, L), out_shape=(pltpu....  5.22 us
    pallas_call x1, Pallas kernels, call_keep_close(): pl.pallas_call(functools.partial(keep_close, G, L), out_shape=(sds((S * L...  5.01 us
  transfers between devices with their start and end apart: 41, of which 13 were waited for; matrix products, arithmetic and copies ran while one was open for 1% of the time, Pallas kernels for 30%

profile of v8, /device:TPU:0, one launch (start us, length us, event | category | flops | bytes accessed | tf_op | source)
XLA Modules:
  0.0 144.6 jit_solution(8945631352291421915)
XLA Ops:
  1.7 5.1 %collective-permute-start.2 = (bf16[64,640]{1,0:T(8,128)(2,1)S(1)}, bf16[64,640]{1,0:T(8,128)(2,1)S(1)}, u32[]{:S(2)}, u32[]{:S(2)}) collective-permute-start(bf16[64,640]{1,0:T(8,128)(2,1)S(1)} %prepare_attention.1), channel_id=1, source_target_pairs={{0,6},{1,7},{2,4},{3,5},{4,2},{5,3},{6,0},{7,1},{8,14},{9,15},{10,... | collective-permute-start | bytes 245768 | tf_op jit(solution)/shard_map/ppermute | solution.py:798
  10.1 3.7 %collective-permute-done.1 = bf16[64,640]{1,0:T(8,128)(2,1)S(1)} collective-permute-done((bf16[64,640]{1,0:T(8,128)(2,1)S(1)}, bf16[64,640]{1,0:T(8,128)(2,1)S(1)}, u32[]{:S(2)}, u32[]{:S(2)}) %collective-permute-start.1) | collective-permute-done | bytes 81952 | tf_op jit(solution)/shard_map/ppermute | solution.py:798
  13.8 1.6 %collective-permute-start.3 = (bf16[4,64,640]{2,1,0:T(8,128)(2,1)S(1)}, bf16[4,64,640]{2,1,0:T(8,128)(2,1)S(1)}, u32[]{:S(2)}, u32[]{:S(2)}) collective-permute-start(bf16[4,64,640]{2,1,0:T(8,128)(2,1)S(1)} %pad_maximum_fusion.2.refs_0_), channel_id=1, source_target_pairs={{0,1},{1,0},{2,3},{3,2},{4,5},{5,4},{6,7},{7,6},{8,9},{9,8},{10,11... | collective-permute-start | bytes 983048 | tf_op jit(solution)/shard_map/ppermute | solution.py:798
  15.3 2.7 %collective-permute-start.7 = (bf16[240,256]{1,0:T(8,128)(2,1)S(1)}, bf16[240,256]{1,0:T(8,128)(2,1)S(1)}, u32[]{:S(2)}, u32[]{:S(2)}) collective-permute-start(bf16[240,256]{1,0:T(8,128)(2,1)S(1)} %get-tuple-element.140), channel_id=1, source_target_pairs={{0,6},{1,7},{2,4},{3,5},{4,2},{5,3},{6,0},{7,1},{8,14},{9,15},{10,... | collective-permute-start | bytes 368648 | tf_op jit(solution)/shard_map/ppermute | solution.py:798
  18.0 1.7 %collective-permute-start.5 = (bf16[240,256]{1,0:T(8,128)(2,1)S(1)}, bf16[240,256]{1,0:T(8,128)(2,1)S(1)}, u32[]{:S(2)}, u32[]{:S(2)}) collective-permute-start(bf16[240,256]{1,0:T(8,128)(2,1)S(1)} %get-tuple-element.140), channel_id=1, source_target_pairs={{0,2},{1,3},{2,0},{3,1},{4,6},{5,7},{6,4},{7,5},{8,10},{9,11},{10,... | collective-permute-start | bytes 368648 | tf_op jit(solution)/shard_map/ppermute | solution.py:798
  20.3 5.0 %keep_close.1 = (bf16[3072,512]{1,0:T(8,128)(2,1)S(1)}, bf16[3072,512]{1,0:T(8,128)(2,1)S(1)}, f32[8,128]{1,0:T(8,128)S(1)}) custom-call(s32[4]{0:T(128)} %pad_add_fusion.place_ref, bf16[48,64,512]{2,1,0:T(8,128)(2,1)} %tok_ref.1, bf16[48,64,512]{2,1,0:T(8,128)(2,1)} %ct_ref.1), custom_call_target="tpu_custom_call" | custom-call | flops 6144 | bytes 12582912 | tf_op jit(solution)/shard_map/keep_close/pallas_call | solution.py:203
  25.3 2.8 %collective-permute-done.6 = bf16[240,256]{1,0:T(8,128)(2,1)S(1)} collective-permute-done((bf16[240,256]{1,0:T(8,128)(2,1)S(1)}, bf16[240,256]{1,0:T(8,128)(2,1)S(1)}, u32[]{:S(2)}, u32[]{:S(2)}) %collective-permute-start.6) | collective-permute-done | bytes 122912 | tf_op jit(solution)/shard_map/ppermute | solution.py:798
  28.7 1.9 %collective-permute-start.14 = (bf16[192,256]{1,0:T(8,128)(2,1)S(1)}, bf16[192,256]{1,0:T(8,128)(2,1)S(1)}, u32[]{:S(2)}, u32[]{:S(2)}) collective-permute-start(bf16[192,256]{1,0:T(8,128)(2,1)S(1)} %get-tuple-element.154), channel_id=1, source_target_pairs={{0,6},{1,7},{2,4},{3,5},{4,2},{5,3},{6,0},{7,1},{8,14},{9,15},{10,... | collective-permute-start | bytes 294920 | tf_op jit(solution)/shard_map/ppermute | solution.py:798
  30.5 2.5 %collective-permute-start.12 = (bf16[192,256]{1,0:T(8,128)(2,1)S(1)}, bf16[192,256]{1,0:T(8,128)(2,1)S(1)}, u32[]{:S(2)}, u32[]{:S(2)}) collective-permute-start(bf16[192,256]{1,0:T(8,128)(2,1)S(1)} %get-tuple-element.154), channel_id=1, source_target_pairs={{0,2},{1,3},{2,0},{3,1},{4,6},{5,7},{6,4},{7,5},{8,10},{9,11},{10,... | collective-permute-start | bytes 294920 | tf_op jit(solution)/shard_map/ppermute | solution.py:798
  33.8 4.5 %attention_forward.1 = (bf16[3072,1152]{1,0:T(8,128)(2,1)S(1)}, bf16[48,3,64,128]{3,2,1,0:T(8,128)(2,1)S(1)}, bf16[3072,384]{1,0:T(8,128)(2,1)S(1)}, bf16[512,1152]{1,0:T(8,128)(2,1)S(1)}, f32[8,512]{1,0:T(8,128)S(1)}) custom-call(s32[4]{0:T(128)} %pad_add_fusion.place_ref, bf16[3072,512]{1,0:T(8,128)(2,1)S(1)} %get-tuple-element.145.tok_ref.refs_6_, ...), custom_call_target="tpu_custom_call" | custom-call | flops 14495514624 | bytes 15360000 | tf_op jit(solution)/shard_map/attention_forward/pallas_call | solution.py:316
  39.5 4.8 %collective-permute-done.10.refs_2_ = bf16[3,240,256]{2,1,0:T(8,128)(2,1)S(1)} collective-permute-done((bf16[3,240,256]{2,1,0:T(8,128)(2,1)S(1)}, bf16[3,240,256]{2,1,0:T(8,128)(2,1)S(1)}, u32[]{:S(2)}, u32[]{:S(2)}) %collective-permute-start.10) | collective-permute-done | bytes 368672 | tf_op jit(solution)/shard_map/ppermute | solution.py:798
  46.8 1.6 %collective-permute-start.17 = (bf16[4,192,256]{2,1,0:T(8,128)(2,1)S(1)}, bf16[4,192,256]{2,1,0:T(8,128)(2,1)S(1)}, u32[]{:S(2)}, u32[]{:S(2)}) collective-permute-start(bf16[4,192,256]{2,1,0:T(8,128)(2,1)S(1)} %pad_maximum_fusion.1.refs_0_), channel_id=1, source_target_pairs={{0,1},{1,0},{2,3},{3,2},{4,5},{5,4},{6,7},{7,6},{8,9},{9,8},{10,11... | collective-permute-start | bytes 1179656 | tf_op jit(solution)/shard_map/ppermute | solution.py:798
  48.4 7.3 %ffn_first.1 = (bf16[3072,512]{1,0:T(8,128)(2,1)S(1)}, bf16[3072,512]{1,0:T(8,128)(2,1)S(1)}, bf16[3072,512]{1,0:T(8,128)(2,1)S(1)}, bf16[512,512]{1,0:T(8,128)(...) custom-call(s32[4]{0:T(128)} %pad_add_fusion.place_ref, ...), custom_call_target="tpu_custom_call" | custom-call | flops 14495514624 | bytes 27648000 | tf_op jit(solution)/shard_map/ffn_first/pallas_call | solution.py:539
  55.8 2.3 %collective-permute-done.17.refs_1_ = bf16[4,192,256]{2,1,0:T(8,128)(2,1)S(1)} collective-permute-done((bf16[4,192,256]{2,1,0:T(8,128)(2,1)S(1)}, bf16[4,192,256]{2,1,0:T(8,128)(2,1)S(1)}, u32[]{:S(2)}, u32[]{:S(2)}) %collective-permute-start.17) | collective-permute-done | bytes 393248 | tf_op jit(solution)/shard_map/ppermute | solution.py:798
  58.1 9.6 %collective-permute-start.19 = (bf16[4,192,256]{2,1,0:T(8,128)(2,1)S(1)}, bf16[4,192,256]{2,1,0:T(8,128)(2,1)S(1)}, u32[]{:S(2)}, u32[]{:S(2)}) collective-permute-start(bf16[4,192,256]{2,1,0:T(8,128)(2,1)S(1)} %collective-permute-done.17.refs_1_), channel_id=1, source_target_pairs={{0,8},{8,0},{16,24},{24,16},{1,9},{9,1},{17,25},{25,17},{2,10},{10... | collective-permute-start | bytes 1179656 | tf_op jit(solution)/shard_map/ppermute | solution.py:801
  69.0 7.7 %ffn_second.1 = (bf16[3072,512]{1,0:T(8,128)(2,1)S(1)}, bf16[3072,384]{1,0:T(8,128)(2,1)S(1)}, bf16[3072,512]{1,0:T(8,128)(2,1)S(1)}, f32[512,1024]{1,0:T(8,128)...) custom-call(s32[4]{0:T(128)} %pad_add_fusion.place_ref, ...), custom_call_target="tpu_custom_call", output_to_operand_aliasing={{0}: (9, {}), {1}: (10, {})} | custom-call | flops 7247757312 | bytes 27648000 | tf_op jit(solution)/shard_map/ffn_second/pallas_call | solution.py:539
  76.8 4.0 %collective-permute-start.21 = (bf16[4,192,256]{2,1,0:T(8,128)(2,1)S(1)}, bf16[4,192,256]{2,1,0:T(8,128)(2,1)S(1)}, u32[]{:S(2)}, u32[]{:S(2)}) collective-permute-start(bf16[4,192,256]{2,1,0:T(8,128)(2,1)S(1)} %fusion.1), channel_id=1, source_target_pairs={{0,1},{1,0},{2,3},{3,2},{4,5},{5,4},{6,7},{7,6},{8,9},{9,8},{10,11... | collective-permute-start | bytes 1179656 | tf_op jit(solution)/shard_map/ppermute | solution.py:798
  82.0 8.2 %collective-permute-done.21 = bf16[4,192,256]{2,1,0:T(8,128)(2,1)S(1)} collective-permute-done((bf16[4,192,256]{2,1,0:T(8,128)(2,1)S(1)}, bf16[4,192,256]{2,1,0:T(8,128)(2,1)S(1)}, u32[]{:S(2)}, u32[]{:S(2)}) %collective-permute-start.21) | collective-permute-done | bytes 393248 | tf_op jit(solution)/shard_map/ppermute | solution.py:798
  90.2 1.5 %collective-permute-start.22 = (bf16[2,4,240,256]{3,2,1,0:T(8,128)(2,1)S(1)}, bf16[2,4,240,256]{3,2,1,0:T(8,128)(2,1)S(1)}, u32[]{:S(2)}, u32[]{:S(2)}) collective-permute-start(bf16[2,4,240,256]{3,2,1,0:T(8,128)(2,1)S(1)} %get-tuple-element.198), channel_id=1, source_target_pairs={{0,8},{8,0},{16,24},{24,16},{1,9},{9,1},{17,25},{25,17},{2,10},{10... | collective-permute-start | bytes 2949128 | tf_op jit(solution)/shard_map/ppermute | solution.py:801
  92.5 3.9 %collective-permute-start.23 = (bf16[192,256]{1,0:T(8,128)(2,1)S(1)}, bf16[192,256]{1,0:T(8,128)(2,1)S(1)}, u32[]{:S(2)}, u32[]{:S(2)}) collective-permute-start(bf16[192,256]{1,0:T(8,128)(2,1)S(1)} %get-tuple-element.261), channel_id=1, source_target_pairs={{0,2},{1,3},{2,0},{3,1},{4,6},{5,7},{6,4},{7,5},{8,10},{9,11},{10,... | collective-permute-start | bytes 294920 | tf_op jit(solution)/shard_map/ppermute | solution.py:798
  96.9 5.9 %attention_backward.1 = (bf16[3072,1152]{1,0:T(8,128)(2,1)S(1)}, bf16[2,4,64,640]{3,2,1,0:T(8,128)(2,1)S(1)}, bf16[2,4,64,640]{3,2,1,0:T(8,128)(2,1)S(1)}) custom-call(s32[4]{0:T(128)} %pad_add_fusion.place_ref, bf16[3072,512]{1,0:T(8,128)(2,1)S(1)} %get-tuple-element.145.tok_ref.refs_6_, ...), custom_call_target="tpu_custom_call", output_to_operand_aliasing={{0}: (2, {})} | custom-call | flops 14495514624 | bytes 18432000 | tf_op jit(solution)/shard_map/attention_backward/pallas_call | solution.py:682
  102.8 6.0 %collective-permute-done.26 = bf16[4,240,256]{2,1,0:T(8,128)(2,1)S(1)} collective-permute-done((bf16[4,240,256]{2,1,0:T(8,128)(2,1)S(1)}, bf16[4,240,256]{2,1,0:T(8,128)(2,1)S(1)}, u32[]{:S(2)}, u32[]{:S(2)}) %collective-permute-start.26) | collective-permute-done | bytes 491552 | tf_op jit(solution)/shard_map/ppermute | solution.py:798
  111.7 2.9 %collective-permute-start.29 = (bf16[240,256]{1,0:T(8,128)(2,1)S(1)}, bf16[240,256]{1,0:T(8,128)(2,1)S(1)}, u32[]{:S(2)}, u32[]{:S(2)}) collective-permute-start(bf16[240,256]{1,0:T(8,128)(2,1)S(1)} %get-tuple-element.258), channel_id=1, source_target_pairs={{0,2},{1,3},{2,0},{3,1},{4,6},{5,7},{6,4},{7,5},{8,10},{9,11},{10,... | collective-permute-start | bytes 368648 | tf_op jit(solution)/shard_map/ppermute | solution.py:798
  114.7 3.5 %collective-permute-start.35 = (bf16[192,256]{1,0:T(8,128)(2,1)S(1)}, bf16[192,256]{1,0:T(8,128)(2,1)S(1)}, u32[]{:S(2)}, u32[]{:S(2)}) collective-permute-start(bf16[192,256]{1,0:T(8,128)(2,1)S(1)} %fusion.10), channel_id=1, source_target_pairs={{0,16},{8,24},{16,0},{24,8},{1,17},{9,25},{17,1},{25,9},{2,18},{10... | collective-permute-start | bytes 294920 | tf_op jit(solution)/shard_map/ppermute | solution.py:801
  118.2 5.2 %token_gradient.1 = (bf16[48,64,512]{2,1,0:T(8,128)(2,1)}, f32[8,512]{1,0:T(8,128)S(1)}) custom-call(s32[4]{0:T(128)} %pad_add_fusion.place_ref, bf16[3072,512]{1,0:T(8,128)(2,1)S(1)} %get-tuple-element.145.tok_ref.refs_6_, bf16[3072,1152]{1,0:T(8,128)(2,1)S(1)} %get-tuple-element.200.dqkv_ref, bf16[3072,512]{1,0:T(8,128)(2,1)S(1)} %get-tuple-element.201.gh_ref, ...), custom_call_target="tpu_custom_call" | custom-call | flops 7247757312 | bytes 15360000 | tf_op jit(solution)/shard_map/token_gradient/pallas_call | solution.py:732
  123.5 3.7 %collective-permute-done.28 = bf16[4,64,640]{2,1,0:T(8,128)(2,1)S(1)} collective-permute-done((bf16[4,64,640]{2,1,0:T(8,128)(2,1)S(1)}, bf16[4,64,640]{2,1,0:T(8,128)(2,1)S(1)}, u32[]{:S(2)}, u32[]{:S(2)}) %collective-permute-start.28) | collective-permute-done | bytes 327712 | tf_op jit(solution)/shard_map/ppermute | solution.py:798
  127.7 2.1 %collective-permute-start.33 = (bf16[64,640]{1,0:T(8,128)(2,1)S(1)}, bf16[64,640]{1,0:T(8,128)(2,1)S(1)}, u32[]{:S(2)}, u32[]{:S(2)}) collective-permute-start(bf16[64,640]{1,0:T(8,128)(2,1)S(1)} %get-tuple-element.220), channel_id=1, source_target_pairs={{0,4},{1,5},{2,6},{3,7},{4,0},{5,1},{6,2},{7,3},{8,12},{9,13},{10,... | collective-permute-start | bytes 245768 | tf_op jit(solution)/shard_map/ppermute | solution.py:798
  129.9 2.0 %collective-permute-start.34 = (bf16[64,640]{1,0:T(8,128)(2,1)S(1)}, bf16[64,640]{1,0:T(8,128)(2,1)S(1)}, u32[]{:S(2)}, u32[]{:S(2)}) collective-permute-start(bf16[64,640]{1,0:T(8,128)(2,1)S(1)} %get-tuple-element.221), channel_id=1, source_target_pairs={{0,6},{1,7},{2,4},{3,5},{4,2},{5,3},{6,0},{7,1},{8,14},{9,15},{10,... | collective-permute-start | bytes 245768 | tf_op jit(solution)/shard_map/ppermute | solution.py:798
  132.3 3.1 %layer_result.2 = (bf16[48,64,512]{2,1,0:T(8,128)(2,1)}, f32[8,512]{1,0:T(8,128)S(1)}) custom-call(s32[4]{0:T(128)} %pad_add_fusion.place_ref, bf16[3072,512]{1,0:T(8,128)(2,1)S(1)} %get-tuple-element.162.refs_4_.refs_0_.hid_ref, bf16[3072,512]{1,0:T(8,128)(2,1)S(1)} %get-tuple-element.163.act_0, bf16[3072,512]{1,0:T(8,128)(2,1)S(1)} %get-tuple-element.186.act_1, ...), custom_call_target="tpu_custom_call" | custom-call | flops 1610612736 | bytes 9216000 | tf_op jit(solution)/shard_map/layer_result/pallas_call | solution.py:583
  136.2 1.6 %collective-permute-start.37 = (bf16[64,640]{1,0:T(8,128)(2,1)S(1)}, bf16[64,640]{1,0:T(8,128)(2,1)S(1)}, u32[]{:S(2)}, u32[]{:S(2)}) collective-permute-start(bf16[64,640]{1,0:T(8,128)(2,1)S(1)} %fusion.14), channel_id=1, source_target_pairs={{0,16},{8,24},{16,0},{24,8},{1,17},{9,25},{17,1},{25,9},{2,18},{10... | collective-permute-start | bytes 245768 | tf_op jit(solution)/shard_map/ppermute | solution.py:801
  137.8 2.4 %layer_result.3 = (bf16[48,64,512]{2,1,0:T(8,128)(2,1)}, f32[8,512]{1,0:T(8,128)S(1)}) custom-call(s32[4]{0:T(128)} %pad_add_fusion.place_ref, bf16[3072,512]{1,0:T(8,128)(2,1)S(1)} %get-tuple-element.162.refs_4_.refs_0_.hid_ref, bf16[3072,512]{1,0:T(8,128)(2,1)S(1)} %get-tuple-element.163.act_0, ...), custom_call_target="tpu_custom_call", output_to_operand_aliasing={{0}: (7, {})} | custom-call | flops 1610612736 | bytes 9216000 | tf_op jit(solution)/shard_map/layer_result/pallas_call | solution.py:583
  142.8 1.8 %finish.1 = (f32[64,384]{1,0:T(8,128)}, f32[64,384]{1,0:T(8,128)}, f32[64,384]{1,0:T(8,128)}, f32[48,512]{1,0:T(8,128)}, f32[64,1024]{1,0:T(8,128)}, /*index=5*/...) custom-call(s32[4]{0:T(128)} %pad_add_fusion.place_ref, ...), custom_call_target="tpu_custom_call" | custom-call | tf_op jit(solution)/shard_map/finish/pallas_call | solution.py:783
  (82 shorter events, 20.4 us)
Async XLA Ops:
  1.7 8.3 %collective-permute-start.2 = (bf16[64,640]{1,0:T(8,128)(2,1)S(1)}, bf16[64,640]{1,0:T(8,128)(2,1)S(1)}, u32[]{:S(2)}, u32[]{:S(2)}) collective-permute-start(bf16[64,640]{1,0:T(8,128)(2,1)S(1)} %prepare_attention.1), channel_id=1, source_target_pairs={{0,6},{1,7},{2,4},{3,5},{4,2},{5,3},{6,0},{7,1},{8,14},{9,15},{10,... | collective-permute-start | bytes 245768 | tf_op jit(solution)/shard_map/ppermute | solution.py:798
  6.8 6.9 %collective-permute-start.1 = (bf16[64,640]{1,0:T(8,128)(2,1)S(1)}, bf16[64,640]{1,0:T(8,128)(2,1)S(1)}, u32[]{:S(2)}, u32[]{:S(2)}) collective-permute-start(bf16[64,640]{1,0:T(8,128)(2,1)S(1)} %prepare_attention.1), channel_id=1, source_target_pairs={{0,4},{1,5},{2,6},{3,7},{4,0},{5,1},{6,2},{7,3},{8,12},{9,13},{10,... | collective-permute-start | bytes 245768 | tf_op jit(solution)/shard_map/ppermute | solution.py:798
  6.8 6.9 %collective-permute-start = (bf16[64,640]{1,0:T(8,128)(2,1)S(1)}, bf16[64,640]{1,0:T(8,128)(2,1)S(1)}, u32[]{:S(2)}, u32[]{:S(2)}) collective-permute-start(bf16[64,640]{1,0:T(8,128)(2,1)S(1)} %prepare_attention.1), channel_id=1, source_target_pairs={{0,2},{1,3},{2,0},{3,1},{4,6},{5,7},{6,4},{7,5},{8,10},{9,11},{10,... | collective-permute-start | bytes 245768 | tf_op jit(solution)/shard_map/ppermute | solution.py:798
  13.8 14.3 %collective-permute-start.3 = (bf16[4,64,640]{2,1,0:T(8,128)(2,1)S(1)}, bf16[4,64,640]{2,1,0:T(8,128)(2,1)S(1)}, u32[]{:S(2)}, u32[]{:S(2)}) collective-permute-start(bf16[4,64,640]{2,1,0:T(8,128)(2,1)S(1)} %pad_maximum_fusion.2.refs_0_), channel_id=1, source_target_pairs={{0,1},{1,0},{2,3},{3,2},{4,5},{5,4},{6,7},{7,6},{8,9},{9,8},{10,11... | collective-permute-start | bytes 983048 | tf_op jit(solution)/shard_map/ppermute | solution.py:798
  15.3 9.9 %collective-permute-start.7 = (bf16[240,256]{1,0:T(8,128)(2,1)S(1)}, bf16[240,256]{1,0:T(8,128)(2,1)S(1)}, u32[]{:S(2)}, u32[]{:S(2)}) collective-permute-start(bf16[240,256]{1,0:T(8,128)(2,1)S(1)} %get-tuple-element.140), channel_id=1, source_target_pairs={{0,6},{1,7},{2,4},{3,5},{4,2},{5,3},{6,0},{7,1},{8,14},{9,15},{10,... | collective-permute-start | bytes 368648 | tf_op jit(solution)/shard_map/ppermute | solution.py:798
  18.0 10.0 %collective-permute-start.6 = (bf16[240,256]{1,0:T(8,128)(2,1)S(1)}, bf16[240,256]{1,0:T(8,128)(2,1)S(1)}, u32[]{:S(2)}, u32[]{:S(2)}) collective-permute-start(bf16[240,256]{1,0:T(8,128)(2,1)S(1)} %get-tuple-element.140), channel_id=1, source_target_pairs={{0,4},{1,5},{2,6},{3,7},{4,0},{5,1},{6,2},{7,3},{8,12},{9,13},{10,... | collective-permute-start | bytes 368648 | tf_op jit(solution)/shard_map/ppermute | solution.py:798
  18.0 10.0 %collective-permute-start.5 = (bf16[240,256]{1,0:T(8,128)(2,1)S(1)}, bf16[240,256]{1,0:T(8,128)(2,1)S(1)}, u32[]{:S(2)}, u32[]{:S(2)}) collective-permute-start(bf16[240,256]{1,0:T(8,128)(2,1)S(1)} %get-tuple-element.140), channel_id=1, source_target_pairs={{0,2},{1,3},{2,0},{3,1},{4,6},{5,7},{6,4},{7,5},{8,10},{9,11},{10,... | collective-permute-start | bytes 368648 | tf_op jit(solution)/shard_map/ppermute | solution.py:798
  19.7 8.4 %collective-permute-start.4 = (bf16[240,256]{1,0:T(8,128)(2,1)S(1)}, bf16[240,256]{1,0:T(8,128)(2,1)S(1)}, u32[]{:S(2)}, u32[]{:S(2)}) collective-permute-start(bf16[240,256]{1,0:T(8,128)(2,1)S(1)} %get-tuple-element.140), channel_id=1, source_target_pairs={{0,1},{1,0},{2,3},{3,2},{4,5},{5,4},{6,7},{7,6},{8,9},{9,8},{10,11... | collective-permute-start | bytes 368648 | tf_op jit(solution)/shard_map/ppermute | solution.py:798
  28.7 9.6 %collective-permute-start.14 = (bf16[192,256]{1,0:T(8,128)(2,1)S(1)}, bf16[192,256]{1,0:T(8,128)(2,1)S(1)}, u32[]{:S(2)}, u32[]{:S(2)}) collective-permute-start(bf16[192,256]{1,0:T(8,128)(2,1)S(1)} %get-tuple-element.154), channel_id=1, source_target_pairs={{0,6},{1,7},{2,4},{3,5},{4,2},{5,3},{6,0},{7,1},{8,14},{9,15},{10,... | collective-permute-start | bytes 294920 | tf_op jit(solution)/shard_map/ppermute | solution.py:798
  30.5 8.9 %collective-permute-start.13 = (bf16[192,256]{1,0:T(8,128)(2,1)S(1)}, bf16[192,256]{1,0:T(8,128)(2,1)S(1)}, u32[]{:S(2)}, u32[]{:S(2)}) collective-permute-start(bf16[192,256]{1,0:T(8,128)(2,1)S(1)} %get-tuple-element.154), channel_id=1, source_target_pairs={{0,4},{1,5},{2,6},{3,7},{4,0},{5,1},{6,2},{7,3},{8,12},{9,13},{10,... | collective-permute-start | bytes 294920 | tf_op jit(solution)/shard_map/ppermute | solution.py:798
  30.5 8.9 %collective-permute-start.12 = (bf16[192,256]{1,0:T(8,128)(2,1)S(1)}, bf16[192,256]{1,0:T(8,128)(2,1)S(1)}, u32[]{:S(2)}, u32[]{:S(2)}) collective-permute-start(bf16[192,256]{1,0:T(8,128)(2,1)S(1)} %get-tuple-element.154), channel_id=1, source_target_pairs={{0,2},{1,3},{2,0},{3,1},{4,6},{5,7},{6,4},{7,5},{8,10},{9,11},{10,... | collective-permute-start | bytes 294920 | tf_op jit(solution)/shard_map/ppermute | solution.py:798
  33.2 11.1 %collective-permute-start.11 = (bf16[4,240,256]{2,1,0:T(8,128)(2,1)S(1)}, bf16[4,240,256]{2,1,0:T(8,128)(2,1)S(1)}, u32[]{:S(2)}, u32[]{:S(2)}) collective-permute-start(bf16[4,240,256]{2,1,0:T(8,128)(2,1)S(1)} %pad_maximum_fusion.refs_0_), channel_id=1, source_target_pairs={{0,8},{8,0},{16,24},{24,16},{1,9},{9,1},{17,25},{25,17},{2,10},{10... | collective-permute-start | bytes 1474568 | tf_op jit(solution)/shard_map/ppermute | solution.py:801
  33.3 11.0 %collective-permute-start.10 = (bf16[3,240,256]{2,1,0:T(8,128)(2,1)S(1)}, bf16[3,240,256]{2,1,0:T(8,128)(2,1)S(1)}, u32[]{:S(2)}, u32[]{:S(2)}) collective-permute-start(bf16[3,240,256]{2,1,0:T(8,128)(2,1)S(1)} %slice.84), channel_id=1, source_target_pairs={{0,1},{1,0},{2,3},{3,2},{4,5},{5,4},{6,7},{7,6},{8,9},{9,8},{10,11... | collective-permute-start | bytes 1105928 | tf_op jit(solution)/shard_map/ppermute | solution.py:798
  46.5 9.3 %collective-permute-start.18 = (bf16[4,192,256]{2,1,0:T(8,128)(2,1)S(1)}, bf16[4,192,256]{2,1,0:T(8,128)(2,1)S(1)}, u32[]{:S(2)}, u32[]{:S(2)}) collective-permute-start(bf16[4,192,256]{2,1,0:T(8,128)(2,1)S(1)} %pad_maximum_fusion.1.refs_0_), channel_id=1, source_target_pairs={{0,8},{8,0},{16,24},{24,16},{1,9},{9,1},{17,25},{25,17},{2,10},{10... | collective-permute-start | bytes 1179656 | tf_op jit(solution)/shard_map/ppermute | solution.py:801
  46.8 11.2 %collective-permute-start.17 = (bf16[4,192,256]{2,1,0:T(8,128)(2,1)S(1)}, bf16[4,192,256]{2,1,0:T(8,128)(2,1)S(1)}, u32[]{:S(2)}, u32[]{:S(2)}) collective-permute-start(bf16[4,192,256]{2,1,0:T(8,128)(2,1)S(1)} %pad_maximum_fusion.1.refs_0_), channel_id=1, source_target_pairs={{0,1},{1,0},{2,3},{3,2},{4,5},{5,4},{6,7},{7,6},{8,9},{9,8},{10,11... | collective-permute-start | bytes 1179656 | tf_op jit(solution)/shard_map/ppermute | solution.py:798
  58.1 11.0 %collective-permute-start.19 = (bf16[4,192,256]{2,1,0:T(8,128)(2,1)S(1)}, bf16[4,192,256]{2,1,0:T(8,128)(2,1)S(1)}, u32[]{:S(2)}, u32[]{:S(2)}) collective-permute-start(bf16[4,192,256]{2,1,0:T(8,128)(2,1)S(1)} %collective-permute-done.17.refs_1_), channel_id=1, source_target_pairs={{0,8},{8,0},{16,24},{24,16},{1,9},{9,1},{17,25},{25,17},{2,10},{10... | collective-permute-start | bytes 1179656 | tf_op jit(solution)/shard_map/ppermute | solution.py:801
  67.7 9.1 %collective-permute-start.20 = (bf16[2,4,192,256]{3,2,1,0:T(8,128)(2,1)S(1)}, bf16[2,4,192,256]{3,2,1,0:T(8,128)(2,1)S(1)}, u32[]{:S(2)}, u32[]{:S(2)}) collective-permute-start(bf16[2,4,192,256]{3,2,1,0:T(8,128)(2,1)S(1)} %get-tuple-element.182), channel_id=1, source_target_pairs={{0,8},{8,0},{16,24},{24,16},{1,9},{9,1},{17,25},{25,17},{2,10},{10... | collective-permute-start | bytes 2359304 | tf_op jit(solution)/shard_map/ppermute | solution.py:801
  76.8 13.4 %collective-permute-start.21 = (bf16[4,192,256]{2,1,0:T(8,128)(2,1)S(1)}, bf16[4,192,256]{2,1,0:T(8,128)(2,1)S(1)}, u32[]{:S(2)}, u32[]{:S(2)}) collective-permute-start(bf16[4,192,256]{2,1,0:T(8,128)(2,1)S(1)} %fusion.1), channel_id=1, source_target_pairs={{0,1},{1,0},{2,3},{3,2},{4,5},{5,4},{6,7},{7,6},{8,9},{9,8},{10,11... | collective-permute-start | bytes 1179656 | tf_op jit(solution)/shard_map/ppermute | solution.py:798
  90.2 6.2 %collective-permute-start.22 = (bf16[2,4,240,256]{3,2,1,0:T(8,128)(2,1)S(1)}, bf16[2,4,240,256]{3,2,1,0:T(8,128)(2,1)S(1)}, u32[]{:S(2)}, u32[]{:S(2)}) collective-permute-start(bf16[2,4,240,256]{3,2,1,0:T(8,128)(2,1)S(1)} %get-tuple-element.198), channel_id=1, source_target_pairs={{0,8},{8,0},{16,24},{24,16},{1,9},{9,1},{17,25},{25,17},{2,10},{10... | collective-permute-start | bytes 2949128 | tf_op jit(solution)/shard_map/ppermute | solution.py:801
  91.9 10.9 %collective-permute-start.25 = (bf16[192,256]{1,0:T(8,128)(2,1)S(1)}, bf16[192,256]{1,0:T(8,128)(2,1)S(1)}, u32[]{:S(2)}, u32[]{:S(2)}) collective-permute-start(bf16[192,256]{1,0:T(8,128)(2,1)S(1)} %get-tuple-element.259), channel_id=1, source_target_pairs={{0,6},{1,7},{2,4},{3,5},{4,2},{5,3},{6,0},{7,1},{8,14},{9,15},{10,... | collective-permute-start | bytes 294920 | tf_op jit(solution)/shard_map/ppermute | solution.py:798
  92.0 10.8 %collective-permute-start.24 = (bf16[192,256]{1,0:T(8,128)(2,1)S(1)}, bf16[192,256]{1,0:T(8,128)(2,1)S(1)}, u32[]{:S(2)}, u32[]{:S(2)}) collective-permute-start(bf16[192,256]{1,0:T(8,128)(2,1)S(1)} %get-tuple-element.260), channel_id=1, source_target_pairs={{0,4},{1,5},{2,6},{3,7},{4,0},{5,1},{6,2},{7,3},{8,12},{9,13},{10,... | collective-permute-start | bytes 294920 | tf_op jit(solution)/shard_map/ppermute | solution.py:798
  92.5 10.3 %collective-permute-start.23 = (bf16[192,256]{1,0:T(8,128)(2,1)S(1)}, bf16[192,256]{1,0:T(8,128)(2,1)S(1)}, u32[]{:S(2)}, u32[]{:S(2)}) collective-permute-start(bf16[192,256]{1,0:T(8,128)(2,1)S(1)} %get-tuple-element.261), channel_id=1, source_target_pairs={{0,2},{1,3},{2,0},{3,1},{4,6},{5,7},{6,4},{7,5},{8,10},{9,11},{10,... | collective-permute-start | bytes 294920 | tf_op jit(solution)/shard_map/ppermute | solution.py:798
  96.5 12.4 %collective-permute-start.26 = (bf16[4,240,256]{2,1,0:T(8,128)(2,1)S(1)}, bf16[4,240,256]{2,1,0:T(8,128)(2,1)S(1)}, u32[]{:S(2)}, u32[]{:S(2)}) collective-permute-start(bf16[4,240,256]{2,1,0:T(8,128)(2,1)S(1)} %fusion), channel_id=1, source_target_pairs={{0,1},{1,0},{2,3},{3,2},{4,5},{5,4},{6,7},{7,6},{8,9},{9,8},{10,11... | collective-permute-start | bytes 1474568 | tf_op jit(solution)/shard_map/ppermute | solution.py:798
  110.1 13.3 %collective-permute-start.31 = (bf16[240,256]{1,0:T(8,128)(2,1)S(1)}, bf16[240,256]{1,0:T(8,128)(2,1)S(1)}, u32[]{:S(2)}, u32[]{:S(2)}) collective-permute-start(bf16[240,256]{1,0:T(8,128)(2,1)S(1)} %get-tuple-element.256), channel_id=1, source_target_pairs={{0,6},{1,7},{2,4},{3,5},{4,2},{5,3},{6,0},{7,1},{8,14},{9,15},{10,... | collective-permute-start | bytes 368648 | tf_op jit(solution)/shard_map/ppermute | solution.py:798
  110.2 13.3 %collective-permute-start.30 = (bf16[240,256]{1,0:T(8,128)(2,1)S(1)}, bf16[240,256]{1,0:T(8,128)(2,1)S(1)}, u32[]{:S(2)}, u32[]{:S(2)}) collective-permute-start(bf16[240,256]{1,0:T(8,128)(2,1)S(1)} %get-tuple-element.257), channel_id=1, source_target_pairs={{0,4},{1,5},{2,6},{3,7},{4,0},{5,1},{6,2},{7,3},{8,12},{9,13},{10,... | collective-permute-start | bytes 368648 | tf_op jit(solution)/shard_map/ppermute | solution.py:798
  111.7 11.8 %collective-permute-start.29 = (bf16[240,256]{1,0:T(8,128)(2,1)S(1)}, bf16[240,256]{1,0:T(8,128)(2,1)S(1)}, u32[]{:S(2)}, u32[]{:S(2)}) collective-permute-start(bf16[240,256]{1,0:T(8,128)(2,1)S(1)} %get-tuple-element.258), channel_id=1, source_target_pairs={{0,2},{1,3},{2,0},{3,1},{4,6},{5,7},{6,4},{7,5},{8,10},{9,11},{10,... | collective-permute-start | bytes 368648 | tf_op jit(solution)/shard_map/ppermute | solution.py:798
  114.7 25.4 %collective-permute-start.35 = (bf16[192,256]{1,0:T(8,128)(2,1)S(1)}, bf16[192,256]{1,0:T(8,128)(2,1)S(1)}, u32[]{:S(2)}, u32[]{:S(2)}) collective-permute-start(bf16[192,256]{1,0:T(8,128)(2,1)S(1)} %fusion.10), channel_id=1, source_target_pairs={{0,16},{8,24},{16,0},{24,8},{1,17},{9,25},{17,1},{25,9},{2,18},{10... | collective-permute-start | bytes 294920 | tf_op jit(solution)/shard_map/ppermute | solution.py:801
  118.2 9.0 %collective-permute-start.28 = (bf16[4,64,640]{2,1,0:T(8,128)(2,1)S(1)}, bf16[4,64,640]{2,1,0:T(8,128)(2,1)S(1)}, u32[]{:S(2)}, u32[]{:S(2)}) collective-permute-start(bf16[4,64,640]{2,1,0:T(8,128)(2,1)S(1)} %fusion.2), channel_id=1, source_target_pairs={{0,1},{1,0},{2,3},{3,2},{4,5},{5,4},{6,7},{7,6},{8,9},{9,8},{10,11... | collective-permute-start | bytes 983048 | tf_op jit(solution)/shard_map/ppermute | solution.py:798
  127.4 8.1 %collective-permute-start.32 = (bf16[64,640]{1,0:T(8,128)(2,1)S(1)}, bf16[64,640]{1,0:T(8,128)(2,1)S(1)}, u32[]{:S(2)}, u32[]{:S(2)}) collective-permute-start(bf16[64,640]{1,0:T(8,128)(2,1)S(1)} %get-tuple-element.219), channel_id=1, source_target_pairs={{0,2},{1,3},{2,0},{3,1},{4,6},{5,7},{6,4},{7,5},{8,10},{9,11},{10,... | collective-permute-start | bytes 245768 | tf_op jit(solution)/shard_map/ppermute | solution.py:798
  127.7 7.7 %collective-permute-start.33 = (bf16[64,640]{1,0:T(8,128)(2,1)S(1)}, bf16[64,640]{1,0:T(8,128)(2,1)S(1)}, u32[]{:S(2)}, u32[]{:S(2)}) collective-permute-start(bf16[64,640]{1,0:T(8,128)(2,1)S(1)} %get-tuple-element.220), channel_id=1, source_target_pairs={{0,4},{1,5},{2,6},{3,7},{4,0},{5,1},{6,2},{7,3},{8,12},{9,13},{10,... | collective-permute-start | bytes 245768 | tf_op jit(solution)/shard_map/ppermute | solution.py:798
  129.9 6.3 %collective-permute-start.34 = (bf16[64,640]{1,0:T(8,128)(2,1)S(1)}, bf16[64,640]{1,0:T(8,128)(2,1)S(1)}, u32[]{:S(2)}, u32[]{:S(2)}) collective-permute-start(bf16[64,640]{1,0:T(8,128)(2,1)S(1)} %get-tuple-element.221), channel_id=1, source_target_pairs={{0,6},{1,7},{2,4},{3,5},{4,2},{5,3},{6,0},{7,1},{8,14},{9,15},{10,... | collective-permute-start | bytes 245768 | tf_op jit(solution)/shard_map/ppermute | solution.py:798
  131.9 8.3 %collective-permute-start.36 = (bf16[240,256]{1,0:T(8,128)(2,1)S(1)}, bf16[240,256]{1,0:T(8,128)(2,1)S(1)}, u32[]{:S(2)}, u32[]{:S(2)}) collective-permute-start(bf16[240,256]{1,0:T(8,128)(2,1)S(1)} %fusion.6), channel_id=1, source_target_pairs={{0,16},{8,24},{16,0},{24,8},{1,17},{9,25},{17,1},{25,9},{2,18},{10... | collective-permute-start | bytes 368648 | tf_op jit(solution)/shard_map/ppermute | solution.py:801
  (9 other events, 31.0 us)

commit v9 on v8

--- a/solution.py
+++ b/solution.py
@@ -350,7 +350,8 @@
     v2 = v * v
     t = jnp.tanh(v * (c + (c * 0.044715) * v2))
     half = 0.5 + 0.5 * t
-    return v * half, half + (0.5 * v) * (1.0 - t * t) * (c + (3 * c * 0.044715) * v2)
+    g = v * half
+    return g, half + g * (1.0 - t) * (c + (3 * c * 0.044715) * v2)
 
 
 def put_weights(place, pieces, wgu, wd, wo=None):
@@ -646,17 +647,17 @@
         n_f = 2 * n_z
         ds, n_b, rest = D // n_f, BUCKETS // n_f, 3 * INNER - CUT
         ids = bucket_table(L)
-        low = lane_low((1, PAIR))
         small[...] = jnp.zeros_like(small)
         for p in range(PAIRS):
             t = ab[p]
+            by_lane = [jnp.sum(jnp.where(ids == b, t, 0.0), axis=0, keepdims=True) for b in range(BUCKETS)]
+            by_lane = jnp.concatenate(by_lane, axis=0)
+            low = lane_low(by_lane.shape)
+            halves = [jnp.sum(jnp.where(mask, by_lane, 0.0), axis=1, keepdims=True) for mask in (low, ~low)]
             for b in range(BUCKETS):
-                by_lane = jnp.sum(jnp.where(ids == b, t, 0.0), axis=0, keepdims=True)
-                one = jnp.sum(jnp.where(low, by_lane, 0.0), axis=1, keepdims=True)
-                two = jnp.sum(jnp.where(low, 0.0, by_lane), axis=1, keepdims=True)
                 row = b // n_b * ds + (b % n_b) * HEADS + 2 * p
-                small[row : row + 1, :] = jnp.broadcast_to(one, (1, PAIR))
-                small[row + 1 : row + 2, :] = jnp.broadcast_to(two, (1, PAIR))
+                for side in range(2):
+                    small[row + side : row + side + 1, :] = jnp.broadcast_to(halves[side][b : b + 1], (1, PAIR))
         gain = jnp.transpose(gains_ref[...])[:, 0:1]
         one = jnp.sum(aw[...] * w_ref[...].astype(f32), axis=1, keepdims=True) / gain
         two = jnp.sum(jnp.transpose(gf_ref[...]), axis=1, keepdims=True)

time: 144 us -> 143 us (level); the launches traced: 145 us -> 142 us
  waiting for transfers between devices: 37.7 us -> 33.4 us
  starting transfers between devices: 56.9 us -> 58.4 us
    ppermute x25, starting transfers between devices: 36.4 us -> 52.2 us  [over_fsdp(): return lax.ppermute(value, 'fsdp', [(i, i ^ distance) for i in range(n_f)])]
    ppermute x16, starting transfers between devices: 20.5 us -> 6.18 us  [over_rep(): return lax.ppermute(value, 'rep', [(i, i ^ distance) for i in range(n_r)])]
    ppermute x25, waiting for transfers between devices: 33.5 us -> 28.8 us  [over_fsdp(): return lax.ppermute(value, 'fsdp', [(i, i ^ distance) for i in range(n_f)])]
  transfers between devices with their start and end apart: 41 -> 41, of which waited for: 13 -> 14; matrix products, arithmetic and copies ran while one was open for 1% -> 1% of each run, Pallas kernels for 30% -> 31%
where the time goes in v9:
time: 143 us; the launch traced here: 142 us
  starting transfers between devices  58.4 us (41%)
  Pallas kernels  46.4 us (32%)
  waiting for transfers between devices  33.4 us (23%)
  other arithmetic  1.79 us (1%)
  between operations  1.61 us (1%)
    ppermute x25, starting transfers between devices, over_fsdp(): return lax.ppermute(value, 'fsdp', [(i, i ^ distance) for i in range(n_f)])  52.2 us
    ppermute x25, waiting for transfers between devices, over_fsdp(): return lax.ppermute(value, 'fsdp', [(i, i ^ distance) for i in range(n_f)])  28.8 us
    pallas_call x3, Pallas kernels, call_ffn_half(): pl.pallas_call(functools.partial(ffn_half, G, L, n_z, stage, shift), out_...  16.1 us
    ppermute x16, starting transfers between devices, over_rep(): return lax.ppermute(value, 'rep', [(i, i ^ distance) for i in range(n_r)])  6.18 us
    pallas_call x1, Pallas kernels, call_attention_backward(): pl.pallas_call(functools.partial(attention_backward, G, L, n_z), out_shap...  5.94 us
    pallas_call x2, Pallas kernels, call_layer_result(): pl.pallas_call(functools.partial(layer_result, G, L, shift), out_shape=(p...  5.48 us
    pallas_call x1, Pallas kernels, call_token_gradient(): pl.pallas_call(functools.partial(token_gradient, G, L), out_shape=(pltpu....  5.23 us
    pallas_call x1, Pallas kernels, call_keep_close(): pl.pallas_call(functools.partial(keep_close, G, L), out_shape=(sds((S * L...  5.01 us
  transfers between devices with their start and end apart: 41, of which 14 were waited for; matrix products, arithmetic and copies ran while one was open for 1% of the time, Pallas kernels for 31%

profile of v9, /device:TPU:0, one launch (start us, length us, event | category | flops | bytes accessed | tf_op | source)
XLA Modules:
  0.0 141.7 jit_solution(11530122556758695804)
XLA Ops:
  1.7 5.1 %collective-permute-start.2 = (bf16[64,640]{1,0:T(8,128)(2,1)S(1)}, bf16[64,640]{1,0:T(8,128)(2,1)S(1)}, u32[]{:S(2)}, u32[]{:S(2)}) collective-permute-start(bf16[64,640]{1,0:T(8,128)(2,1)S(1)} %prepare_attention.1), channel_id=1, source_target_pairs={{0,6},{1,7},{2,4},{3,5},{4,2},{5,3},{6,0},{7,1},{8,14},{9,15},{10,... | collective-permute-start | bytes 245768 | tf_op jit(solution)/shard_map/ppermute | solution.py:799
  10.1 3.7 %collective-permute-done.1 = bf16[64,640]{1,0:T(8,128)(2,1)S(1)} collective-permute-done((bf16[64,640]{1,0:T(8,128)(2,1)S(1)}, bf16[64,640]{1,0:T(8,128)(2,1)S(1)}, u32[]{:S(2)}, u32[]{:S(2)}) %collective-permute-start.1) | collective-permute-done | bytes 81952 | tf_op jit(solution)/shard_map/ppermute | solution.py:799
  13.8 1.6 %collective-permute-start.3 = (bf16[4,64,640]{2,1,0:T(8,128)(2,1)S(1)}, bf16[4,64,640]{2,1,0:T(8,128)(2,1)S(1)}, u32[]{:S(2)}, u32[]{:S(2)}) collective-permute-start(bf16[4,64,640]{2,1,0:T(8,128)(2,1)S(1)} %pad_maximum_fusion.2.refs_0_), channel_id=1, source_target_pairs={{0,1},{1,0},{2,3},{3,2},{4,5},{5,4},{6,7},{7,6},{8,9},{9,8},{10,11... | collective-permute-start | bytes 983048 | tf_op jit(solution)/shard_map/ppermute | solution.py:799
  15.3 2.7 %collective-permute-start.7 = (bf16[240,256]{1,0:T(8,128)(2,1)S(1)}, bf16[240,256]{1,0:T(8,128)(2,1)S(1)}, u32[]{:S(2)}, u32[]{:S(2)}) collective-permute-start(bf16[240,256]{1,0:T(8,128)(2,1)S(1)} %get-tuple-element.140), channel_id=1, source_target_pairs={{0,6},{1,7},{2,4},{3,5},{4,2},{5,3},{6,0},{7,1},{8,14},{9,15},{10,... | collective-permute-start | bytes 368648 | tf_op jit(solution)/shard_map/ppermute | solution.py:799
  18.0 1.7 %collective-permute-start.5 = (bf16[240,256]{1,0:T(8,128)(2,1)S(1)}, bf16[240,256]{1,0:T(8,128)(2,1)S(1)}, u32[]{:S(2)}, u32[]{:S(2)}) collective-permute-start(bf16[240,256]{1,0:T(8,128)(2,1)S(1)} %get-tuple-element.140), channel_id=1, source_target_pairs={{0,2},{1,3},{2,0},{3,1},{4,6},{5,7},{6,4},{7,5},{8,10},{9,11},{10,... | collective-permute-start | bytes 368648 | tf_op jit(solution)/shard_map/ppermute | solution.py:799
  20.3 5.0 %keep_close.1 = (bf16[3072,512]{1,0:T(8,128)(2,1)S(1)}, bf16[3072,512]{1,0:T(8,128)(2,1)S(1)}, f32[8,128]{1,0:T(8,128)S(1)}) custom-call(s32[4]{0:T(128)} %pad_add_fusion.place_ref, bf16[48,64,512]{2,1,0:T(8,128)(2,1)} %tok_ref.1, bf16[48,64,512]{2,1,0:T(8,128)(2,1)} %ct_ref.1), custom_call_target="tpu_custom_call" | custom-call | flops 6144 | bytes 12582912 | tf_op jit(solution)/shard_map/keep_close/pallas_call | solution.py:203
  25.3 2.8 %collective-permute-done.6 = bf16[240,256]{1,0:T(8,128)(2,1)S(1)} collective-permute-done((bf16[240,256]{1,0:T(8,128)(2,1)S(1)}, bf16[240,256]{1,0:T(8,128)(2,1)S(1)}, u32[]{:S(2)}, u32[]{:S(2)}) %collective-permute-start.6) | collective-permute-done | bytes 122912 | tf_op jit(solution)/shard_map/ppermute | solution.py:799
  28.7 1.9 %collective-permute-start.14 = (bf16[192,256]{1,0:T(8,128)(2,1)S(1)}, bf16[192,256]{1,0:T(8,128)(2,1)S(1)}, u32[]{:S(2)}, u32[]{:S(2)}) collective-permute-start(bf16[192,256]{1,0:T(8,128)(2,1)S(1)} %get-tuple-element.154), channel_id=1, source_target_pairs={{0,6},{1,7},{2,4},{3,5},{4,2},{5,3},{6,0},{7,1},{8,14},{9,15},{10,... | collective-permute-start | bytes 294920 | tf_op jit(solution)/shard_map/ppermute | solution.py:799
  30.5 2.5 %collective-permute-start.12 = (bf16[192,256]{1,0:T(8,128)(2,1)S(1)}, bf16[192,256]{1,0:T(8,128)(2,1)S(1)}, u32[]{:S(2)}, u32[]{:S(2)}) collective-permute-start(bf16[192,256]{1,0:T(8,128)(2,1)S(1)} %get-tuple-element.154), channel_id=1, source_target_pairs={{0,2},{1,3},{2,0},{3,1},{4,6},{5,7},{6,4},{7,5},{8,10},{9,11},{10,... | collective-permute-start | bytes 294920 | tf_op jit(solution)/shard_map/ppermute | solution.py:799
  33.8 4.5 %attention_forward.1 = (bf16[3072,1152]{1,0:T(8,128)(2,1)S(1)}, bf16[48,3,64,128]{3,2,1,0:T(8,128)(2,1)S(1)}, bf16[3072,384]{1,0:T(8,128)(2,1)S(1)}, bf16[512,1152]{1,0:T(8,128)(2,1)S(1)}, f32[8,512]{1,0:T(8,128)S(1)}) custom-call(s32[4]{0:T(128)} %pad_add_fusion.place_ref, bf16[3072,512]{1,0:T(8,128)(2,1)S(1)} %get-tuple-element.145.tok_ref.refs_6_, ...), custom_call_target="tpu_custom_call" | custom-call | flops 14495514624 | bytes 15360000 | tf_op jit(solution)/shard_map/attention_forward/pallas_call | solution.py:316
  39.5 4.8 %collective-permute-done.10.refs_2_ = bf16[3,240,256]{2,1,0:T(8,128)(2,1)S(1)} collective-permute-done((bf16[3,240,256]{2,1,0:T(8,128)(2,1)S(1)}, bf16[3,240,256]{2,1,0:T(8,128)(2,1)S(1)}, u32[]{:S(2)}, u32[]{:S(2)}) %collective-permute-start.10) | collective-permute-done | bytes 368672 | tf_op jit(solution)/shard_map/ppermute | solution.py:799
  46.1 2.3 %collective-permute-start.17 = (bf16[4,192,256]{2,1,0:T(8,128)(2,1)S(1)}, bf16[4,192,256]{2,1,0:T(8,128)(2,1)S(1)}, u32[]{:S(2)}, u32[]{:S(2)}) collective-permute-start(bf16[4,192,256]{2,1,0:T(8,128)(2,1)S(1)} %pad_maximum_fusion.1.refs_0_), channel_id=1, source_target_pairs={{0,1},{1,0},{2,3},{3,2},{4,5},{5,4},{6,7},{7,6},{8,9},{9,8},{10,11... | collective-permute-start | bytes 1179656 | tf_op jit(solution)/shard_map/ppermute | solution.py:799
  48.4 7.3 %ffn_first.1 = (bf16[3072,512]{1,0:T(8,128)(2,1)S(1)}, bf16[3072,512]{1,0:T(8,128)(2,1)S(1)}, bf16[3072,512]{1,0:T(8,128)(2,1)S(1)}, bf16[512,512]{1,0:T(8,128)(...) custom-call(s32[4]{0:T(128)} %pad_add_fusion.place_ref, ...), custom_call_target="tpu_custom_call" | custom-call | flops 14495514624 | bytes 27648000 | tf_op jit(solution)/shard_map/ffn_first/pallas_call | solution.py:540
  55.7 2.3 %collective-permute-done.17.refs_1_ = bf16[4,192,256]{2,1,0:T(8,128)(2,1)S(1)} collective-permute-done((bf16[4,192,256]{2,1,0:T(8,128)(2,1)S(1)}, bf16[4,192,256]{2,1,0:T(8,128)(2,1)S(1)}, u32[]{:S(2)}, u32[]{:S(2)}) %collective-permute-start.17) | collective-permute-done | bytes 393248 | tf_op jit(solution)/shard_map/ppermute | solution.py:799
  59.8 7.6 %ffn_second.1 = (bf16[3072,512]{1,0:T(8,128)(2,1)S(1)}, bf16[3072,384]{1,0:T(8,128)(2,1)S(1)}, bf16[3072,512]{1,0:T(8,128)(2,1)S(1)}, f32[512,1024]{1,0:T(8,128)...) custom-call(s32[4]{0:T(128)} %pad_add_fusion.place_ref, ...), custom_call_target="tpu_custom_call", output_to_operand_aliasing={{0}: (9, {}), {1}: (10, {})} | custom-call | flops 7247757312 | bytes 27648000 | tf_op jit(solution)/shard_map/ffn_second/pallas_call | solution.py:540
  67.5 12.7 %collective-permute-start.21 = (bf16[4,192,256]{2,1,0:T(8,128)(2,1)S(1)}, bf16[4,192,256]{2,1,0:T(8,128)(2,1)S(1)}, u32[]{:S(2)}, u32[]{:S(2)}) collective-permute-start(bf16[4,192,256]{2,1,0:T(8,128)(2,1)S(1)} %fusion.1), channel_id=1, source_target_pairs={{0,1},{1,0},{2,3},{3,2},{4,5},{5,4},{6,7},{7,6},{8,9},{9,8},{10,11... | collective-permute-start | bytes 1179656 | tf_op jit(solution)/shard_map/ppermute | solution.py:799
  81.4 4.6 %collective-permute-done.21 = bf16[4,192,256]{2,1,0:T(8,128)(2,1)S(1)} collective-permute-done((bf16[4,192,256]{2,1,0:T(8,128)(2,1)S(1)}, bf16[4,192,256]{2,1,0:T(8,128)(2,1)S(1)}, u32[]{:S(2)}, u32[]{:S(2)}) %collective-permute-start.21) | collective-permute-done | bytes 393248 | tf_op jit(solution)/shard_map/ppermute | solution.py:799
  86.2 2.5 %collective-permute-start.25 = (bf16[192,256]{1,0:T(8,128)(2,1)S(1)}, bf16[192,256]{1,0:T(8,128)(2,1)S(1)}, u32[]{:S(2)}, u32[]{:S(2)}) collective-permute-start(bf16[192,256]{1,0:T(8,128)(2,1)S(1)} %get-tuple-element.259), channel_id=1, source_target_pairs={{0,6},{1,7},{2,4},{3,5},{4,2},{5,3},{6,0},{7,1},{8,14},{9,15},{10,... | collective-permute-start | bytes 294920 | tf_op jit(solution)/shard_map/ppermute | solution.py:799
  88.7 3.7 %collective-permute-start.24 = (bf16[192,256]{1,0:T(8,128)(2,1)S(1)}, bf16[192,256]{1,0:T(8,128)(2,1)S(1)}, u32[]{:S(2)}, u32[]{:S(2)}) collective-permute-start(bf16[192,256]{1,0:T(8,128)(2,1)S(1)} %get-tuple-element.260), channel_id=1, source_target_pairs={{0,4},{1,5},{2,6},{3,7},{4,0},{5,1},{6,2},{7,3},{8,12},{9,13},{10,... | collective-permute-start | bytes 294920 | tf_op jit(solution)/shard_map/ppermute | solution.py:799
  93.1 3.0 %collective-permute-start.26 = (bf16[4,240,256]{2,1,0:T(8,128)(2,1)S(1)}, bf16[4,240,256]{2,1,0:T(8,128)(2,1)S(1)}, u32[]{:S(2)}, u32[]{:S(2)}) collective-permute-start(bf16[4,240,256]{2,1,0:T(8,128)(2,1)S(1)} %fusion), channel_id=1, source_target_pairs={{0,1},{1,0},{2,3},{3,2},{4,5},{5,4},{6,7},{7,6},{8,9},{9,8},{10,11... | collective-permute-start | bytes 1474568 | tf_op jit(solution)/shard_map/ppermute | solution.py:799
  96.1 5.9 %attention_backward.1 = (bf16[3072,1152]{1,0:T(8,128)(2,1)S(1)}, bf16[2,4,64,640]{3,2,1,0:T(8,128)(2,1)S(1)}, bf16[2,4,64,640]{3,2,1,0:T(8,128)(2,1)S(1)}) custom-call(s32[4]{0:T(128)} %pad_add_fusion.place_ref, bf16[3072,512]{1,0:T(8,128)(2,1)S(1)} %get-tuple-element.145.tok_ref.refs_6_, ...), custom_call_target="tpu_custom_call", output_to_operand_aliasing={{0}: (2, {})} | custom-call | flops 14495514624 | bytes 18432000 | tf_op jit(solution)/shard_map/attention_backward/pallas_call | solution.py:683
  102.0 5.1 %collective-permute-done.26 = bf16[4,240,256]{2,1,0:T(8,128)(2,1)S(1)} collective-permute-done((bf16[4,240,256]{2,1,0:T(8,128)(2,1)S(1)}, bf16[4,240,256]{2,1,0:T(8,128)(2,1)S(1)}, u32[]{:S(2)}, u32[]{:S(2)}) %collective-permute-start.26) | collective-permute-done | bytes 491552 | tf_op jit(solution)/shard_map/ppermute | solution.py:799
  107.3 1.6 %collective-permute-start.31 = (bf16[240,256]{1,0:T(8,128)(2,1)S(1)}, bf16[240,256]{1,0:T(8,128)(2,1)S(1)}, u32[]{:S(2)}, u32[]{:S(2)}) collective-permute-start(bf16[240,256]{1,0:T(8,128)(2,1)S(1)} %get-tuple-element.256), channel_id=1, source_target_pairs={{0,6},{1,7},{2,4},{3,5},{4,2},{5,3},{6,0},{7,1},{8,14},{9,15},{10,... | collective-permute-start | bytes 368648 | tf_op jit(solution)/shard_map/ppermute | solution.py:799
  108.9 2.7 %collective-permute-start.30 = (bf16[240,256]{1,0:T(8,128)(2,1)S(1)}, bf16[240,256]{1,0:T(8,128)(2,1)S(1)}, u32[]{:S(2)}, u32[]{:S(2)}) collective-permute-start(bf16[240,256]{1,0:T(8,128)(2,1)S(1)} %get-tuple-element.257), channel_id=1, source_target_pairs={{0,4},{1,5},{2,6},{3,7},{4,0},{5,1},{6,2},{7,3},{8,12},{9,13},{10,... | collective-permute-start | bytes 368648 | tf_op jit(solution)/shard_map/ppermute | solution.py:799
  112.2 2.1 %collective-permute-start.35 = (bf16[192,256]{1,0:T(8,128)(2,1)S(1)}, bf16[192,256]{1,0:T(8,128)(2,1)S(1)}, u32[]{:S(2)}, u32[]{:S(2)}) collective-permute-start(bf16[192,256]{1,0:T(8,128)(2,1)S(1)} %fusion.10), channel_id=1, source_target_pairs={{0,16},{8,24},{16,0},{24,8},{1,17},{9,25},{17,1},{25,9},{2,18},{10... | collective-permute-start | bytes 294920 | tf_op jit(solution)/shard_map/ppermute | solution.py:802
  115.5 5.2 %token_gradient.1 = (bf16[48,64,512]{2,1,0:T(8,128)(2,1)}, f32[8,512]{1,0:T(8,128)S(1)}) custom-call(s32[4]{0:T(128)} %pad_add_fusion.place_ref, bf16[3072,512]{1,0:T(8,128)(2,1)S(1)} %get-tuple-element.145.tok_ref.refs_6_, bf16[3072,1152]{1,0:T(8,128)(2,1)S(1)} %get-tuple-element.200.dqkv_ref, bf16[3072,512]{1,0:T(8,128)(2,1)S(1)} %get-tuple-element.201.gh_ref, ...), custom_call_target="tpu_custom_call" | custom-call | flops 7247757312 | bytes 15360000 | tf_op jit(solution)/shard_map/token_gradient/pallas_call | solution.py:733
  120.7 2.1 %collective-permute-done.30 = bf16[240,256]{1,0:T(8,128)(2,1)S(1)} collective-permute-done((bf16[240,256]{1,0:T(8,128)(2,1)S(1)}, bf16[240,256]{1,0:T(8,128)(2,1)S(1)}, u32[]{:S(2)}, u32[]{:S(2)}) %collective-permute-start.30) | collective-permute-done | bytes 122912 | tf_op jit(solution)/shard_map/ppermute | solution.py:799
  123.8 1.8 %collective-permute-start.32 = (bf16[64,640]{1,0:T(8,128)(2,1)S(1)}, bf16[64,640]{1,0:T(8,128)(2,1)S(1)}, u32[]{:S(2)}, u32[]{:S(2)}) collective-permute-start(bf16[64,640]{1,0:T(8,128)(2,1)S(1)} %get-tuple-element.219), channel_id=1, source_target_pairs={{0,2},{1,3},{2,0},{3,1},{4,6},{5,7},{6,4},{7,5},{8,10},{9,11},{10,... | collective-permute-start | bytes 245768 | tf_op jit(solution)/shard_map/ppermute | solution.py:799
  125.8 2.4 %collective-permute-start.34 = (bf16[64,640]{1,0:T(8,128)(2,1)S(1)}, bf16[64,640]{1,0:T(8,128)(2,1)S(1)}, u32[]{:S(2)}, u32[]{:S(2)}) collective-permute-start(bf16[64,640]{1,0:T(8,128)(2,1)S(1)} %get-tuple-element.221), channel_id=1, source_target_pairs={{0,6},{1,7},{2,4},{3,5},{4,2},{5,3},{6,0},{7,1},{8,14},{9,15},{10,... | collective-permute-start | bytes 245768 | tf_op jit(solution)/shard_map/ppermute | solution.py:799
  128.7 3.1 %layer_result.2 = (bf16[48,64,512]{2,1,0:T(8,128)(2,1)}, f32[8,512]{1,0:T(8,128)S(1)}) custom-call(s32[4]{0:T(128)} %pad_add_fusion.place_ref, bf16[3072,512]{1,0:T(8,128)(2,1)S(1)} %get-tuple-element.162.refs_4_.refs_0_.hid_ref, bf16[3072,512]{1,0:T(8,128)(2,1)S(1)} %get-tuple-element.163.act_0, bf16[3072,512]{1,0:T(8,128)(2,1)S(1)} %get-tuple-element.186.act_1, ...), custom_call_target="tpu_custom_call" | custom-call | flops 1610612736 | bytes 9216000 | tf_op jit(solution)/shard_map/layer_result/pallas_call | solution.py:584
  134.5 2.4 %layer_result.3 = (bf16[48,64,512]{2,1,0:T(8,128)(2,1)}, f32[8,512]{1,0:T(8,128)S(1)}) custom-call(s32[4]{0:T(128)} %pad_add_fusion.place_ref, bf16[3072,512]{1,0:T(8,128)(2,1)S(1)} %get-tuple-element.162.refs_4_.refs_0_.hid_ref, bf16[3072,512]{1,0:T(8,128)(2,1)S(1)} %get-tuple-element.163.act_0, ...), custom_call_target="tpu_custom_call", output_to_operand_aliasing={{0}: (7, {})} | custom-call | flops 1610612736 | bytes 9216000 | tf_op jit(solution)/shard_map/layer_result/pallas_call | solution.py:584
  139.9 1.8 %finish.1 = (f32[64,384]{1,0:T(8,128)}, f32[64,384]{1,0:T(8,128)}, f32[64,384]{1,0:T(8,128)}, f32[48,512]{1,0:T(8,128)}, f32[64,1024]{1,0:T(8,128)}, /*index=5*/...) custom-call(s32[4]{0:T(128)} %pad_add_fusion.place_ref, ...), custom_call_target="tpu_custom_call" | custom-call | tf_op jit(solution)/shard_map/finish/pallas_call | solution.py:784
  (82 shorter events, 21.7 us)
Async XLA Ops:
  1.7 8.3 %collective-permute-start.2 = (bf16[64,640]{1,0:T(8,128)(2,1)S(1)}, bf16[64,640]{1,0:T(8,128)(2,1)S(1)}, u32[]{:S(2)}, u32[]{:S(2)}) collective-permute-start(bf16[64,640]{1,0:T(8,128)(2,1)S(1)} %prepare_attention.1), channel_id=1, source_target_pairs={{0,6},{1,7},{2,4},{3,5},{4,2},{5,3},{6,0},{7,1},{8,14},{9,15},{10,... | collective-permute-start | bytes 245768 | tf_op jit(solution)/shard_map/ppermute | solution.py:799
  6.8 6.9 %collective-permute-start.1 = (bf16[64,640]{1,0:T(8,128)(2,1)S(1)}, bf16[64,640]{1,0:T(8,128)(2,1)S(1)}, u32[]{:S(2)}, u32[]{:S(2)}) collective-permute-start(bf16[64,640]{1,0:T(8,128)(2,1)S(1)} %prepare_attention.1), channel_id=1, source_target_pairs={{0,4},{1,5},{2,6},{3,7},{4,0},{5,1},{6,2},{7,3},{8,12},{9,13},{10,... | collective-permute-start | bytes 245768 | tf_op jit(solution)/shard_map/ppermute | solution.py:799
  6.8 6.9 %collective-permute-start = (bf16[64,640]{1,0:T(8,128)(2,1)S(1)}, bf16[64,640]{1,0:T(8,128)(2,1)S(1)}, u32[]{:S(2)}, u32[]{:S(2)}) collective-permute-start(bf16[64,640]{1,0:T(8,128)(2,1)S(1)} %prepare_attention.1), channel_id=1, source_target_pairs={{0,2},{1,3},{2,0},{3,1},{4,6},{5,7},{6,4},{7,5},{8,10},{9,11},{10,... | collective-permute-start | bytes 245768 | tf_op jit(solution)/shard_map/ppermute | solution.py:799
  13.8 14.3 %collective-permute-start.3 = (bf16[4,64,640]{2,1,0:T(8,128)(2,1)S(1)}, bf16[4,64,640]{2,1,0:T(8,128)(2,1)S(1)}, u32[]{:S(2)}, u32[]{:S(2)}) collective-permute-start(bf16[4,64,640]{2,1,0:T(8,128)(2,1)S(1)} %pad_maximum_fusion.2.refs_0_), channel_id=1, source_target_pairs={{0,1},{1,0},{2,3},{3,2},{4,5},{5,4},{6,7},{7,6},{8,9},{9,8},{10,11... | collective-permute-start | bytes 983048 | tf_op jit(solution)/shard_map/ppermute | solution.py:799
  15.3 9.9 %collective-permute-start.7 = (bf16[240,256]{1,0:T(8,128)(2,1)S(1)}, bf16[240,256]{1,0:T(8,128)(2,1)S(1)}, u32[]{:S(2)}, u32[]{:S(2)}) collective-permute-start(bf16[240,256]{1,0:T(8,128)(2,1)S(1)} %get-tuple-element.140), channel_id=1, source_target_pairs={{0,6},{1,7},{2,4},{3,5},{4,2},{5,3},{6,0},{7,1},{8,14},{9,15},{10,... | collective-permute-start | bytes 368648 | tf_op jit(solution)/shard_map/ppermute | solution.py:799
  18.0 10.0 %collective-permute-start.6 = (bf16[240,256]{1,0:T(8,128)(2,1)S(1)}, bf16[240,256]{1,0:T(8,128)(2,1)S(1)}, u32[]{:S(2)}, u32[]{:S(2)}) collective-permute-start(bf16[240,256]{1,0:T(8,128)(2,1)S(1)} %get-tuple-element.140), channel_id=1, source_target_pairs={{0,4},{1,5},{2,6},{3,7},{4,0},{5,1},{6,2},{7,3},{8,12},{9,13},{10,... | collective-permute-start | bytes 368648 | tf_op jit(solution)/shard_map/ppermute | solution.py:799
  18.0 10.0 %collective-permute-start.5 = (bf16[240,256]{1,0:T(8,128)(2,1)S(1)}, bf16[240,256]{1,0:T(8,128)(2,1)S(1)}, u32[]{:S(2)}, u32[]{:S(2)}) collective-permute-start(bf16[240,256]{1,0:T(8,128)(2,1)S(1)} %get-tuple-element.140), channel_id=1, source_target_pairs={{0,2},{1,3},{2,0},{3,1},{4,6},{5,7},{6,4},{7,5},{8,10},{9,11},{10,... | collective-permute-start | bytes 368648 | tf_op jit(solution)/shard_map/ppermute | solution.py:799
  19.7 8.4 %collective-permute-start.4 = (bf16[240,256]{1,0:T(8,128)(2,1)S(1)}, bf16[240,256]{1,0:T(8,128)(2,1)S(1)}, u32[]{:S(2)}, u32[]{:S(2)}) collective-permute-start(bf16[240,256]{1,0:T(8,128)(2,1)S(1)} %get-tuple-element.140), channel_id=1, source_target_pairs={{0,1},{1,0},{2,3},{3,2},{4,5},{5,4},{6,7},{7,6},{8,9},{9,8},{10,11... | collective-permute-start | bytes 368648 | tf_op jit(solution)/shard_map/ppermute | solution.py:799
  28.2 5.1 %collective-permute-start.9 = (bf16[4,64,640]{2,1,0:T(8,128)(2,1)S(1)}, bf16[4,64,640]{2,1,0:T(8,128)(2,1)S(1)}, u32[]{:S(2)}, u32[]{:S(2)}) collective-permute-start(bf16[4,64,640]{2,1,0:T(8,128)(2,1)S(1)} %pad_maximum_fusion.2.refs_0_), channel_id=1, source_target_pairs={{0,8},{8,0},{16,24},{24,16},{1,9},{9,1},{17,25},{25,17},{2,10},{10... | collective-permute-start | bytes 983048 | tf_op jit(solution)/shard_map/ppermute | solution.py:802
  28.7 9.6 %collective-permute-start.14 = (bf16[192,256]{1,0:T(8,128)(2,1)S(1)}, bf16[192,256]{1,0:T(8,128)(2,1)S(1)}, u32[]{:S(2)}, u32[]{:S(2)}) collective-permute-start(bf16[192,256]{1,0:T(8,128)(2,1)S(1)} %get-tuple-element.154), channel_id=1, source_target_pairs={{0,6},{1,7},{2,4},{3,5},{4,2},{5,3},{6,0},{7,1},{8,14},{9,15},{10,... | collective-permute-start | bytes 294920 | tf_op jit(solution)/shard_map/ppermute | solution.py:799
  30.5 8.9 %collective-permute-start.13 = (bf16[192,256]{1,0:T(8,128)(2,1)S(1)}, bf16[192,256]{1,0:T(8,128)(2,1)S(1)}, u32[]{:S(2)}, u32[]{:S(2)}) collective-permute-start(bf16[192,256]{1,0:T(8,128)(2,1)S(1)} %get-tuple-element.154), channel_id=1, source_target_pairs={{0,4},{1,5},{2,6},{3,7},{4,0},{5,1},{6,2},{7,3},{8,12},{9,13},{10,... | collective-permute-start | bytes 294920 | tf_op jit(solution)/shard_map/ppermute | solution.py:799
  30.5 8.9 %collective-permute-start.12 = (bf16[192,256]{1,0:T(8,128)(2,1)S(1)}, bf16[192,256]{1,0:T(8,128)(2,1)S(1)}, u32[]{:S(2)}, u32[]{:S(2)}) collective-permute-start(bf16[192,256]{1,0:T(8,128)(2,1)S(1)} %get-tuple-element.154), channel_id=1, source_target_pairs={{0,2},{1,3},{2,0},{3,1},{4,6},{5,7},{6,4},{7,5},{8,10},{9,11},{10,... | collective-permute-start | bytes 294920 | tf_op jit(solution)/shard_map/ppermute | solution.py:799
  33.2 11.1 %collective-permute-start.11 = (bf16[4,240,256]{2,1,0:T(8,128)(2,1)S(1)}, bf16[4,240,256]{2,1,0:T(8,128)(2,1)S(1)}, u32[]{:S(2)}, u32[]{:S(2)}) collective-permute-start(bf16[4,240,256]{2,1,0:T(8,128)(2,1)S(1)} %pad_maximum_fusion.refs_0_), channel_id=1, source_target_pairs={{0,8},{8,0},{16,24},{24,16},{1,9},{9,1},{17,25},{25,17},{2,10},{10... | collective-permute-start | bytes 1474568 | tf_op jit(solution)/shard_map/ppermute | solution.py:802
  33.3 11.0 %collective-permute-start.10 = (bf16[3,240,256]{2,1,0:T(8,128)(2,1)S(1)}, bf16[3,240,256]{2,1,0:T(8,128)(2,1)S(1)}, u32[]{:S(2)}, u32[]{:S(2)}) collective-permute-start(bf16[3,240,256]{2,1,0:T(8,128)(2,1)S(1)} %slice.84), channel_id=1, source_target_pairs={{0,1},{1,0},{2,3},{3,2},{4,5},{5,4},{6,7},{7,6},{8,9},{9,8},{10,11... | collective-permute-start | bytes 1105928 | tf_op jit(solution)/shard_map/ppermute | solution.py:799
  45.9 9.8 %collective-permute-start.18 = (bf16[4,192,256]{2,1,0:T(8,128)(2,1)S(1)}, bf16[4,192,256]{2,1,0:T(8,128)(2,1)S(1)}, u32[]{:S(2)}, u32[]{:S(2)}) collective-permute-start(bf16[4,192,256]{2,1,0:T(8,128)(2,1)S(1)} %pad_maximum_fusion.1.refs_0_), channel_id=1, source_target_pairs={{0,8},{8,0},{16,24},{24,16},{1,9},{9,1},{17,25},{25,17},{2,10},{10... | collective-permute-start | bytes 1179656 | tf_op jit(solution)/shard_map/ppermute | solution.py:802
  46.1 12.0 %collective-permute-start.17 = (bf16[4,192,256]{2,1,0:T(8,128)(2,1)S(1)}, bf16[4,192,256]{2,1,0:T(8,128)(2,1)S(1)}, u32[]{:S(2)}, u32[]{:S(2)}) collective-permute-start(bf16[4,192,256]{2,1,0:T(8,128)(2,1)S(1)} %pad_maximum_fusion.1.refs_0_), channel_id=1, source_target_pairs={{0,1},{1,0},{2,3},{3,2},{4,5},{5,4},{6,7},{7,6},{8,9},{9,8},{10,11... | collective-permute-start | bytes 1179656 | tf_op jit(solution)/shard_map/ppermute | solution.py:799
  58.1 9.4 %collective-permute-start.20 = (bf16[2,4,192,256]{3,2,1,0:T(8,128)(2,1)S(1)}, bf16[2,4,192,256]{3,2,1,0:T(8,128)(2,1)S(1)}, u32[]{:S(2)}, u32[]{:S(2)}) collective-permute-start(bf16[2,4,192,256]{3,2,1,0:T(8,128)(2,1)S(1)} %get-tuple-element.182), channel_id=1, source_target_pairs={{0,8},{8,0},{16,24},{24,16},{1,9},{9,1},{17,25},{25,17},{2,10},{10... | collective-permute-start | bytes 2359304 | tf_op jit(solution)/shard_map/ppermute | solution.py:802
  67.5 18.5 %collective-permute-start.21 = (bf16[4,192,256]{2,1,0:T(8,128)(2,1)S(1)}, bf16[4,192,256]{2,1,0:T(8,128)(2,1)S(1)}, u32[]{:S(2)}, u32[]{:S(2)}) collective-permute-start(bf16[4,192,256]{2,1,0:T(8,128)(2,1)S(1)} %fusion.1), channel_id=1, source_target_pairs={{0,1},{1,0},{2,3},{3,2},{4,5},{5,4},{6,7},{7,6},{8,9},{9,8},{10,11... | collective-permute-start | bytes 1179656 | tf_op jit(solution)/shard_map/ppermute | solution.py:799
  86.0 6.9 %collective-permute-start.22 = (bf16[2,4,240,256]{3,2,1,0:T(8,128)(2,1)S(1)}, bf16[2,4,240,256]{3,2,1,0:T(8,128)(2,1)S(1)}, u32[]{:S(2)}, u32[]{:S(2)}) collective-permute-start(bf16[2,4,240,256]{3,2,1,0:T(8,128)(2,1)S(1)} %get-tuple-element.198), channel_id=1, source_target_pairs={{0,8},{8,0},{16,24},{24,16},{1,9},{9,1},{17,25},{25,17},{2,10},{10... | collective-permute-start | bytes 2949128 | tf_op jit(solution)/shard_map/ppermute | solution.py:802
  86.2 15.8 %collective-permute-start.25 = (bf16[192,256]{1,0:T(8,128)(2,1)S(1)}, bf16[192,256]{1,0:T(8,128)(2,1)S(1)}, u32[]{:S(2)}, u32[]{:S(2)}) collective-permute-start(bf16[192,256]{1,0:T(8,128)(2,1)S(1)} %get-tuple-element.259), channel_id=1, source_target_pairs={{0,6},{1,7},{2,4},{3,5},{4,2},{5,3},{6,0},{7,1},{8,14},{9,15},{10,... | collective-permute-start | bytes 294920 | tf_op jit(solution)/shard_map/ppermute | solution.py:799
  88.7 13.3 %collective-permute-start.24 = (bf16[192,256]{1,0:T(8,128)(2,1)S(1)}, bf16[192,256]{1,0:T(8,128)(2,1)S(1)}, u32[]{:S(2)}, u32[]{:S(2)}) collective-permute-start(bf16[192,256]{1,0:T(8,128)(2,1)S(1)} %get-tuple-element.260), channel_id=1, source_target_pairs={{0,4},{1,5},{2,6},{3,7},{4,0},{5,1},{6,2},{7,3},{8,12},{9,13},{10,... | collective-permute-start | bytes 294920 | tf_op jit(solution)/shard_map/ppermute | solution.py:799
  92.5 9.6 %collective-permute-start.23 = (bf16[192,256]{1,0:T(8,128)(2,1)S(1)}, bf16[192,256]{1,0:T(8,128)(2,1)S(1)}, u32[]{:S(2)}, u32[]{:S(2)}) collective-permute-start(bf16[192,256]{1,0:T(8,128)(2,1)S(1)} %get-tuple-element.261), channel_id=1, source_target_pairs={{0,2},{1,3},{2,0},{3,1},{4,6},{5,7},{6,4},{7,5},{8,10},{9,11},{10,... | collective-permute-start | bytes 294920 | tf_op jit(solution)/shard_map/ppermute | solution.py:799
  93.1 14.0 %collective-permute-start.26 = (bf16[4,240,256]{2,1,0:T(8,128)(2,1)S(1)}, bf16[4,240,256]{2,1,0:T(8,128)(2,1)S(1)}, u32[]{:S(2)}, u32[]{:S(2)}) collective-permute-start(bf16[4,240,256]{2,1,0:T(8,128)(2,1)S(1)} %fusion), channel_id=1, source_target_pairs={{0,1},{1,0},{2,3},{3,2},{4,5},{5,4},{6,7},{7,6},{8,9},{9,8},{10,11... | collective-permute-start | bytes 1474568 | tf_op jit(solution)/shard_map/ppermute | solution.py:799
  107.3 13.4 %collective-permute-start.31 = (bf16[240,256]{1,0:T(8,128)(2,1)S(1)}, bf16[240,256]{1,0:T(8,128)(2,1)S(1)}, u32[]{:S(2)}, u32[]{:S(2)}) collective-permute-start(bf16[240,256]{1,0:T(8,128)(2,1)S(1)} %get-tuple-element.256), channel_id=1, source_target_pairs={{0,6},{1,7},{2,4},{3,5},{4,2},{5,3},{6,0},{7,1},{8,14},{9,15},{10,... | collective-permute-start | bytes 368648 | tf_op jit(solution)/shard_map/ppermute | solution.py:799
  108.9 13.9 %collective-permute-start.30 = (bf16[240,256]{1,0:T(8,128)(2,1)S(1)}, bf16[240,256]{1,0:T(8,128)(2,1)S(1)}, u32[]{:S(2)}, u32[]{:S(2)}) collective-permute-start(bf16[240,256]{1,0:T(8,128)(2,1)S(1)} %get-tuple-element.257), channel_id=1, source_target_pairs={{0,4},{1,5},{2,6},{3,7},{4,0},{5,1},{6,2},{7,3},{8,12},{9,13},{10,... | collective-permute-start | bytes 368648 | tf_op jit(solution)/shard_map/ppermute | solution.py:799
  111.6 11.2 %collective-permute-start.29 = (bf16[240,256]{1,0:T(8,128)(2,1)S(1)}, bf16[240,256]{1,0:T(8,128)(2,1)S(1)}, u32[]{:S(2)}, u32[]{:S(2)}) collective-permute-start(bf16[240,256]{1,0:T(8,128)(2,1)S(1)} %get-tuple-element.258), channel_id=1, source_target_pairs={{0,2},{1,3},{2,0},{3,1},{4,6},{5,7},{6,4},{7,5},{8,10},{9,11},{10,... | collective-permute-start | bytes 368648 | tf_op jit(solution)/shard_map/ppermute | solution.py:799
  112.2 24.6 %collective-permute-start.35 = (bf16[192,256]{1,0:T(8,128)(2,1)S(1)}, bf16[192,256]{1,0:T(8,128)(2,1)S(1)}, u32[]{:S(2)}, u32[]{:S(2)}) collective-permute-start(bf16[192,256]{1,0:T(8,128)(2,1)S(1)} %fusion.10), channel_id=1, source_target_pairs={{0,16},{8,24},{16,0},{24,8},{1,17},{9,25},{17,1},{25,9},{2,18},{10... | collective-permute-start | bytes 294920 | tf_op jit(solution)/shard_map/ppermute | solution.py:802
  114.3 9.3 %collective-permute-start.28 = (bf16[4,64,640]{2,1,0:T(8,128)(2,1)S(1)}, bf16[4,64,640]{2,1,0:T(8,128)(2,1)S(1)}, u32[]{:S(2)}, u32[]{:S(2)}) collective-permute-start(bf16[4,64,640]{2,1,0:T(8,128)(2,1)S(1)} %fusion.2), channel_id=1, source_target_pairs={{0,1},{1,0},{2,3},{3,2},{4,5},{5,4},{6,7},{7,6},{8,9},{9,8},{10,11... | collective-permute-start | bytes 983048 | tf_op jit(solution)/shard_map/ppermute | solution.py:799
  123.8 8.1 %collective-permute-start.32 = (bf16[64,640]{1,0:T(8,128)(2,1)S(1)}, bf16[64,640]{1,0:T(8,128)(2,1)S(1)}, u32[]{:S(2)}, u32[]{:S(2)}) collective-permute-start(bf16[64,640]{1,0:T(8,128)(2,1)S(1)} %get-tuple-element.219), channel_id=1, source_target_pairs={{0,2},{1,3},{2,0},{3,1},{4,6},{5,7},{6,4},{7,5},{8,10},{9,11},{10,... | collective-permute-start | bytes 245768 | tf_op jit(solution)/shard_map/ppermute | solution.py:799
  125.6 7.8 %collective-permute-start.33 = (bf16[64,640]{1,0:T(8,128)(2,1)S(1)}, bf16[64,640]{1,0:T(8,128)(2,1)S(1)}, u32[]{:S(2)}, u32[]{:S(2)}) collective-permute-start(bf16[64,640]{1,0:T(8,128)(2,1)S(1)} %get-tuple-element.220), channel_id=1, source_target_pairs={{0,4},{1,5},{2,6},{3,7},{4,0},{5,1},{6,2},{7,3},{8,12},{9,13},{10,... | collective-permute-start | bytes 245768 | tf_op jit(solution)/shard_map/ppermute | solution.py:799
  125.8 7.5 %collective-permute-start.34 = (bf16[64,640]{1,0:T(8,128)(2,1)S(1)}, bf16[64,640]{1,0:T(8,128)(2,1)S(1)}, u32[]{:S(2)}, u32[]{:S(2)}) collective-permute-start(bf16[64,640]{1,0:T(8,128)(2,1)S(1)} %get-tuple-element.221), channel_id=1, source_target_pairs={{0,6},{1,7},{2,4},{3,5},{4,2},{5,3},{6,0},{7,1},{8,14},{9,15},{10,... | collective-permute-start | bytes 245768 | tf_op jit(solution)/shard_map/ppermute | solution.py:799
  128.3 8.6 %collective-permute-start.36 = (bf16[240,256]{1,0:T(8,128)(2,1)S(1)}, bf16[240,256]{1,0:T(8,128)(2,1)S(1)}, u32[]{:S(2)}, u32[]{:S(2)}) collective-permute-start(bf16[240,256]{1,0:T(8,128)(2,1)S(1)} %fusion.6), channel_id=1, source_target_pairs={{0,16},{8,24},{16,0},{24,8},{1,17},{9,25},{17,1},{25,9},{2,18},{10... | collective-permute-start | bytes 368648 | tf_op jit(solution)/shard_map/ppermute | solution.py:802
  (9 other events, 27.3 us)
